TPU v7x, 32 devices: a whole 2x2x4 slice. The times are simulated.
32 devices in a mesh: ulysses: 4 (over y, x), blk: 8 (over z, core).
Axes of the slice: x: 2, y: 2, z: 4, core: 2. Of those that a mesh axis runs over, the one named last changes fastest.
Arguments:
- tokens: int32 [4, 2048], P(None, 'blk'), may hold values from 0 to 151935
- lengths: int32 [4], replicated, may hold values from 1024 to 2048, as said below
- picked: int32 [4, 128], P(None, 'blk'), may hold values from 0 to 2047, as said below
- targets: int32 [4, 128], P(None, 'blk'), may hold values from 0 to 151935
- advantages: float32 [4, 128], P(None, 'blk'), may hold values from -6 to 6
- step_count: int32 [1], replicated, may hold values from 1 to 20
- embedding: float32 [151936, 1024], P(('ulysses', 'blk')), may hold values from -0.54 to 0.54
- first_embedding: float32 [151936, 1024], P(('ulysses', 'blk')), may hold values from -1.0161426e-06 to 1.0161426e-06
- second_embedding: float32 [151936, 1024], P(('ulysses', 'blk')), may hold values from 8.697458e-15 to 8.6974574e-13
- inflow: float32 [1024, 4096], P(('ulysses', 'blk')), may hold values from -0.1875 to 0.1875
- inflow_first_moment: float32 [1024, 4096], P(('ulysses', 'blk')), may hold values from -3.010227e-06 to 3.010227e-06
- inflow_second_moment: float32 [1024, 4096], P(('ulysses', 'blk')), may hold values from 7.588386e-14 to 7.588386e-12
- outflow: float32 [2048, 1024], P(('ulysses', 'blk')), may hold values from -3 to 3
- first_outflow: float32 [2048, 1024], P(('ulysses', 'blk')), may hold values from -1.9711639e-07 to 1.9711639e-07
- second_outflow: float32 [2048, 1024], P(('ulysses', 'blk')), may hold values from 3.268843e-16 to 3.268843e-14
- expand: float32 [1024, 6144], P(('ulysses', 'blk')), may hold values from -0.1875 to 0.1875
- first_expand: float32 [1024, 6144], P(('ulysses', 'blk')), may hold values from -5.0883534e-07 to 5.0883534e-07
- second_expand: float32 [1024, 6144], P(('ulysses', 'blk')), may hold values from 2.177283e-15 to 2.177283e-13
- contract: float32 [3072, 1024], P(('ulysses', 'blk')), may hold values from -0.109375 to 0.109375
- first_contract: float32 [3072, 1024], P(('ulysses', 'blk')), may hold values from -5.0883534e-07 to 5.0883534e-07
- second_contract: float32 [3072, 1024], P(('ulysses', 'blk')), may hold values from 2.177283e-15 to 2.177283e-13
- scales: float32 [3328], P(('ulysses', 'blk')), may hold values from 0.5 to 1.5
- first_scales: float32 [3328], P(('ulysses', 'blk')), may hold values from -4.461859e-06 to 4.461859e-06
- second_scales: float32 [3328], P(('ulysses', 'blk')), may hold values from 1.6752821e-13 to 1.6752821e-11
Outputs:
- policy_loss: float32 [], replicated
- gradient_norm: float32 [], replicated
- change_embedding: float32 [151936, 1024], P(('ulysses', 'blk'))
- mean_embedding: float32 [151936, 1024], P(('ulysses', 'blk'))
- square_embedding: float32 [151936, 1024], P(('ulysses', 'blk'))
- change_inflow: float32 [1024, 4096], P(('ulysses', 'blk'))
- mean_inflow: float32 [1024, 4096], P(('ulysses', 'blk'))
- square_inflow: float32 [1024, 4096], P(('ulysses', 'blk'))
- change_outflow: float32 [2048, 1024], P(('ulysses', 'blk'))
- mean_outflow: float32 [2048, 1024], P(('ulysses', 'blk'))
- square_outflow: float32 [2048, 1024], P(('ulysses', 'blk'))
- change_expand: float32 [1024, 6144], P(('ulysses', 'blk'))
- mean_expand: float32 [1024, 6144], P(('ulysses', 'blk'))
- square_expand: float32 [1024, 6144], P(('ulysses', 'blk'))
- change_contract: float32 [3072, 1024], P(('ulysses', 'blk'))
- mean_contract: float32 [3072, 1024], P(('ulysses', 'blk'))
- square_contract: float32 [3072, 1024], P(('ulysses', 'blk'))
- change_scales: float32 [3328], P(('ulysses', 'blk'))
- mean_scales: float32 [3328], P(('ulysses', 'blk'))
- square_scales: float32 [3328], P(('ulysses', 'blk'))
Inputs may be any that keep to these rules, and one draw needn't show every extreme that they name: lengths[s] counts the valid leading positions of slot s; later positions are padding. Some slot has exactly 2048. `picked`: the entries in columns k * 16 to (k + 1) * 16 - 1 are positions k * 256 to (k + 1) * 256 - 1 of the slot; a position may repeat.
All inputs are finite; a program needn't handle non-finite values.
Results may differ from a plain program's by a relative error of at most 0.03.
The roundings to bfloat16 on the way count: a program that leaves them out, or rounds other values in their place, can miss the bound.
Values may be sent and summed in bfloat16 or wider, within the bound.
A program may use at most 832 MiB of HBM per device.

v0:
```python
import jax
import jax.numpy as jnp
from jax import lax
from jax.sharding import PartitionSpec as P

MODEL_WIDTH = 1024
QUERY_HEADS = 16
KEY_VALUE_HEADS = 8
HEAD_WIDTH = 128
FF = 3072


norm_eps = 1e-06
rope_base = 1000000.0
clip_limit = 0.01
beta_first = 0.9
beta_second = 0.95
adam_eps = 1e-08
learning_rates = (0.01, 0.003, 0.07, 0.003, 0.002, 0.01)
weight_decays = (0.1, 0.1, 0.1, 0.1, 0.1, 0.0)


def merged(array, axis, combine):
    everything = jax.tree.map(lambda part: lax.all_gather(part, axis), array)
    first = jax.tree.map(lambda part: part[0], everything)

    def turn(k, so_far):
        return combine(so_far, jax.tree.map(lambda part: part[k], everything))

    return lax.fori_loop(1, lax.axis_size(axis), turn, first)


def inverse_root(values):
    return lax.rsqrt(jnp.mean(values * values, axis=-1, keepdims=True) + norm_eps)


def norm_back(inputs, gain_vec, upstream):
    root_scale = inverse_root(inputs)
    unit_rows = inputs * root_scale
    weighted = upstream * gain_vec
    grad_inputs = root_scale * (
        weighted - unit_rows * jnp.mean(weighted * unit_rows, axis=-1, keepdims=True)
    )
    grad_gain = jnp.sum((upstream * unit_rows).reshape(-1, gain_vec.shape[-1]), axis=0)
    return (grad_inputs, grad_gain)


def rope_angles(positions, head_width):
    half_width = head_width // 2
    frequency = rope_base ** (
        -(jnp.arange(half_width, dtype=jnp.int32).astype(jnp.float32) * 2.0 / head_width)
    )
    angles = positions.astype(jnp.float32)[:, None] * frequency[None, :]
    return (jnp.cos(angles), jnp.sin(angles))


def rotate(values, cosine_table, sine_table, sign_value):
    half_width = values.shape[-1] // 2
    front_half = values[..., :half_width]
    back_half = values[..., half_width:]
    cosine_part = cosine_table[:, None, :]
    sine_part = sine_table[:, None, :] * sign_value
    return jnp.concatenate(
        [
            front_half * cosine_part - back_half * sine_part,
            back_half * cosine_part + front_half * sine_part,
        ],
        axis=-1,
    )


def score_block(query_part, key_portion, query_pos, key_pos, length, score_scale):
    raw_scores = (
        jnp.einsum("kqd,kjd->kqj", query_part, key_portion, preferred_element_type=jnp.float32)
        * score_scale
    )
    allowed = (key_pos[None, :] <= query_pos[:, None]) & (key_pos[None, :] < length)
    return (raw_scores, allowed[None, :, :])


def combine_stats(earlier, later):
    row_max = jnp.maximum(earlier[0], later[0])
    row_sum = earlier[1] * jnp.exp(earlier[0] - row_max) + later[1] * jnp.exp(later[0] - row_max)
    return (row_max, row_sum, earlier[2] + later[2])


def outer_sum(left, right):
    return lax.dot_general(
        left, right, (((0,), (0,)), ((), ())), preferred_element_type=jnp.float32
    )


def times_back(left, right):
    return lax.dot_general(
        left, right, (((1,), (1,)), ((), ())), preferred_element_type=jnp.float32
    )


def adam_update(weight_now, first_now, second_now, gradient, rate_value, decay_value, step_float):
    new_first = beta_first * first_now + (1.0 - beta_first) * gradient
    new_second = beta_second * second_now + (1.0 - beta_second) * gradient * gradient
    first_hat = new_first / (1.0 - beta_first**step_float)
    second_hat = new_second / (1.0 - beta_second**step_float)
    change = -rate_value * (
        first_hat / (jnp.sqrt(second_hat) + adam_eps) + decay_value * weight_now
    )
    return (change, new_first, new_second)


def local(
    tokens,
    lengths,
    picked,
    targets,
    advantages,
    step_count,
    embedding,
    first_embedding,
    second_embedding,
    inflow,
    inflow_first_moment,
    inflow_second_moment,
    outflow,
    first_outflow,
    second_outflow,
    expand,
    first_expand,
    second_expand,
    contract,
    first_contract,
    second_contract,
    scales,
    first_scales,
    second_scales,
):
    sequence_split_count = lax.axis_size("ulysses")
    ulysses_rank = lax.axis_index("ulysses")
    block_rank = lax.axis_index("blk")
    slot_count, block_len = tokens.shape
    own_slots = slot_count // sequence_split_count
    row_share = embedding.shape[0]
    query_group_width = QUERY_HEADS // KEY_VALUE_HEADS
    local_key_value = KEY_VALUE_HEADS // sequence_split_count
    local_q = QUERY_HEADS // sequence_split_count
    query_rows = query_group_width * block_len
    owned_row_span = own_slots * block_len
    score_scale = HEAD_WIDTH ** (-0.5)
    bf16 = jnp.bfloat16
    single_float = jnp.float32
    weight_in, weight_out, weight_expand, weight_contract, gains_low = (
        lax.all_gather(inflow.astype(bf16), ("ulysses", "blk"), axis=0, tiled=True),
        lax.all_gather(outflow.astype(bf16), ("ulysses", "blk"), axis=0, tiled=True),
        lax.all_gather(expand.astype(bf16), ("ulysses", "blk"), axis=0, tiled=True),
        lax.all_gather(contract.astype(bf16), ("ulysses", "blk"), axis=0, tiled=True),
        lax.all_gather(scales.astype(bf16), ("ulysses", "blk"), axis=0, tiled=True),
    )
    gains_wide = gains_low.astype(single_float)
    gain_attn = gains_wide[:MODEL_WIDTH]
    gain_mlp = gains_wide[MODEL_WIDTH : 2 * MODEL_WIDTH]
    gain_final = gains_wide[2 * MODEL_WIDTH : 3 * MODEL_WIDTH]
    gain_query = gains_wide[3 * MODEL_WIDTH : 3 * MODEL_WIDTH + HEAD_WIDTH]
    gain_key = gains_wide[3 * MODEL_WIDTH + HEAD_WIDTH :]
    table_whole = lax.all_gather(embedding.astype(bf16), "blk", axis=0, tiled=True)
    vocab_share = table_whole.shape[0]
    vocab_base = ulysses_rank * vocab_share
    local_ids = tokens - vocab_base
    owned = (local_ids >= 0) & (local_ids < vocab_share)
    safe_ids = jnp.clip(local_ids, 0, vocab_share - 1)
    looked = jnp.where(
        owned[..., None], jnp.take(table_whole, safe_ids, axis=0), jnp.zeros((), bf16)
    ).astype(single_float)
    embedded = (
        lax.psum_scatter(looked.astype(jnp.bfloat16), "ulysses", scatter_dimension=0, tiled=True)
        .astype(jnp.float32)
        .reshape(owned_row_span, MODEL_WIDTH)
    )
    normed_in = (embedded * inverse_root(embedded) * gain_attn).astype(bf16)
    blended_rows = jnp.dot(normed_in, weight_in, preferred_element_type=single_float)
    queries = blended_rows[:, : QUERY_HEADS * HEAD_WIDTH].reshape(
        owned_row_span, QUERY_HEADS, HEAD_WIDTH
    )
    key_portion = blended_rows[
        :, QUERY_HEADS * HEAD_WIDTH : (QUERY_HEADS + KEY_VALUE_HEADS) * HEAD_WIDTH
    ].reshape(owned_row_span, KEY_VALUE_HEADS, HEAD_WIDTH)
    value_portion = blended_rows[:, (QUERY_HEADS + KEY_VALUE_HEADS) * HEAD_WIDTH :].reshape(
        owned_row_span, KEY_VALUE_HEADS, HEAD_WIDTH
    )
    positions = block_rank * block_len + jnp.arange(owned_row_span, dtype=jnp.int32) % block_len
    cosine_table, sine_table = rope_angles(positions, HEAD_WIDTH)
    query_unit = queries * inverse_root(queries)
    key_unit = key_portion * inverse_root(key_portion)
    query_rot = rotate(query_unit * gain_query, cosine_table, sine_table, 1.0).astype(bf16)
    rotated_key = rotate(key_unit * gain_key, cosine_table, sine_table, 1.0).astype(bf16)
    value_reduced = value_portion.astype(bf16)

    def rows_into_heads(array, heads):
        return array.reshape(own_slots, block_len, heads, HEAD_WIDTH).transpose(0, 2, 1, 3)

    def heads_into_rows(array):
        return array.transpose(0, 2, 1, 3).reshape(owned_row_span, array.shape[1], HEAD_WIDTH)

    query_heads, heads_of_keys, heads_of_values = (
        lax.all_to_all(
            rows_into_heads(query_rot, QUERY_HEADS),
            "ulysses",
            split_axis=1,
            concat_axis=0,
            tiled=True,
        ),
        lax.all_to_all(
            rows_into_heads(rotated_key, KEY_VALUE_HEADS),
            "ulysses",
            split_axis=1,
            concat_axis=0,
            tiled=True,
        ),
        lax.all_to_all(
            rows_into_heads(value_reduced, KEY_VALUE_HEADS),
            "ulysses",
            split_axis=1,
            concat_axis=0,
            tiled=True,
        ),
    )
    key_all, value_all = (
        lax.all_gather(heads_of_keys, "blk", axis=2, tiled=True),
        lax.all_gather(heads_of_values, "blk", axis=2, tiled=True),
    )
    query_groups = query_heads.reshape(slot_count, local_key_value, query_rows, HEAD_WIDTH)
    query_pos = block_rank * block_len + jnp.arange(query_rows, dtype=jnp.int32) % block_len
    key_pos = jnp.arange(key_all.shape[2], dtype=jnp.int32)

    def attend(inputs):
        query_part, key_block, value_block, length = inputs
        scores, allowed = score_block(
            query_part, key_block, query_pos, key_pos, length, score_scale
        )
        masked = jnp.where(allowed, scores, -1e30)
        row_max = jnp.max(masked, axis=-1, keepdims=True)
        weights = jnp.where(allowed, jnp.exp(masked - row_max), 0.0)
        row_sum = jnp.sum(weights, axis=-1, keepdims=True)
        attn_probs = weights / row_sum
        result = jnp.einsum(
            "kqj,kjd->kqd",
            attn_probs.astype(bf16),
            value_block,
            preferred_element_type=single_float,
        )
        return (result.astype(bf16), (row_max + jnp.log(row_sum))[..., 0])

    attended, log_total = lax.map(attend, (query_groups, key_all, value_all, lengths))
    out_rows = lax.all_to_all(
        attended.reshape(slot_count, local_q, block_len, HEAD_WIDTH),
        "ulysses",
        split_axis=0,
        concat_axis=1,
        tiled=True,
    )
    out_flat = heads_into_rows(out_rows).reshape(owned_row_span, QUERY_HEADS * HEAD_WIDTH)
    after_attn = embedded + jnp.dot(out_flat, weight_out, preferred_element_type=single_float)
    normed_mlp = (after_attn * inverse_root(after_attn) * gain_mlp).astype(bf16)
    gate_up = jnp.dot(normed_mlp, weight_expand, preferred_element_type=single_float)
    gate_part = gate_up[:, :FF]
    up_part = gate_up[:, FF:]
    activated = (jax.nn.silu(gate_part) * up_part).astype(bf16)
    after_mlp = after_attn + jnp.dot(
        activated, weight_contract, preferred_element_type=single_float
    )
    final_normed = after_mlp * inverse_root(after_mlp) * gain_final
    own_picked = lax.dynamic_slice_in_dim(picked, ulysses_rank * own_slots, own_slots, 0)
    pick_rows = (
        own_picked
        - block_rank * block_len
        + jnp.arange(own_slots, dtype=jnp.int32)[:, None] * block_len
    ).reshape(-1)
    chosen = jnp.take(final_normed, pick_rows, axis=0).astype(bf16)
    chosen_all = lax.all_gather(chosen, "ulysses", axis=0, tiled=True)
    logits = times_back(chosen_all, table_whole)
    target_local = targets.reshape(-1) - vocab_base
    is_target = jnp.arange(vocab_share, dtype=jnp.int32)[None, :] == target_local[:, None]
    local_max = jnp.max(logits, axis=1)
    local_sum = jnp.sum(jnp.exp(logits - local_max[:, None]), axis=1)
    local_target = jnp.sum(jnp.where(is_target, logits, 0.0), axis=1)
    full_max, full_sum, target_logit = merged(
        (local_max, local_sum, local_target), "ulysses", combine_stats
    )
    log_norm = full_max + jnp.log(full_sum)
    log_prob = target_logit - log_norm
    is_valid = (picked < lengths[:, None]).reshape(-1)
    row_weight = jnp.where(is_valid, advantages.reshape(-1), 0.0)
    grad_logits = (
        row_weight[:, None] * (jnp.exp(logits - log_norm[:, None]) - is_target.astype(single_float))
    ).astype(bf16)
    own_valid = lax.dynamic_slice_in_dim(
        is_valid.reshape(slot_count, -1), ulysses_rank * own_slots, own_slots, 0
    )
    own_terms = lax.dynamic_slice_in_dim(
        (row_weight * log_prob).reshape(slot_count, -1), ulysses_rank * own_slots, own_slots, 0
    )
    count_local = jnp.sum(own_valid.astype(single_float))
    loss_local = -jnp.sum(own_terms)
    grad_chosen = lax.psum_scatter(
        jnp.dot(grad_logits, table_whole, preferred_element_type=single_float).astype(jnp.bfloat16),
        "ulysses",
        scatter_dimension=0,
        tiled=True,
    ).astype(jnp.float32)
    grad_final = (
        jnp.zeros((owned_row_span, MODEL_WIDTH), single_float).at[pick_rows].add(grad_chosen)
    )
    grad_after_mlp, grad_gain_final = norm_back(after_mlp, gain_final, grad_final)
    grad_branch = grad_after_mlp.astype(bf16)
    grad_contract = outer_sum(activated, grad_branch)
    grad_act = times_back(grad_branch, weight_contract)
    sigmoid_gate = jax.nn.sigmoid(gate_part)
    grad_gate = grad_act * up_part * sigmoid_gate * (1.0 + gate_part * (1.0 - sigmoid_gate))
    grad_up = grad_act * gate_part * sigmoid_gate
    grad_gate_up = jnp.concatenate([grad_gate, grad_up], axis=1).astype(bf16)
    grad_expand = outer_sum(normed_mlp, grad_gate_up)
    grad_mid_part, grad_gain_mlp = norm_back(
        after_attn, gain_mlp, times_back(grad_gate_up, weight_expand)
    )
    grad_after_attn = grad_after_mlp + grad_mid_part
    grad_attn_branch = grad_after_attn.astype(bf16)
    grad_outflow = outer_sum(out_flat, grad_attn_branch)
    grad_attended = (
        times_back(grad_attn_branch, weight_out)
        .astype(bf16)
        .reshape(owned_row_span, QUERY_HEADS, HEAD_WIDTH)
    )
    grad_heads_in = lax.all_to_all(
        rows_into_heads(grad_attended, QUERY_HEADS),
        "ulysses",
        split_axis=1,
        concat_axis=0,
        tiled=True,
    )
    grad_groups = grad_heads_in.reshape(slot_count, local_key_value, query_rows, HEAD_WIDTH)
    keys_back, values_back = (key_all, value_all)

    def query_side(inputs):
        query_part, key_block, value_block, grad_part, log_part, length = inputs
        scores, allowed = score_block(
            query_part, key_block, query_pos, key_pos, length, score_scale
        )
        attn_probs = jnp.where(allowed, jnp.exp(scores - log_part[..., None]), 0.0)
        grad_probs = jnp.einsum(
            "kqd,kjd->kqj", grad_part, value_block, preferred_element_type=single_float
        )
        row_delta = jnp.sum(attn_probs * grad_probs, axis=-1)
        grad_scores = (attn_probs * (grad_probs - row_delta[..., None]) * score_scale).astype(bf16)
        grad_query = jnp.einsum(
            "kqj,kjd->kqd", grad_scores, key_block, preferred_element_type=single_float
        )
        return (grad_query.astype(bf16), row_delta)

    grad_queries, row_deltas = lax.map(
        query_side, (query_groups, keys_back, values_back, grad_groups, log_total, lengths)
    )
    slice_pos = jnp.arange(block_len * lax.axis_size("blk"), dtype=jnp.int32)

    def per_slot(inputs):
        query_part, key_block, value_block, grad_part, log_part, delta_part, length = inputs
        scores, allowed = score_block(
            query_part, key_block, query_pos, slice_pos, length, score_scale
        )
        attn_probs = jnp.where(allowed, jnp.exp(scores - log_part[..., None]), 0.0)
        grad_probs = jnp.einsum(
            "kqd,kjd->kqj", grad_part, value_block, preferred_element_type=single_float
        )
        grad_scores = (attn_probs * (grad_probs - delta_part[..., None]) * score_scale).astype(bf16)
        grad_key = jnp.einsum(
            "kqj,kqd->kjd", grad_scores, query_part, preferred_element_type=single_float
        )
        grad_value = jnp.einsum(
            "kqj,kqd->kjd", attn_probs.astype(bf16), grad_part, preferred_element_type=single_float
        )
        return jnp.concatenate([grad_key, grad_value], axis=-1)

    stacked = lax.map(
        per_slot,
        (query_groups, keys_back, values_back, grad_groups, log_total, row_deltas, lengths),
    )
    key_sums = lax.psum_scatter(
        jnp.transpose(stacked, (2, 0, 1, 3)).astype(jnp.bfloat16),
        "blk",
        scatter_dimension=0,
        tiled=True,
    ).astype(jnp.float32)
    key_sums = jnp.transpose(key_sums, (1, 2, 0, 3)).astype(bf16)
    back_query, back_key, value_backward = (
        lax.all_to_all(
            grad_queries.reshape(slot_count, local_q, block_len, HEAD_WIDTH),
            "ulysses",
            split_axis=0,
            concat_axis=1,
            tiled=True,
        ),
        lax.all_to_all(
            key_sums[..., :HEAD_WIDTH], "ulysses", split_axis=0, concat_axis=1, tiled=True
        ),
        lax.all_to_all(
            key_sums[..., HEAD_WIDTH:], "ulysses", split_axis=0, concat_axis=1, tiled=True
        ),
    )
    grad_query_unit = rotate(
        heads_into_rows(back_query).astype(single_float), cosine_table, sine_table, -1.0
    )
    grad_key_unit = rotate(
        heads_into_rows(back_key).astype(single_float), cosine_table, sine_table, -1.0
    )
    grad_query_raw, grad_gain_query = norm_back(queries, gain_query, grad_query_unit)
    unrotated_key_gradient, grad_gain_key = norm_back(key_portion, gain_key, grad_key_unit)
    grad_mixed = jnp.concatenate(
        [
            grad_query_raw.reshape(owned_row_span, QUERY_HEADS * HEAD_WIDTH),
            unrotated_key_gradient.reshape(owned_row_span, KEY_VALUE_HEADS * HEAD_WIDTH),
            heads_into_rows(value_backward)
            .reshape(owned_row_span, KEY_VALUE_HEADS * HEAD_WIDTH)
            .astype(single_float),
        ],
        axis=1,
    ).astype(bf16)
    grad_inflow = outer_sum(normed_in, grad_mixed)
    grad_embed_part, grad_gain_attn = norm_back(
        embedded, gain_attn, times_back(grad_mixed, weight_in)
    )
    grad_embedded = (grad_after_attn + grad_embed_part).astype(bf16)
    grad_scales = jnp.concatenate(
        [grad_gain_attn, grad_gain_mlp, grad_gain_final, grad_gain_query, grad_gain_key]
    )
    layer_grads = (
        lax.psum_scatter(grad_inflow, ("ulysses", "blk"), scatter_dimension=0, tiled=True),
        lax.psum_scatter(grad_outflow, ("ulysses", "blk"), scatter_dimension=0, tiled=True),
        lax.psum_scatter(grad_expand, ("ulysses", "blk"), scatter_dimension=0, tiled=True),
        lax.psum_scatter(grad_contract, ("ulysses", "blk"), scatter_dimension=0, tiled=True),
        lax.psum_scatter(grad_scales, ("ulysses", "blk"), scatter_dimension=0, tiled=True),
    )
    grad_tokens = lax.all_gather(
        grad_embedded.reshape(own_slots, block_len, MODEL_WIDTH), "ulysses", axis=0, tiled=True
    ).reshape(slot_count * block_len, MODEL_WIDTH)
    flat_ids = safe_ids.reshape(-1)
    flat_owned = owned.reshape(-1)
    head_part = outer_sum(grad_logits, chosen_all)
    in_range = flat_owned & (flat_ids >= 0) & (flat_ids < row_share * lax.axis_size("blk"))
    target_rows = jnp.clip(flat_ids, 0, row_share * lax.axis_size("blk") - 1)
    token_rows = jnp.where(in_range[:, None], grad_tokens.astype(single_float), 0.0)
    table_grad = lax.psum_scatter(
        head_part.at[target_rows].add(token_rows).astype(jnp.bfloat16),
        "blk",
        scatter_dimension=0,
        tiled=True,
    ).astype(jnp.float32)
    raw_grads = (table_grad,) + tuple(layer_grads)
    squares = jnp.zeros((), single_float)
    for grad_piece in raw_grads:
        squares = squares + jnp.sum(grad_piece * grad_piece)
    square_total, count_total, loss_total = lax.psum(
        (squares, count_local, loss_local), ("ulysses", "blk")
    )
    gradient_norm = jnp.sqrt(square_total) / count_total
    factor = jnp.minimum(1.0, clip_limit / gradient_norm) / count_total
    step_float = step_count[0].astype(single_float)
    weights_now = (embedding, inflow, outflow, expand, contract, scales)
    firsts = (
        first_embedding,
        inflow_first_moment,
        first_outflow,
        first_expand,
        first_contract,
        first_scales,
    )
    seconds = (
        second_embedding,
        inflow_second_moment,
        second_outflow,
        second_expand,
        second_contract,
        second_scales,
    )
    outputs = [loss_total / count_total, gradient_norm]
    for position in range(6):
        change, new_first, new_second = adam_update(
            weights_now[position],
            firsts[position],
            seconds[position],
            raw_grads[position] * factor,
            learning_rates[position],
            weight_decays[position],
            step_float,
        )
        outputs = outputs + [change, new_first, new_second]
    return tuple(outputs)


def solution(mesh):
    return jax.shard_map(
        local,
        mesh=mesh,
        in_specs=(
            P(None, "blk"),
            P(),
            P(None, "blk"),
            P(None, "blk"),
            P(None, "blk"),
            P(),
            P(("ulysses", "blk"), None),
            P(("ulysses", "blk"), None),
            P(("ulysses", "blk"), None),
            P(("ulysses", "blk"), None),
            P(("ulysses", "blk"), None),
            P(("ulysses", "blk"), None),
            P(("ulysses", "blk"), None),
            P(("ulysses", "blk"), None),
            P(("ulysses", "blk"), None),
            P(("ulysses", "blk"), None),
            P(("ulysses", "blk"), None),
            P(("ulysses", "blk"), None),
            P(("ulysses", "blk"), None),
            P(("ulysses", "blk"), None),
            P(("ulysses", "blk"), None),
            P(("ulysses", "blk")),
            P(("ulysses", "blk")),
            P(("ulysses", "blk")),
        ),
        out_specs=(
            P(),
            P(),
            P(("ulysses", "blk"), None),
            P(("ulysses", "blk"), None),
            P(("ulysses", "blk"), None),
            P(("ulysses", "blk"), None),
            P(("ulysses", "blk"), None),
            P(("ulysses", "blk"), None),
            P(("ulysses", "blk"), None),
            P(("ulysses", "blk"), None),
            P(("ulysses", "blk"), None),
            P(("ulysses", "blk"), None),
            P(("ulysses", "blk"), None),
            P(("ulysses", "blk"), None),
            P(("ulysses", "blk"), None),
            P(("ulysses", "blk"), None),
            P(("ulysses", "blk"), None),
            P(("ulysses", "blk")),
            P(("ulysses", "blk")),
            P(("ulysses", "blk")),
        ),
        check_vma=False,
    )
```

profile of v0, /device:TPU:0, one launch (start us, length us, event | category | flops | bytes accessed | tf_op | source)
XLA Modules:
  0.0 3391.7 jit_solution(15034152015748346368)
XLA Ops:
  8.1 11.7 convert_bitcast_fusion
  21.6 654.6 %all-gather.28.cloned.1.call-done = bf16[8,4748,1024]{2,1,0:T(8,128)(2,1)} async-done(((bf16[1,4748,1024]{2,1,0:T(8,128)(2,1)}), bf16[8,4748,1024]{2,1,0:T(8,128)(2,1)}) %all-gather.28.cloned.1.call-update) | async-done | bytes 77791248 | tf_op jit(solution)/shard_map/all_gather | solution.py:163
  676.2 67.4 %reshape.754 = bf16[37984,1024]{1,0:T(8,128)(2,1)} reshape(bf16[8,4748,1024]{2,1,0:T(8,128)(2,1)} %all-gather.28.cloned.1.call-done) | data formatting | bytes 155582464
  743.6 38.0 %gather_fusion = bf16[1024,1024]{1,0:T(8,128)(2,1)S(1)} fusion(bf16[37984,1024]{1,0:T(8,128)(2,1)} %reshape.754, s32[1024]{0:T(1024)S(1)} %broadcast_clamp_fusion), kind=kCustom, calls=%fused_computation | custom fusion | bytes 4198400 | tf_op jit(solution)/shard_map/jit(_take)/gather | solution.py:170
  784.4 38.9 %all-reduce = bf16[3328]{0:T(1024)(128)(2,1)S(1)} all-reduce(bf16[3328]{0:T(1024)(128)(2,1)S(1)} %dynamic-update-slice), channel_id=1, replica_groups=mesh['ulysses'=4,'blk'=8] {'ulysses','blk'}, use_global_device_ids=true, to_apply=%add | all-reduce | flops 3328 | bytes 13312
  824.6 43.0 %all-gather.14.cloned.1.call-done = bf16[1024,4096]{1,0:T(8,128)(2,1)} async-done(((bf16[32,4096]{1,0:T(8,128)(2,1)}), bf16[1024,4096]{1,0:T(8,128)(2,1)}) %all-gather.14.cloned.1.call-update) | async-done | bytes 8388624 | tf_op jit(solution)/shard_map/all_gather | solution.py:151
  875.9 12.3 all_to_all.81
  894.1 11.1 all_to_all.82
  919.0 11.0 all-to-all-done
  933.6 47.4 %all-gather.16.cloned.1.call-done = bf16[4,2,2048,128]{3,2,1,0:T(8,128)(2,1)} async-done(((bf16[4,2,256,128]{3,2,1,0:T(8,128)(2,1)}), bf16[4,2,2048,128]{3,2,1,0:T(8,128)(2,1)}) %all-gather.16.cloned.1.call-update) | async-done | bytes 4194320 | tf_op jit(solution)/shard_map/all_gather | solution.py:226
  981.2 51.0 %while.60 = (s32[]{:T(128)}, bf16[4,2,512,128]{3,2,1,0:T(8,128)(2,1)S(1)}, f32[4,2,512]{2,1,0:T(2,128)S(1)}, s32[4]{0:T(128)S(1)}, bf16[4,2,512,128]{3,2,1,0:T(8...) while((s32[]{:T(128)}, ...), condition=%wide.region_7.8_spmd.clone.clone, body=%wide.region_4.7_spmd.clone.clone.sunk | while | flops 1105334784 | bytes 32024700 | solution.py:251
  1055.5 88.8 %all-gather.22.cloned.1.call-done = bf16[1024,6144]{1,0:T(8,128)(2,1)} async-done(((bf16[32,6144]{1,0:T(8,128)(2,1)}), bf16[1024,6144]{1,0:T(8,128)(2,1)}) %all-gather.22.cloned.1.call-update) | async-done | bytes 12582928 | tf_op jit(solution)/shard_map/all_gather | solution.py:153
  1155.8 60.4 %all-gather.24.cloned.1.call-done = bf16[3072,1024]{1,0:T(8,128)(2,1)} async-done(((bf16[96,1024]{1,0:T(8,128)(2,1)}), bf16[3072,1024]{1,0:T(8,128)(2,1)}) %all-gather.24.cloned.1.call-update) | async-done | bytes 6291472 | tf_op jit(solution)/shard_map/all_gather | solution.py:154
  1224.2 8.4 all_gather.56
  1232.6 34.9 %fusion.189 = (f32[64]{0:T(128)S(1)}, f32[64,37984]{1,0:T(8,128)}) fusion(bf16[64,1024]{1,0:T(8,128)(2,1)S(1)} %all_gather.56, bf16[37984,1024]{1,0:T(8,128)(2,1)} %reshape.754), kind=kOutput, calls=%fused_computation.332 | convolution fusion | flops 4981069824 | bytes 87646464 | tf_op jit(solution)/shard_map/dot_general | solution.py:94
  1274.4 9.3 all-reduce.9
  1284.6 30.7 convolution_convert_fusion.1
  1315.3 21.6 reduce-scatter.12.cloned.1.call-done
  1342.8 9.0 multiply_convert_fusion.11
  1351.8 8.4 multiply_reduce_fusion.4
  1369.7 13.3 all-to-all-done.4
  1384.1 91.6 %while.61 = (s32[]{:T(128)}, bf16[4,2,512,128]{3,2,1,0:T(8,128)(2,1)}, f32[4,2,512]{2,1,0:T(2,128)S(1)}, s32[4]{0:T(128)S(1)}, bf16[4,2,512,128]{3,2,1,0:T(8,128...) while((s32[]{:T(128)}, ...), condition=%wide.region_25.26_spmd.clone.clone, body=%wide.region_23.25_spmd.clone.clone.sunk | while | flops 1638011392 | bytes 82619568 | solution.py:357
  1388.6 8.8 multiply_reduce_fusion.17
  1397.4 9.7 fusion.247
  1411.6 8.8 multiply_reduce_fusion.17
  1420.4 9.6 fusion.247
  1434.5 8.8 multiply_reduce_fusion.17
  1443.3 9.5 fusion.247
  1457.3 8.8 multiply_reduce_fusion.17
  1466.1 9.5 fusion.247
  1475.6 91.4 %while.62 = (s32[]{:T(128)}, bf16[4,2,2048,256]{2,3,1,0:T(8,128)(2,1)}, s32[4]{0:T(128)S(1)}, bf16[4,2,512,128]{3,2,1,0:T(8,128)(2,1)S(1)}, bf16[4,2,2048,128]{3...) while((s32[]{:T(128)}, ...), condition=%wide.region_28.29_spmd.clone.clone, body=%wide.region_27.28_spmd.clone.clone.sunk | while | flops 2176849408 | bytes 37788308 | solution.py:380
  1483.7 7.6 fusion.259
  1587.3 11.8 all-to-all-done.5
  1602.0 54.8 %reduce-scatter.14.cloned.1.call-done = bf16[256,4,2,256]{0,3,2,1:T(8,128)(2,1)} async-done(((bf16[2048,4,2,256]{0,3,2,1:T(8,128)(2,1)}), bf16[256,4,2,256]{0,3,2,1:T(8,128)(2,1)}) %reduce-scatter.14.cloned.1.call-update) | async-done | bytes 1048592 | tf_op jit(solution)/shard_map/reduce_scatter | solution.py:384
  1699.2 12.3 fusion.114
  1726.3 55.4 %fusion.175 = f32[37984,1024]{1,0:T(8,128)} fusion(bf16[64,1024]{1,0:T(8,128)(2,1)S(1)} %copy-done.53, f32[64,37984]{1,0:T(8,128)} %get-tuple-element.695, f32[64]{0:T(128)S(1)} %copy-done.80, f32[64]{0:T(128)S(1)} %copy-done.74, s32[64]{0:T(128)S(1)} %copy-done.76), kind=kOutput, calls=%fused_computation.326 | convolution fusion | flops 4993224704 | bytes 165438208 | tf_op jit(solution)/shard_map/dot_general | solution.py:88
  1785.9 22.8 reduce-scatter.18.cloned.1.call-done
  1810.4 158.4 %reduce-scatter.22.cloned.1.call-done = f32[96,1024]{1,0:T(8,128)} async-done(((f32[3072,1024]{1,0:T(8,128)}), f32[96,1024]{1,0:T(8,128)}) %reduce-scatter.22.cloned.1.call-update) | async-done | bytes 393232 | tf_op jit(solution)/shard_map/reduce_scatter | solution.py:436
  1973.2 8.6 fusion.137
  1981.9 23.8 all-gather.26.cloned.1.call-done
  2009.6 151.8 %scatter_fusion = f32[37984,1024]{1,0:T(8,128)} fusion(f32[37984,1024]{1,0:T(8,128)} %fusion.175, s32[1024]{0:T(1024)S(1)} %bitcast.358, f32[1024,1024]{1,0:T(8,128)} %convert_select_fusion), kind=kCustom, calls=%fused_computation.3 | custom fusion | flops 1048576 | bytes 12587008 | tf_op jit(solution)/shard_map/scatter-add | solution.py:449
  2161.4 75.2 %convert_element_type.224 = bf16[37984,1024]{1,0:T(8,128)(2,1)} convert(f32[37984,1024]{1,0:T(8,128)} %scatter_fusion) | non-fusion elementwise | flops 38895616 | bytes 233373696 | tf_op jit(solution)/shard_map/convert_element_type | solution.py:449
  2236.7 940.4 %fusion.12 = bf16[4768,1024]{1,0:T(8,128)(2,1)} fusion(bf16[37984,1024]{1,0:T(8,128)(2,1)} %convert_element_type.224), kind=kCustom, calls=%all-reduce-scatter | all-reduce-scatter fusion | flops 39059456 | bytes 87556608
  3180.8 39.5 %all-reduce.6 = f32[3328]{0:T(1024)S(1)} all-reduce(f32[3328]{0:T(1024)S(1)} %constant_dynamic-update-slice_fusion), channel_id=14, replica_groups=mesh['ulysses'=4,'blk'=8] {'ulysses','blk'}, use_global_device_ids=true, to_apply=%region_48.49.clone | all-reduce | flops 3328 | bytes 26624
  3220.9 47.1 %concatenate.89 = bf16[4908,1024]{1,0:T(8,128)(2,1)} concatenate(bf16[140,1024]{1,0:T(8,128)(2,1)} %collective-permute-done, bf16[4768,1024]{1,0:T(8,128)(2,1)} %fusion.12), dimensions={0} | concatenate | bytes 20103168
  3268.1 9.4 fusion.108
  3285.1 40.7 %all-reduce.8 = (f32[]{:T(128)}, f32[]{:T(128)}, f32[]{:T(128)}) all-reduce(f32[]{:T(128)S(6)} %neg.17, f32[]{:T(128)} %fusion.167, f32[]{:T(128)S(6)} %add.396), channel_id=1, replica_groups=mesh['ulysses'=4,'blk'=8] {'ulysses','blk'}, use_global_device_ids=true, to_apply=%region_16.17 | all-reduce | flops 3 | bytes 24 | tf_op jit(solution)/shard_map/psum | solution.py:458
  3330.6 45.9 %add_multiply_fusion = (f32[4748,1024]{1,0:T(8,128)}, f32[4748,1024]{1,0:T(8,128)}, f32[4748,1024]{1,0:T(8,128)}) fusion(f32[4748,1024]{1,0:T(8,128)} %param.38, f32[]{:T(128)} %bitcast.54, f32[]{:T(128)} %bitcast.53, f32[]{:T(128)S(6)} %div.160, bf16[4908,1024]{1,0:T(8,128)(2,1)} %concatenate.89, u32[]{:S(6)} %subtract, f32[4748,1024]{1,0:T(8,128)} %param.40, ...), kind=kLoop, calls=%fused_computation.133 | loop fusion | flops 77791232 | bytes 126410768 | tf_op jit(solution)/shard_map/mul | solution.py:104
  (507 shorter events, 361.7 us)
Async XLA Ops:
  8.0 668.2 %all-gather.28.cloned.1.call-start = ((), (), s32[]{:S(2)}) async-start(), calls=%async_computation.28 | async-start | bytes 87588864 | tf_op jit(solution)/shard_map/all_gather | solution.py:163
  19.8 803.6 %reduce-scatter.24.cloned.1.call-start = ((), (), s32[]{:S(2)}) async-start(), calls=%async_computation.29 | async-start | bytes 2621440
  783.3 84.3 %all-gather.14.cloned.1.call-start = ((), (), s32[]{:S(2)}) async-start(), calls=%async_computation.15 | async-start | bytes 8650752 | tf_op jit(solution)/shard_map/all_gather | solution.py:151
  784.1 149.5 %all-gather.18.cloned.1.call-start = ((), (), s32[]{:S(2)}) async-start(), calls=%async_computation.17 | async-start | bytes 4718592 | tf_op jit(solution)/shard_map/all_gather | solution.py:227
  823.3 50.2 %copy-start.63 = (f32[1024]{0:T(1024)}, f32[1024]{0:T(1024)S(1)}, u32[]{:S(2)}) copy-start(f32[1024]{0:T(1024)S(1)} %get-tuple-element.679) | copy-start | bytes 12292
  823.3 536.9 %copy-start.54 = (f32[1024]{0:T(1024)}, f32[1024]{0:T(1024)S(1)}, u32[]{:S(2)}) copy-start(f32[1024]{0:T(1024)S(1)} %get-tuple-element.678) | copy-start | bytes 12292
  824.6 49.0 %copy-start.81 = (f32[256]{0:T(256)}, f32[256]{0:T(256)S(1)}, u32[]{:S(2)}) copy-start(f32[256]{0:T(256)S(1)} %add_rsqrt_fusion.4) | copy-start | bytes 3076
  888.2 92.8 %all-gather.16.cloned.1.call-start = ((), (), s32[]{:S(2)}) async-start(), calls=%async_computation.16 | async-start | bytes 4718592 | tf_op jit(solution)/shard_map/all_gather | solution.py:226
  905.2 140.6 %all-gather.20.cloned.1.call-start = ((), (), s32[]{:S(2)}) async-start(), calls=%async_computation.18 | async-start | bytes 4325376 | tf_op jit(solution)/shard_map/all_gather | solution.py:152
  905.9 238.4 %all-gather.22.cloned.1.call-start = ((), (), s32[]{:S(2)}) async-start(), calls=%async_computation.19 | async-start | bytes 12976128 | tf_op jit(solution)/shard_map/all_gather | solution.py:153
  913.1 68.1 %copy-start.98 = (s32[4]{0:T(128)S(1)}, s32[4]{0:T(128)}, u32[]{:S(2)}) copy-start(s32[4]{0:T(128)} %param.33) | copy-start | bytes 52
  914.7 15.3 all-to-all-start
  918.2 297.9 %all-gather.24.cloned.1.call-start = ((), (), s32[]{:S(2)}) async-start(), calls=%async_computation.20 | async-start | bytes 6488064 | tf_op jit(solution)/shard_map/all_gather | solution.py:154
  1033.6 17.8 all-to-all-start.3
  1037.3 299.5 %reduce-scatter.12.cloned.1.call-start = ((), (), s32[]{:S(2)}) async-start(), calls=%async_computation.21 | async-start | bytes 163840 | tf_op jit(solution)/shard_map/reduce_scatter | solution.py:302
  1038.3 246.4 %copy-start.75 = (s32[64]{0:T(128)}, s32[64]{0:T(128)S(1)}, u32[]{:S(2)}) copy-start(s32[64]{0:T(128)S(1)} %sub.177) | copy-start | bytes 772
  1038.9 245.7 %copy-start.73 = (f32[64]{0:T(128)}, f32[64]{0:T(128)S(1)}, u32[]{:S(2)}) copy-start(f32[64]{0:T(128)S(1)} %select_n.111) | copy-start | bytes 772
  1051.4 99.4 %copy-start.23 = (bf16[4,4,256,128]{2,3,1,0:T(8,128)(2,1)}, bf16[4,4,256,128]{2,3,1,0:T(8,128)(2,1)S(1)}, u32[]{:S(2)}) copy-start(bf16[4,4,256,128]{2,3,1,0:T(8,128)(2,1)S(1)} %all-to-all-done.3) | copy-start | bytes 3145732
  1055.5 304.8 %copy-start.8 = (f32[256,1024]{1,0:T(8,128)}, f32[256,1024]{1,0:T(8,128)S(1)}, u32[]{:S(2)}) copy-start(f32[256,1024]{1,0:T(8,128)S(1)} %get-tuple-element.691) | copy-start | bytes 3145732
  1055.5 304.8 %copy-start.77 = (f32[256]{0:T(256)}, f32[256]{0:T(256)S(1)}, u32[]{:S(2)}) copy-start(f32[256]{0:T(256)S(1)} %add_rsqrt_fusion.3) | copy-start | bytes 3076
  1221.3 117.6 %copy-start.16 = (f32[256,1024]{1,0:T(8,128)}, f32[256,1024]{1,0:T(8,128)S(1)}, u32[]{:S(2)}) copy-start(f32[256,1024]{1,0:T(8,128)S(1)} %get-tuple-element.693) | copy-start | bytes 3145732
  1365.2 17.7 all-to-all-start.4
  1369.5 287.3 %reduce-scatter.14.cloned.1.call-start = ((), (), s32[]{:S(2)}) async-start(), calls=%async_computation.22 | async-start | bytes 9437184 | tf_op jit(solution)/shard_map/reduce_scatter | solution.py:384
  1567.0 241.7 %reduce-scatter.18.cloned.1.call-start = ((), (), s32[]{:S(2)}) async-start(), calls=%async_computation.24 | async-start | bytes 8650752 | tf_op jit(solution)/shard_map/reduce_scatter | solution.py:434
  1573.2 395.6 %reduce-scatter.22.cloned.1.call-start = ((), (), s32[]{:S(2)}) async-start(), calls=%async_computation.26 | async-start | bytes 12976128 | tf_op jit(solution)/shard_map/reduce_scatter | solution.py:436
  1581.8 17.3 all-to-all-start.5
  1599.3 63.4 %copy-start.3 = (f32[32,16,8,128]{3,2,1,0:T(8,128)S(1)}, f32[32,16,8,128]{3,2,1,0:T(8,128)}, u32[]{:S(2)}) copy-start(f32[32,16,8,128]{3,2,1,0:T(8,128)} %copy-done.2) | copy-start | bytes 6291460
  1659.1 11.6 all-to-all-start.7
  1670.7 12.5 all-to-all-start.6
  1674.2 331.5 %all-gather.26.cloned.1.call-start = ((), (), s32[]{:S(2)}) async-start(), calls=%async_computation.27 | async-start | bytes 2621440 | tf_op jit(solution)/shard_map/all_gather | solution.py:439
  1699.1 1578.3 %reduce-scatter.20.cloned.1.call-start = ((), (), s32[]{:S(2)}) async-start(), calls=%async_computation.25 | async-start | bytes 25952256 | tf_op jit(solution)/shard_map/reduce_scatter | solution.py:435
  1711.6 1567.9 %reduce-scatter.16.cloned.1.call-start = ((), (), s32[]{:S(2)}) async-start(), calls=%async_computation.23 | async-start | bytes 17301504 | tf_op jit(solution)/shard_map/reduce_scatter | solution.py:433
  1726.3 55.4 %copy-start.5 = (f32[256,16,64]{2,0,1:T(8,128)S(1)}, f32[256,16,64]{2,0,1:T(8,128)}, u32[]{:S(2)}) copy-start(f32[256,16,64]{2,0,1:T(8,128)} %get-tuple-element.665) | copy-start | bytes 3145732
  1784.6 186.0 %copy-start.94 = (f32[1024]{0:T(1024)S(1)}, f32[1024]{0:T(1024)}, u32[]{:S(2)}) copy-start(f32[1024]{0:T(1024)} %get-tuple-element.546) | copy-start | bytes 12292
  1784.6 186.0 %copy-start.93 = (f32[1024]{0:T(1024)S(1)}, f32[1024]{0:T(1024)}, u32[]{:S(2)}) copy-start(f32[1024]{0:T(1024)} %get-tuple-element.544) | copy-start | bytes 12292
  1784.6 186.0 %copy-start.85 = (f32[1024]{0:T(1024)S(1)}, f32[1024]{0:T(1024)}, u32[]{:S(2)}) copy-start(f32[1024]{0:T(1024)} %get-tuple-element.542) | copy-start | bytes 12292
  1784.6 186.0 %copy-start.15 = (f32[256,8,64]{2,0,1:T(8,128)S(1)}, f32[256,8,64]{2,0,1:T(8,128)}, u32[]{:S(2)}) copy-start(f32[256,8,64]{2,0,1:T(8,128)} %copy-done.14) | copy-start | bytes 1572868
  1784.6 188.6 %copy-start.27 = (bf16[1,256,1024]{2,1,0:T(8,128)(2,1)S(1)}, bf16[1,256,1024]{2,1,0:T(8,128)(2,1)}, u32[]{:S(2)}) copy-start(bf16[1,256,1024]{2,1,0:T(8,128)(2,1)} %reduce-scatter.24.cloned.1.call-done) | copy-start | bytes 1572868
  1784.7 188.5 %copy-start.39 = (bf16[32,8,8,128]{3,1,2,0:T(8,128)(2,1)S(1)}, bf16[32,8,8,128]{3,1,2,0:T(8,128)(2,1)}, u32[]{:S(2)}) copy-start(bf16[32,8,8,128]{3,1,2,0:T(8,128)(2,1)} %copy.214) | copy-start | bytes 1572868
  1784.7 188.5 %copy-start.83 = (f32[256]{0:T(256)S(1)}, f32[256]{0:T(256)}, u32[]{:S(2)}) copy-start(f32[256]{0:T(256)} %copy-done.81) | copy-start | bytes 3076
  2236.6 943.5 %copy-start.28 = (f32[2048,128]{1,0:T(8,128)S(1)}, f32[2048,128]{1,0:T(8,128)}, u32[]{:S(2)}) copy-start(f32[2048,128]{1,0:T(8,128)} %reshape.688) | copy-start | bytes 3145732
  2236.6 943.5 %copy-start.29 = (f32[2048,64]{1,0:T(8,128)S(1)}, f32[2048,64]{1,0:T(8,128)}, u32[]{:S(2)}) copy-start(f32[2048,64]{1,0:T(8,128)} %get-tuple-element.698) | copy-start | bytes 1572868
  2236.6 943.5 %copy-start.30 = (f32[2048,64]{1,0:T(8,128)S(1)}, f32[2048,64]{1,0:T(8,128)}, u32[]{:S(2)}) copy-start(f32[2048,64]{1,0:T(8,128)} %get-tuple-element.699) | copy-start | bytes 1572868
  2236.6 943.5 %copy-start.84 = (f32[2048]{0:T(1024)S(1)}, f32[2048]{0:T(1024)}, u32[]{:S(2)}) copy-start(f32[2048]{0:T(1024)} %rsqrt.59) | copy-start | bytes 24580
  3178.1 42.8 %collective-permute-start = (bf16[140,1024]{1,0:T(8,128)(2,1)S(1)}, bf16[140,1024]{1,0:T(8,128)(2,1)}, u32[]{:S(2)}, u32[]{:S(2)}) collective-permute-start(bf16[140,1024]{1,0:T(8,128)(2,1)S(1)} %slice.120), channel_id=1, source_target_pairs={{0,1},{1,2},{2,3},{3,4},{4,5},{5,6},{6,7},{8,9},{9,10},{10,11},{11... | collective-permute-start | bytes 860168
  3268.1 61.8 %copy-start.100 = (f32[104]{0:T(128)S(1)}, f32[104]{0:T(128)}, u32[]{:S(2)}) copy-start(f32[104]{0:T(128)} %param.53) | copy-start | bytes 1252
  3268.1 61.8 %copy-start.101 = (f32[104]{0:T(128)S(1)}, f32[104]{0:T(128)}, u32[]{:S(2)}) copy-start(f32[104]{0:T(128)} %param.55) | copy-start | bytes 1252
  3268.1 61.8 %copy-start.102 = (f32[104]{0:T(128)S(1)}, f32[104]{0:T(128)}, u32[]{:S(2)}) copy-start(f32[104]{0:T(128)} %param.54) | copy-start | bytes 1252
  (82 other events, 1020.6 us)
Sparse Core Ops, SparseCore 0:
  19.9 656.2 all-gather.27
  783.4 36.3 reduce-scatter.23
  888.4 45.2 all-gather.17
  935.2 45.8 all-gather.15
  984.9 60.8 all-gather.19
  1049.7 94.6 all-gather.21
  1148.3 67.7 all-gather.23
  1315.4 21.3 reduce-scatter.11
  1567.1 89.6 reduce-scatter.13
  1659.0 149.7 reduce-scatter.17
  1815.4 153.3 reduce-scatter.21
  1971.2 34.4 all-gather.25
  2013.2 252.9 reduce-scatter.19
  2269.0 364.9 reduce-scatter.15
Sparse Core Ops, SparseCore 1:
  787.3 80.2 all-gather.13
where the time goes:
time: 3410 us; the launch traced here: 3390 us
  waiting for transfers between devices  1230 us (36%)
  blocking collectives  1100 us (32%)
  other arithmetic  399 us (12%)
  matrix products  393 us (12%)
  local copies, waits for them, and re-layouts  211 us (6%)
    unnamed x4, blocking collectives  1030 us
    all_gather x1, waiting for transfers between devices, local(): lax.all_gather(embedding.astype(bf16), 'blk', axis=0, tiled=True)  655 us
    reduce_scatter x1, waiting for transfers between devices, local(): lax.psum_scatter(grad_contract, ('ulysses', 'blk'), scatter_dimension=0,...  158 us
    scatter-add x1, other arithmetic, local(): head_part.at[target_rows].add(token_rows).astype(jnp.bfloat16)  152 us
    unnamed x235, local copies, waits for them, and re-layouts  135 us
    all_gather x1, waiting for transfers between devices, local(): lax.all_gather(expand.astype(bf16), ('ulysses', 'blk'), axis=0, tiled=True)  88.8 us
    dot_general x5, matrix products, outer_sum(): lax.dot_general(left, right, (((0,), (0,)), ((), ())), preferred_element_...  87.6 us
    convert_element_type x1, other arithmetic, local(): head_part.at[target_rows].add(token_rows).astype(jnp.bfloat16)  75.2 us
  transfers between devices with their start and end apart: 22, of which 18 were waited for; matrix products, arithmetic and copies ran while one was open for 43% of the time, Pallas kernels for 0%

commit v1 on v0

v1 whole, which is shorter than its diff:
```python
import functools
import math

import jax
import jax.numpy as jnp
from jax import lax
from jax.experimental import pallas as pl
from jax.experimental.pallas import tpu as pltpu
from jax.sharding import PartitionSpec as P

MODEL_WIDTH = 1024
QUERY_HEADS = 16
KEY_VALUE_HEADS = 8
HEAD_WIDTH = 128
FF = 3072
QUERY_WIDTH = QUERY_HEADS * HEAD_WIDTH

norm_eps = 1e-06
rope_base = 1000000.0
clip_limit = 0.01
beta_first = 0.9
beta_second = 0.95
adam_eps = 1e-08
learning_rates = (0.01, 0.003, 0.07, 0.003, 0.002, 0.01)
weight_decays = (0.1, 0.1, 0.1, 0.1, 0.1, 0.0)
masked_score = -1e30

bf16 = jnp.bfloat16
f32 = jnp.float32
BOTH = ("ulysses", "blk")


def inverse_root(values):
    return lax.rsqrt(jnp.mean(values * values, axis=-1, keepdims=True) + norm_eps)


def norm_back(inputs, gain_vec, upstream):
    root_scale = inverse_root(inputs)
    unit_rows = inputs * root_scale
    weighted = upstream * gain_vec
    grad_inputs = root_scale * (
        weighted - unit_rows * jnp.mean(weighted * unit_rows, axis=-1, keepdims=True)
    )
    grad_gain = jnp.sum((upstream * unit_rows).reshape(-1, gain_vec.shape[-1]), axis=0)
    return (grad_inputs, grad_gain)


def rope_angles(positions):
    half_width = HEAD_WIDTH // 2
    frequency = rope_base ** (
        -(jnp.arange(half_width, dtype=jnp.int32).astype(f32) * 2.0 / HEAD_WIDTH)
    )
    angles = positions.astype(f32)[:, None] * frequency[None, :]
    return (jnp.cos(angles), jnp.sin(angles))


def rotate(values, tables, sign_value):
    half_width = values.shape[-1] // 2
    front_half = values[..., :half_width]
    back_half = values[..., half_width:]
    cosine_part = tables[0][:, None, :]
    sine_part = tables[1][:, None, :] * sign_value
    return jnp.concatenate(
        [
            front_half * cosine_part - back_half * sine_part,
            back_half * cosine_part + front_half * sine_part,
        ],
        axis=-1,
    )


def mm(left, right):
    return lax.dot_general(left, right, (((1,), (0,)), ((), ())), preferred_element_type=f32)


def mm_outer(left, right):
    return lax.dot_general(left, right, (((0,), (0,)), ((), ())), preferred_element_type=f32)


def mm_back(left, right):
    return lax.dot_general(left, right, (((1,), (1,)), ((), ())), preferred_element_type=f32)


def spread_rows(onehot, rows):
    return lax.dot_general(
        onehot.astype(f32),
        rows,
        (((0,), (0,)), ((), ())),
        precision=lax.Precision.HIGHEST,
        preferred_element_type=f32,
    )


def adam_update(weight_now, first_now, second_now, gradient, rate_value, decay_value, step_float):
    new_first = beta_first * first_now + (1.0 - beta_first) * gradient
    new_second = beta_second * second_now + (1.0 - beta_second) * gradient * gradient
    first_hat = new_first / (1.0 - beta_first**step_float)
    second_hat = new_second / (1.0 - beta_second**step_float)
    change = -rate_value * (
        first_hat / (jnp.sqrt(second_hat) + adam_eps) + decay_value * weight_now
    )
    return (change, new_first, new_second)


def exchange_kernel(axis, blk_count, kinds, *refs):
    parts = len(kinds)
    sources, landings = refs[:parts], refs[parts : 2 * parts]
    send_sems, recv_sems, own_sems = refs[2 * parts :]
    row, column = lax.axis_index("ulysses"), lax.axis_index("blk")
    if axis == "all":
        me = row * blk_count + column
    else:
        me = row if axis == "ulysses" else column
    count = landings[0].shape[0]

    def place(peer):
        if axis == "all":
            return {"ulysses": peer // blk_count, "blk": lax.rem(peer, blk_count)}
        return {axis: peer}

    barrier = pltpu.get_barrier_semaphore()

    def greet(step, carry):
        pl.semaphore_signal(
            barrier,
            inc=1,
            device_id=place(lax.rem(me + step, count)),
            device_id_type=pl.DeviceIdType.MESH,
        )
        return carry

    lax.fori_loop(1, count, greet, 0)
    pl.semaphore_wait(barrier, count - 1)

    def copies(step):
        peer = lax.rem(me + step, count)
        return [
            pltpu.make_async_remote_copy(
                src_ref=sources[k].at[peer] if kinds[k] == "s" else sources[k],
                dst_ref=landings[k].at[me],
                send_sem=send_sems.at[k, step],
                recv_sem=recv_sems.at[k, step],
                device_id=place(peer),
                device_id_type=pl.DeviceIdType.MESH,
            )
            for k in range(parts)
        ]

    def send(step, carry):
        for copy in copies(step):
            copy.start()
        return carry

    lax.fori_loop(1, count, send, 0)
    own = [
        pltpu.make_async_copy(
            sources[k].at[me] if kinds[k] == "s" else sources[k],
            landings[k].at[me],
            own_sems.at[k],
        )
        for k in range(parts)
    ]
    for copy in own:
        copy.start()
    for copy in own:
        copy.wait()

    def finish(step, carry):
        for copy in copies(step):
            copy.wait()
        return carry

    lax.fori_loop(1, count, finish, 0)


class Exchanger:
    def __init__(self):
        self.used = 0

    def __call__(self, axis, kinds, *arrays):
        blk_count = lax.axis_size("blk")
        count = lax.axis_size("ulysses") * blk_count if axis == "all" else lax.axis_size(axis)
        shapes = [
            jax.ShapeDtypeStruct(
                array.shape if kind == "s" else (count,) + array.shape, array.dtype
            )
            for kind, array in zip(kinds, arrays)
        ]
        parts = len(arrays)
        collective_id = self.used
        self.used += 1
        return pl.pallas_call(
            functools.partial(exchange_kernel, axis, blk_count, kinds),
            out_shape=shapes,
            in_specs=[pl.BlockSpec(memory_space=pltpu.VMEM)] * parts,
            out_specs=[pl.BlockSpec(memory_space=pltpu.VMEM)] * parts,
            scratch_shapes=[
                pltpu.SemaphoreType.DMA((parts, count)),
                pltpu.SemaphoreType.DMA((parts, count)),
                pltpu.SemaphoreType.DMA((parts,)),
            ],
            compiler_params=pltpu.CompilerParams(
                collective_id=collective_id,
                has_side_effects=True,
                vmem_limit_bytes=32 * 1024 * 1024,
            ),
            name="exchange_" + str(collective_id),
        )(*arrays)


def lookup_kernel(slots, fills_ref, ids_ref, table_ref, rows_ref, wide, sem):
    wide[...] = jnp.zeros_like(wide)

    def row_copy(place, row):
        return pltpu.make_async_copy(
            table_ref.at[pl.ds(row, 1), :], wide.at[pl.ds(place, 1), :], sem
        )

    def of_peer(peer, total):
        fill = fills_ref[peer]

        def fetch(k, carry):
            place = peer * slots + k
            row_copy(place, ids_ref[place]).start()
            return carry

        lax.fori_loop(0, fill, fetch, 0)
        return total + fill

    total = lax.fori_loop(0, fills_ref.shape[0], of_peer, 0)

    def drain(k, carry):
        row_copy(0, 0).wait()
        return carry

    lax.fori_loop(0, total, drain, 0)
    rows_ref[...] = wide[...].astype(rows_ref.dtype)


def lookup(fills, ids, table, slots):
    places = ids.shape[0]
    return pl.pallas_call(
        functools.partial(lookup_kernel, slots),
        out_shape=jax.ShapeDtypeStruct((places, table.shape[1]), bf16),
        in_specs=[
            pl.BlockSpec(memory_space=pltpu.SMEM),
            pl.BlockSpec(memory_space=pltpu.SMEM),
            pl.BlockSpec(memory_space=pl.ANY),
        ],
        out_specs=pl.BlockSpec(memory_space=pltpu.VMEM),
        scratch_shapes=[
            pltpu.VMEM((places, table.shape[1]), f32),
            pltpu.SemaphoreType.DMA,
        ],
        compiler_params=pltpu.CompilerParams(vmem_limit_bytes=40 * 1024 * 1024),
        name="lookup",
    )(fills, ids, table)


def local(
    tokens,
    lengths,
    picked,
    targets,
    advantages,
    step_count,
    embedding,
    first_embedding,
    second_embedding,
    inflow,
    inflow_first_moment,
    inflow_second_moment,
    outflow,
    first_outflow,
    second_outflow,
    expand,
    first_expand,
    second_expand,
    contract,
    first_contract,
    second_contract,
    scales,
    first_scales,
    second_scales,
):
    exchange = Exchanger()
    n_u, n_b = lax.axis_size("ulysses"), lax.axis_size("blk")
    n_all = n_u * n_b
    u, b = lax.axis_index("ulysses"), lax.axis_index("blk")
    me = u * n_b + b
    slot_count, block_len = tokens.shape
    assert slot_count == n_u
    picks = picked.shape[1]
    slot_picks = picks * n_b
    all_picks = slot_picks * n_u
    row_share = embedding.shape[0]
    group = QUERY_HEADS // KEY_VALUE_HEADS
    score_scale = HEAD_WIDTH ** (-0.5)
    in_rows, out_share, ff_share = inflow.shape[0], outflow.shape[0], contract.shape[0]
    q_share = QUERY_WIDTH // n_b
    heads_share = q_share // HEAD_WIDTH

    inflow_low = inflow.astype(bf16)
    kv_weight = lax.all_gather(inflow_low[:, QUERY_WIDTH:], BOTH, axis=0, tiled=True)
    q_cols = inflow_low[:, :QUERY_WIDTH].reshape(in_rows, n_b, q_share).transpose(1, 0, 2)
    ff_cols = (
        expand.astype(bf16)
        .reshape(in_rows, 2, n_u, n_b, ff_share)
        .transpose(3, 0, 1, 2, 4)
        .reshape(n_b, in_rows, 2 * n_u * ff_share)
    )
    (split_cols,) = exchange("blk", "s", jnp.concatenate([q_cols, ff_cols], axis=2))
    in_block = n_b * in_rows
    mixed_share = q_share + 2 * n_u * ff_share
    wide_rows = in_block * mixed_share // MODEL_WIDTH
    layer_rows = jnp.concatenate(
        [
            split_cols.reshape(wide_rows, MODEL_WIDTH),
            outflow.astype(bf16),
            contract.astype(bf16),
        ],
        axis=0,
    )
    layer_all = lax.all_gather(layer_rows, "ulysses", axis=0)
    mixed_in = layer_all[:, :wide_rows].reshape(n_u * in_block, mixed_share)
    q_weight = mixed_in[:, :q_share]
    ff_weight = mixed_in[:, q_share:]
    out_weight = layer_all[:, wide_rows : wide_rows + out_share].reshape(n_u * out_share, MODEL_WIDTH)
    contract_weight = layer_all[:, wide_rows + out_share :].reshape(n_u * ff_share, MODEL_WIDTH)

    packed = jnp.concatenate(
        [tokens.astype(f32), targets.astype(f32), picked.astype(f32), advantages], axis=1
    )
    scale_share = scales.shape[0]
    gains_mine = jnp.pad(scales, (0, 128 - scale_share)).reshape(1, 128)
    packed_all, = exchange("blk", "g", packed)
    gains_all, = exchange("all", "g", gains_mine)
    gains_wide = gains_all[:, 0, :scale_share].reshape(-1).astype(bf16).astype(f32)
    gain_attn = gains_wide[:MODEL_WIDTH]
    gain_mlp = gains_wide[MODEL_WIDTH : 2 * MODEL_WIDTH]
    gain_final = gains_wide[2 * MODEL_WIDTH : 3 * MODEL_WIDTH]
    gain_query = gains_wide[3 * MODEL_WIDTH : 3 * MODEL_WIDTH + HEAD_WIDTH]
    gain_key = gains_wide[3 * MODEL_WIDTH + HEAD_WIDTH :]

    wants_count = block_len + picks
    wants = (
        packed_all[:, :, :wants_count]
        .astype(jnp.int32)
        .transpose(1, 0, 2)
        .reshape(n_all, wants_count)
    )
    picked_all = packed_all[:, :, wants_count : wants_count + picks].astype(jnp.int32)
    targets_all = packed_all[:, :, block_len:wants_count].astype(jnp.int32)
    advantages_all = packed_all[:, :, wants_count + picks :]
    valid_all = picked_all < lengths[None, :, None]
    weights_all = jnp.where(valid_all, advantages_all, 0.0)
    my_length = lax.dynamic_index_in_dim(lengths, u, 0, keepdims=False)
    slot_picked = lax.dynamic_index_in_dim(picked_all, u, 1, keepdims=False).reshape(-1)
    my_picked = lax.dynamic_index_in_dim(picked, u, 0, keepdims=False)
    my_valid = my_picked < my_length
    my_weight = jnp.where(
        my_valid, lax.dynamic_index_in_dim(advantages, u, 0, keepdims=False), 0.0
    )

    fill_mean = wants_count / n_all
    slots = -(-int(fill_mean + 8 * math.sqrt(fill_mean)) // 16) * 16
    places = n_all * slots
    owner_all = wants // row_share
    counts = jnp.sum(
        (owner_all[:, None, :] == jnp.arange(n_all, dtype=jnp.int32)[None, :, None]).astype(
            jnp.int32
        ),
        axis=-1,
    )
    rounds = (jnp.max(counts) + slots - 1) // slots
    wants_mine = owner_all == me
    earlier = (
        jnp.arange(wants_count)[:, None] < jnp.arange(wants_count)[None, :]
    ).astype(bf16)
    rank_mine = mm(wants_mine.astype(bf16), earlier).astype(jnp.int32)
    total_mine = jnp.sum(wants_mine.astype(jnp.int32), axis=1)
    rows_mine = jnp.where(wants_mine, wants - me * row_share, 0)
    own_wants = lax.dynamic_index_in_dim(wants, me, 0, keepdims=False)
    own_owner = own_wants // row_share
    same_owner = own_owner[:, None] == own_owner[None, :]
    own_rank = jnp.sum(
        jnp.where(
            same_owner & (jnp.arange(wants_count)[:, None] < jnp.arange(wants_count)[None, :]),
            1,
            0,
        ),
        axis=0,
    )

    def slot_ids(turn):
        slot_rank = turn * slots + jnp.arange(slots, dtype=jnp.int32)
        chosen = wants_mine[:, None, :] & (rank_mine[:, None, :] == slot_rank[None, :, None])
        ids = jnp.sum(jnp.where(chosen, rows_mine[:, None, :], 0), axis=-1)
        fills = jnp.clip(total_mine - turn * slots, 0, slots)
        filled = jnp.arange(slots)[None, :] < fills[:, None]
        return (ids, fills, filled)

    def landing(turn):
        rank = own_rank - turn * slots
        place = jnp.where((rank >= 0) & (rank < slots), own_owner * slots + rank, -1)
        return (place[:, None] == jnp.arange(places, dtype=jnp.int32)[None, :]).astype(bf16)

    rows_out = exchange.used
    exchange.used += 1

    def fetch_turn(state):
        turn, so_far = state
        ids, fills, _ = slot_ids(turn)
        rows = lookup(fills, ids.reshape(-1), embedding, slots)
        mine = Exchanger()
        mine.used = rows_out
        (arrived,) = mine("all", "s", rows.reshape(n_all, slots, MODEL_WIDTH))
        return (turn + 1, so_far + mm(landing(turn), arrived.reshape(places, MODEL_WIDTH)))

    _, fetched = lax.while_loop(
        lambda state: state[0] < rounds,
        fetch_turn,
        (jnp.int32(0), jnp.zeros((wants_count, MODEL_WIDTH), f32)),
    )
    embedded = fetched[:block_len]
    target_rows = fetched[block_len:]

    unit_in = embedded * inverse_root(embedded)
    normed_in = (unit_in * gain_attn).astype(bf16)
    pick_hot = (my_picked - b * block_len)[:, None] == jnp.arange(block_len)[None, :]
    picked_both = mm(
        pick_hot.astype(bf16), jnp.concatenate([embedded.astype(bf16), normed_in], axis=1)
    )
    embedded_picks = picked_both[:, :MODEL_WIDTH]
    (normed_slot,) = exchange("blk", "g", picked_both[:, MODEL_WIDTH:].astype(bf16))
    normed_slot = normed_slot.reshape(slot_picks, MODEL_WIDTH)
    mixed_kv = mm(normed_in, kv_weight)
    key_raw = mixed_kv[:, : KEY_VALUE_HEADS * HEAD_WIDTH].reshape(
        block_len, KEY_VALUE_HEADS, HEAD_WIDTH
    )
    values_low = (
        mixed_kv[:, KEY_VALUE_HEADS * HEAD_WIDTH :]
        .reshape(block_len, KEY_VALUE_HEADS, HEAD_WIDTH)
        .astype(bf16)
        .transpose(1, 0, 2)
    )
    key_pos = b * block_len + jnp.arange(block_len, dtype=jnp.int32)
    key_tables = rope_angles(key_pos)
    key_rot = (
        rotate(key_raw * inverse_root(key_raw) * gain_key, key_tables, 1.0)
        .astype(bf16)
        .transpose(1, 0, 2)
    )

    query_raw = mm(normed_slot, q_weight).reshape(slot_picks, heads_share, HEAD_WIDTH)
    query_tables = rope_angles(slot_picked)
    query_mine = rotate(query_raw * inverse_root(query_raw) * gain_query, query_tables, 1.0)
    (query_all,) = exchange("blk", "g", query_mine.astype(bf16).reshape(slot_picks, q_share))

    def into_groups(array):
        return (
            array.reshape(n_b, slot_picks, heads_share, HEAD_WIDTH)
            .transpose(0, 2, 1, 3)
            .reshape(KEY_VALUE_HEADS, group * slot_picks, HEAD_WIDTH)
        )

    query_groups = into_groups(query_all)
    query_pos = jnp.tile(slot_picked, group)
    allowed = ((key_pos[None, :] <= query_pos[:, None]) & (key_pos[None, :] < my_length))[None]
    scores = (
        jnp.einsum("kqd,kjd->kqj", query_groups, key_rot, preferred_element_type=f32)
        * score_scale
    )
    scores = jnp.where(allowed, scores, masked_score)
    part_max = jnp.max(scores, axis=-1, keepdims=True)
    part_weights = jnp.where(allowed, jnp.exp(scores - part_max), 0.0)
    part_sum = jnp.sum(part_weights, axis=-1)
    part_out = jnp.einsum(
        "kqj,kjd->kqd", part_weights.astype(bf16), values_low, preferred_element_type=f32
    )
    out_cut = QUERY_WIDTH // n_all
    part_send = (
        part_out.astype(bf16)
        .reshape(QUERY_HEADS, slot_picks, HEAD_WIDTH)
        .transpose(1, 0, 2)
        .reshape(slot_picks, n_u, n_b, out_cut)
        .transpose(2, 0, 1, 3)
        .reshape(n_b, slot_picks, n_u * out_cut)
    )
    stats = jnp.stack([part_max[..., 0], part_sum]).reshape(2 * QUERY_HEADS, slot_picks)
    part_got, stats_all = exchange("blk", "sg", part_send, stats)
    stats_all = stats_all.reshape(n_b, 2, QUERY_HEADS, slot_picks)
    full_max = jnp.max(stats_all[:, 0], axis=0)
    shrink = jnp.exp(stats_all[:, 0] - full_max[None])
    full_sum = jnp.sum(stats_all[:, 1] * shrink, axis=0)
    log_total = full_max + jnp.log(full_sum)
    share_of = shrink / full_sum[None]
    heads_row = QUERY_HEADS // n_u
    cut_head = (b * out_cut) // HEAD_WIDTH
    my_share = lax.dynamic_index_in_dim(
        share_of.reshape(n_b, n_u, heads_row, slot_picks), cut_head, 2, keepdims=False
    )
    attended_wide = jnp.sum(
        part_got.astype(f32).reshape(n_b, slot_picks, n_u, out_cut)
        * my_share.transpose(0, 2, 1)[..., None],
        axis=0,
    )
    attended = attended_wide.astype(bf16).reshape(slot_picks, n_u * out_cut)

    def sum_to_picks(partial):
        (got,) = exchange("blk", "s", partial.astype(bf16).reshape(n_b, picks, MODEL_WIDTH))
        return jnp.sum(got.astype(f32), axis=0)

    def to_slot(rows):
        (got,) = exchange("blk", "g", rows)
        return got.reshape(slot_picks, rows.shape[1])

    after_attn = embedded_picks + sum_to_picks(mm(attended, out_weight))
    normed_mlp = to_slot((after_attn * inverse_root(after_attn) * gain_mlp).astype(bf16))
    gate_up = mm(normed_mlp, ff_weight)
    ff_mine = n_u * ff_share
    gate_part, up_part = gate_up[:, :ff_mine], gate_up[:, ff_mine:]
    sigmoid_gate = jax.nn.sigmoid(gate_part)
    activated = (gate_part * sigmoid_gate * up_part).astype(bf16)
    after_mlp = after_attn + sum_to_picks(mm(activated, contract_weight))
    final_rows = (after_mlp * inverse_root(after_mlp) * gain_final).astype(bf16)

    (final_all,) = exchange("ulysses", "g", to_slot(final_rows))
    final_all = final_all.reshape(all_picks, MODEL_WIDTH)
    table_low = embedding.astype(bf16)
    logits = mm_back(final_all, table_low)
    local_max = jnp.max(logits, axis=1)
    head_weights = jnp.exp(logits - local_max[:, None])
    local_sum = jnp.sum(head_weights, axis=1)
    head_rows = mm(head_weights.astype(bf16), table_low).astype(bf16)
    head_stats = jnp.stack([local_max, local_sum], axis=1).reshape(n_u, slot_picks, 2)

    def merge_rows(rows, stats_in):
        top = jnp.max(stats_in[..., 0], axis=0)
        factor = jnp.exp(stats_in[..., 0] - top[None])
        total = jnp.sum(stats_in[..., 1] * factor, axis=0)
        return (jnp.sum(rows.astype(f32) * factor[..., None], axis=0), top, total)

    got_rows, got_stats = exchange(
        "ulysses",
        "ss",
        head_rows.reshape(n_u, slot_picks, MODEL_WIDTH),
        jnp.pad(head_stats, ((0, 0), (0, 0), (0, 126))),
    )
    slot_rows, slot_top, slot_total = merge_rows(got_rows, got_stats)
    slot_stats = jnp.stack([slot_top, slot_total], axis=1).reshape(n_b, picks, 2)
    got_rows, got_stats = exchange(
        "blk",
        "ss",
        slot_rows.astype(bf16).reshape(n_b, picks, MODEL_WIDTH),
        jnp.pad(slot_stats, ((0, 0), (0, 0), (0, 126))),
    )
    mean_rows, top, total = merge_rows(got_rows, got_stats)
    log_norm = top + jnp.log(total)
    target_logit = jnp.sum(final_rows.astype(f32) * target_rows, axis=1)
    loss_local = -jnp.sum(my_weight * (target_logit - log_norm))
    count_local = jnp.sum(my_valid.astype(f32))
    grad_final = my_weight[:, None] * (mean_rows / total[:, None] - target_rows)

    grad_after_mlp, grad_gain_final = norm_back(after_mlp, gain_final, grad_final)
    (got_branch, norms_slot) = exchange(
        "blk",
        "gg",
        grad_after_mlp.astype(bf16),
        jnp.broadcast_to(log_norm[:, None], (picks, 128)),
    )
    grad_branch = got_branch.reshape(slot_picks, MODEL_WIDTH)
    (norms_all,) = exchange("ulysses", "g", norms_slot[:, :, 0].reshape(n_b, picks))
    norms_all = norms_all.reshape(all_picks)
    grad_contract = mm_outer(activated, grad_branch)
    grad_act = mm_back(grad_branch, contract_weight)
    grad_gate = grad_act * up_part * sigmoid_gate * (1.0 + gate_part * (1.0 - sigmoid_gate))
    grad_up = grad_act * gate_part * sigmoid_gate
    grad_gate_up = jnp.concatenate([grad_gate, grad_up], axis=1).astype(bf16)
    grad_expand = mm_outer(normed_mlp, grad_gate_up)
    grad_mid_part, grad_gain_mlp = norm_back(
        after_attn, gain_mlp, sum_to_picks(mm_back(grad_gate_up, ff_weight))
    )
    grad_after_attn = grad_after_mlp + grad_mid_part
    grad_attn_branch = to_slot(grad_after_attn.astype(bf16))
    grad_outflow = mm_outer(attended, grad_attn_branch)
    grad_attended = mm_back(grad_attn_branch, out_weight).astype(bf16)
    delta_part = jnp.sum(
        attended_wide * grad_attended.astype(f32).reshape(slot_picks, n_u, out_cut), axis=-1
    )
    got_attended, got_delta = exchange("blk", "gg", grad_attended, delta_part.T)
    grad_heads = (
        got_attended.reshape(n_b, slot_picks, n_u, out_cut)
        .transpose(1, 2, 0, 3)
        .reshape(slot_picks, QUERY_HEADS, HEAD_WIDTH)
        .transpose(1, 0, 2)
        .reshape(KEY_VALUE_HEADS, group * slot_picks, HEAD_WIDTH)
    )
    row_delta = jnp.sum(
        got_delta.transpose(1, 0, 2).reshape(QUERY_HEADS, HEAD_WIDTH // out_cut, slot_picks), axis=1
    ).reshape(KEY_VALUE_HEADS, group * slot_picks, 1)
    log_groups = log_total.reshape(KEY_VALUE_HEADS, group * slot_picks, 1)
    attn_probs = jnp.where(allowed, jnp.exp(scores - log_groups), 0.0)
    grad_probs = jnp.einsum("kqd,kjd->kqj", grad_heads, values_low, preferred_element_type=f32)
    grad_scores = (attn_probs * (grad_probs - row_delta) * score_scale).astype(bf16)
    grad_query_part = jnp.einsum(
        "kqj,kjd->kqd", grad_scores, key_rot, preferred_element_type=f32
    )
    grad_key_rot = jnp.einsum(
        "kqj,kqd->kjd", grad_scores, query_groups, preferred_element_type=f32
    ).astype(bf16)
    grad_value = jnp.einsum(
        "kqj,kqd->kjd", attn_probs.astype(bf16), grad_heads, preferred_element_type=f32
    ).astype(bf16)
    (got_query,) = exchange(
        "blk",
        "s",
        grad_query_part.astype(bf16)
        .reshape(n_b, heads_share, slot_picks, HEAD_WIDTH)
        .transpose(0, 2, 1, 3)
        .reshape(n_b, slot_picks, q_share),
    )
    grad_query_rot = jnp.sum(got_query.astype(f32), axis=0).astype(bf16).astype(f32)
    grad_query_raw, grad_gain_query = norm_back(
        query_raw,
        gain_query,
        rotate(grad_query_rot.reshape(slot_picks, heads_share, HEAD_WIDTH), query_tables, -1.0),
    )
    grad_query_low = grad_query_raw.reshape(slot_picks, q_share).astype(bf16)
    grad_q_weight = mm_outer(normed_slot, grad_query_low)
    grad_normed_picks = sum_to_picks(mm_back(grad_query_low, q_weight))
    grad_key_raw, grad_gain_key = norm_back(
        key_raw, gain_key, rotate(grad_key_rot.astype(f32).transpose(1, 0, 2), key_tables, -1.0)
    )
    grad_kv = jnp.concatenate(
        [
            grad_key_raw.reshape(block_len, -1).astype(bf16),
            grad_value.transpose(1, 0, 2).reshape(block_len, -1),
        ],
        axis=1,
    )
    grad_kv_weight = mm_outer(normed_in, grad_kv)
    back_both = spread_rows(
        pick_hot, jnp.concatenate([grad_normed_picks, grad_after_attn], axis=1)
    )
    grad_normed = mm_back(grad_kv, kv_weight) + back_both[:, :MODEL_WIDTH]
    grad_embed_part, grad_gain_attn = norm_back(embedded, gain_attn, grad_normed)
    grad_embedded = (back_both[:, MODEL_WIDTH:] + grad_embed_part).astype(bf16)

    grad_layer = jnp.concatenate(
        [
            jnp.concatenate([grad_q_weight, grad_expand], axis=1)
            .astype(bf16)
            .reshape(n_u, wide_rows, MODEL_WIDTH),
            grad_outflow.astype(bf16).reshape(n_u, out_share, MODEL_WIDTH),
            grad_contract.astype(bf16).reshape(n_u, ff_share, MODEL_WIDTH),
        ],
        axis=1,
    )
    got_layer = lax.all_to_all(grad_layer, "ulysses", 0, 0, tiled=True)
    sum_layer = jnp.sum(got_layer.astype(f32), axis=0)
    sum_outflow = sum_layer[wide_rows : wide_rows + out_share]
    sum_contract = sum_layer[wide_rows + out_share :]
    (got_cols,) = exchange("blk", "s", sum_layer[:wide_rows].astype(bf16).reshape(n_b, in_rows, mixed_share))
    got_cols = got_cols.astype(f32)
    sum_q = got_cols[:, :, :q_share].transpose(1, 0, 2).reshape(in_rows, QUERY_WIDTH)
    sum_expand = (
        got_cols[:, :, q_share:]
        .reshape(n_b, in_rows, 2, n_u, ff_share)
        .transpose(1, 2, 3, 0, 4)
        .reshape(in_rows, 2 * FF)
    )
    kv_first = lax.all_to_all(
        grad_kv_weight.astype(bf16).reshape(n_u, in_block, -1), "ulysses", 0, 0, tiled=True
    )
    kv_second = lax.all_to_all(
        jnp.sum(kv_first.astype(f32), axis=0).astype(bf16).reshape(n_b, in_rows, -1),
        "blk",
        0,
        0,
        tiled=True,
    )
    sum_kv = jnp.sum(kv_second.astype(f32), axis=0)
    sum_inflow = jnp.concatenate([sum_q, sum_kv], axis=1)
    grad_scales = jnp.concatenate(
        [grad_gain_attn, grad_gain_mlp, grad_gain_final, grad_gain_query, grad_gain_key]
    )
    (got_scales,) = exchange(
        "all",
        "s",
        jnp.pad(grad_scales.reshape(n_all, scale_share), ((0, 0), (0, 128 - scale_share))).reshape(
            n_all, 1, 128
        ),
    )
    sum_scales = jnp.sum(got_scales, axis=0)[0, :scale_share]

    def flat(array):
        return array.transpose(1, 0, 2).reshape(-1)

    target_local = flat(targets_all) - me * row_share
    is_target = target_local[:, None] == jnp.arange(row_share, dtype=jnp.int32)[None, :]
    grad_logits = (
        flat(weights_all)[:, None]
        * (jnp.exp(logits - norms_all[:, None]) - is_target.astype(f32))
    ).astype(bf16)
    table_head = mm_outer(grad_logits, final_all)
    rows_back = exchange.used
    exchange.used += 1

    def return_turn(state):
        turn, so_far = state
        ids, _, filled = slot_ids(turn)
        sent = mm_outer(landing(turn)[:block_len], grad_embedded).astype(bf16)
        mine = Exchanger()
        mine.used = rows_back
        (arrived,) = mine("all", "s", sent.reshape(n_all, slots, MODEL_WIDTH))
        row_of = jnp.where(filled, ids, -1).reshape(-1)
        hot = (
            jnp.arange(row_share, dtype=jnp.int32)[:, None] == row_of[None, :]
        ).astype(bf16)
        return (turn + 1, so_far + mm(hot, arrived.reshape(places, MODEL_WIDTH)))

    _, table_grad = lax.while_loop(
        lambda state: state[0] < rounds, return_turn, (jnp.int32(0), table_head)
    )

    raw_grads = (table_grad, sum_inflow, sum_outflow, sum_expand, sum_contract, sum_scales)
    squares = jnp.zeros((), f32)
    for grad_piece in raw_grads:
        squares = squares + jnp.sum(grad_piece * grad_piece)
    (totals,) = exchange(
        "all",
        "g",
        jnp.pad(jnp.stack([squares, count_local, loss_local]), (0, 125)).reshape(1, 128),
    )
    totals = jnp.sum(totals, axis=(0, 1))
    square_total, count_total, loss_total = totals[0], totals[1], totals[2]
    gradient_norm = jnp.sqrt(square_total) / count_total
    factor = jnp.minimum(1.0, clip_limit / gradient_norm) / count_total
    step_float = step_count[0].astype(f32)
    weights_now = (embedding, inflow, outflow, expand, contract, scales)
    firsts = (
        first_embedding,
        inflow_first_moment,
        first_outflow,
        first_expand,
        first_contract,
        first_scales,
    )
    seconds = (
        second_embedding,
        inflow_second_moment,
        second_outflow,
        second_expand,
        second_contract,
        second_scales,
    )
    outputs = [loss_total / count_total, gradient_norm]
    for position in range(6):
        change, new_first, new_second = adam_update(
            weights_now[position],
            firsts[position],
            seconds[position],
            raw_grads[position] * factor,
            learning_rates[position],
            weight_decays[position],
            step_float,
        )
        outputs = outputs + [change, new_first, new_second]
    return tuple(outputs)


def solution(mesh):
    rows = P(("ulysses", "blk"), None)
    flat_rows = P(("ulysses", "blk"))
    column = P(None, "blk")
    return jax.shard_map(
        local,
        mesh=mesh,
        in_specs=(column, P(), column, column, column, P()) + (rows,) * 15 + (flat_rows,) * 3,
        out_specs=(P(), P()) + (rows,) * 15 + (flat_rows,) * 3,
        check_vma=False,
    )
```

time: 3410 us -> 729 us (0.21)
  waiting for transfers between devices: 1230 us -> 45.4 us
  blocking collectives: 1100 us -> 0 us
  Pallas kernels: 0 us -> 383 us
  matrix products: 393 us -> 85.2 us
  other arithmetic: 399 us -> 117 us
  local copies, waits for them, and re-layouts: 211 us -> 48.2 us
    unnamed x4 -> x0, blocking collectives: 1030 us -> none
    all_gather x8 -> x2, waiting for transfers between devices: 928 us -> 18.7 us  [the longest x1 18.7 us: local(): lax.all_gather(inflow_low[:, QUERY_WIDTH:], BOTH, axis=0, tiled=True)]
    pallas_call x0 -> x26, Pallas kernels: none -> 383 us  [the longest x25 378 us: __call__(): pl.pallas_call(functools.partial(exchange_kernel, axis, blk_count, kinds)...]
    dot_general x47 -> x30, matrix products: 393 us -> 85.2 us  [the longest x10 40.3 us: mm(): lax.dot_general(left, right, (((1,), (0,)), ((), ())), preferred_element_...]
    reduce_scatter x6 -> x0, waiting for transfers between devices: 258 us -> none  [the longest x1 158 us: local(): lax.psum_scatter(grad_contract, ('ulysses', 'blk'), scatter_dimension=0,...]
    scatter-add x2 -> x0, other arithmetic: 154 us -> none  [the longest x1 152 us: local(): head_part.at[target_rows].add(token_rows).astype(jnp.bfloat16)]
    unnamed x235 -> x262, local copies, waits for them, and re-layouts: 135 us -> 10.7 us
    convert_element_type x9 -> x18, other arithmetic: 80.3 us -> 5.22 us  [the longest x1 1.23 us: local(): expand.astype(bf16).reshape(in_rows, 2, n_u, n_b, ff_share)]
  transfers between devices with their start and end apart: 22 -> 5, of which waited for: 18 -> 2; matrix products, arithmetic and copies ran while one was open for 43% -> 13% of each run, Pallas kernels for 0% -> 26%
where the time goes in v1:
time: 729 us; the launch traced here: 722 us
  Pallas kernels  383 us (53%)
  other arithmetic  117 us (16%)
  matrix products  85.2 us (12%)
  local copies, waits for them, and re-layouts  48.2 us (7%)
  waiting for transfers between devices  45.4 us (6%)
  between operations  29.2 us (4%)
  starting transfers between devices  14.3 us (2%)
    pallas_call x25, Pallas kernels, __call__(): pl.pallas_call(functools.partial(exchange_kernel, axis, blk_count, kinds)...  378 us
    mul x6, other arithmetic, adam_update(): -rate_value  55 us
    dot_general x10, matrix products, mm(): lax.dot_general(left, right, (((1,), (0,)), ((), ())), preferred_element_...  40.3 us
    all_to_all x1, waiting for transfers between devices, local(): lax.all_to_all(grad_kv_weight.astype(bf16).reshape(n_u, in_block, -1), 'u...  25.9 us
    all_gather x1, waiting for transfers between devices, local(): lax.all_gather(inflow_low[:, QUERY_WIDTH:], BOTH, axis=0, tiled=True)  18.7 us
    dot_general x7, matrix products, mm_outer(): lax.dot_general(left, right, (((0,), (0,)), ((), ())), preferred_element_...  17.5 us
    dot_general x6, matrix products, mm_back(): lax.dot_general(left, right, (((1,), (1,)), ((), ())), preferred_element_...  16.9 us
    reduce_sum x6, other arithmetic, local(): squares = squares + jnp.sum(grad_piece * grad_piece)  15.6 us
  transfers between devices with their start and end apart: 5, of which 2 were waited for; matrix products, arithmetic and copies ran while one was open for 13% of the time, Pallas kernels for 26%

profile of v1, /device:TPU:0, one launch (start us, length us, event | category | flops | bytes accessed | tf_op | source)
XLA Modules:
  0.0 722.5 jit_solution(14135228064251900068)
XLA Ops:
  12.5 14.3 %exchange_0.1 = bf16[8,32,1024]{2,1,0:T(8,128)(2,1)S(1)} custom-call(bf16[8,32,1024]{2,1,0:T(8,128)(2,1)S(1)} %pad_maximum_fusion.6.refs_0_), custom_call_target="tpu_custom_call" | custom-call | tf_op jit(solution)/shard_map/exchange_0/pallas_call | solution.py:192
  28.7 8.1 %exchange_1.1 = f32[8,4,304]{2,1,0:T(4,128)S(1)} custom-call(f32[4,304]{1,0:T(4,128)S(1)} %pad_maximum_fusion.15.refs_0_), custom_call_target="tpu_custom_call" | custom-call | tf_op jit(solution)/shard_map/exchange_1/pallas_call | solution.py:192
  39.5 8.7 %exchange_2.1 = f32[32,1,128]{2,1,0:T(1,128)S(1)} custom-call(f32[1,128]{1,0:T(1,128)S(1)} %pad_bitcast_fusion.refs_0_), custom_call_target="tpu_custom_call" | custom-call | tf_op jit(solution)/shard_map/exchange_2/pallas_call | solution.py:192
  48.7 54.9 %while.20 = (s32[]{:T(128)}, f32[272,1024]{1,0:T(8,128)S(1)}, s32[]{:T(128)}, s32[272]{0:T(512)S(1)}, s32[272]{0:T(512)S(1)}, /*index=5*/s32[32]{0:T(128)S(1)}, ...) while((s32[]{:T(128)}, f32[272,1024]{1,0:T(8,128)S(1)}, ...), condition=%wide.region_6.7_spmd, body=%wide.region_4.6_spmd.sunk | while | flops 572097472 | bytes 4438417 | solution.py:420
  49.5 5.4 lookup.1
  55.0 47.6 %exchange_3.1 = bf16[32,32,1024]{2,1,0:T(8,128)(2,1)S(1)} custom-call(bf16[32,32,1024]{2,1,0:T(8,128)(2,1)S(1)} %bitcast.281), custom_call_target="tpu_custom_call" | custom-call | tf_op jit(solution)/shard_map/while/body/exchange_3/pallas_call | solution.py:192
  105.8 12.7 %exchange_4.1 = bf16[8,16,1024]{2,1,0:T(8,128)(2,1)S(1)} custom-call(bf16[16,1024]{1,0:T(8,128)(2,1)S(1)} %slice.359.refs_0_), custom_call_target="tpu_custom_call" | custom-call | tf_op jit(solution)/shard_map/exchange_4/pallas_call | solution.py:192
  128.9 2.7 slice.238
  134.3 14.2 %exchange_5.1 = bf16[8,128,256]{2,1,0:T(8,128)(2,1)S(1)} custom-call(bf16[128,256]{1,0:T(8,128)(2,1)S(1)} %copy.369.refs_0_), custom_call_target="tpu_custom_call" | custom-call | tf_op jit(solution)/shard_map/exchange_5/pallas_call | solution.py:192
  151.1 18.7 %all-gather.4.cloned.1.call-done = bf16[1024,2048]{1,0:T(8,128)(2,1)} async-done(((bf16[32,2048]{1,0:T(8,128)(2,1)}), bf16[1024,2048]{1,0:T(8,128)(2,1)}) %all-gather.4.cloned.1.call-update) | async-done | bytes 4194320 | tf_op jit(solution)/shard_map/all_gather | solution.py:304
  169.8 3.4 fusion.122
  181.8 13.6 %exchange_6.1 = (bf16[8,128,256]{2,1,0:T(8,128)(2,1)S(1)}, f32[8,32,128]{2,1,0:T(8,128)S(1)}) custom-call(bf16[8,128,256]{2,1,0:T(8,128)(2,1)S(1)} %copy.327.refs_0_, f32[32,128]{1,0:T(8,128)S(1)} %reshape.754.refs_1_), custom_call_target="tpu_custom_call" | custom-call | tf_op jit(solution)/shard_map/exchange_6/pallas_call | solution.py:192
  201.1 11.9 %exchange_7.1 = bf16[8,16,1024]{2,1,0:T(8,128)(2,1)S(1)} custom-call(bf16[8,16,1024]{2,1,0:T(8,128)(2,1)S(1)} %bitcast.298), custom_call_target="tpu_custom_call" | custom-call | tf_op jit(solution)/shard_map/exchange_7/pallas_call | solution.py:192
  215.4 9.1 %exchange_8.1 = bf16[8,16,1024]{2,1,0:T(8,128)(2,1)S(1)} custom-call(bf16[16,1024]{1,0:T(8,128)(2,1)S(1)} %multiply_convert_fusion.9.refs_0_), custom_call_target="tpu_custom_call" | custom-call | tf_op jit(solution)/shard_map/exchange_8/pallas_call | solution.py:192
  225.7 9.1 %exchange_9.1 = bf16[8,16,1024]{2,1,0:T(8,128)(2,1)S(1)} custom-call(bf16[8,16,1024]{2,1,0:T(8,128)(2,1)S(1)} %bitcast.300), custom_call_target="tpu_custom_call" | custom-call | tf_op jit(solution)/shard_map/exchange_9/pallas_call | solution.py:192
  235.7 9.3 %exchange_10.1 = bf16[8,16,1024]{2,1,0:T(8,128)(2,1)S(1)} custom-call(bf16[16,1024]{1,0:T(8,128)(2,1)S(1)} %get-tuple-element.229.refs_0_), custom_call_target="tpu_custom_call" | custom-call | tf_op jit(solution)/shard_map/exchange_10/pallas_call | solution.py:192
  244.9 15.4 %exchange_11.1 = bf16[4,128,1024]{2,1,0:T(8,128)(2,1)S(1)} custom-call(bf16[128,1024]{1,0:T(8,128)(2,1)S(1)} %bitcast.295), custom_call_target="tpu_custom_call" | custom-call | tf_op jit(solution)/shard_map/exchange_11/pallas_call | solution.py:192
  260.4 10.0 %fusion.121 = (f32[512]{0:T(512)S(1)}, f32[512,4748]{0,1:T(8,128)S(1)}) fusion(bf16[512,1024]{1,0:T(8,128)(2,1)S(1)} %bitcast.285, f32[4748,1024]{1,0:T(8,128)} %get-tuple-element.493), kind=kOutput, calls=%fused_computation.329 | convolution fusion | flops 4985931264 | bytes 30222336 | tf_op jit(solution)/shard_map/dot_general | solution.py:81
  270.5 13.6 %fusion.22 = bf16[512,1024]{1,0:T(8,128)(2,1)S(1)} fusion(f32[4748,1024]{1,0:T(8,128)} %get-tuple-element.493, f32[512,4748]{0,1:T(8,128)S(1)} %get-tuple-element.281, f32[512]{0:T(512)S(1)} %get-tuple-element.280), kind=kOutput, calls=%fused_computation.54 | convolution fusion | flops 4988887040 | bytes 30222336 | tf_op jit(solution)/shard_map/dot_general | solution.py:73
  285.7 17.2 %exchange_12.1 = (bf16[4,128,1024]{2,1,0:T(8,128)(2,1)S(1)}, f32[4,128,128]{2,1,0:T(8,128)S(1)}) custom-call(bf16[4,128,1024]{2,1,0:T(8,128)(2,1)S(1)} %bitcast.294, f32[4,128,128]{2,1,0:T(8,128)S(1)} %pad.21.refs_1_), custom_call_target="tpu_custom_call" | custom-call | tf_op jit(solution)/shard_map/exchange_12/pallas_call | solution.py:192
  304.7 10.2 %exchange_13.1 = (bf16[8,16,1024]{2,1,0:T(8,128)(2,1)S(1)}, f32[8,16,128]{2,1,0:T(8,128)S(1)}) custom-call(bf16[8,16,1024]{2,1,0:T(8,128)(2,1)S(1)} %bitcast.293, f32[8,16,128]{2,1,0:T(8,128)S(1)} %pad.22.refs_1_), custom_call_target="tpu_custom_call" | custom-call | tf_op jit(solution)/shard_map/exchange_13/pallas_call | solution.py:192
  319.0 10.5 %exchange_14.1 = (bf16[8,16,1024]{2,1,0:T(8,128)(2,1)S(1)}, f32[8,16,128]{2,1,0:T(8,128)S(1)}) custom-call(bf16[16,1024]{1,0:T(8,128)(2,1)S(1)} %fusion.80.refs_0_, f32[16,128]{1,0:T(8,128)S(1)} %broadcast_in_dim.88.refs_1_), custom_call_target="tpu_custom_call" | custom-call | tf_op jit(solution)/shard_map/exchange_14/pallas_call | solution.py:192
  330.7 9.7 %exchange_16.1 = bf16[8,16,1024]{2,1,0:T(8,128)(2,1)S(1)} custom-call(bf16[8,16,1024]{2,1,0:T(8,128)(2,1)S(1)} %bitcast.304), custom_call_target="tpu_custom_call" | custom-call | tf_op jit(solution)/shard_map/exchange_16/pallas_call | solution.py:192
  341.9 9.4 %exchange_17.1 = bf16[8,16,1024]{2,1,0:T(8,128)(2,1)S(1)} custom-call(bf16[16,1024]{1,0:T(8,128)(2,1)S(1)} %get-tuple-element.222.refs_0_), custom_call_target="tpu_custom_call" | custom-call | tf_op jit(solution)/shard_map/exchange_17/pallas_call | solution.py:192
  351.8 14.3 %exchange_18.1 = (bf16[8,128,256]{2,1,0:T(8,128)(2,1)S(1)}, f32[8,4,128]{2,1,0:T(4,128)S(1)}) custom-call(bf16[128,256]{1,0:T(8,128)(2,1)S(1)} %get-tuple-element.283.refs_0_, f32[4,128]{1,0:T(4,128)S(1)} %bitcast.309), custom_call_target="tpu_custom_call" | custom-call | tf_op jit(solution)/shard_map/exchange_18/pallas_call | solution.py:192
  369.3 3.0 convolution_convert_fusion.4
  372.3 2.2 multiply_convert_fusion.2
  379.5 4.7 exchange_15.1
  385.7 14.5 %exchange_19.1 = bf16[8,128,256]{2,1,0:T(8,128)(2,1)S(1)} custom-call(bf16[8,128,256]{2,1,0:T(8,128)(2,1)S(1)} %reshape.772.refs_0_), custom_call_target="tpu_custom_call" | custom-call | tf_op jit(solution)/shard_map/exchange_19/pallas_call | solution.py:192
  406.0 10.9 %exchange_20.1 = bf16[8,16,1024]{2,1,0:T(8,128)(2,1)S(1)} custom-call(bf16[8,16,1024]{2,1,0:T(8,128)(2,1)S(1)} %bitcast.299), custom_call_target="tpu_custom_call" | custom-call | tf_op jit(solution)/shard_map/exchange_20/pallas_call | solution.py:192
  423.7 3.3 convolution_convert_fusion.1
  427.0 5.0 all-to-all-start.1
  436.4 4.2 multiply_reduce_fusion.2
  444.5 10.0 %fusion.11 = f32[4748,1024]{1,0:T(8,128)} fusion(bf16[512,1024]{1,0:T(8,128)(2,1)S(1)} %bitcast.286, f32[512,4748]{0,1:T(8,128)S(1)} %bitcast.311, s32[512]{0:T(512)S(1)} %copy-done.111, f32[512]{0:T(512)S(1)} %copy-done.113, f32[512]{0:T(512)S(1)} %copy-done.112), kind=kOutput, calls=%fused_computation.32 | convolution fusion | flops 4993224704 | bytes 30226432 | tf_op jit(solution)/shard_map/dot_general | solution.py:77
  454.4 25.9 %all-to-all-done.1 = bf16[4,256,2048]{2,1,0:T(8,128)(2,1)} async-done(((bf16[4,256,2048]{2,1,0:T(8,128)(2,1)}), bf16[4,256,2048]{2,1,0:T(8,128)(2,1)}, u32[]{:S(2)}, u32[]{:S(2)}) %all-to-all-start.1) | async-done | bytes 4194336 | tf_op jit(solution)/shard_map/all_to_all | solution.py:673
  480.4 4.7 all-to-all-start
  485.1 85.2 %while.21 = (s32[]{:T(128)}, f32[4748,1024]{1,0:T(8,128)}, s32[]{:T(128)}, s32[32]{0:T(128)S(1)}, pred[32,272]{1,0:T(32,128)(4,1)S(1)}, /*index=5*/s32[32,272]{1...) while((s32[]{:T(128)}, f32[4748,1024]{1,0:T(8,128)}, ...), condition=%wide.region_39.40_spmd, body=%wide.region_37.39_spmd.sunk | while | flops 10506300416 | bytes 43741648 | solution.py:723
  486.0 64.0 %exchange_23.1 = bf16[32,32,1024]{2,1,0:T(8,128)(2,1)S(1)} custom-call(bf16[32,32,1024]{2,1,0:T(8,128)(2,1)S(1)} %bitcast.282), custom_call_target="tpu_custom_call" | custom-call | tf_op jit(solution)/shard_map/while/body/exchange_23/pallas_call | solution.py:192
  550.9 19.5 %fusion.170 = f32[4748,1024]{1,0:T(8,128)} fusion(f32[4748,1024]{1,0:T(8,128)} %get-tuple-element.468, bf16[1024,1024]{1,0:T(8,128)(2,1)S(1)} %bitcast.283, s32[1024]{0:T(1024)S(1)} %select_n.180), kind=kOutput, calls=%fused_computation.9.clone.1 | convolution fusion | flops 9967001600 | bytes 40996864 | tf_op jit(solution)/shard_map/while/body/dot_general | solution.py:73
  575.9 9.1 %exchange_22.1 = f32[32,1,128]{2,1,0:T(1,128)S(1)} custom-call(f32[32,1,128]{2,1,0:T(1,128)S(1)} %bitcast.307), custom_call_target="tpu_custom_call" | custom-call | tf_op jit(solution)/shard_map/exchange_22/pallas_call | solution.py:192
  585.1 4.3 reduce_sum.502
  589.3 4.5 all-to-all-start.2
  594.4 12.1 %multiply_reduce_fusion = f32[]{:T(128)} fusion(f32[4748,1024]{1,0:T(8,128)} %get-tuple-element.147), kind=kLoop, calls=%fused_computation.24 | loop fusion | flops 9723903 | bytes 19447812 | tf_op jit(solution)/shard_map/reduce_sum | solution.py:730
  606.6 2.8 convert_reduce_fusion
  609.5 18.6 %exchange_21.1 = bf16[8,32,1024]{2,1,0:T(8,128)(2,1)S(1)} custom-call(bf16[8,32,1024]{2,1,0:T(8,128)(2,1)S(1)} %bitcast.292), custom_call_target="tpu_custom_call" | custom-call | tf_op jit(solution)/shard_map/exchange_21/pallas_call | solution.py:192
  637.9 10.7 %exchange_24.1 = f32[32,1,128]{2,1,0:T(1,128)S(1)} custom-call(f32[1,128]{1,0:T(1,128)S(1)} %fusion.89.refs_0_), custom_call_target="tpu_custom_call" | custom-call | tf_op jit(solution)/shard_map/exchange_24/pallas_call | solution.py:192
  657.9 47.8 %add_multiply_fusion = (f32[4748,1024]{1,0:T(8,128)}, f32[4748,1024]{1,0:T(8,128)}, f32[4748,1024]{1,0:T(8,128)}) fusion(f32[4748,1024]{1,0:T(8,128)} %get-tuple-element.493, f32[]{:T(128)} %bitcast.100, f32[]{:T(128)} %bitcast.99, f32[4748,1024]{1,0:T(8,128)} %get-tuple-element.147, f32[]{:T(128)S(6)} %div.228, f32[4748,1024]{1,0:T(8,128)} %param.36, ...), kind=kLoop, calls=%fused_computation.22 | loop fusion | flops 72929280 | bytes 136134672 | tf_op jit(solution)/shard_map/mul | solution.py:99
  705.8 2.7 add_multiply_fusion.2
  (494 shorter events, 109.4 us)
Async XLA Ops:
  7.2 119.9 %all-gather.6.cloned.1.call-start = ((), (), s32[]{:S(2)}) async-start(), calls=%async_computation.4 | async-start | bytes 4259840 | tf_op jit(solution)/shard_map/all_gather | solution.py:324
  12.4 16.1 %copy-start.103 = (s32[4,16]{1,0:T(4,128)S(1)}, s32[4,16]{1,0:T(4,128)}, u32[]{:S(2)}) copy-start(s32[4,16]{1,0:T(4,128)} %param.30) | copy-start | bytes 772
  12.5 16.1 %copy-start.116 = (s32[4,16]{1,0:T(4,128)S(1)}, s32[4,16]{1,0:T(4,128)}, u32[]{:S(2)}) copy-start(s32[4,16]{1,0:T(4,128)} %param.31) | copy-start | bytes 772
  12.5 16.1 %copy-start.106 = (s32[4,256]{1,0:T(4,128)S(1)}, s32[4,256]{1,0:T(4,128)}, u32[]{:S(2)}) copy-start(s32[4,256]{1,0:T(4,128)} %param.28) | copy-start | bytes 12292
  12.5 16.1 %copy-start.107 = (f32[4,16]{1,0:T(4,128)S(1)}, f32[4,16]{1,0:T(4,128)}, u32[]{:S(2)}) copy-start(f32[4,16]{1,0:T(4,128)} %param.32) | copy-start | bytes 772
  12.5 27.0 %copy-start.119 = (f32[104]{0:T(128)S(1)}, f32[104]{0:T(128)}, u32[]{:S(2)}) copy-start(f32[104]{0:T(128)} %param.49) | copy-start | bytes 1252
  27.8 142.0 %all-gather.4.cloned.1.call-start = ((), (), s32[]{:S(2)}) async-start(), calls=%async_computation.3 | async-start | bytes 4325376 | tf_op jit(solution)/shard_map/all_gather | solution.py:304
  104.2 130.8 %copy-start.3 = (f32[272,1024]{1,0:T(8,128)}, f32[272,1024]{1,0:T(8,128)S(1)}, u32[]{:S(2)}) copy-start(f32[272,1024]{1,0:T(8,128)S(1)} %get-tuple-element.136) | copy-start | bytes 3342340
  104.3 14.2 %copy-start.117 = (s32[4]{0:T(128)S(1)}, s32[4]{0:T(128)}, u32[]{:S(2)}) copy-start(s32[4]{0:T(128)} %param.29) | copy-start | bytes 52
  105.4 64.4 %copy-start.28 = (bf16[256,1024]{1,0:T(8,128)(2,1)}, bf16[256,1024]{1,0:T(8,128)(2,1)S(1)}, u32[]{:S(2)}) copy-start(bf16[256,1024]{1,0:T(8,128)(2,1)S(1)} %multiply_convert_fusion.3) | copy-start | bytes 1572868
  105.8 23.1 %copy-start.80 = (f32[16,2048]{1,0:T(8,128)}, f32[16,2048]{1,0:T(8,128)S(1)}, u32[]{:S(2)}) copy-start(f32[16,2048]{1,0:T(8,128)S(1)} %fusion.43) | copy-start | bytes 393220
  125.0 55.8 %copy-start.45 = (pred[256,256]{0,1:T(8,128)(4,1)}, pred[256,256]{0,1:T(8,128)(4,1)S(1)}, u32[]{:S(2)}) copy-start(pred[256,256]{0,1:T(8,128)(4,1)S(1)} %compare_and_fusion) | copy-start | bytes 196612
  134.0 17.1 %copy-start.38 = (f32[128,2,128]{0,2,1:T(8,128)}, f32[128,2,128]{0,2,1:T(8,128)S(1)}, u32[]{:S(2)}) copy-start(f32[128,2,128]{0,2,1:T(8,128)S(1)} %get-tuple-element.277) | copy-start | bytes 393220
  134.0 17.0 %copy-start.89 = (f32[128,2]{0,1:T(2,128)}, f32[128,2]{0,1:T(2,128)S(1)}, u32[]{:S(2)}) copy-start(f32[128,2]{0,1:T(2,128)S(1)} %add_rsqrt_fusion.1) | copy-start | bytes 3076
  151.1 26.5 %copy-start.13 = (bf16[8,256,128]{1,2,0:T(8,128)(2,1)}, bf16[8,256,128]{1,2,0:T(8,128)(2,1)S(1)}, u32[]{:S(2)}) copy-start(bf16[8,256,128]{1,2,0:T(8,128)(2,1)S(1)} %reshape.749) | copy-start | bytes 1572868
  199.5 25.0 %copy-start.20 = (bf16[4,256,1024]{2,1,0:T(8,128)(2,1)S(1)}, bf16[4,256,1024]{2,1,0:T(8,128)(2,1)}, u32[]{:S(2)}) copy-start(bf16[4,256,1024]{2,1,0:T(8,128)(2,1)} %copy-done.19) | copy-start | bytes 6291460
  199.6 14.5 %copy-start.64 = (bf16[128,256]{1,0:T(8,128)(2,1)}, bf16[128,256]{1,0:T(8,128)(2,1)S(1)}, u32[]{:S(2)}) copy-start(bf16[128,256]{1,0:T(8,128)(2,1)S(1)} %convert_element_type.309) | copy-start | bytes 196612
  201.1 23.9 %copy-start.25 = (bf16[4,96,1024]{2,1,0:T(8,128)(2,1)S(1)}, bf16[4,96,1024]{2,1,0:T(8,128)(2,1)}, u32[]{:S(2)}) copy-start(bf16[4,96,1024]{2,1,0:T(8,128)(2,1)} %slice.238) | copy-start | bytes 2359300
  214.0 20.8 %copy-start.47 = (f32[16,1024]{1,0:T(8,128)}, f32[16,1024]{1,0:T(8,128)S(1)}, u32[]{:S(2)}) copy-start(f32[16,1024]{1,0:T(8,128)S(1)} %get-tuple-element.233) | copy-start | bytes 196612
  234.9 25.4 %copy-start.49 = (f32[16,1024]{1,0:T(8,128)}, f32[16,1024]{1,0:T(8,128)S(1)}, u32[]{:S(2)}) copy-start(f32[16,1024]{1,0:T(8,128)S(1)} %get-tuple-element.231) | copy-start | bytes 196612
  235.0 35.5 %copy-start.96 = (f32[16]{0:T(128)}, f32[16]{0:T(128)S(1)}, u32[]{:S(2)}) copy-start(f32[16]{0:T(128)S(1)} %add_rsqrt_fusion.3) | copy-start | bytes 196
  270.4 13.7 %copy-start = (f32[512,4748]{0,1:T(8,128)}, f32[512,4748]{0,1:T(8,128)S(1)}, u32[]{:S(2)}) copy-start(f32[512,4748]{0,1:T(8,128)S(1)} %get-tuple-element.281) | copy-start | bytes 29171716
  285.5 18.0 %copy-start.79 = (f32[16,128]{1,0:T(8,128)S(1)}, f32[16,128]{1,0:T(8,128)}, u32[]{:S(2)}) copy-start(f32[16,128]{1,0:T(8,128)} %copy-done.78) | copy-start | bytes 24580
  285.5 18.0 %copy-start.85 = (f32[16,128]{1,0:T(8,128)S(1)}, f32[16,128]{1,0:T(8,128)}, u32[]{:S(2)}) copy-start(f32[16,128]{1,0:T(8,128)} %copy-done.84) | copy-start | bytes 24580
  302.9 12.3 %copy-start.108 = (f32[16]{0:T(128)S(1)}, f32[16]{0:T(128)}, u32[]{:S(2)}) copy-start(f32[16]{0:T(128)} %get-tuple-element.228) | copy-start | bytes 196
  302.9 14.4 %copy-start.50 = (f32[16,1024]{1,0:T(8,128)S(1)}, f32[16,1024]{1,0:T(8,128)}, u32[]{:S(2)}) copy-start(f32[16,1024]{1,0:T(8,128)} %copy-done.49) | copy-start | bytes 196612
  302.9 14.4 %copy-start.97 = (f32[16]{0:T(128)S(1)}, f32[16]{0:T(128)}, u32[]{:S(2)}) copy-start(f32[16]{0:T(128)} %copy-done.96) | copy-start | bytes 196
  302.9 26.6 %copy-start.26 = (bf16[4,96,1024]{2,1,0:T(8,128)(2,1)S(1)}, bf16[4,96,1024]{2,1,0:T(8,128)(2,1)}, u32[]{:S(2)}) copy-start(bf16[4,96,1024]{2,1,0:T(8,128)(2,1)} %slice.238) | copy-start | bytes 2359300
  304.4 25.2 %copy-start.67 = (f32[128,768]{1,0:T(8,128)S(1)}, f32[128,768]{1,0:T(8,128)}, u32[]{:S(2)}) copy-start(f32[128,768]{1,0:T(8,128)} %copy-done.66) | copy-start | bytes 1179652
  304.7 25.4 %copy-start.21 = (bf16[4,256,1024]{2,1,0:T(8,128)(2,1)S(1)}, bf16[4,256,1024]{2,1,0:T(8,128)(2,1)}, u32[]{:S(2)}) copy-start(bf16[4,256,1024]{2,1,0:T(8,128)(2,1)} %copy-done.19) | copy-start | bytes 6291460
  330.0 11.2 %copy-start.98 = (f32[16]{0:T(128)S(1)}, f32[16]{0:T(128)}, u32[]{:S(2)}) copy-start(f32[16]{0:T(128)} %copy-done.96) | copy-start | bytes 196
  330.0 21.3 %copy-start.37 = (bf16[4,64,1024]{2,1,0:T(8,128)(2,1)S(1)}, bf16[4,64,1024]{2,1,0:T(8,128)(2,1)}, u32[]{:S(2)}) copy-start(bf16[4,64,1024]{2,1,0:T(8,128)(2,1)} %slice.233) | copy-start | bytes 1572868
  330.0 21.3 %copy-start.55 = (f32[128,256]{1,0:T(8,128)S(1)}, f32[128,256]{1,0:T(8,128)}, u32[]{:S(2)}) copy-start(f32[128,256]{1,0:T(8,128)} %copy-done.54) | copy-start | bytes 393220
  351.7 16.9 %copy-start.88 = (f32[16,128]{1,0:T(8,128)S(1)}, f32[16,128]{1,0:T(8,128)}, u32[]{:S(2)}) copy-start(f32[16,128]{1,0:T(8,128)} %log_add_fusion) | copy-start | bytes 24580
  351.7 17.7 %copy-start.46 = (pred[256,256]{0,1:T(8,128)(4,1)S(1)}, pred[256,256]{0,1:T(8,128)(4,1)}, u32[]{:S(2)}) copy-start(pred[256,256]{0,1:T(8,128)(4,1)} %copy-done.45) | copy-start | bytes 196612
  384.8 17.2 %copy-start.90 = (f32[128,2]{0,1:T(2,128)S(1)}, f32[128,2]{0,1:T(2,128)}, u32[]{:S(2)}) copy-start(f32[128,2]{0,1:T(2,128)} %copy-done.89) | copy-start | bytes 3076
  385.7 31.3 %copy-start.34 = (bf16[8,256,128]{1,2,0:T(8,128)(2,1)S(1)}, bf16[8,256,128]{1,2,0:T(8,128)(2,1)}, u32[]{:S(2)}) copy-start(bf16[8,256,128]{1,2,0:T(8,128)(2,1)} %convolution_convert_fusion.4) | copy-start | bytes 1572868
  400.3 17.7 %copy-start.57 = (f32[256,64]{1,0:T(8,128)S(1)}, f32[256,64]{1,0:T(8,128)}, u32[]{:S(2)}) copy-start(f32[256,64]{1,0:T(8,128)} %get-tuple-element.269) | copy-start | bytes 196612
  400.4 17.6 %copy-start.10 = (f32[256,8,128]{2,0,1:T(8,128)S(1)}, f32[256,8,128]{2,0,1:T(8,128)}, u32[]{:S(2)}) copy-start(f32[256,8,128]{2,0,1:T(8,128)} %fusion.32) | copy-start | bytes 3145732
  427.0 53.4 %all-to-all-start.1 = ((bf16[4,256,2048]{2,1,0:T(8,128)(2,1)}), bf16[4,256,2048]{2,1,0:T(8,128)(2,1)}, u32[]{:S(2)}, u32[]{:S(2)}) async-start(bf16[4,256,2048]{2,1,0:T(8,128)(2,1)} %bitcast.312), calls=%async_computation.1 | async-start | bytes 8388608 | tf_op jit(solution)/shard_map/all_to_all | solution.py:673
  454.4 30.7 %copy-start.12 = (s32[32,272]{1,0:T(8,128)S(1)}, s32[32,272]{1,0:T(8,128)}, u32[]{:S(2)}) copy-start(s32[32,272]{1,0:T(8,128)} %copy-done.11) | copy-start | bytes 104452
  454.4 30.7 %copy-start.83 = (s32[32]{0:T(128)S(1)}, s32[32]{0:T(128)}, u32[]{:S(2)}) copy-start(s32[32]{0:T(128)} %copy-done.82) | copy-start | bytes 388
  480.4 109.0 %all-to-all-start = ((bf16[4,416,1024]{2,1,0:T(8,128)(2,1)}), bf16[4,416,1024]{2,1,0:T(8,128)(2,1)}, u32[]{:S(2)}, u32[]{:S(2)}) async-start(bf16[4,416,1024]{2,1,0:T(8,128)(2,1)} %pad_maximum_fusion), calls=%async_computation | async-start | bytes 6815744 | tf_op jit(solution)/shard_map/all_to_all | solution.py:660
  589.3 41.0 %all-to-all-start.2 = ((bf16[8,32,2048]{2,1,0:T(8,128)(2,1)}), bf16[8,32,2048]{2,1,0:T(8,128)(2,1)}, u32[]{:S(2)}, u32[]{:S(2)}) async-start(bf16[8,32,2048]{2,1,0:T(8,128)(2,1)} %bitcast.87), calls=%async_computation.2 | async-start | bytes 2097152 | tf_op jit(solution)/shard_map/all_to_all | solution.py:676
  628.2 24.4 %copy-start.32 = (f32[8,4,8,256]{3,2,0,1:T(8,128)}, f32[8,4,8,256]{3,2,0,1:T(8,128)S(1)}, u32[]{:S(2)}) copy-start(f32[8,4,8,256]{3,2,0,1:T(8,128)S(1)} %copy.378) | copy-start | bytes 786436
  657.9 47.9 %copy-start.31 = (f32[32,2048]{1,0:T(8,128)S(1)}, f32[32,2048]{1,0:T(8,128)}, u32[]{:S(2)}) copy-start(f32[32,2048]{1,0:T(8,128)} %copy-done.30) | copy-start | bytes 786436
  657.9 47.9 %copy-start.33 = (f32[8,4,8,256]{3,2,0,1:T(8,128)S(1)}, f32[8,4,8,256]{3,2,0,1:T(8,128)}, u32[]{:S(2)}) copy-start(f32[8,4,8,256]{3,2,0,1:T(8,128)} %copy-done.32) | copy-start | bytes 786436
  657.9 47.9 %copy-start.40 = (f32[32,4096]{1,0:T(8,128)S(1)}, f32[32,4096]{1,0:T(8,128)}, u32[]{:S(2)}) copy-start(f32[32,4096]{1,0:T(8,128)} %param.37) | copy-start | bytes 1572868
  (83 other events, 239.1 us)
Sparse Core Ops, SparseCore 0:
  27.9 72.9 all-gather.5
  104.4 65.3 all-gather.3

commit v2 on v1

v2 whole, which is shorter than its diff:
```python
import functools
import math

import jax
import jax.numpy as jnp
from jax import lax
from jax.experimental import pallas as pl
from jax.experimental.pallas import tpu as pltpu
from jax.sharding import PartitionSpec as P

MODEL_WIDTH = 1024
QUERY_HEADS = 16
KEY_VALUE_HEADS = 8
HEAD_WIDTH = 128
FF = 3072
QUERY_WIDTH = QUERY_HEADS * HEAD_WIDTH

norm_eps = 1e-06
rope_base = 1000000.0
clip_limit = 0.01
beta_first = 0.9
beta_second = 0.95
adam_eps = 1e-08
learning_rates = (0.01, 0.003, 0.07, 0.003, 0.002, 0.01)
weight_decays = (0.1, 0.1, 0.1, 0.1, 0.1, 0.0)
masked_score = -1e30

bf16 = jnp.bfloat16
f32 = jnp.float32
BOTH = ("ulysses", "blk")


def inverse_root(values):
    return lax.rsqrt(jnp.mean(values * values, axis=-1, keepdims=True) + norm_eps)


def norm_back(inputs, gain_vec, upstream):
    root_scale = inverse_root(inputs)
    unit_rows = inputs * root_scale
    weighted = upstream * gain_vec
    grad_inputs = root_scale * (
        weighted - unit_rows * jnp.mean(weighted * unit_rows, axis=-1, keepdims=True)
    )
    grad_gain = jnp.sum((upstream * unit_rows).reshape(-1, gain_vec.shape[-1]), axis=0)
    return (grad_inputs, grad_gain)


def rope_angles(positions):
    half_width = HEAD_WIDTH // 2
    frequency = rope_base ** (
        -(jnp.arange(half_width, dtype=jnp.int32).astype(f32) * 2.0 / HEAD_WIDTH)
    )
    angles = positions.astype(f32)[:, None] * frequency[None, :]
    return (jnp.cos(angles), jnp.sin(angles))


def rotate(values, tables, sign_value):
    half_width = values.shape[-1] // 2
    front_half = values[..., :half_width]
    back_half = values[..., half_width:]
    cosine_part = tables[0][:, None, :]
    sine_part = tables[1][:, None, :] * sign_value
    return jnp.concatenate(
        [
            front_half * cosine_part - back_half * sine_part,
            back_half * cosine_part + front_half * sine_part,
        ],
        axis=-1,
    )


def mm(left, right):
    return lax.dot_general(left, right, (((1,), (0,)), ((), ())), preferred_element_type=f32)


def mm_outer(left, right):
    return lax.dot_general(left, right, (((0,), (0,)), ((), ())), preferred_element_type=f32)


def mm_back(left, right):
    return lax.dot_general(left, right, (((1,), (1,)), ((), ())), preferred_element_type=f32)


def spread_rows(onehot, rows):
    return lax.dot_general(
        onehot.astype(f32),
        rows,
        (((0,), (0,)), ((), ())),
        precision=lax.Precision.HIGHEST,
        preferred_element_type=f32,
    )


def adam_update(weight_now, first_now, second_now, gradient, rate_value, decay_value, step_float):
    new_first = beta_first * first_now + (1.0 - beta_first) * gradient
    new_second = beta_second * second_now + (1.0 - beta_second) * gradient * gradient
    first_hat = new_first / (1.0 - beta_first**step_float)
    second_hat = new_second / (1.0 - beta_second**step_float)
    change = -rate_value * (
        first_hat / (jnp.sqrt(second_hat) + adam_eps) + decay_value * weight_now
    )
    return (change, new_first, new_second)


def place_of(axis, blk_count, peer):
    if axis == "all":
        return {"ulysses": peer // blk_count, "blk": lax.rem(peer, blk_count)}
    return {axis: peer}


def rank_of(axis, blk_count):
    row, column = lax.axis_index("ulysses"), lax.axis_index("blk")
    return {"ulysses": row, "blk": column, "all": row * blk_count + column}[axis]


def greet(axes, blk_count, counts):
    barrier = pltpu.get_barrier_semaphore()
    axes = ("all",) if "all" in axes else tuple(axes)
    total = 0
    for axis in axes:
        me, count = rank_of(axis, blk_count), counts[axis]

        def call(step, carry, axis=axis, me=me, count=count):
            pl.semaphore_signal(
                barrier,
                inc=1,
                device_id=place_of(axis, blk_count, lax.rem(me + step, count)),
                device_id_type=pl.DeviceIdType.MESH,
            )
            return carry

        lax.fori_loop(1, count, call, 0)
        total += count - 1
    pl.semaphore_wait(barrier, total)


def each(count, body, first=0):
    def step(k, carry):
        body(k)
        return carry

    lax.fori_loop(first, count, step, 0)


def remote(source, target, send_sem, recv_sem, device_id):
    return pltpu.make_async_remote_copy(
        src_ref=source,
        dst_ref=target,
        send_sem=send_sem,
        recv_sem=recv_sem,
        device_id=device_id,
        device_id_type=pl.DeviceIdType.MESH,
    )


class Part:
    def __init__(self, axis, kind, source, landing, send_sems, recv_sems, own_sem, blk_count):
        self.axis, self.kind, self.blk_count = axis, kind, blk_count
        self.source, self.landing = source, landing
        self.send_sems, self.recv_sems, self.own_sem = send_sems, recv_sems, own_sem
        self.me, self.count = rank_of(axis, blk_count), landing.shape[0]

    def copy(self, step):
        peer = lax.rem(self.me + step, self.count)
        return remote(
            self.source.at[peer] if self.kind == "s" else self.source,
            self.landing.at[self.me],
            self.send_sems.at[step],
            self.recv_sems.at[step],
            place_of(self.axis, self.blk_count, peer),
        )

    def own(self):
        return pltpu.make_async_copy(
            self.source.at[self.me] if self.kind == "s" else self.source,
            self.landing.at[self.me],
            self.own_sem,
        )

    def start(self):
        each(self.count, lambda step: self.copy(step).start(), 1)
        self.own().start()

    def finish(self):
        self.own().wait()
        each(self.count, lambda step: self.copy(step).wait(), 1)


def sems(count):
    return [
        pltpu.SemaphoreType.DMA((count,)),
        pltpu.SemaphoreType.DMA((count,)),
        pltpu.SemaphoreType.DMA,
    ]


def exchange_kernel(plan, blk_count, counts, *refs):
    parts = len(plan)
    entries = [
        Part(axis, kind, refs[k], refs[parts + k], *refs[2 * parts + 3 * k :][:3], blk_count)
        for k, (axis, kind) in enumerate(plan)
    ]
    greet({axis for axis, _ in plan}, blk_count, counts)
    for entry in entries:
        entry.start()
    for entry in entries:
        entry.finish()


def axis_counts():
    n_u, n_b = lax.axis_size("ulysses"), lax.axis_size("blk")
    return {"ulysses": n_u, "blk": n_b, "all": n_u * n_b}


VMEM = pl.BlockSpec(memory_space=pltpu.VMEM)


def remote_call(kernel, collective_id, shapes, scratch, arrays, name):
    return pl.pallas_call(
        kernel,
        out_shape=shapes,
        in_specs=[VMEM] * len(arrays),
        out_specs=[VMEM] * len(shapes),
        scratch_shapes=scratch,
        compiler_params=pltpu.CompilerParams(
            collective_id=collective_id,
            has_side_effects=True,
            vmem_limit_bytes=40 * 1024 * 1024,
        ),
        name=name,
    )(*arrays)


class Exchanger:
    def __init__(self):
        self.used = 0

    def next_id(self):
        self.used += 1
        return self.used - 1

    def many(self, plan, *arrays, collective_id=None):
        counts = axis_counts()
        shapes = [
            jax.ShapeDtypeStruct(
                array.shape if kind == "s" else (counts[axis],) + array.shape, array.dtype
            )
            for (axis, kind), array in zip(plan, arrays)
        ]
        scratch = []
        for axis, _ in plan:
            scratch += sems(counts[axis])
        if collective_id is None:
            collective_id = self.next_id()
        return remote_call(
            functools.partial(exchange_kernel, plan, counts["blk"], counts),
            collective_id,
            shapes,
            scratch,
            arrays,
            "exchange_" + str(collective_id),
        )

    def __call__(self, axis, kinds, *arrays):
        return self.many(tuple((axis, kind) for kind in kinds), *arrays)


def start_kernel(
    blk_count,
    counts,
    rows_in,
    kv_in,
    q_in,
    ff_in,
    rows_out,
    kv_out,
    q_out,
    ff_out,
    q_split,
    z_send,
    z_recv,
    own_sem,
    xy_send,
    xy_recv,
    core_send,
    core_recv,
    *part_sems,
):
    u, b = lax.axis_index("ulysses"), lax.axis_index("blk")
    n_u, n_z = kv_out.shape[0], kv_out.shape[1]
    z, c = b // 2, lax.rem(b, 2)
    greet({"ulysses", "blk"}, blk_count, counts)
    rows = Part("ulysses", "s", rows_in, rows_out, *part_sems[0:3], blk_count)
    first_q = Part("blk", "s", q_in, q_split, *part_sems[3:6], blk_count)
    then_q = Part("ulysses", "g", q_split, q_out, *part_sems[6:9], blk_count)
    split_ff = Part("blk", "s", ff_in, ff_out, *part_sems[9:12], blk_count)

    def along_z(step):
        mine = kv_out.at[u, z, c]
        return remote(
            kv_in,
            mine,
            z_send.at[step],
            z_recv.at[step],
            {"blk": lax.rem(z + step, n_z) * 2 + c},
        )

    def own_copy():
        return pltpu.make_async_copy(kv_in, kv_out.at[u, z, c], own_sem)

    def block(hop, step):
        return kv_out.at[lax.rem(u - hop + n_u, n_u), lax.rem(z - step + n_z, n_z), c]

    def across(hop, step):
        place = block(0, step)
        return remote(
            place,
            place,
            xy_send.at[hop, step],
            xy_recv.at[hop, step],
            {"ulysses": lax.rem(u + hop, n_u)},
        )

    def to_core(hop, step):
        place = block(hop, step)
        return remote(
            place,
            place,
            core_send.at[hop, step],
            core_recv.at[hop, step],
            {"blk": z * 2 + 1 - c},
        )

    own_copy().start()
    each(n_z, lambda step: along_z(step).start(), 1)
    first_q.start()
    rows.start()
    own_copy().wait()
    each(n_u, lambda hop: across(hop, 0).start(), 1)
    to_core(0, 0).start()
    split_ff.start()

    def pass_on(step):
        along_z(step).wait_recv()
        each(n_u, lambda hop: across(hop, step).start(), 1)
        to_core(0, step).start()

    each(n_z, pass_on, 1)
    first_q.finish()
    then_q.start()

    def share(step):
        def one(hop):
            across(hop, step).wait_recv()
            to_core(hop, step).start()

        each(n_u, one, 1)

    each(n_z, share)
    rows.finish()
    split_ff.finish()
    then_q.finish()
    each(n_z, lambda step: along_z(step).wait_send(), 1)
    each(n_z, lambda step: each(n_u, lambda hop: across(hop, step).wait_send(), 1))
    each(n_z, lambda step: each(n_u, lambda hop: to_core(hop, step).wait()))


def start_call(exchange, rows, kv_low, q_cols, ff_cols):
    counts = axis_counts()
    n_u, n_b = counts["ulysses"], counts["blk"]
    n_z = n_b // 2
    dma = pltpu.SemaphoreType.DMA
    return remote_call(
        functools.partial(start_kernel, n_b, counts),
        exchange.next_id(),
        [
            jax.ShapeDtypeStruct(rows.shape, bf16),
            jax.ShapeDtypeStruct((n_u, n_z, 2) + kv_low.shape, bf16),
            jax.ShapeDtypeStruct((n_u,) + q_cols.shape, bf16),
            jax.ShapeDtypeStruct(ff_cols.shape, bf16),
        ],
        [
            pltpu.VMEM(q_cols.shape, bf16),
            dma((n_z,)),
            dma((n_z,)),
            dma,
            dma((n_u, n_z)),
            dma((n_u, n_z)),
            dma((n_u, n_z)),
            dma((n_u, n_z)),
        ]
        + sems(n_u)
        + sems(n_b)
        + sems(n_u)
        + sems(n_b),
        (rows, kv_low, q_cols, ff_cols),
        "start",
    )


def settle_kernel(
    blk_count,
    counts,
    kv_in,
    rows_in,
    q_in,
    gains_in,
    kv_out,
    rows_out,
    q_out,
    gains_out,
    kv_core,
    kv_pair,
    kv_cross,
    kv_plane,
    kv_line,
    q_got,
    q_sum,
    core_send,
    core_recv,
    xy_send,
    xy_recv,
    z_send,
    z_recv,
    *part_sems,
):
    u, b = lax.axis_index("ulysses"), lax.axis_index("blk")
    n_u, n_z = kv_in.shape[0], kv_in.shape[1]
    z, c = b // 2, lax.rem(b, 2)
    greet({"all"}, blk_count, counts)
    rows = Part("ulysses", "s", rows_in, rows_out, *part_sems[0:3], blk_count)
    first_q = Part("ulysses", "s", q_in, q_got, *part_sems[3:6], blk_count)
    then_q = Part("blk", "s", q_sum, q_out, *part_sems[6:9], blk_count)
    gains = Part("all", "s", gains_in, gains_out, *part_sems[9:12], blk_count)

    def place(hop, step):
        return (lax.rem(u + hop, n_u), lax.rem(z + step, n_z))

    def to_core(hop, step):
        row, line = place(hop, step)
        return remote(
            kv_in.at[row, line, 1 - c],
            kv_core.at[hop, step],
            core_send.at[hop, step],
            core_recv.at[hop, step],
            {"blk": z * 2 + 1 - c},
        )

    def across(hop, step):
        return remote(
            kv_pair.at[hop, step],
            kv_cross.at[hop, step],
            xy_send.at[hop, step],
            xy_recv.at[hop, step],
            {"ulysses": lax.rem(u + hop, n_u)},
        )

    def along_z(step):
        return remote(
            kv_plane.at[step],
            kv_line.at[step],
            z_send.at[step],
            z_recv.at[step],
            {"blk": lax.rem(z + step, n_z) * 2 + c},
        )

    each(n_z, lambda step: each(n_u, lambda hop: to_core(hop, step).start()))
    first_q.start()

    def add_pair(step):
        def one(hop):
            row, line = place(hop, step)
            to_core(hop, step).wait_recv()
            kv_pair[hop, step] = (
                kv_in[row, line, c].astype(f32) + kv_core[hop, step].astype(f32)
            ).astype(bf16)

        def forward(hop):
            one(hop)
            across(hop, step).start()

        one(0)
        each(n_u, forward, 1)

    each(n_z, add_pair, 1)
    add_pair(0)
    rows.start()
    gains.start()
    first_q.finish()
    q_sum[...] = jnp.sum(q_got[...].astype(f32), axis=0).astype(bf16)
    then_q.start()

    def plane_sum(step):
        total = kv_pair[0, step].astype(f32)
        for hop in range(1, n_u):
            across(hop, step).wait_recv()
            total = total + kv_cross[hop, step].astype(f32)
        return total

    def add_plane(step):
        kv_plane[step] = plane_sum(step).astype(bf16)
        along_z(step).start()

    each(n_z, add_plane, 1)
    total = plane_sum(0)
    for step in range(1, n_z):
        along_z(step).wait_recv()
        total = total + kv_line[step].astype(f32)
    kv_out[...] = total
    then_q.finish()
    gains.finish()
    rows.finish()
    each(n_z, lambda step: each(n_u, lambda hop: to_core(hop, step).wait_send()))
    each(n_z, lambda step: each(n_u, lambda hop: across(hop, step).wait_send(), 1))
    each(n_z, lambda step: along_z(step).wait_send(), 1)


def settle_call(exchange, kv_grad, rows, q_grad, gains):
    counts = axis_counts()
    n_u, n_b = counts["ulysses"], counts["blk"]
    n_z = n_b // 2
    block = kv_grad.shape[3:]
    dma = pltpu.SemaphoreType.DMA
    return remote_call(
        functools.partial(settle_kernel, n_b, counts),
        exchange.next_id(),
        [
            jax.ShapeDtypeStruct(block, f32),
            jax.ShapeDtypeStruct(rows.shape, bf16),
            jax.ShapeDtypeStruct(q_grad.shape[1:], bf16),
            jax.ShapeDtypeStruct(gains.shape, f32),
        ],
        [
            pltpu.VMEM((n_u, n_z) + block, bf16),
            pltpu.VMEM((n_u, n_z) + block, bf16),
            pltpu.VMEM((n_u, n_z) + block, bf16),
            pltpu.VMEM((n_z,) + block, bf16),
            pltpu.VMEM((n_z,) + block, bf16),
            pltpu.VMEM(q_grad.shape, bf16),
            pltpu.VMEM(q_grad.shape[1:], bf16),
            dma((n_u, n_z)),
            dma((n_u, n_z)),
            dma((n_u, n_z)),
            dma((n_u, n_z)),
            dma((n_z,)),
            dma((n_z,)),
        ]
        + sems(n_u)
        + sems(n_u)
        + sems(n_b)
        + sems(n_u * n_b),
        (kv_grad, rows, q_grad, gains),
        "settle",
    )


def lookup_kernel(slots, fills_ref, ids_ref, table_ref, rows_ref, wide, sem):
    wide[...] = jnp.zeros_like(wide)

    def row_copy(place, row):
        return pltpu.make_async_copy(
            table_ref.at[pl.ds(row, 1), :], wide.at[pl.ds(place, 1), :], sem
        )

    def of_peer(peer, total):
        fill = fills_ref[peer]

        def fetch(k, carry):
            place = peer * slots + k
            row_copy(place, ids_ref[place]).start()
            return carry

        lax.fori_loop(0, fill, fetch, 0)
        return total + fill

    total = lax.fori_loop(0, fills_ref.shape[0], of_peer, 0)

    def drain(k, carry):
        row_copy(0, 0).wait()
        return carry

    lax.fori_loop(0, total, drain, 0)
    rows_ref[...] = wide[...].astype(rows_ref.dtype)


def lookup(fills, ids, table, slots):
    places = ids.shape[0]
    return pl.pallas_call(
        functools.partial(lookup_kernel, slots),
        out_shape=jax.ShapeDtypeStruct((places, table.shape[1]), bf16),
        in_specs=[
            pl.BlockSpec(memory_space=pltpu.SMEM),
            pl.BlockSpec(memory_space=pltpu.SMEM),
            pl.BlockSpec(memory_space=pl.ANY),
        ],
        out_specs=VMEM,
        scratch_shapes=[
            pltpu.VMEM((places, table.shape[1]), f32),
            pltpu.SemaphoreType.DMA,
        ],
        compiler_params=pltpu.CompilerParams(vmem_limit_bytes=40 * 1024 * 1024),
        name="lookup",
    )(fills, ids, table)


TABLE_TILE = 256


def table_grad_kernel(
    limit, logits, finals, norms, weights, targets, rows, row_ids, grad_out, squares
):
    tile = grad_out.shape[0]
    start = pl.program_id(0) * tile
    ids = start + lax.broadcasted_iota(jnp.int32, (tile, 1), 0)
    grad_logits = (
        weights[...]
        * (jnp.exp(logits[...] - norms[...]) - jnp.where(targets[...] == ids, 1.0, 0.0))
    ).astype(bf16)
    hot = jnp.where(row_ids[...] == ids, 1.0, 0.0).astype(bf16)
    grad = mm(grad_logits, finals[...]) + mm(hot, rows[...])
    grad_out[...] = grad.astype(bf16)

    @pl.when(pl.program_id(0) == 0)
    def _():
        squares[...] = jnp.zeros_like(squares)

    squares[...] += jnp.sum(jnp.where(ids < limit, grad * grad, 0.0), axis=0, keepdims=True)


def table_grad_call(logits, finals, norms, weights, targets, rows, row_ids):
    share, picks = logits.shape
    places, width = rows.shape
    whole = lambda *shape: pl.BlockSpec(shape, lambda i: (0, 0))
    return pl.pallas_call(
        functools.partial(table_grad_kernel, share),
        grid=(pl.cdiv(share, TABLE_TILE),),
        out_shape=[
            jax.ShapeDtypeStruct((share, width), bf16),
            jax.ShapeDtypeStruct((1, width), f32),
        ],
        in_specs=[
            pl.BlockSpec((TABLE_TILE, picks), lambda i: (i, 0)),
            whole(picks, width),
            whole(1, picks),
            whole(1, picks),
            whole(1, picks),
            whole(places, width),
            whole(1, places),
        ],
        out_specs=[
            pl.BlockSpec((TABLE_TILE, width), lambda i: (i, 0)),
            whole(1, width),
        ],
        compiler_params=pltpu.CompilerParams(vmem_limit_bytes=40 * 1024 * 1024),
        cost_estimate=pl.CostEstimate(
            flops=2 * share * width * (picks + places),
            bytes_accessed=share * (4 * picks + 2 * width),
            transcendentals=share * picks,
        ),
        name="table_grad",
    )(logits, finals, norms, weights, targets, rows, row_ids)


def adam_kernel(rate, decay, numbers, weight, first, second, grad, change, new_first, new_second):
    gradient = grad[...].astype(f32) * numbers[0]
    mean = beta_first * first[...] + (1.0 - beta_first) * gradient
    square = beta_second * second[...] + (1.0 - beta_second) * gradient * gradient
    new_first[...] = mean
    new_second[...] = square
    change[...] = -rate * (
        mean * numbers[1] / (jnp.sqrt(square * numbers[2]) + adam_eps) + decay * weight[...]
    )


def adam_call(numbers, weight, first, second, grad, rate, decay):
    share, width = weight.shape
    block = pl.BlockSpec((TABLE_TILE, width), lambda i: (i, 0))
    return pl.pallas_call(
        functools.partial(adam_kernel, rate, decay),
        grid=(pl.cdiv(share, TABLE_TILE),),
        out_shape=[jax.ShapeDtypeStruct((share, width), f32)] * 3,
        in_specs=[pl.BlockSpec(memory_space=pltpu.SMEM)] + [block] * 4,
        out_specs=[block] * 3,
        compiler_params=pltpu.CompilerParams(vmem_limit_bytes=48 * 1024 * 1024),
        name="adam",
    )(numbers, weight, first, second, grad)


def local(
    tokens,
    lengths,
    picked,
    targets,
    advantages,
    step_count,
    embedding,
    first_embedding,
    second_embedding,
    inflow,
    inflow_first_moment,
    inflow_second_moment,
    outflow,
    first_outflow,
    second_outflow,
    expand,
    first_expand,
    second_expand,
    contract,
    first_contract,
    second_contract,
    scales,
    first_scales,
    second_scales,
):
    exchange = Exchanger()
    n_u, n_b = lax.axis_size("ulysses"), lax.axis_size("blk")
    n_all = n_u * n_b
    n_z = n_b // 2
    u, b = lax.axis_index("ulysses"), lax.axis_index("blk")
    me = u * n_b + b
    slot_count, block_len = tokens.shape
    assert slot_count == n_u and n_b % 2 == 0
    picks = picked.shape[1]
    slot_picks = picks * n_b
    all_picks = slot_picks * n_u
    row_share = embedding.shape[0]
    group = QUERY_HEADS // KEY_VALUE_HEADS
    score_scale = HEAD_WIDTH ** (-0.5)
    in_rows, out_share, ff_share = inflow.shape[0], outflow.shape[0], contract.shape[0]
    q_share = QUERY_WIDTH // n_b
    heads_share = q_share // HEAD_WIDTH
    ff_mine = n_u * ff_share
    out_cut = QUERY_WIDTH // n_all
    scale_share = scales.shape[0]

    packed = jnp.concatenate(
        [tokens.astype(f32), targets.astype(f32), picked.astype(f32), advantages], axis=1
    )
    packed_all, gains_all = exchange.many(
        (("blk", "g"), ("all", "g")),
        packed,
        jnp.pad(scales, (0, 128 - scale_share)).reshape(1, 128),
    )
    gains_wide = gains_all[:, 0, :scale_share].reshape(-1).astype(bf16).astype(f32)
    gain_attn = gains_wide[:MODEL_WIDTH]
    gain_mlp = gains_wide[MODEL_WIDTH : 2 * MODEL_WIDTH]
    gain_final = gains_wide[2 * MODEL_WIDTH : 3 * MODEL_WIDTH]
    gain_query = gains_wide[3 * MODEL_WIDTH : 3 * MODEL_WIDTH + HEAD_WIDTH]
    gain_key = gains_wide[3 * MODEL_WIDTH + HEAD_WIDTH :]

    wants_block = block_len + picks
    wants_count = n_b * wants_block
    wants = (
        packed_all[:, :, :wants_block]
        .astype(jnp.int32)
        .transpose(1, 0, 2)
        .reshape(n_u, wants_count)
    )
    picked_all = packed_all[:, :, wants_block : wants_block + picks].astype(jnp.int32)
    targets_all = packed_all[:, :, block_len:wants_block].astype(jnp.int32)
    advantages_all = packed_all[:, :, wants_block + picks :]
    weights_all = jnp.where(picked_all < lengths[None, :, None], advantages_all, 0.0)
    my_length = lax.dynamic_index_in_dim(lengths, u, 0, keepdims=False)
    slot_picked = lax.dynamic_index_in_dim(picked_all, u, 1, keepdims=False).reshape(-1)
    my_picked = lax.dynamic_index_in_dim(picked, u, 0, keepdims=False)
    my_valid = my_picked < my_length
    my_weight = jnp.where(
        my_valid, lax.dynamic_index_in_dim(advantages, u, 0, keepdims=False), 0.0
    )

    fill_mean = wants_count / n_all
    slots = -(-int(fill_mean + 5.2 * math.sqrt(fill_mean)) // 16) * 16
    places = n_u * slots
    owners = wants // row_share
    counts = jnp.sum(
        (owners[:, None, :] == jnp.arange(n_all, dtype=jnp.int32)[None, :, None]).astype(f32),
        axis=-1,
    )
    rounds = (jnp.max(counts).astype(jnp.int32) + slots - 1) // slots
    own_owners = lax.dynamic_index_in_dim(owners, u, 0, keepdims=True)
    sent_mask = owners == me
    got_mask = own_owners == jnp.arange(n_u, dtype=jnp.int32)[:, None] * n_b + b
    masks = jnp.concatenate([sent_mask, got_mask], axis=0)
    totals_sent = jnp.sum(sent_mask.astype(f32), axis=1).astype(jnp.int32)
    lanes = math.gcd(wants_count, 128)
    blocks = masks.astype(bf16).reshape(2 * n_u, wants_count // lanes, lanes)
    before = (jnp.arange(lanes)[:, None] < jnp.arange(lanes)[None, :]).astype(bf16)
    block_sums = jnp.sum(blocks.astype(f32), axis=-1)
    chunk = jnp.arange(wants_count // lanes)
    block_base = mm(block_sums.astype(bf16), (chunk[:, None] < chunk[None, :]).astype(bf16))
    ranks = (
        mm(blocks.reshape(-1, lanes), before).reshape(blocks.shape) + block_base[:, :, None]
    ).reshape(2 * n_u, wants_count)
    ranks = jnp.where(masks, ranks.astype(jnp.int32), -1)
    labels = jnp.concatenate(
        [
            wants - me * row_share,
            jnp.broadcast_to(
                jnp.arange(wants_count, dtype=jnp.int32)[None, :], (n_u, wants_count)
            ),
        ],
        axis=0,
    )

    def slot_tables(turn):
        slot_rank = turn * slots + jnp.arange(slots, dtype=jnp.int32)
        hit = ranks[:, None, :] == slot_rank[None, :, None]
        found = jnp.sum(jnp.where(hit, labels[:, None, :] + 1, 0), axis=-1) - 1
        fills = jnp.clip(totals_sent - turn * slots, 0, slots)
        row_ids = found[:n_u].reshape(-1)
        entry = found[n_u:].reshape(-1)
        block, inside = entry // wants_block, entry % wants_block
        is_token = (entry >= 0) & (inside < block_len)
        key_pos = jnp.where(is_token, block * block_len + inside, 1 << 30)
        target_of = jnp.where(
            (entry >= 0) & (inside >= block_len), block * picks + inside - block_len, -1
        )
        pick_hot = (slot_picked[:, None] == key_pos[None, :]).astype(bf16)
        target_hot = (jnp.arange(slot_picks)[:, None] == target_of[None, :]).astype(bf16)
        return (row_ids, fills, key_pos, pick_hot, target_hot)

    def fetch(fills, row_ids):
        rows = lookup(fills, jnp.maximum(row_ids, 0), embedding, slots)
        return rows.reshape(n_u, slots, MODEL_WIDTH)

    tables = slot_tables(jnp.int32(0))
    row_ids, fills, key_pos, pick_hot, target_hot = tables

    inflow_low = inflow.astype(bf16)
    q_cols = inflow_low[:, :QUERY_WIDTH].reshape(in_rows, n_b, q_share).transpose(1, 0, 2)
    ff_cols = (
        expand.astype(bf16)
        .reshape(in_rows, 2, n_u, n_b, ff_share)
        .transpose(3, 0, 1, 2, 4)
        .reshape(n_b, in_rows, 2 * ff_mine)
    )
    arrived, kv_weight, q_weight, ff_split = start_call(
        exchange, fetch(fills, row_ids), inflow_low[:, QUERY_WIDTH:], q_cols, ff_cols
    )
    arrived = arrived.reshape(places, MODEL_WIDTH)
    kv_weight = kv_weight.reshape(MODEL_WIDTH, -1)
    q_weight = q_weight.reshape(MODEL_WIDTH, q_share)
    in_block = n_b * in_rows
    wide_rows = in_block * 2 * ff_mine // MODEL_WIDTH
    layer_rows = jnp.concatenate(
        [
            ff_split.reshape(wide_rows, MODEL_WIDTH),
            outflow.astype(bf16),
            contract.astype(bf16),
        ],
        axis=0,
    )
    layer_all = lax.all_to_all(
        jnp.broadcast_to(layer_rows[None], (n_u,) + layer_rows.shape), "ulysses", 0, 0, tiled=True
    )
    ff_weight = layer_all[:, :wide_rows].reshape(MODEL_WIDTH, 2 * ff_mine)
    out_weight = layer_all[:, wide_rows : wide_rows + out_share].reshape(
        n_u * out_share, MODEL_WIDTH
    )
    contract_weight = layer_all[:, wide_rows + out_share :].reshape(ff_mine, MODEL_WIDTH)

    def picked_rows(pick_hot, target_hot, arrived):
        return jnp.concatenate([mm(pick_hot, arrived), mm(target_hot, arrived)], axis=1)

    refetch_id = [exchange.next_id() for _ in range(5)]

    def refetch(turn, which):
        tables = slot_tables(turn)
        (got,) = exchange.many(
            (("ulysses", "s"),), fetch(tables[1], tables[0]), collective_id=refetch_id[which]
        )
        return (tables, got.reshape(places, MODEL_WIDTH))

    def more(state):
        return state[0] < rounds

    def picks_turn(state):
        tables, got = refetch(state[0], 0)
        return (state[0] + 1, state[1] + picked_rows(tables[3], tables[4], got))

    pick_part = picked_rows(pick_hot, target_hot, arrived)
    _, pick_part = lax.while_loop(more, picks_turn, (jnp.int32(1), pick_part))
    (got_picks,) = exchange(
        "blk", "s", pick_part.astype(bf16).reshape(n_b, picks, 2 * MODEL_WIDTH)
    )
    got_picks = jnp.sum(got_picks.astype(f32), axis=0)
    embedded_picks, target_rows = got_picks[:, :MODEL_WIDTH], got_picks[:, MODEL_WIDTH:]

    def to_slot(rows):
        (got,) = exchange("blk", "g", rows)
        return got.reshape(slot_picks, rows.shape[1])

    def sum_to_picks(partial):
        (got,) = exchange("blk", "s", partial.astype(bf16).reshape(n_b, picks, MODEL_WIDTH))
        return jnp.sum(got.astype(f32), axis=0)

    normed_slot = to_slot(
        (embedded_picks * inverse_root(embedded_picks) * gain_attn).astype(bf16)
    )

    def keys_of(arrived, key_pos):
        embedded = arrived.astype(f32)
        normed = (embedded * inverse_root(embedded) * gain_attn).astype(bf16)
        mixed = mm(normed, kv_weight)
        half = KEY_VALUE_HEADS * HEAD_WIDTH
        key_raw = mixed[:, :half].reshape(places, KEY_VALUE_HEADS, HEAD_WIDTH)
        values = mixed[:, half:].reshape(places, KEY_VALUE_HEADS, HEAD_WIDTH)
        angle_tables = rope_angles(jnp.where(key_pos < (1 << 30), key_pos, 0))
        key_rot = rotate(key_raw * inverse_root(key_raw) * gain_key, angle_tables, 1.0)
        return (
            embedded,
            normed,
            key_raw,
            angle_tables,
            key_rot.astype(bf16).transpose(1, 0, 2),
            values.astype(bf16).transpose(1, 0, 2),
        )

    query_pos = jnp.tile(slot_picked, group)

    def allowed_of(key_pos):
        return ((key_pos[None, :] <= query_pos[:, None]) & (key_pos[None, :] < my_length))[None]

    def scores_of(query_groups, key_rot, allowed):
        scores = (
            jnp.einsum("kqd,kjd->kqj", query_groups, key_rot, preferred_element_type=f32)
            * score_scale
        )
        return jnp.where(allowed, scores, masked_score)

    def attend(scores, allowed, values):
        part_max = jnp.max(scores, axis=-1, keepdims=True)
        weights = jnp.where(allowed, jnp.exp(scores - part_max), 0.0)
        out = jnp.einsum("kqj,kjd->kqd", weights.astype(bf16), values, preferred_element_type=f32)
        return (part_max, jnp.sum(weights, axis=-1, keepdims=True), out)

    keys = keys_of(arrived, key_pos)

    query_raw = mm(normed_slot, q_weight).reshape(slot_picks, heads_share, HEAD_WIDTH)
    query_tables = rope_angles(slot_picked)
    query_mine = rotate(query_raw * inverse_root(query_raw) * gain_query, query_tables, 1.0)
    (query_all,) = exchange("blk", "g", query_mine.astype(bf16).reshape(slot_picks, q_share))
    query_groups = (
        query_all.reshape(n_b, slot_picks, heads_share, HEAD_WIDTH)
        .transpose(0, 2, 1, 3)
        .reshape(KEY_VALUE_HEADS, group * slot_picks, HEAD_WIDTH)
    )
    allowed = allowed_of(key_pos)
    scores = scores_of(query_groups, keys[4], allowed)

    def attend_turn(state):
        turn, top, total, out = state
        tables, got = refetch(turn, 1)
        keys_now = keys_of(got, tables[2])
        allowed_now = allowed_of(tables[2])
        new = attend(scores_of(query_groups, keys_now[4], allowed_now), allowed_now, keys_now[5])
        both = jnp.maximum(top, new[0])
        old_factor, new_factor = jnp.exp(top - both), jnp.exp(new[0] - both)
        return (
            turn + 1,
            both,
            total * old_factor + new[1] * new_factor,
            out * old_factor + new[2] * new_factor,
        )

    _, part_max, part_sum, part_out = lax.while_loop(
        more, attend_turn, (jnp.int32(1),) + attend(scores, allowed, keys[5])
    )
    part_send = (
        part_out.astype(bf16)
        .reshape(QUERY_HEADS, slot_picks, HEAD_WIDTH)
        .transpose(1, 0, 2)
        .reshape(slot_picks, n_u, n_b, out_cut)
        .transpose(2, 0, 1, 3)
        .reshape(n_b, slot_picks, n_u * out_cut)
    )
    stats = jnp.stack([part_max[..., 0], part_sum[..., 0]]).reshape(2 * QUERY_HEADS, slot_picks)
    part_got, stats_all = exchange("blk", "sg", part_send, stats)
    stats_all = stats_all.reshape(n_b, 2, QUERY_HEADS, slot_picks)
    full_max = jnp.max(stats_all[:, 0], axis=0)
    shrink = jnp.exp(stats_all[:, 0] - full_max[None])
    full_sum = jnp.sum(stats_all[:, 1] * shrink, axis=0)
    log_total = full_max + jnp.log(full_sum)
    share_of = shrink / full_sum[None]
    heads_row = QUERY_HEADS // n_u
    cut_head = (b * out_cut) // HEAD_WIDTH
    my_share = lax.dynamic_index_in_dim(
        share_of.reshape(n_b, n_u, heads_row, slot_picks), cut_head, 2, keepdims=False
    )
    attended_wide = jnp.sum(
        part_got.astype(f32).reshape(n_b, slot_picks, n_u, out_cut)
        * my_share.transpose(0, 2, 1)[..., None],
        axis=0,
    )
    attended = attended_wide.astype(bf16).reshape(slot_picks, n_u * out_cut)

    after_attn = embedded_picks + sum_to_picks(mm(attended, out_weight))
    normed_mlp = to_slot((after_attn * inverse_root(after_attn) * gain_mlp).astype(bf16))
    gate_up = mm(normed_mlp, ff_weight)
    gate_part, up_part = gate_up[:, :ff_mine], gate_up[:, ff_mine:]
    sigmoid_gate = jax.nn.sigmoid(gate_part)
    activated = (gate_part * sigmoid_gate * up_part).astype(bf16)
    after_mlp = after_attn + sum_to_picks(mm(activated, contract_weight))
    final_rows = (after_mlp * inverse_root(after_mlp) * gain_final).astype(bf16)

    (final_all,) = exchange("ulysses", "g", to_slot(final_rows))
    final_all = final_all.reshape(all_picks, MODEL_WIDTH)
    table_low = embedding.astype(bf16)
    logits = mm_back(table_low, final_all)
    local_max = jnp.max(logits, axis=0)
    head_weights = jnp.exp(logits - local_max[None, :])
    local_sum = jnp.sum(head_weights, axis=0)
    head_rows = mm_outer(head_weights.astype(bf16), table_low).astype(bf16)
    head_stats = jnp.stack([local_max, local_sum], axis=1).reshape(n_u, slot_picks, 2)

    def merge_rows(rows, stats_in):
        top = jnp.max(stats_in[..., 0], axis=0)
        factor = jnp.exp(stats_in[..., 0] - top[None])
        total = jnp.sum(stats_in[..., 1] * factor, axis=0)
        return (jnp.sum(rows.astype(f32) * factor[..., None], axis=0), top, total)

    got_rows, got_stats = exchange(
        "ulysses",
        "ss",
        head_rows.reshape(n_u, slot_picks, MODEL_WIDTH),
        jnp.pad(head_stats, ((0, 0), (0, 0), (0, 126))),
    )
    slot_rows, slot_top, slot_total = merge_rows(got_rows, got_stats)
    slot_stats = jnp.stack([slot_top, slot_total], axis=1).reshape(n_b, picks, 2)
    got_rows, got_stats = exchange(
        "blk",
        "ss",
        slot_rows.astype(bf16).reshape(n_b, picks, MODEL_WIDTH),
        jnp.pad(slot_stats, ((0, 0), (0, 0), (0, 126))),
    )
    mean_rows, top, total = merge_rows(got_rows, got_stats)
    log_norm = top + jnp.log(total)
    target_logit = jnp.sum(final_rows.astype(f32) * target_rows, axis=1)
    loss_local = -jnp.sum(my_weight * (target_logit - log_norm))
    count_local = jnp.sum(my_valid.astype(f32))
    grad_final = my_weight[:, None] * (mean_rows / total[:, None] - target_rows)

    grad_after_mlp, grad_gain_final = norm_back(after_mlp, gain_final, grad_final)
    got_branch, norms_slot = exchange(
        "blk",
        "gg",
        grad_after_mlp.astype(bf16),
        jnp.broadcast_to(log_norm[:, None], (picks, 128)),
    )
    grad_branch = got_branch.reshape(slot_picks, MODEL_WIDTH)
    grad_contract = mm_outer(activated, grad_branch)
    grad_act = mm_back(grad_branch, contract_weight)
    grad_gate = grad_act * up_part * sigmoid_gate * (1.0 + gate_part * (1.0 - sigmoid_gate))
    grad_up = grad_act * gate_part * sigmoid_gate
    grad_gate_up = jnp.concatenate([grad_gate, grad_up], axis=1).astype(bf16)
    grad_expand = mm_outer(normed_mlp, grad_gate_up)
    grad_mid_part, grad_gain_mlp = norm_back(
        after_attn, gain_mlp, sum_to_picks(mm_back(grad_gate_up, ff_weight))
    )
    grad_after_attn = grad_after_mlp + grad_mid_part
    grad_attn_branch = to_slot(grad_after_attn.astype(bf16))
    grad_outflow = mm_outer(attended, grad_attn_branch)
    grad_layer = jnp.concatenate(
        [
            grad_expand.astype(bf16).reshape(n_u, wide_rows, MODEL_WIDTH),
            grad_outflow.astype(bf16).reshape(n_u, out_share, MODEL_WIDTH),
            grad_contract.astype(bf16).reshape(n_u, ff_share, MODEL_WIDTH),
        ],
        axis=1,
    )
    got_layer = lax.all_to_all(grad_layer, "ulysses", 0, 0, tiled=True)
    grad_attended = mm_back(grad_attn_branch, out_weight).astype(bf16)
    delta_part = jnp.sum(
        attended_wide * grad_attended.astype(f32).reshape(slot_picks, n_u, out_cut), axis=-1
    )
    got_attended, got_delta = exchange("blk", "gg", grad_attended, delta_part.T)
    grad_heads = (
        got_attended.reshape(n_b, slot_picks, n_u, out_cut)
        .transpose(1, 2, 0, 3)
        .reshape(slot_picks, QUERY_HEADS, HEAD_WIDTH)
        .transpose(1, 0, 2)
        .reshape(KEY_VALUE_HEADS, group * slot_picks, HEAD_WIDTH)
    )
    row_delta = jnp.sum(
        got_delta.transpose(1, 0, 2).reshape(QUERY_HEADS, HEAD_WIDTH // out_cut, slot_picks), axis=1
    ).reshape(KEY_VALUE_HEADS, group * slot_picks, 1)
    log_groups = log_total.reshape(KEY_VALUE_HEADS, group * slot_picks, 1)

    def score_grads(scores, allowed, values):
        probs = jnp.where(allowed, jnp.exp(scores - log_groups), 0.0)
        grad_probs = jnp.einsum("kqd,kjd->kqj", grad_heads, values, preferred_element_type=f32)
        return (probs, (probs * (grad_probs - row_delta) * score_scale).astype(bf16))

    def query_grads(grad_scores, key_rot):
        return jnp.einsum("kqj,kjd->kqd", grad_scores, key_rot, preferred_element_type=f32)

    def key_grads(probs, grad_scores, keys):
        grad_key = jnp.einsum(
            "kqj,kqd->kjd", grad_scores, query_groups, preferred_element_type=f32
        )
        grad_value = jnp.einsum(
            "kqj,kqd->kjd", probs.astype(bf16), grad_heads, preferred_element_type=f32
        )
        upstream = rotate(
            grad_key.astype(bf16).astype(f32).transpose(1, 0, 2), keys[3], -1.0
        )
        grad_raw, grad_gain = norm_back(keys[2], gain_key, upstream)
        grad_kv = jnp.concatenate(
            [
                grad_raw.reshape(places, -1).astype(bf16),
                grad_value.astype(bf16).transpose(1, 0, 2).reshape(places, -1),
            ],
            axis=1,
        )
        return (grad_kv, grad_gain)

    def row_grads(grad_kv, keys):
        return norm_back(keys[0], gain_attn, mm_back(grad_kv, kv_weight))

    def redo(turn, which):
        tables, got = refetch(turn, which)
        keys_now = keys_of(got, tables[2])
        allowed_now = allowed_of(tables[2])
        scores_now = scores_of(query_groups, keys_now[4], allowed_now)
        return (tables, keys_now) + score_grads(scores_now, allowed_now, keys_now[5])

    def query_turn(state):
        _, keys_now, _, grad_scores_now = redo(state[0], 2)
        return (state[0] + 1, state[1] + query_grads(grad_scores_now, keys_now[4]))

    probs, grad_scores = score_grads(scores, allowed, keys[5])
    _, grad_query_part = lax.while_loop(
        more, query_turn, (jnp.int32(1), query_grads(grad_scores, keys[4]))
    )
    (got_query,) = exchange(
        "blk",
        "s",
        grad_query_part.astype(bf16)
        .reshape(n_b, heads_share, slot_picks, HEAD_WIDTH)
        .transpose(0, 2, 1, 3)
        .reshape(n_b, slot_picks, q_share),
    )
    grad_query_rot = jnp.sum(got_query.astype(f32), axis=0).astype(bf16).astype(f32)
    grad_query_raw, grad_gain_query = norm_back(
        query_raw,
        gain_query,
        rotate(grad_query_rot.reshape(slot_picks, heads_share, HEAD_WIDTH), query_tables, -1.0),
    )
    grad_query_low = grad_query_raw.reshape(slot_picks, q_share).astype(bf16)
    grad_q_weight = mm_outer(normed_slot, grad_query_low)
    grad_normed_picks = sum_to_picks(mm_back(grad_query_low, q_weight))
    grad_pick_part, grad_gain_picks = norm_back(embedded_picks, gain_attn, grad_normed_picks)
    pick_back = to_slot((grad_after_attn + grad_pick_part).astype(bf16))

    grad_kv, grad_gain_key = key_grads(probs, grad_scores, keys)
    grad_kv_weight = mm_outer(keys[1], grad_kv)
    grad_rows, grad_gain_attn = row_grads(grad_kv, keys)

    def weight_turn(state):
        turn, weight_sum, key_sum, attn_sum = state
        _, keys_now, probs_now, grad_scores_now = redo(turn, 3)
        grad_kv_now, gain_key_now = key_grads(probs_now, grad_scores_now, keys_now)
        _, gain_attn_now = row_grads(grad_kv_now, keys_now)
        return (
            turn + 1,
            weight_sum + mm_outer(keys_now[1], grad_kv_now),
            key_sum + gain_key_now,
            attn_sum + gain_attn_now,
        )

    _, grad_kv_weight, grad_gain_key, grad_gain_attn = lax.while_loop(
        more, weight_turn, (jnp.int32(1), grad_kv_weight, grad_gain_key, grad_gain_attn)
    )
    grad_scales = jnp.concatenate(
        [
            grad_gain_attn + grad_gain_picks,
            grad_gain_mlp,
            grad_gain_final,
            grad_gain_query,
            grad_gain_key,
        ]
    )

    sum_layer = jnp.sum(got_layer.astype(f32), axis=0)
    sum_outflow = sum_layer[wide_rows : wide_rows + out_share]
    sum_contract = sum_layer[wide_rows + out_share :]
    got_ff = lax.all_to_all(
        sum_layer[:wide_rows].astype(bf16).reshape(n_b, in_rows, 2 * ff_mine),
        "blk",
        0,
        0,
        tiled=True,
    )
    sum_expand = (
        got_ff.astype(f32)
        .reshape(n_b, in_rows, 2, n_u, ff_share)
        .transpose(1, 2, 3, 0, 4)
        .reshape(in_rows, 2 * FF)
    )
    rows_low = (grad_rows + mm_outer(pick_hot, pick_back)).astype(bf16)
    sum_kv, rows_back, got_q, got_scales = settle_call(
        exchange,
        grad_kv_weight.astype(bf16).reshape(n_u, n_z, 2, in_rows, -1),
        rows_low.reshape(n_u, slots, MODEL_WIDTH),
        grad_q_weight.astype(bf16).reshape(n_u, n_b, in_rows, q_share),
        jnp.pad(
            grad_scales.reshape(n_all, scale_share), ((0, 0), (0, 128 - scale_share))
        ).reshape(n_all, 1, 128),
    )
    sum_q = got_q.astype(f32).transpose(1, 0, 2).reshape(in_rows, QUERY_WIDTH)
    sum_inflow = jnp.concatenate([sum_q, sum_kv], axis=1)
    sum_scales = jnp.sum(got_scales, axis=0)[0, :scale_share]

    def flat(array):
        return array.transpose(1, 0, 2).reshape(1, -1)

    (norms_all,) = exchange("ulysses", "g", norms_slot[:, :, 0].reshape(n_b, picks))
    table_grad, table_squares = table_grad_call(
        logits,
        final_all,
        norms_all.reshape(1, all_picks),
        flat(weights_all),
        flat(targets_all) - me * row_share,
        rows_back.reshape(places, MODEL_WIDTH),
        row_ids.reshape(1, places),
    )
    return_id = exchange.next_id()

    def return_turn(state):
        turn, so_far, _ = state
        tables, keys_now, probs_now, grad_scores_now = redo(turn, 4)
        grad_kv_now, _ = key_grads(probs_now, grad_scores_now, keys_now)
        rows_now, _ = row_grads(grad_kv_now, keys_now)
        rows_now = (rows_now + mm_outer(tables[3], pick_back)).astype(bf16)
        (back,) = exchange.many(
            (("ulysses", "s"),),
            rows_now.reshape(n_u, slots, MODEL_WIDTH),
            collective_id=return_id,
        )
        hot = (
            jnp.arange(row_share, dtype=jnp.int32)[:, None] == tables[0][None, :]
        ).astype(bf16)
        grown = so_far.astype(f32) + mm(hot, back.reshape(places, MODEL_WIDTH))
        return (turn + 1, grown.astype(bf16), jnp.sum(grown * grown, axis=0, keepdims=True))

    _, table_grad, table_squares = lax.while_loop(
        more, return_turn, (jnp.int32(1), table_grad, table_squares)
    )

    layer_grads = (sum_inflow, sum_outflow, sum_expand, sum_contract, sum_scales)
    squares = jnp.sum(table_squares)
    for grad_piece in layer_grads:
        squares = squares + jnp.sum(grad_piece * grad_piece)
    (totals,) = exchange(
        "all",
        "g",
        jnp.pad(jnp.stack([squares, count_local, loss_local]), (0, 125)).reshape(1, 128),
    )
    totals = jnp.sum(totals, axis=(0, 1))
    square_total, count_total, loss_total = totals[0], totals[1], totals[2]
    gradient_norm = jnp.sqrt(square_total) / count_total
    factor = jnp.minimum(1.0, clip_limit / gradient_norm) / count_total
    step_float = step_count[0].astype(f32)
    outputs = [loss_total / count_total, gradient_norm]
    outputs += adam_call(
        jnp.stack(
            [factor, 1.0 / (1.0 - beta_first**step_float), 1.0 / (1.0 - beta_second**step_float)]
        ),
        embedding,
        first_embedding,
        second_embedding,
        table_grad,
        learning_rates[0],
        weight_decays[0],
    )
    weights_now = (inflow, outflow, expand, contract, scales)
    firsts = (inflow_first_moment, first_outflow, first_expand, first_contract, first_scales)
    seconds = (inflow_second_moment, second_outflow, second_expand, second_contract, second_scales)
    for position in range(5):
        outputs += adam_update(
            weights_now[position],
            firsts[position],
            seconds[position],
            layer_grads[position] * factor,
            learning_rates[position + 1],
            weight_decays[position + 1],
            step_float,
        )
    return tuple(outputs)


def solution(mesh):
    rows = P(("ulysses", "blk"), None)
    flat_rows = P(("ulysses", "blk"))
    column = P(None, "blk")
    return jax.shard_map(
        local,
        mesh=mesh,
        in_specs=(column, P(), column, column, column, P()) + (rows,) * 15 + (flat_rows,) * 3,
        out_specs=(P(), P()) + (rows,) * 15 + (flat_rows,) * 3,
        check_vma=False,
    )
```

time: 729 us -> 699 us (0.959)
  Pallas kernels: 383 us -> 437 us
  other arithmetic: 117 us -> 71.3 us
  waiting for transfers between devices: 45.4 us -> 7.88 us
  matrix products: 85.2 us -> 64.2 us
  local copies, waits for them, and re-layouts: 48.2 us -> 68.6 us
  between operations: 29.2 us -> 16 us
  loops' own time: 0.3 us -> 10.9 us
    pallas_call x25, Pallas kernels: 378 us -> 432 us  [the longest x23 366 us: remote_call(): pl.pallas_call(kernel, out_shape=shapes, in_specs=[VMEM] * len(arrays), o...]
    mul x6 -> x5, other arithmetic: 55 us -> 7.3 us  [adam_update(): -rate_value]
    dot_general x10 -> x9, matrix products: 40.3 us -> 8.67 us  [mm(): lax.dot_general(left, right, (((1,), (0,)), ((), ())), preferred_element_...]
    all_gather x2 -> x0, waiting for transfers between devices: 18.7 us -> none  [the longest x1 18.7 us: local(): lax.all_gather(inflow_low[:, QUERY_WIDTH:], BOTH, axis=0, tiled=True)]
    all_to_all x2, waiting for transfers between devices: 25.9 us -> 7.88 us  [the longest x1 7.88 us: local(): lax.all_to_all(sum_layer[:wide_rows].astype(bf16).reshape(n_b, in_rows, 2...]
    reduce_sum x6 -> x5, other arithmetic: 15.6 us -> 3.5 us  [local(): squares = squares + jnp.sum(grad_piece * grad_piece)]
    convert_element_type x4 -> x10, other arithmetic: 1.27 us -> 12.6 us  [the longest x1 6.18 us: local(): grad_kv_weight.astype(bf16).reshape(n_u, n_z, 2, in_rows, -1)]
    another operation x2 -> x5, loops' own time: 0.3 us -> 10.9 us  [the longest x1 5.56 us: local(): lax.while_loop(more, return_turn, (jnp.int32(1), table_grad, table_squares))]
  transfers between devices with their start and end apart: 5 -> 3, of which waited for: 2 -> 1; matrix products, arithmetic and copies ran while one was open for 13% -> 8% of each run, Pallas kernels for 26% -> 22%
where the time goes in v2:
time: 699 us; the launch traced here: 691 us
  Pallas kernels  437 us (63%)
  other arithmetic  71.3 us (10%)
  local copies, waits for them, and re-layouts  68.6 us (10%)
  matrix products  64.2 us (9%)
  between operations  16 us (2%)
  starting transfers between devices  14.7 us (2%)
  loops' own time  10.9 us (2%)
  waiting for transfers between devices  7.88 us (1%)
    pallas_call x23, Pallas kernels, remote_call(): pl.pallas_call(kernel, out_shape=shapes, in_specs=[VMEM] * len(arrays), o...  366 us
    pallas_call x1, Pallas kernels, adam_call(): pl.pallas_call(functools.partial(adam_kernel, rate, decay), grid=(pl.cdiv...  48.9 us
    dot_general x7, matrix products, mm_outer(): lax.dot_general(left, right, (((0,), (0,)), ((), ())), preferred_element_...  26.2 us
    pallas_call x1, Pallas kernels, table_grad_call(): pl.pallas_call(functools.partial(table_grad_kernel, share), grid=(pl.cdiv...  17.9 us
    dot_general x6, matrix products, mm_back(): lax.dot_general(left, right, (((1,), (1,)), ((), ())), preferred_element_...  17.4 us
  transfers between devices with their start and end apart: 3, of which 1 were waited for; matrix products, arithmetic and copies ran while one was open for 8% of the time, Pallas kernels for 22%

profile of v2, /device:TPU:0, one launch (start us, length us, event | category | flops | bytes accessed | tf_op | source)
XLA Modules:
  0.0 690.6 jit_solution(3999249664315283381)
XLA Ops:
  4.3 11.1 %exchange_0.1 = (f32[8,4,304]{2,1,0:T(4,128)S(1)}, f32[32,1,128]{2,1,0:T(1,128)S(1)}) custom-call(f32[4,304]{1,0:T(4,128)S(1)} %pad_maximum_fusion.19.refs_0_, f32[1,128]{1,0:T(1,128)S(1)} %pad_bitcast_fusion.refs_1_), custom_call_target="tpu_custom_call" | custom-call | tf_op jit(solution)/shard_map/exchange_0/pallas_call | solution.py:219
  20.1 4.6 lookup.26
  24.7 47.3 %start.1 = (bf16[4,112,1024]{2,1,0:T(8,128)(2,1)S(1)}, bf16[4,4,2,32,2048]{4,3,2,1,0:T(8,128)(2,1)}, bf16[4,8,32,256]{3,2,1,0:T(8,128)(2,1)S(1)}, bf16[8,32,768]{2,1,0:T(8,128)(2,1)S(1)}) custom-call(bf16[4,112,1024]{2,1,0:T(8,128)(2,1)S(1)} %bitcast.919, bf16[32,2048]{1,0:T(8,128)(2,1)S(1)} %get-tuple-element.1719.kv_in, bf16[8,32,256]{2,1,0:T(8,128)(2,1)S(1)} %bitcast.938, ...), custom_call_target="tpu_custom_call" | custom-call | tf_op jit(solution)/shard_map/start/pallas_call | solution.py:219
  74.3 4.7 all-to-all-start
  91.8 11.7 %exchange_7.1 = bf16[8,16,2048]{2,1,0:T(8,128)(2,1)S(1)} custom-call(bf16[8,16,2048]{2,1,0:T(8,128)(2,1)S(1)} %bitcast.927), custom_call_target="tpu_custom_call" | custom-call | tf_op jit(solution)/shard_map/exchange_7/pallas_call | solution.py:219
  103.8 10.5 %exchange_8.1 = bf16[8,16,1024]{2,1,0:T(8,128)(2,1)S(1)} custom-call(bf16[16,1024]{1,0:T(8,128)(2,1)S(1)} %multiply_convert_fusion.12.refs_0_), custom_call_target="tpu_custom_call" | custom-call | tf_op jit(solution)/shard_map/exchange_8/pallas_call | solution.py:219
  116.0 12.8 %exchange_9.1 = bf16[8,128,256]{2,1,0:T(8,128)(2,1)S(1)} custom-call(bf16[128,256]{1,0:T(8,128)(2,1)S(1)} %copy.442.refs_0_), custom_call_target="tpu_custom_call" | custom-call | tf_op jit(solution)/shard_map/exchange_9/pallas_call | solution.py:219
  129.4 4.2 fusion.298
  150.0 27.0 %exchange_10.1 = (bf16[8,128,256]{2,1,0:T(8,128)(2,1)S(1)}, f32[8,32,128]{2,1,0:T(8,128)S(1)}) custom-call(bf16[8,128,256]{2,1,0:T(8,128)(2,1)S(1)} %copy.416.refs_0_, f32[32,128]{1,0:T(8,128)S(1)} %reshape.2450.refs_1_), custom_call_target="tpu_custom_call" | custom-call | tf_op jit(solution)/shard_map/exchange_10/pallas_call | solution.py:219
  195.1 2.9 reshape.2455
  199.7 8.7 %exchange_11.1 = bf16[8,16,1024]{2,1,0:T(8,128)(2,1)S(1)} custom-call(bf16[8,16,1024]{2,1,0:T(8,128)(2,1)S(1)} %bitcast.934), custom_call_target="tpu_custom_call" | custom-call | tf_op jit(solution)/shard_map/exchange_11/pallas_call | solution.py:219
  208.7 9.2 %exchange_12.1 = bf16[8,16,1024]{2,1,0:T(8,128)(2,1)S(1)} custom-call(bf16[16,1024]{1,0:T(8,128)(2,1)S(1)} %multiply_convert_fusion.11.refs_0_), custom_call_target="tpu_custom_call" | custom-call | tf_op jit(solution)/shard_map/exchange_12/pallas_call | solution.py:219
  220.0 9.2 %exchange_13.1 = bf16[8,16,1024]{2,1,0:T(8,128)(2,1)S(1)} custom-call(bf16[8,16,1024]{2,1,0:T(8,128)(2,1)S(1)} %bitcast.936), custom_call_target="tpu_custom_call" | custom-call | tf_op jit(solution)/shard_map/exchange_13/pallas_call | solution.py:219
  229.5 9.3 %exchange_14.1 = bf16[8,16,1024]{2,1,0:T(8,128)(2,1)S(1)} custom-call(bf16[16,1024]{1,0:T(8,128)(2,1)S(1)} %multiply_convert_fusion.10.refs_0_), custom_call_target="tpu_custom_call" | custom-call | tf_op jit(solution)/shard_map/exchange_14/pallas_call | solution.py:219
  238.8 16.3 %exchange_15.1 = bf16[4,128,1024]{2,1,0:T(8,128)(2,1)S(1)} custom-call(bf16[128,1024]{1,0:T(8,128)(2,1)S(1)} %bitcast.933), custom_call_target="tpu_custom_call" | custom-call | tf_op jit(solution)/shard_map/exchange_15/pallas_call | solution.py:219
  255.1 10.2 %fusion.294 = (f32[512]{0:T(512)S(1)}, f32[512,4748]{0,1:T(8,128)S(1)}) fusion(bf16[512,1024]{1,0:T(8,128)(2,1)S(1)} %bitcast.917, f32[4748,1024]{1,0:T(8,128)} %get-tuple-element.2805), kind=kOutput, calls=%fused_computation.674 | convolution fusion | flops 4985931264 | bytes 30222336 | tf_op jit(solution)/shard_map/dot_general | solution.py:81
  265.4 13.6 %fusion.202 = bf16[512,1024]{1,0:T(8,128)(2,1)S(1)} fusion(f32[4748,1024]{1,0:T(8,128)} %get-tuple-element.2805, f32[512]{0:T(512)S(1)} %get-tuple-element.1755, f32[512,4748]{0,1:T(8,128)S(1)} %get-tuple-element.1756), kind=kOutput, calls=%fused_computation.408 | convolution fusion | flops 4988887040 | bytes 30222336 | tf_op jit(solution)/shard_map/dot_general | solution.py:77
  280.6 17.8 %exchange_16.1 = (bf16[4,128,1024]{2,1,0:T(8,128)(2,1)S(1)}, f32[4,128,128]{2,1,0:T(8,128)S(1)}) custom-call(bf16[4,128,1024]{2,1,0:T(8,128)(2,1)S(1)} %bitcast.932, f32[4,128,128]{2,1,0:T(8,128)S(1)} %pad.21.refs_1_), custom_call_target="tpu_custom_call" | custom-call | tf_op jit(solution)/shard_map/exchange_16/pallas_call | solution.py:219
  299.5 12.6 %exchange_17.1 = (bf16[8,16,1024]{2,1,0:T(8,128)(2,1)S(1)}, f32[8,16,128]{2,1,0:T(8,128)S(1)}) custom-call(bf16[8,16,1024]{2,1,0:T(8,128)(2,1)S(1)} %bitcast.931, f32[8,16,128]{2,1,0:T(8,128)S(1)} %pad.22.refs_1_), custom_call_target="tpu_custom_call" | custom-call | tf_op jit(solution)/shard_map/exchange_17/pallas_call | solution.py:219
  313.5 11.8 %exchange_18.1 = (bf16[8,16,1024]{2,1,0:T(8,128)(2,1)S(1)}, f32[8,16,128]{2,1,0:T(8,128)S(1)}) custom-call(bf16[16,1024]{1,0:T(8,128)(2,1)S(1)} %fusion.254.refs_0_, f32[16,128]{1,0:T(8,128)S(1)} %broadcast_in_dim.479.refs_1_), custom_call_target="tpu_custom_call" | custom-call | tf_op jit(solution)/shard_map/exchange_18/pallas_call | solution.py:219
  327.6 8.2 %exchange_19.1 = bf16[8,16,1024]{2,1,0:T(8,128)(2,1)S(1)} custom-call(bf16[8,16,1024]{2,1,0:T(8,128)(2,1)S(1)} %bitcast.937), custom_call_target="tpu_custom_call" | custom-call | tf_op jit(solution)/shard_map/exchange_19/pallas_call | solution.py:219
  337.2 9.1 %exchange_20.1 = bf16[8,16,1024]{2,1,0:T(8,128)(2,1)S(1)} custom-call(bf16[16,1024]{1,0:T(8,128)(2,1)S(1)} %get-tuple-element.1619.refs_0_), custom_call_target="tpu_custom_call" | custom-call | tf_op jit(solution)/shard_map/exchange_20/pallas_call | solution.py:219
  347.9 17.3 %exchange_21.1 = (bf16[8,128,256]{2,1,0:T(8,128)(2,1)S(1)}, f32[8,4,128]{2,1,0:T(4,128)S(1)}) custom-call(bf16[128,256]{1,0:T(8,128)(2,1)S(1)} %get-tuple-element.1758.refs_0_, f32[4,128]{1,0:T(4,128)S(1)} %bitcast.946), custom_call_target="tpu_custom_call" | custom-call | tf_op jit(solution)/shard_map/exchange_21/pallas_call | solution.py:219
  367.9 2.9 fusion.210
  371.0 3.0 multiply_convert_fusion.3
  380.5 2.7 fusion.225
  390.8 2.7 fusion.193
  393.6 5.9 fusion.215
  399.5 4.3 multiply_reduce_fusion.14
  410.6 12.0 %exchange_22.1 = bf16[8,128,256]{2,1,0:T(8,128)(2,1)S(1)} custom-call(bf16[8,128,256]{2,1,0:T(8,128)(2,1)S(1)} %reshape.2476.refs_0_), custom_call_target="tpu_custom_call" | custom-call | tf_op jit(solution)/shard_map/exchange_22/pallas_call | solution.py:219
  427.1 10.8 %exchange_23.1 = bf16[8,16,1024]{2,1,0:T(8,128)(2,1)S(1)} custom-call(bf16[8,16,1024]{2,1,0:T(8,128)(2,1)S(1)} %bitcast.935), custom_call_target="tpu_custom_call" | custom-call | tf_op jit(solution)/shard_map/exchange_23/pallas_call | solution.py:219
  439.6 4.7 exchange_26.1
  444.3 3.6 fusion.194
  447.9 4.3 while.82
  452.4 6.2 convert_element_type.756
  458.7 9.1 %exchange_24.1 = bf16[8,16,1024]{2,1,0:T(8,128)(2,1)S(1)} custom-call(bf16[16,1024]{1,0:T(8,128)(2,1)S(1)} %add_convert_fusion.7.refs_0_), custom_call_target="tpu_custom_call" | custom-call | tf_op jit(solution)/shard_map/exchange_24/pallas_call | solution.py:219
  468.5 4.0 reshape.2486
  472.5 3.3 pad_maximum_fusion.5
  475.8 4.7 all-to-all-start.1
  485.0 70.9 %settle.1 = (f32[32,2048]{1,0:T(8,128)S(1)}, bf16[4,112,1024]{2,1,0:T(8,128)(2,1)S(1)}, bf16[8,32,256]{2,1,0:T(8,128)(2,1)S(1)}, f32[32,1,128]{2,1,0:T(1,128)S(1)}) custom-call(bf16[4,4,2,32,2048]{4,3,2,1,0:T(8,128)(2,1)S(1)} %bitcast.916, bf16[4,112,1024]{2,1,0:T(8,128)(2,1)S(1)} %bitcast.920, bf16[4,8,32,256]{3,2,1,0:T(8,128)(2,1)S(1)} %bitcast.930, ...), custom_call_target="tpu_custom_call" | custom-call | tf_op jit(solution)/shard_map/settle/pallas_call | solution.py:219
  555.9 3.8 copy-done.1
  559.7 17.9 %table_grad.1 = (bf16[4748,1024]{1,0:T(8,128)(2,1)}, f32[1,1024]{1,0:T(1,128)}) custom-call(f32[4748,512]{1,0:T(8,128)S(1)} %bitcast.909, bf16[512,1024]{1,0:T(8,128)(2,1)S(1)} %bitcast.918, f32[1,512]{1,0:T(1,128)S(1)} %reshape.2461.norms, f32[1,512]{1,0:T(1,128)S(1)} %reshape.2462.weights, s32[1,512]{1,0:T(1,128)S(1)} %sub.580.targets, ...), custom_call_target="tpu_custom_call" | custom-call | flops 9334947840 | bytes 19447808 | tf_op jit(solution)/shard_map/table_grad/pallas_call | solution.py:634
  577.6 5.6 while.85
  590.1 5.2 all-to-all-start.2
  600.0 7.9 %all-to-all-done.2 = bf16[8,32,768]{2,1,0:T(8,128)(2,1)S(1)} async-done(((bf16[8,32,768]{2,1,0:T(8,128)(2,1)}), bf16[8,32,768]{2,1,0:T(8,128)(2,1)S(1)}, u32[]{:S(2)}, u32[]{:S(2)}) %all-to-all-start.2) | async-done | bytes 393248 | tf_op jit(solution)/shard_map/all_to_all | solution.py:1187
  611.3 8.5 %exchange_28.1 = f32[32,1,128]{2,1,0:T(1,128)S(1)} custom-call(f32[1,128]{1,0:T(1,128)S(1)} %fusion.259.refs_0_), custom_call_target="tpu_custom_call" | custom-call | tf_op jit(solution)/shard_map/exchange_28/pallas_call | solution.py:219
  630.9 2.8 add_multiply_fusion.1
  639.1 48.9 %adam.1 = (f32[4748,1024]{1,0:T(8,128)}, f32[4748,1024]{1,0:T(8,128)}, f32[4748,1024]{1,0:T(8,128)}) custom-call(f32[3]{0:T(128)S(1)} %pad_maximum_fusion.21.numbers, f32[4748,1024]{1,0:T(8,128)} %get-tuple-element.2848, f32[4748,1024]{1,0:T(8,128)} %first.1, f32[4748,1024]{1,0:T(8,128)} %second.1, bf16[4748,1024]{1,0:T(8,128)(2,1)} %get-tuple-element.2842), custom_call_target="tpu_custom_call" | custom-call | tf_op jit(solution)/shard_map/adam/pallas_call | solution.py:678
  (511 shorter events, 129.0 us)
Async XLA Ops:
  0.7 18.1 %copy-start.75 = (f32[32,4096]{1,0:T(8,128)S(1)}, f32[32,4096]{1,0:T(8,128)}, u32[]{:S(2)}) copy-start(f32[32,4096]{1,0:T(8,128)} %param.43) | copy-start | bytes 1572868
  0.7 18.1 %copy-start.66 = (f32[32,6144]{1,0:T(8,128)S(1)}, f32[32,6144]{1,0:T(8,128)}, u32[]{:S(2)}) copy-start(f32[32,6144]{1,0:T(8,128)} %param.49) | copy-start | bytes 2359300
  15.4 64.3 %copy-start.12 = (f32[8,4,304]{2,1,0:T(4,128)}, f32[8,4,304]{2,1,0:T(4,128)S(1)}, u32[]{:S(2)}) copy-start(f32[8,4,304]{2,1,0:T(4,128)S(1)} %get-tuple-element.1239) | copy-start | bytes 116740
  72.0 42.4 %copy-start.10 = (bf16[4,8,32,256]{3,2,1,0:T(8,128)(2,1)}, bf16[4,8,32,256]{3,2,1,0:T(8,128)(2,1)S(1)}, u32[]{:S(2)}) copy-start(bf16[4,8,32,256]{3,2,1,0:T(8,128)(2,1)S(1)} %get-tuple-element.1243) | copy-start | bytes 1572868
  72.0 57.1 %copy-start.2 = (bf16[4,112,1024]{2,1,0:T(8,128)(2,1)}, bf16[4,112,1024]{2,1,0:T(8,128)(2,1)S(1)}, u32[]{:S(2)}) copy-start(bf16[4,112,1024]{2,1,0:T(8,128)(2,1)S(1)} %get-tuple-element.1240) | copy-start | bytes 2752516
  74.3 118.1 %all-to-all-start = ((bf16[4,352,1024]{2,1,0:T(8,128)(2,1)}), bf16[4,352,1024]{2,1,0:T(8,128)(2,1)}, u32[]{:S(2)}, u32[]{:S(2)}) async-start(bf16[4,352,1024]{2,1,0:T(8,128)(2,1)} %broadcast_in_dim.477), calls=%async_computation | async-start | bytes 5767168 | tf_op jit(solution)/shard_map/all_to_all | solution.py:853
  91.8 23.1 %copy-start.170 = (f32[64]{0:T(128)S(1)}, f32[64]{0:T(128)}, u32[]{:S(2)}) copy-start(f32[64]{0:T(128)} %negate_power_fusion.4) | copy-start | bytes 772
  91.8 23.1 %copy-start.177 = (f32[128]{0:T(128)S(1)}, f32[128]{0:T(128)}, u32[]{:S(2)}) copy-start(f32[128]{0:T(128)} %convert_element_type.710) | copy-start | bytes 1540
  103.6 209.0 %copy-start.70 = (f32[16,2048]{1,0:T(8,128)}, f32[16,2048]{1,0:T(8,128)S(1)}, u32[]{:S(2)}) copy-start(f32[16,2048]{1,0:T(8,128)S(1)} %convert_reduce_fusion.2) | copy-start | bytes 393220
  114.3 14.6 %copy-start.8 = (bf16[8,16,1024]{2,1,0:T(8,128)(2,1)}, bf16[8,16,1024]{2,1,0:T(8,128)(2,1)S(1)}, u32[]{:S(2)}) copy-start(bf16[8,16,1024]{2,1,0:T(8,128)(2,1)S(1)} %exchange_8.1) | copy-start | bytes 786436
  114.9 14.5 %copy-start.73 = (f32[128,2,128]{0,2,1:T(8,128)}, f32[128,2,128]{0,2,1:T(8,128)S(1)}, u32[]{:S(2)}) copy-start(f32[128,2,128]{0,2,1:T(8,128)S(1)} %get-tuple-element.1752) | copy-start | bytes 393220
  114.9 14.2 %copy-start.147 = (f32[4,112]{1,0:T(4,128)S(1)}, f32[4,112]{1,0:T(4,128)}, u32[]{:S(2)}) copy-start(f32[4,112]{1,0:T(4,128)} %fusion.184) | copy-start | bytes 5380
  114.9 14.5 %copy-start.139 = (f32[128,2]{0,1:T(2,128)}, f32[128,2]{0,1:T(2,128)S(1)}, u32[]{:S(2)}) copy-start(f32[128,2]{0,1:T(2,128)S(1)} %add_rsqrt_fusion.10) | copy-start | bytes 3076
  115.8 13.7 %copy-start.113 = (f32[128,64]{0,1:T(8,128)}, f32[128,64]{0,1:T(8,128)S(1)}, u32[]{:S(2)}) copy-start(f32[128,64]{0,1:T(8,128)S(1)} %get-tuple-element.1747) | copy-start | bytes 98308
  137.2 41.1 %copy-start.115 = (f32[448,8]{0,1:T(8,128)}, f32[448,8]{0,1:T(8,128)S(1)}, u32[]{:S(2)}) copy-start(f32[448,8]{0,1:T(8,128)S(1)} %add_rsqrt_fusion.8) | copy-start | bytes 43012
  149.8 30.1 %copy-start.136 = (s32[8,16]{1,0:T(8,128)S(1)}, s32[8,16]{1,0:T(8,128)}, u32[]{:S(2)}) copy-start(s32[8,16]{1,0:T(8,128)} %get-tuple-element.2833) | copy-start | bytes 1540
  191.8 120.8 %copy-start.161 = (f32[16]{0:T(128)}, f32[16]{0:T(128)S(1)}, u32[]{:S(2)}) copy-start(f32[16]{0:T(128)S(1)} %get-tuple-element.1744) | copy-start | bytes 196
  198.0 20.3 %copy-start.47 = (bf16[1024,768]{1,0:T(8,128)(2,1)}, bf16[1024,768]{1,0:T(8,128)(2,1)S(1)}, u32[]{:S(2)}) copy-start(bf16[1024,768]{1,0:T(8,128)(2,1)S(1)} %reshape.2455) | copy-start | bytes 4718596
  219.7 35.4 %copy-start.65 = (bf16[4,96,1024]{2,1,0:T(8,128)(2,1)}, bf16[4,96,1024]{2,1,0:T(8,128)(2,1)S(1)}, u32[]{:S(2)}) copy-start(bf16[4,96,1024]{2,1,0:T(8,128)(2,1)S(1)} %slice.468) | copy-start | bytes 2359300
  229.4 107.1 %copy-start.143 = (f32[16]{0:T(128)}, f32[16]{0:T(128)S(1)}, u32[]{:S(2)}) copy-start(f32[16]{0:T(128)S(1)} %add_rsqrt_fusion.11) | copy-start | bytes 196
  265.4 13.7 %copy-start = (f32[512,4748]{0,1:T(8,128)}, f32[512,4748]{0,1:T(8,128)S(1)}, u32[]{:S(2)}) copy-start(f32[512,4748]{0,1:T(8,128)S(1)} %get-tuple-element.1756) | copy-start | bytes 29171716
  299.5 27.4 %copy-start.48 = (bf16[1024,768]{1,0:T(8,128)(2,1)S(1)}, bf16[1024,768]{1,0:T(8,128)(2,1)}, u32[]{:S(2)}) copy-start(bf16[1024,768]{1,0:T(8,128)(2,1)} %copy-done.47) | copy-start | bytes 4718596
  312.4 15.1 %copy-start.172 = (f32[16]{0:T(128)}, f32[16]{0:T(128)S(1)}, u32[]{:S(2)}) copy-start(f32[16]{0:T(128)S(1)} %log_add_fusion.1) | copy-start | bytes 196
  326.9 19.4 %copy-start.107 = (bf16[128,384]{1,0:T(8,128)(2,1)}, bf16[128,384]{1,0:T(8,128)(2,1)S(1)}, u32[]{:S(2)}) copy-start(bf16[128,384]{1,0:T(8,128)(2,1)S(1)} %get-tuple-element.1716) | copy-start | bytes 294916
  326.9 19.4 %copy-start.109 = (bf16[128,384]{1,0:T(8,128)(2,1)}, bf16[128,384]{1,0:T(8,128)(2,1)S(1)}, u32[]{:S(2)}) copy-start(bf16[128,384]{1,0:T(8,128)(2,1)S(1)} %get-tuple-element.1717) | copy-start | bytes 294916
  347.8 20.1 %copy-start.81 = (pred[256,448]{0,1:T(8,128)(4,1)S(1)}, pred[256,448]{0,1:T(8,128)(4,1)}, u32[]{:S(2)}) copy-start(pred[256,448]{0,1:T(8,128)(4,1)} %copy-done.80) | copy-start | bytes 344068
  347.8 20.1 %copy-start.155 = (f32[8,256]{1,0:T(8,128)S(1)}, f32[8,256]{1,0:T(8,128)}, u32[]{:S(2)}) copy-start(f32[8,256]{1,0:T(8,128)} %add.1124) | copy-start | bytes 24580
  409.7 13.8 %copy-start.114 = (f32[128,64]{0,1:T(8,128)S(1)}, f32[128,64]{0,1:T(8,128)}, u32[]{:S(2)}) copy-start(f32[128,64]{0,1:T(8,128)} %copy-done.113) | copy-start | bytes 98308
  410.2 14.1 %copy-start.74 = (f32[128,2,128]{0,2,1:T(8,128)S(1)}, f32[128,2,128]{0,2,1:T(8,128)}, u32[]{:S(2)}) copy-start(f32[128,2,128]{0,2,1:T(8,128)} %copy-done.73) | copy-start | bytes 393220
  410.3 16.2 %copy-start.11 = (bf16[4,8,32,256]{3,2,1,0:T(8,128)(2,1)S(1)}, bf16[4,8,32,256]{3,2,1,0:T(8,128)(2,1)}, u32[]{:S(2)}) copy-start(bf16[4,8,32,256]{3,2,1,0:T(8,128)(2,1)} %copy-done.10) | copy-start | bytes 1572868
  422.6 15.4 %copy-start.71 = (f32[16,2048]{1,0:T(8,128)S(1)}, f32[16,2048]{1,0:T(8,128)}, u32[]{:S(2)}) copy-start(f32[16,2048]{1,0:T(8,128)} %copy-done.70) | copy-start | bytes 393220
  422.6 15.4 %copy-start.125 = (f32[1024]{0:T(1024)S(1)}, f32[1024]{0:T(1024)}, u32[]{:S(2)}) copy-start(f32[1024]{0:T(1024)} %get-tuple-element.1728) | copy-start | bytes 12292
  422.6 21.7 %copy-start.129 = (f32[3584]{0:T(1024)S(1)}, f32[3584]{0:T(1024)}, u32[]{:S(2)}) copy-start(f32[3584]{0:T(1024)} %rsqrt.188) | copy-start | bytes 43012
  422.7 21.6 %copy-start.60 = (f32[3584,128]{1,0:T(8,128)S(1)}, f32[3584,128]{1,0:T(8,128)}, u32[]{:S(2)}) copy-start(f32[3584,128]{1,0:T(8,128)} %reshape.2472) | copy-start | bytes 5505028
  452.3 15.5 %copy-start.171 = (f32[448]{0:T(512)S(1)}, f32[448]{0:T(512)}, u32[]{:S(2)}) copy-start(f32[448]{0:T(512)} %get-tuple-element.1425) | copy-start | bytes 5380
  452.3 15.5 %copy-start.9 = (bf16[8,16,1024]{2,1,0:T(8,128)(2,1)S(1)}, bf16[8,16,1024]{2,1,0:T(8,128)(2,1)}, u32[]{:S(2)}) copy-start(bf16[8,16,1024]{2,1,0:T(8,128)(2,1)} %copy-done.8) | copy-start | bytes 786436
  452.4 15.5 %copy-start.102 = (bf16[128,2,128]{0,2,1:T(8,128)(2,1)S(1)}, bf16[128,2,128]{0,2,1:T(8,128)(2,1)}, u32[]{:S(2)}) copy-start(bf16[128,2,128]{0,2,1:T(8,128)(2,1)} %copy-done.101) | copy-start | bytes 196612
  452.4 15.9 %copy-start.128 = (f32[1024]{0:T(1024)S(1)}, f32[1024]{0:T(1024)}, u32[]{:S(2)}) copy-start(f32[1024]{0:T(1024)} %get-tuple-element.1261) | copy-start | bytes 12292
  452.4 15.9 %copy-start.140 = (f32[1024]{0:T(1024)S(1)}, f32[1024]{0:T(1024)}, u32[]{:S(2)}) copy-start(f32[1024]{0:T(1024)} %get-tuple-element.1432) | copy-start | bytes 12292
  452.4 15.9 %copy-start.142 = (f32[1024]{0:T(1024)S(1)}, f32[1024]{0:T(1024)}, u32[]{:S(2)}) copy-start(f32[1024]{0:T(1024)} %get-tuple-element.1436) | copy-start | bytes 12292
  452.4 15.9 %copy-start.141 = (f32[1024]{0:T(1024)S(1)}, f32[1024]{0:T(1024)}, u32[]{:S(2)}) copy-start(f32[1024]{0:T(1024)} %get-tuple-element.1434) | copy-start | bytes 12292
  452.4 15.9 %copy-start.175 = (f32[128]{0:T(128)S(1)}, f32[128]{0:T(128)}, u32[]{:S(2)}) copy-start(f32[128]{0:T(128)} %get-tuple-element.1427) | copy-start | bytes 1540
  452.4 15.9 %copy-start.180 = (f32[128]{0:T(128)S(1)}, f32[128]{0:T(128)}, u32[]{:S(2)}) copy-start(f32[128]{0:T(128)} %get-tuple-element.1262) | copy-start | bytes 1540
  475.8 110.7 %all-to-all-start.1 = ((bf16[4,352,1024]{2,1,0:T(8,128)(2,1)}), bf16[4,352,1024]{2,1,0:T(8,128)(2,1)}, u32[]{:S(2)}, u32[]{:S(2)}) async-start(bf16[4,352,1024]{2,1,0:T(8,128)(2,1)} %pad_maximum_fusion.5), calls=%async_computation.1 | async-start | bytes 5767168 | tf_op jit(solution)/shard_map/all_to_all | solution.py:1071
  485.0 70.9 %copy-start.7 = (bf16[4,128,1024]{2,1,0:T(8,128)(2,1)S(1)}, bf16[4,128,1024]{2,1,0:T(8,128)(2,1)}, u32[]{:S(2)}) copy-start(bf16[4,128,1024]{2,1,0:T(8,128)(2,1)} %copy-done.6) | copy-start | bytes 3145732
  559.7 17.9 %copy-start.137 = (s32[128]{0:T(128)S(1)}, s32[128]{0:T(128)}, u32[]{:S(2)}) copy-start(s32[128]{0:T(128)} %eq.531) | copy-start | bytes 1540
  559.7 17.9 %copy-start.152 = (f32[8,256,1]{1,0,2:T(8,128)S(1)}, f32[8,256,1]{1,0,2:T(8,128)}, u32[]{:S(2)}) copy-start(f32[8,256,1]{1,0,2:T(8,128)} %get-tuple-element.2835) | copy-start | bytes 24580
  590.1 17.7 %all-to-all-start.2 = ((bf16[8,32,768]{2,1,0:T(8,128)(2,1)}), bf16[8,32,768]{2,1,0:T(8,128)(2,1)S(1)}, u32[]{:S(2)}, u32[]{:S(2)}) async-start(bf16[8,32,768]{2,1,0:T(8,128)(2,1)} %reshape.2489), calls=%async_computation.2 | async-start | bytes 786432 | tf_op jit(solution)/shard_map/all_to_all | solution.py:1187
  (82 other events, 316.7 us)

commit v3 on v2

v3 whole, which is shorter than its diff:
```python
import functools
import math

import jax
import jax.numpy as jnp
from jax import lax
from jax.experimental import pallas as pl
from jax.experimental.pallas import tpu as pltpu
from jax.sharding import PartitionSpec as P

MODEL_WIDTH = 1024
QUERY_HEADS = 16
KEY_VALUE_HEADS = 8
HEAD_WIDTH = 128
FF = 3072
QUERY_WIDTH = QUERY_HEADS * HEAD_WIDTH

norm_eps = 1e-06
rope_base = 1000000.0
clip_limit = 0.01
beta_first = 0.9
beta_second = 0.95
adam_eps = 1e-08
learning_rates = (0.01, 0.003, 0.07, 0.003, 0.002, 0.01)
weight_decays = (0.1, 0.1, 0.1, 0.1, 0.1, 0.0)
masked_score = -1e30

bf16 = jnp.bfloat16
f32 = jnp.float32
BOTH = ("ulysses", "blk")


def inverse_root(values):
    return lax.rsqrt(jnp.mean(values * values, axis=-1, keepdims=True) + norm_eps)


def norm_back(inputs, gain_vec, upstream):
    root_scale = inverse_root(inputs)
    unit_rows = inputs * root_scale
    weighted = upstream * gain_vec
    grad_inputs = root_scale * (
        weighted - unit_rows * jnp.mean(weighted * unit_rows, axis=-1, keepdims=True)
    )
    grad_gain = jnp.sum((upstream * unit_rows).reshape(-1, gain_vec.shape[-1]), axis=0)
    return (grad_inputs, grad_gain)


def rope_angles(positions):
    half_width = HEAD_WIDTH // 2
    frequency = rope_base ** (
        -(jnp.arange(half_width, dtype=jnp.int32).astype(f32) * 2.0 / HEAD_WIDTH)
    )
    angles = positions.astype(f32)[:, None] * frequency[None, :]
    return (jnp.cos(angles), jnp.sin(angles))


def rotate(values, tables, sign_value):
    half_width = values.shape[-1] // 2
    front_half = values[..., :half_width]
    back_half = values[..., half_width:]
    cosine_part = tables[0][:, None, :]
    sine_part = tables[1][:, None, :] * sign_value
    return jnp.concatenate(
        [
            front_half * cosine_part - back_half * sine_part,
            back_half * cosine_part + front_half * sine_part,
        ],
        axis=-1,
    )


def mm(left, right):
    return lax.dot_general(left, right, (((1,), (0,)), ((), ())), preferred_element_type=f32)


def mm_outer(left, right):
    return lax.dot_general(left, right, (((0,), (0,)), ((), ())), preferred_element_type=f32)


def mm_back(left, right):
    return lax.dot_general(left, right, (((1,), (1,)), ((), ())), preferred_element_type=f32)


def spread_rows(onehot, rows):
    return lax.dot_general(
        onehot.astype(f32),
        rows,
        (((0,), (0,)), ((), ())),
        precision=lax.Precision.HIGHEST,
        preferred_element_type=f32,
    )


def adam_update(weight_now, first_now, second_now, gradient, rate_value, decay_value, step_float):
    new_first = beta_first * first_now + (1.0 - beta_first) * gradient
    new_second = beta_second * second_now + (1.0 - beta_second) * gradient * gradient
    first_hat = new_first / (1.0 - beta_first**step_float)
    second_hat = new_second / (1.0 - beta_second**step_float)
    change = -rate_value * (
        first_hat / (jnp.sqrt(second_hat) + adam_eps) + decay_value * weight_now
    )
    return (change, new_first, new_second)


def place_of(axis, blk_count, peer):
    if axis == "all":
        return {"ulysses": peer // blk_count, "blk": lax.rem(peer, blk_count)}
    return {axis: peer}


def rank_of(axis, blk_count):
    row, column = lax.axis_index("ulysses"), lax.axis_index("blk")
    return {"ulysses": row, "blk": column, "all": row * blk_count + column}[axis]


def greet(axes, blk_count, counts):
    barrier = pltpu.get_barrier_semaphore()
    axes = ("all",) if "all" in axes else tuple(axes)
    total = 0
    for axis in axes:
        me, count = rank_of(axis, blk_count), counts[axis]

        def call(step, carry, axis=axis, me=me, count=count):
            pl.semaphore_signal(
                barrier,
                inc=1,
                device_id=place_of(axis, blk_count, lax.rem(me + step, count)),
                device_id_type=pl.DeviceIdType.MESH,
            )
            return carry

        lax.fori_loop(1, count, call, 0)
        total += count - 1
    pl.semaphore_wait(barrier, total)


def each(count, body, first=0):
    def step(k, carry):
        body(k)
        return carry

    lax.fori_loop(first, count, step, 0)


def remote(source, target, send_sem, recv_sem, device_id):
    return pltpu.make_async_remote_copy(
        src_ref=source,
        dst_ref=target,
        send_sem=send_sem,
        recv_sem=recv_sem,
        device_id=device_id,
        device_id_type=pl.DeviceIdType.MESH,
    )


class Part:
    def __init__(self, axis, kind, source, landing, send_sems, recv_sems, own_sem, blk_count):
        self.axis, self.kind, self.blk_count = axis, kind, blk_count
        self.source, self.landing = source, landing
        self.send_sems, self.recv_sems, self.own_sem = send_sems, recv_sems, own_sem
        self.me, self.count = rank_of(axis, blk_count), landing.shape[0]

    def copy(self, step):
        peer = lax.rem(self.me + step, self.count)
        return remote(
            self.source.at[peer] if self.kind == "s" else self.source,
            self.landing.at[self.me],
            self.send_sems.at[step],
            self.recv_sems.at[step],
            place_of(self.axis, self.blk_count, peer),
        )

    def own(self):
        return pltpu.make_async_copy(
            self.source.at[self.me] if self.kind == "s" else self.source,
            self.landing.at[self.me],
            self.own_sem,
        )

    def start(self):
        each(self.count, lambda step: self.copy(step).start(), 1)
        self.own().start()

    def finish(self):
        self.own().wait()
        each(self.count, lambda step: self.copy(step).wait(), 1)


def sems(count):
    return [
        pltpu.SemaphoreType.DMA((count,)),
        pltpu.SemaphoreType.DMA((count,)),
        pltpu.SemaphoreType.DMA,
    ]


def exchange_kernel(plan, blk_count, counts, *refs):
    parts = len(plan)
    entries = [
        Part(axis, kind, refs[k], refs[parts + k], *refs[2 * parts + 3 * k :][:3], blk_count)
        for k, (axis, kind) in enumerate(plan)
    ]
    greet({axis for axis, _ in plan}, blk_count, counts)
    for entry in entries:
        entry.start()
    for entry in entries:
        entry.finish()


def axis_counts():
    n_u, n_b = lax.axis_size("ulysses"), lax.axis_size("blk")
    return {"ulysses": n_u, "blk": n_b, "all": n_u * n_b}


VMEM = pl.BlockSpec(memory_space=pltpu.VMEM)


def remote_call(kernel, collective_id, shapes, scratch, arrays, name):
    return pl.pallas_call(
        kernel,
        out_shape=shapes,
        in_specs=[VMEM] * len(arrays),
        out_specs=[VMEM] * len(shapes),
        scratch_shapes=scratch,
        compiler_params=pltpu.CompilerParams(
            collective_id=collective_id,
            has_side_effects=True,
            vmem_limit_bytes=56 * 1024 * 1024,
        ),
        name=name,
    )(*arrays)


class Exchanger:
    def __init__(self):
        self.used = 0

    def next_id(self):
        self.used += 1
        return self.used - 1

    def many(self, plan, *arrays, collective_id=None):
        counts = axis_counts()
        shapes = [
            jax.ShapeDtypeStruct(
                array.shape if kind == "s" else (counts[axis],) + array.shape, array.dtype
            )
            for (axis, kind), array in zip(plan, arrays)
        ]
        scratch = []
        for axis, _ in plan:
            scratch += sems(counts[axis])
        if collective_id is None:
            collective_id = self.next_id()
        return remote_call(
            functools.partial(exchange_kernel, plan, counts["blk"], counts),
            collective_id,
            shapes,
            scratch,
            arrays,
            "exchange_" + str(collective_id),
        )

    def __call__(self, axis, kinds, *arrays):
        return self.many(tuple((axis, kind) for kind in kinds), *arrays)


def start_kernel(
    blk_count,
    counts,
    rows_in,
    kv_in,
    q_in,
    ff_in,
    rows_out,
    kv_out,
    q_out,
    ff_out,
    q_split,
    z_send,
    z_recv,
    own_sem,
    xy_send,
    xy_recv,
    core_send,
    core_recv,
    *part_sems,
):
    u, b = lax.axis_index("ulysses"), lax.axis_index("blk")
    n_u, n_z = kv_out.shape[0], kv_out.shape[1]
    z, c = b // 2, lax.rem(b, 2)
    greet({"ulysses", "blk"}, blk_count, counts)
    rows = Part("ulysses", "s", rows_in, rows_out, *part_sems[0:3], blk_count)
    first_q = Part("blk", "s", q_in, q_split, *part_sems[3:6], blk_count)
    then_q = Part("ulysses", "g", q_split, q_out, *part_sems[6:9], blk_count)
    split_ff = Part("blk", "s", ff_in, ff_out, *part_sems[9:12], blk_count)

    def along_z(step):
        mine = kv_out.at[u, z, c]
        return remote(
            kv_in,
            mine,
            z_send.at[step],
            z_recv.at[step],
            {"blk": lax.rem(z + step, n_z) * 2 + c},
        )

    def own_copy():
        return pltpu.make_async_copy(kv_in, kv_out.at[u, z, c], own_sem)

    def block(hop, step):
        return kv_out.at[lax.rem(u - hop + n_u, n_u), lax.rem(z - step + n_z, n_z), c]

    def across(hop, step):
        place = block(0, step)
        return remote(
            place,
            place,
            xy_send.at[hop, step],
            xy_recv.at[hop, step],
            {"ulysses": lax.rem(u + hop, n_u)},
        )

    def to_core(hop, step):
        place = block(hop, step)
        return remote(
            place,
            place,
            core_send.at[hop, step],
            core_recv.at[hop, step],
            {"blk": z * 2 + 1 - c},
        )

    own_copy().start()
    each(n_z, lambda step: along_z(step).start(), 1)
    first_q.start()
    rows.start()
    own_copy().wait()
    each(n_u, lambda hop: across(hop, 0).start(), 1)
    to_core(0, 0).start()
    split_ff.start()

    def pass_on(step):
        along_z(step).wait_recv()
        each(n_u, lambda hop: across(hop, step).start(), 1)
        to_core(0, step).start()

    each(n_z, pass_on, 1)
    first_q.finish()
    then_q.start()

    def share(step):
        def one(hop):
            across(hop, step).wait_recv()
            to_core(hop, step).start()

        each(n_u, one, 1)

    each(n_z, share)
    rows.finish()
    split_ff.finish()
    then_q.finish()
    each(n_z, lambda step: along_z(step).wait_send(), 1)
    each(n_z, lambda step: each(n_u, lambda hop: across(hop, step).wait_send(), 1))
    each(n_z, lambda step: each(n_u, lambda hop: to_core(hop, step).wait()))


def start_call(exchange, rows, kv_low, q_cols, ff_cols):
    counts = axis_counts()
    n_u, n_b = counts["ulysses"], counts["blk"]
    n_z = n_b // 2
    dma = pltpu.SemaphoreType.DMA
    return remote_call(
        functools.partial(start_kernel, n_b, counts),
        exchange.next_id(),
        [
            jax.ShapeDtypeStruct(rows.shape, bf16),
            jax.ShapeDtypeStruct((n_u, n_z, 2) + kv_low.shape, bf16),
            jax.ShapeDtypeStruct((n_u,) + q_cols.shape, bf16),
            jax.ShapeDtypeStruct(ff_cols.shape, bf16),
        ],
        [
            pltpu.VMEM(q_cols.shape, bf16),
            dma((n_z,)),
            dma((n_z,)),
            dma,
            dma((n_u, n_z)),
            dma((n_u, n_z)),
            dma((n_u, n_z)),
            dma((n_u, n_z)),
        ]
        + sems(n_u)
        + sems(n_b)
        + sems(n_u)
        + sems(n_b),
        (rows, kv_low, q_cols, ff_cols),
        "start",
    )


def settle_kernel(
    blk_count,
    counts,
    kv_in,
    rows_in,
    q_in,
    ff_in,
    gains_in,
    kv_out,
    rows_out,
    q_out,
    ff_out,
    gains_out,
    kv_core,
    kv_pair,
    kv_cross,
    kv_plane,
    kv_line,
    q_got,
    q_sum,
    core_send,
    core_recv,
    xy_send,
    xy_recv,
    z_send,
    z_recv,
    *part_sems,
):
    u, b = lax.axis_index("ulysses"), lax.axis_index("blk")
    n_u, n_z = kv_in.shape[0], kv_in.shape[1]
    z, c = b // 2, lax.rem(b, 2)
    greet({"all"}, blk_count, counts)
    rows = Part("ulysses", "s", rows_in, rows_out, *part_sems[0:3], blk_count)
    first_q = Part("ulysses", "s", q_in, q_got, *part_sems[3:6], blk_count)
    then_q = Part("blk", "s", q_sum, q_out, *part_sems[6:9], blk_count)
    gains = Part("all", "s", gains_in, gains_out, *part_sems[9:12], blk_count)
    split_ff = Part("blk", "s", ff_in, ff_out, *part_sems[12:15], blk_count)

    def place(hop, step):
        return (lax.rem(u + hop, n_u), lax.rem(z + step, n_z))

    def to_core(hop, step):
        row, line = place(hop, step)
        return remote(
            kv_in.at[row, line, 1 - c],
            kv_core.at[hop, step],
            core_send.at[hop, step],
            core_recv.at[hop, step],
            {"blk": z * 2 + 1 - c},
        )

    def across(hop, step):
        return remote(
            kv_pair.at[hop, step],
            kv_cross.at[hop, step],
            xy_send.at[hop, step],
            xy_recv.at[hop, step],
            {"ulysses": lax.rem(u + hop, n_u)},
        )

    def along_z(step):
        return remote(
            kv_plane.at[step],
            kv_line.at[step],
            z_send.at[step],
            z_recv.at[step],
            {"blk": lax.rem(z + step, n_z) * 2 + c},
        )

    each(n_z, lambda step: each(n_u, lambda hop: to_core(hop, step).start()))
    first_q.start()
    split_ff.start()

    def add_pair(step):
        def one(hop):
            row, line = place(hop, step)
            to_core(hop, step).wait_recv()
            kv_pair[hop, step] = (
                kv_in[row, line, c].astype(f32) + kv_core[hop, step].astype(f32)
            ).astype(bf16)

        def forward(hop):
            one(hop)
            across(hop, step).start()

        one(0)
        each(n_u, forward, 1)

    each(n_z, add_pair, 1)
    add_pair(0)
    rows.start()
    gains.start()
    first_q.finish()
    q_sum[...] = jnp.sum(q_got[...].astype(f32), axis=0).astype(bf16)
    then_q.start()

    def plane_sum(step):
        total = kv_pair[0, step].astype(f32)
        for hop in range(1, n_u):
            across(hop, step).wait_recv()
            total = total + kv_cross[hop, step].astype(f32)
        return total

    def add_plane(step):
        kv_plane[step] = plane_sum(step).astype(bf16)
        along_z(step).start()

    each(n_z, add_plane, 1)
    total = plane_sum(0)
    for step in range(1, n_z):
        along_z(step).wait_recv()
        total = total + kv_line[step].astype(f32)
    kv_out[...] = total
    then_q.finish()
    split_ff.finish()
    gains.finish()
    rows.finish()
    each(n_z, lambda step: each(n_u, lambda hop: to_core(hop, step).wait_send()))
    each(n_z, lambda step: each(n_u, lambda hop: across(hop, step).wait_send(), 1))
    each(n_z, lambda step: along_z(step).wait_send(), 1)


def settle_call(exchange, kv_grad, rows, q_grad, ff_grad, gains):
    counts = axis_counts()
    n_u, n_b = counts["ulysses"], counts["blk"]
    n_z = n_b // 2
    block = kv_grad.shape[3:]
    dma = pltpu.SemaphoreType.DMA
    return remote_call(
        functools.partial(settle_kernel, n_b, counts),
        exchange.next_id(),
        [
            jax.ShapeDtypeStruct(block, f32),
            jax.ShapeDtypeStruct(rows.shape, bf16),
            jax.ShapeDtypeStruct(q_grad.shape[1:], bf16),
            jax.ShapeDtypeStruct(ff_grad.shape, bf16),
            jax.ShapeDtypeStruct(gains.shape, f32),
        ],
        [
            pltpu.VMEM((n_u, n_z) + block, bf16),
            pltpu.VMEM((n_u, n_z) + block, bf16),
            pltpu.VMEM((n_u, n_z) + block, bf16),
            pltpu.VMEM((n_z,) + block, bf16),
            pltpu.VMEM((n_z,) + block, bf16),
            pltpu.VMEM(q_grad.shape, bf16),
            pltpu.VMEM(q_grad.shape[1:], bf16),
            dma((n_u, n_z)),
            dma((n_u, n_z)),
            dma((n_u, n_z)),
            dma((n_u, n_z)),
            dma((n_z,)),
            dma((n_z,)),
        ]
        + sems(n_u)
        + sems(n_u)
        + sems(n_b)
        + sems(n_u * n_b)
        + sems(n_b),
        (kv_grad, rows, q_grad, ff_grad, gains),
        "settle",
    )


def norm_back_rows(inputs, gain_vec, upstream):
    root_scale = inverse_root(inputs)
    unit_rows = inputs * root_scale
    weighted = upstream * gain_vec
    grad_inputs = root_scale * (
        weighted - unit_rows * jnp.mean(weighted * unit_rows, axis=-1, keepdims=True)
    )
    return (grad_inputs, jnp.sum(upstream * unit_rows, axis=0, keepdims=True))


class Links:
    def __init__(self, plan, blk_count, sem_refs):
        self.plan, self.blk_count, self.sem_refs = plan, blk_count, sem_refs

    def __call__(self, k, source, landing):
        axis, kind = self.plan[k]
        part = Part(axis, kind, source, landing, *self.sem_refs[3 * k : 3 * k + 3], self.blk_count)
        part.start()
        return part

    def now(self, k, source, landing):
        self(k, source, landing).finish()


def fused_call(exchange, body, plan, arrays, outs, scratch, name):
    counts = axis_counts()
    n_in, n_out, n_scratch = len(arrays), len(outs), len(scratch)
    sem_shapes = []
    for axis, _ in plan:
        sem_shapes += sems(counts[axis])

    def kernel(*refs):
        ins, refs = refs[:n_in], refs[n_in:]
        results, refs = refs[:n_out], refs[n_out:]
        kept, sem_refs = refs[:n_scratch], refs[n_scratch:]
        greet({axis for axis, _ in plan}, counts["blk"], counts)
        body(Links(plan, counts["blk"], sem_refs), ins, results, kept)

    return remote_call(
        kernel,
        exchange.next_id(),
        [jax.ShapeDtypeStruct(shape, dtype) for shape, dtype in outs],
        [pltpu.VMEM(shape, dtype) for shape, dtype in scratch] + sem_shapes,
        arrays,
        name,
    )


def sum_blocks(landing):
    total = landing[0].astype(f32)
    for k in range(1, landing.shape[0]):
        total = total + landing[k].astype(f32)
    return total


def flat_rows_of(ref):
    return ref[...].reshape(-1, ref.shape[-1])


def turned(values, cosines, sines):
    return values * cosines + pltpu.roll(values, HEAD_WIDTH // 2, 1) * sines


def lanes_of(columns, width, count):
    group = lax.broadcasted_iota(jnp.int32, (columns[0].shape[0], width * count), 1) // width
    spread = columns[0]
    for k in range(1, count):
        spread = jnp.where(group == k, columns[k], spread)
    return spread


def query_body(n_b, links, ins, outs, scratch):
    pick_part, gain_attn, gain_query, q_weight, cosines, sines, ff_rows, out_rows, down_rows = ins
    picks_out, normed_all, query_raw, query_all, ff_all, out_all, down_all = outs
    pick_got, normed_mine, query_mine = scratch
    first = links(0, pick_part, pick_got)
    behind = [
        links(3, ff_rows, ff_all),
        links(4, out_rows, out_all),
        links(5, down_rows, down_all),
    ]
    first.finish()
    rows = sum_blocks(pick_got)
    picks_out[...] = rows
    mine = rows[:, :MODEL_WIDTH]
    normed_mine[...] = (mine * inverse_root(mine) * gain_attn[...]).astype(bf16)
    links.now(1, normed_mine, normed_all)
    raw = mm(flat_rows_of(normed_all), q_weight[...])
    query_raw[...] = raw
    for k in range(raw.shape[1] // HEAD_WIDTH):
        head = raw[:, k * HEAD_WIDTH : (k + 1) * HEAD_WIDTH]
        query_mine[:, k * HEAD_WIDTH : (k + 1) * HEAD_WIDTH] = turned(
            head * inverse_root(head) * gain_query[...], cosines[...], sines[...]
        ).astype(bf16)
    links.now(2, query_mine, query_all)
    for part in behind:
        part.finish()


def forward_body(n_u, n_b, links, ins, outs, scratch):
    part_send, stats, mine, out_weight, ff_weight, down_weight, gain_mlp, gain_final = ins
    attended_out, log_out, after_out, normed_all, gate_up_out, top_out, final_mine, final_all = outs
    part_got, stats_all, shares, partial, partial_got, normed_mine, final_slot = scratch
    picks = after_out.shape[0]
    out_cut = attended_out.shape[1] // n_u
    heads_row = QUERY_HEADS // n_u
    cut_head = (lax.axis_index("blk") * out_cut) // HEAD_WIDTH
    sent = links(0, part_send, part_got)
    links.now(1, stats, stats_all)
    full_max = stats_all[0, :QUERY_HEADS]
    for k in range(1, n_b):
        full_max = jnp.maximum(full_max, stats_all[k, :QUERY_HEADS])
    full_sum = jnp.zeros_like(full_max)
    for k in range(n_b):
        full_sum += stats_all[k, QUERY_HEADS:] * jnp.exp(stats_all[k, :QUERY_HEADS] - full_max)
    log_total = full_max + jnp.log(full_sum)
    log_out[...] = log_total
    for row in range(n_u):
        head = row * heads_row + cut_head
        row_log = log_out[pl.ds(head, 1), :]
        for k in range(n_b):
            shares[pl.ds(k * n_u + row, 1), :] = jnp.exp(
                stats_all[k, pl.ds(head, 1), :] - row_log
            )
    columns = shares[...].T
    sent.finish()
    attended = jnp.zeros(attended_out.shape, f32)
    for k in range(n_b):
        attended += part_got[k].astype(f32) * lanes_of(
            [columns[:, k * n_u + row : k * n_u + row + 1] for row in range(n_u)], out_cut, n_u
        )
    attended_out[...] = attended

    def to_picks(which, rows):
        partial[...] = rows.astype(bf16).reshape(partial.shape)
        links.now(which, partial, partial_got.at[which // 4])
        return sum_blocks(partial_got.at[which // 4])

    after_attn = mine[:, :MODEL_WIDTH] + to_picks(2, mm(attended.astype(bf16), out_weight[...]))
    after_out[...] = after_attn
    normed_mine[...] = (after_attn * inverse_root(after_attn) * gain_mlp[...]).astype(bf16)
    links.now(3, normed_mine, normed_all)
    gate_up = mm(flat_rows_of(normed_all), ff_weight[...])
    gate_up_out[...] = gate_up
    half = gate_up.shape[1] // 2
    gate_part, up_part = gate_up[:, :half], gate_up[:, half:]
    activated = (gate_part * jax.nn.sigmoid(gate_part) * up_part).astype(bf16)
    after_mlp = after_attn + to_picks(4, mm(activated, down_weight[...]))
    top_out[...] = after_mlp
    final_mine[...] = (after_mlp * inverse_root(after_mlp) * gain_final[...]).astype(bf16)
    links.now(5, final_mine, final_slot)
    links.now(6, final_slot, final_all)


def backward_body(n_u, n_b, links, ins, outs, scratch):
    (
        head_rows,
        head_stats,
        final_mine,
        picks_in,
        weights,
        after_mlp,
        after_attn,
        gate_up_in,
        normed_all,
        attended,
        out_weight,
        ff_weight,
        down_weight,
        gain_mlp,
        gain_final,
    ) = ins
    (
        norms_all,
        terms,
        gain_mlp_out,
        gain_final_out,
        grad_ff,
        grad_out,
        grad_down,
        grad_after,
        branch_all,
        attended_all,
        delta_all,
    ) = outs
    (
        rows_got,
        stats_got,
        slot_stats,
        slot_got,
        factors,
        columns,
        norms_mine,
        partial,
        partial_got,
        mine_low,
        grad_all,
        attended_mine,
        deltas,
        delta_mine,
    ) = scratch
    picks = after_mlp.shape[0]
    slot_picks = n_b * picks
    b = lax.axis_index("blk")
    factors[...] = jnp.zeros_like(factors)
    first = links(0, head_rows, rows_got)
    links.now(1, head_stats, stats_got)
    tops = stats_got[0, 0:1, :]
    for k in range(1, n_u):
        tops = jnp.maximum(tops, stats_got[k, 0:1, :])
    total = jnp.zeros_like(tops)
    for k in range(n_u):
        factor = jnp.exp(stats_got[k, 0:1, :] - tops)
        factors[k : k + 1, :] = factor
        total += stats_got[k, 1:2, :] * factor
    slot_stats[...] = jnp.zeros_like(slot_stats)
    slot_stats[0:1, :] = tops
    slot_stats[1:2, :] = total
    slot_part = links(3, slot_stats, slot_got)
    by_row = factors[...].T
    first.finish()
    rows = rows_got[0].astype(f32) * by_row[:, 0:1]
    for k in range(1, n_u):
        rows += rows_got[k].astype(f32) * by_row[:, k : k + 1]
    partial[...] = rows.astype(bf16).reshape(partial.shape)
    back = links(2, partial, partial_got.at[0])
    slot_part.finish()
    tops = slot_got[0, 0:1, :]
    for k in range(1, n_b):
        tops = jnp.maximum(tops, slot_got[k, 0:1, :])
    total = jnp.zeros_like(tops)
    for k in range(n_b):
        factor = jnp.exp(slot_got[k, 0:1, :] - tops)
        factors[k : k + 1, :] = factor
        total += slot_got[k, 1:2, :] * factor
    log_norm = tops + jnp.log(total)
    for k in range(n_b):
        factors[k : k + 1, :] = factors[k : k + 1, :] / total
    factors[n_b : n_b + 1, :] = log_norm
    norms_mine[...] = jnp.broadcast_to(log_norm, norms_mine.shape)
    norms_part = links(4, norms_mine, norms_all)
    columns[...] = factors[...].T
    mine = columns[pl.ds(pl.multiple_of(b * picks, picks), picks), :]
    back.finish()
    target_rows = picks_in[:, MODEL_WIDTH:]
    grad_final = -target_rows
    for k in range(n_b):
        grad_final += partial_got[0, k].astype(f32) * mine[:, k : k + 1]
    grad_final = grad_final * weights[:, 0:1]
    target_logit = jnp.sum(
        final_mine[...].astype(f32) * target_rows, axis=-1, keepdims=True
    )
    terms[...] = weights[...] * (target_logit - mine[:, n_b : n_b + 1])
    grad_mlp, gain_rows = norm_back_rows(after_mlp[...], gain_final[...], grad_final)
    gain_final_out[...] = gain_rows
    mine_low[...] = grad_mlp.astype(bf16)
    links.now(5, mine_low, grad_all)
    branch = flat_rows_of(grad_all)
    gate_up = gate_up_in[...]
    half = gate_up.shape[1] // 2
    gate_part, up_part = gate_up[:, :half], gate_up[:, half:]
    sigmoid_gate = jax.nn.sigmoid(gate_part)
    grad_act = mm_back(branch, down_weight[...])
    grad_gate = grad_act * up_part * sigmoid_gate * (1.0 + gate_part * (1.0 - sigmoid_gate))
    grad_up = grad_act * gate_part * sigmoid_gate
    grad_gate_up = jnp.concatenate([grad_gate, grad_up], axis=1).astype(bf16)
    partial[...] = mm_back(grad_gate_up, ff_weight[...]).astype(bf16).reshape(partial.shape)
    back = links(6, partial, partial_got.at[1])
    activated = (gate_part * sigmoid_gate * up_part).astype(bf16)
    grad_down[...] = mm_outer(activated, branch).astype(bf16).reshape(grad_down.shape)
    back.finish()
    grad_mid, gain_rows = norm_back_rows(after_attn[...], gain_mlp[...], sum_blocks(partial_got.at[1]))
    gain_mlp_out[...] = gain_rows
    grad_attn = grad_mlp + grad_mid
    grad_after[...] = grad_attn
    mine_low[...] = grad_attn.astype(bf16)
    again = links(7, mine_low, branch_all)
    grad_ff[...] = (
        mm_outer(flat_rows_of(normed_all), grad_gate_up).astype(bf16).reshape(grad_ff.shape)
    )
    again.finish()
    branch = flat_rows_of(branch_all)
    grad_low = mm_back(branch, out_weight[...]).astype(bf16)
    attended_mine[...] = grad_low
    last = links(8, attended_mine, attended_all)
    out_cut = attended.shape[1] // n_u
    product = attended[...] * grad_low.astype(f32)
    group = lax.broadcasted_iota(jnp.int32, product.shape, 1) // out_cut
    lane = lax.broadcasted_iota(jnp.int32, deltas.shape, 1)
    sums = jnp.zeros(deltas.shape, f32)
    for row in range(n_u):
        one = jnp.sum(jnp.where(group == row, product, 0.0), axis=-1, keepdims=True)
        sums = jnp.where(lane == row, one, sums)
    deltas[...] = sums
    delta_mine[...] = deltas[...].T[:8, :]
    delta_part = links(9, delta_mine, delta_all)
    grad_out[...] = mm_outer(attended[...].astype(bf16), branch).astype(bf16).reshape(
        grad_out.shape
    )
    last.finish()
    delta_part.finish()
    norms_part.finish()


def query_back_body(links, ins, outs, scratch):
    (
        query_send,
        query_raw,
        cosines,
        sines,
        gain_query,
        q_weight,
        normed_all,
        picks_in,
        gain_attn,
        grad_after,
        grad_ff,
        grad_out,
        grad_down,
    ) = ins
    gain_query_out, gain_attn_out, grad_q, pick_back, ff_sum, out_sum, down_sum = outs
    query_got, grad_low, partial, partial_got, mine_low, ff_got, out_got, down_got = scratch
    first = links(0, query_send, query_got)
    behind = [
        links(3, grad_ff, ff_got),
        links(4, grad_out, out_got),
        links(5, grad_down, down_got),
    ]
    first.finish()
    upstream = sum_blocks(query_got).astype(bf16).astype(f32)
    gain_sum = jnp.zeros(gain_query_out.shape, f32)
    for k in range(upstream.shape[1] // HEAD_WIDTH):
        part = slice(k * HEAD_WIDTH, (k + 1) * HEAD_WIDTH)
        grad_head, gain_head = norm_back_rows(
            query_raw[:, part], gain_query[...], turned(upstream[:, part], cosines[...], -sines[...])
        )
        grad_low[:, part] = grad_head.astype(bf16)
        gain_sum += gain_head
    gain_query_out[...] = gain_sum
    partial[...] = mm_back(grad_low[...], q_weight[...]).astype(bf16).reshape(partial.shape)
    back = links(1, partial, partial_got)
    grad_q[...] = (
        mm_outer(flat_rows_of(normed_all), grad_low[...]).astype(bf16).reshape(grad_q.shape)
    )
    back.finish()
    grad_mine, gain_rows = norm_back_rows(
        picks_in[:, :MODEL_WIDTH], gain_attn[...], sum_blocks(partial_got)
    )
    gain_attn_out[...] = gain_rows
    mine_low[...] = (grad_after[...] + grad_mine).astype(bf16)
    links.now(2, mine_low, pick_back)
    for part in behind:
        part.finish()
    ff_sum[...] = sum_blocks(ff_got).astype(bf16)
    out_sum[...] = sum_blocks(out_got)
    down_sum[...] = sum_blocks(down_got)


class Named:
    pass


def named_call(exchange, body, plan, extra_sems, ins, outs, scratch, name):
    counts = axis_counts()
    sem_shapes = []
    for axis, _ in plan.values():
        sem_shapes += sems(counts[axis])
    order = {key: k for k, key in enumerate(plan)}
    extra = list(extra_sems)

    def kernel(*refs):
        r, s = Named(), Named()
        names = list(ins) + list(outs) + list(scratch)
        for key, ref in zip(names, refs):
            setattr(r, key, ref)
        sem_refs = refs[len(names) :]
        for key, ref in zip(extra, sem_refs[3 * len(plan) :]):
            setattr(s, key, ref)
        base = Links(list(plan.values()), counts["blk"], sem_refs)
        greet({axis for axis, _ in plan.values()}, counts["blk"], counts)
        body(r, lambda key, source, landing: base(order[key], source, landing), s)

    results = remote_call(
        kernel,
        exchange.next_id(),
        [jax.ShapeDtypeStruct(shape, dtype) for shape, dtype in outs.values()],
        [pltpu.VMEM(shape, dtype) for shape, dtype in scratch.values()]
        + sem_shapes
        + [pltpu.SemaphoreType.DMA(extra_sems[key]) for key in extra],
        list(ins.values()),
        name,
    )
    found = Named()
    for key, value in zip(outs, results):
        setattr(found, key, value)
    return found


def column_of(lane_row):
    count = lane_row.shape[1]
    down = lax.broadcasted_iota(jnp.int32, (count, count), 0)
    across = lax.broadcasted_iota(jnp.int32, (count, count), 1)
    return jnp.sum(jnp.where(down == across, lane_row, 0.0), axis=1, keepdims=True)


def begin_body(n_u, n_b, row_share, slots, r, links, s):
    u, b = lax.axis_index("ulysses"), lax.axis_index("blk")
    me = u * n_b + b
    block_len, picks = r.tokens.shape[1], r.picked.shape[1]
    places = n_u * slots
    gathers = [
        links("tokens", r.tokens, r.tokens_all),
        links("targets", r.targets, r.targets_all),
        links("picked", r.picked, r.picked_all),
        links("advantages", r.advantages, r.advantages_all),
    ]
    links("near", r.scales, r.near).finish()
    far = links("far", r.near, r.far)
    for part in gathers:
        part.finish()

    width = block_len + picks
    lane = lax.broadcasted_iota(jnp.int32, (1, width), 1)
    before = jnp.where(
        lax.broadcasted_iota(jnp.int32, (width, width), 0)
        < lax.broadcasted_iota(jnp.int32, (width, width), 1),
        1.0,
        0.0,
    ).astype(bf16)
    base = jnp.zeros((2 * n_u, 1), f32)
    found = [jnp.zeros((slots, width), f32) for _ in range(2 * n_u)]
    rank_of_slot = lax.broadcasted_iota(jnp.int32, (slots, width), 0).astype(f32)
    owner_first = lax.broadcasted_iota(jnp.int32, (n_u, 1), 0) * n_b + b
    most = jnp.zeros((n_u, 1), f32)
    counts = [jnp.zeros((n_u, width), f32) for _ in range(n_u * n_b)]
    for k in range(n_b):
        r.wants[:, :block_len] = r.tokens_all[k]
        r.wants[:, block_len:] = r.targets_all[k]
        wants = r.wants[...]
        local = wants - me * row_share
        sent = (local >= 0) & (local < row_share)
        own = r.wants[pl.ds(u, 1), :] - owner_first * row_share
        got = (own >= 0) & (own < row_share)
        r.masks[:n_u, :] = jnp.where(sent, 1.0, 0.0)
        r.masks[n_u:, :] = jnp.where(got, 1.0, 0.0)
        r.labels[:n_u, :] = (local + 1).astype(f32)
        r.labels[n_u:, :] = jnp.broadcast_to(k * width + lane + 1, (n_u, width)).astype(f32)
        masks = r.masks[...]
        ranks = mm(masks.astype(bf16), before) + base
        r.ranks[...] = jnp.where(masks > 0.0, ranks, -1.0)
        base += jnp.sum(masks, axis=1, keepdims=True)
        for row in range(2 * n_u):
            hit = r.ranks[row : row + 1, :] == rank_of_slot
            found[row] += jnp.where(hit, r.labels[row : row + 1, :], 0.0)
        for owner in range(n_u * n_b):
            far_row = wants - owner * row_share
            counts[owner] += jnp.where((far_row >= 0) & (far_row < row_share), 1.0, 0.0)
        r.slot_picked[:, k * picks : (k + 1) * picks] = r.picked_all[k, pl.ds(u, 1), :]
        valid = r.picked_all[k] < r.lengths[...]
        weights = jnp.where(valid, r.advantages_all[k], 0.0)
        for row in range(n_u):
            at = slice((row * n_b + k) * picks, (row * n_b + k + 1) * picks)
            r.weights[:, at] = weights[row : row + 1, :]
            r.target_ids[:, at] = r.targets_all[k, row : row + 1, :] - me * row_share
    for owner in range(n_u * n_b):
        most = jnp.maximum(most, jnp.sum(counts[owner], axis=1, keepdims=True))
    r.meta[...] = jnp.zeros_like(r.meta)
    r.meta[0:n_u, :] = jnp.broadcast_to(base[:n_u], (n_u, 128))
    r.meta[8 : 8 + n_u, :] = jnp.broadcast_to(most, (n_u, 128))
    mine_valid = r.picked[pl.ds(u, 1), :] < r.lengths[pl.ds(u, 1), :]
    mine_weight = jnp.where(mine_valid, r.advantages[pl.ds(u, 1), :], 0.0)
    r.meta[16:17, :] = jnp.broadcast_to(
        jnp.sum(jnp.where(mine_valid, 1.0, 0.0), axis=1, keepdims=True), (1, 128)
    )
    r.weight_wide[...] = jnp.broadcast_to(column_of(mine_weight), r.weight_wide.shape)
    my_length = r.lengths[pl.ds(u, 1), :]
    for row in range(n_u):
        here = slice(row * slots, (row + 1) * slots)
        r.row_ids[here, :] = jnp.sum(found[row], axis=1, keepdims=True).astype(jnp.int32) - 1
        entry = jnp.sum(found[n_u + row], axis=1, keepdims=True) - 1.0
        block = jnp.floor((entry + 0.5) * (1.0 / width))
        inside = entry - block * width
        token = (entry >= 0.0) & (inside < block_len)
        position = (block * block_len + inside).astype(jnp.int32)
        key_pos = jnp.where(token, position, 1 << 30)
        r.key_pos[here, :] = key_pos
        r.key_lim[here, :] = jnp.where(key_pos < my_length, key_pos, 1 << 30)
        r.positions[here, :] = jnp.where(token, position, 0)
        target = (block * picks + inside - block_len).astype(jnp.int32)
        r.target_of[here, :] = jnp.where((entry >= 0.0) & (inside >= block_len), target, -1)
    r.positions[places:, :] = column_of(r.slot_picked[...].astype(f32)).astype(jnp.int32)

    far.finish()
    share = r.scales.shape[1]
    for row in range(n_u):
        for k in range(n_b):
            at = (row * n_b + k) * share
            r.gains[:, at : at + share] = r.far[row, k].astype(bf16).astype(f32)
    r.gain_attn[...] = r.gains[:, :MODEL_WIDTH]
    r.gain_mlp[...] = r.gains[:, MODEL_WIDTH : 2 * MODEL_WIDTH]
    r.gain_final[...] = r.gains[:, 2 * MODEL_WIDTH : 3 * MODEL_WIDTH]
    r.gain_query[...] = r.gains[:, 3 * MODEL_WIDTH : 3 * MODEL_WIDTH + HEAD_WIDTH]
    r.gain_key[...] = r.gains[:, 3 * MODEL_WIDTH + HEAD_WIDTH :]


def totals_body(r, links, s):
    links("near", r.mine, r.near_all).finish()
    r.near[...] = sum_blocks(r.near_all)
    links("far", r.near, r.far_all).finish()
    r.total[...] = sum_blocks(r.far_all)


def head_of(ref, head):
    share = ref.shape[2] // HEAD_WIDTH
    at = head % share * HEAD_WIDTH
    return ref[head // share, :, at : at + HEAD_WIDTH]


def cuts_of(head, n_u, n_b):
    cut = QUERY_WIDTH // (n_u * n_b)
    heads_row, pieces = QUERY_HEADS // n_u, HEAD_WIDTH // cut
    row = head // heads_row
    return [
        (head % heads_row * pieces + t, slice(row * cut, (row + 1) * cut), slice(t * cut, (t + 1) * cut))
        for t in range(pieces)
    ]


def ff_cuts(n_u, n_b):
    cut = FF // (n_u * n_b)
    return [
        (
            k,
            slice((half * n_u + row) * cut, (half * n_u + row + 1) * cut),
            slice(half * FF + (row * n_b + k) * cut, half * FF + (row * n_b + k + 1) * cut),
        )
        for k in range(n_b)
        for half in range(2)
        for row in range(n_u)
    ]


def rise_body(n_u, n_b, r, links, s):
    u, b = lax.axis_index("ulysses"), lax.axis_index("blk")
    n_z = n_b // 2
    z, c = b // 2, lax.rem(b, 2)
    score_scale = HEAD_WIDTH ** (-0.5)

    def along_z(step):
        return remote(
            r.kv_in,
            r.kv_weight.at[u, z, c],
            s.z_send.at[step],
            s.z_recv.at[step],
            {"blk": lax.rem(z + step, n_z) * 2 + c},
        )

    def own_copy():
        return pltpu.make_async_copy(r.kv_in, r.kv_weight.at[u, z, c], s.own.at[0])

    def block(hop, step):
        return r.kv_weight.at[lax.rem(u - hop + n_u, n_u), lax.rem(z - step + n_z, n_z), c]

    def across(hop, step):
        place = block(0, step)
        return remote(
            place,
            place,
            s.xy_send.at[hop, step],
            s.xy_recv.at[hop, step],
            {"ulysses": lax.rem(u + hop, n_u)},
        )

    def to_core(hop, step):
        place = block(hop, step)
        return remote(
            place,
            place,
            s.core_send.at[hop, step],
            s.core_recv.at[hop, step],
            {"blk": z * 2 + 1 - c},
        )

    places = r.key_raw.shape[0]
    half = KEY_VALUE_HEADS * HEAD_WIDTH
    r.kv_in[...] = r.inflow[:, QUERY_WIDTH:].astype(bf16)
    own_copy().start()
    rows = links("rows", r.rows_in, r.arrived)
    each(n_z, lambda step: along_z(step).start(), 1)
    q_share = r.q_in.shape[2]
    for k in range(n_b):
        r.q_in[k] = r.inflow[:, k * q_share : (k + 1) * q_share].astype(bf16)
    q_split = links("q_split", r.q_in, r.q_part)
    own_copy().wait()
    each(n_u, lambda hop: across(hop, 0).start(), 1)
    to_core(0, 0).start()
    for k, there, here in ff_cuts(n_u, n_b):
        r.ff_in[k, :, there] = r.expand[:, here].astype(bf16)
    ff_split = links("ff_split", r.ff_in, r.ff_part)
    r.out_in[...] = r.outflow[...].astype(bf16)
    r.down_in[...] = r.contract[...].astype(bf16)
    rows.finish()

    arrived = flat_rows_of(r.arrived)
    pick_hot = jnp.where(r.key_pos[...] == r.slot_picked[...], 1.0, 0.0).astype(bf16)
    pick_lane = lax.broadcasted_iota(jnp.int32, pick_hot.shape, 1)
    target_hot = jnp.where(r.target_of[...] == pick_lane, 1.0, 0.0).astype(bf16)
    r.pick_send[:, :, :MODEL_WIDTH] = (
        mm_outer(pick_hot, arrived).astype(bf16).reshape(r.normed_slot.shape)
    )
    r.pick_send[:, :, MODEL_WIDTH:] = (
        mm_outer(target_hot, arrived).astype(bf16).reshape(r.normed_slot.shape)
    )
    picked = links("picks", r.pick_send, r.pick_got)

    def pass_on(step):
        along_z(step).wait_recv()
        each(n_u, lambda hop: across(hop, step).start(), 1)
        to_core(0, step).start()

    each(n_z, pass_on, 1)
    q_split.finish()
    q_all = links("q_all", r.q_part, r.q_weight)
    wide = arrived.astype(f32)
    r.normed_keys[...] = (wide * inverse_root(wide) * r.gain_attn[...]).astype(bf16)
    picked.finish()
    pick_rows = sum_blocks(r.pick_got)
    r.pick_rows[...] = pick_rows
    mine = pick_rows[:, :MODEL_WIDTH]
    r.normed_mine[...] = (mine * inverse_root(mine) * r.gain_attn[...]).astype(bf16)
    links("normed", r.normed_mine, r.normed_slot).finish()
    q_all.finish()
    raw = mm(flat_rows_of(r.normed_slot), r.q_weight[...].reshape(MODEL_WIDTH, -1))
    r.query_raw[...] = raw
    for k in range(raw.shape[1] // HEAD_WIDTH):
        part = slice(k * HEAD_WIDTH, (k + 1) * HEAD_WIDTH)
        head = raw[:, part]
        r.query_mine[:, part] = turned(
            head * inverse_root(head) * r.gain_query[...], r.rope_cos[places:], r.rope_sin[places:]
        ).astype(bf16)
    queries = links("queries", r.query_mine, r.query_all)

    def share(step):
        def one(hop):
            across(hop, step).wait_recv()
            to_core(hop, step).start()

        each(n_u, one, 1)

    each(n_z, share)
    out_all = links("out_all", r.out_in, r.out_weight)
    ff_split.finish()
    ff_all = links("ff_all", r.ff_part, r.ff_weight)
    down_all = links("down_all", r.down_in, r.down_weight)
    each(n_z, lambda step: each(n_u, lambda hop: to_core(hop, step).wait_recv()))

    wide_head = 2 * HEAD_WIDTH

    def project(k):
        for first in (0, half):
            at = pl.multiple_of(first + k * wide_head, wide_head)
            weight = r.kv_weight[:, :, :, :, pl.ds(at, wide_head)].reshape(MODEL_WIDTH, wide_head)
            got = mm(r.normed_keys[...], weight)
            here = pl.ds(pl.multiple_of(k * wide_head, wide_head), wide_head)
            if first:
                r.values[:, here] = got.astype(bf16)
            else:
                r.key_raw[:, here] = got
                turned_both = []
                for j in range(2):
                    head = got[:, j * HEAD_WIDTH : (j + 1) * HEAD_WIDTH]
                    turned_both.append(
                        turned(
                            head * inverse_root(head) * r.gain_key[...],
                            r.rope_cos[:places],
                            r.rope_sin[:places],
                        )
                    )
                r.key_rot[:, here] = jnp.concatenate(turned_both, axis=1).astype(bf16)

    each(KEY_VALUE_HEADS // 2, project)
    queries.finish()
    allowed = r.key_lim[...] <= r.slot_picked[...]
    for head in range(QUERY_HEADS):
        at = head // (QUERY_HEADS // KEY_VALUE_HEADS) * HEAD_WIDTH
        part = slice(at, at + HEAD_WIDTH)
        scores = mm_back(r.key_rot[:, part], head_of(r.query_all, head)) * score_scale
        scores = jnp.where(allowed, scores, masked_score)
        top = jnp.max(scores, axis=0, keepdims=True)
        weights = jnp.where(allowed, jnp.exp(scores - top), 0.0)
        r.stats[head : head + 1, :] = top
        r.stats[QUERY_HEADS + head : QUERY_HEADS + head + 1, :] = jnp.sum(
            weights, axis=0, keepdims=True
        )
        out = mm_outer(weights.astype(bf16), r.values[:, part]).astype(bf16)
        for target, there, here in cuts_of(head, n_u, n_b):
            r.part_send[target, :, there] = out[:, here]

    picks = r.after_attn.shape[0]
    out_cut = r.attended.shape[1] // n_u
    heads_row = QUERY_HEADS // n_u
    cut_head = (b * out_cut) // HEAD_WIDTH
    sent = links("parts", r.part_send, r.part_got)
    links("stats", r.stats, r.stats_all).finish()
    full_max = r.stats_all[0, :QUERY_HEADS]
    for k in range(1, n_b):
        full_max = jnp.maximum(full_max, r.stats_all[k, :QUERY_HEADS])
    full_sum = jnp.zeros_like(full_max)
    for k in range(n_b):
        full_sum += r.stats_all[k, QUERY_HEADS:] * jnp.exp(
            r.stats_all[k, :QUERY_HEADS] - full_max
        )
    r.log_total[...] = full_max + jnp.log(full_sum)
    for row in range(n_u):
        head = row * heads_row + cut_head
        row_log = r.log_total[pl.ds(head, 1), :]
        for k in range(n_b):
            r.shares[k * n_u + row : k * n_u + row + 1, :] = jnp.exp(
                r.stats_all[k, pl.ds(head, 1), :] - row_log
            )
    columns = r.shares[...].T
    sent.finish()
    attended = jnp.zeros(r.attended.shape, f32)
    for k in range(n_b):
        attended += r.part_got[k].astype(f32) * lanes_of(
            [columns[:, k * n_u + row : k * n_u + row + 1] for row in range(n_u)], out_cut, n_u
        )
    r.attended[...] = attended
    out_all.finish()

    def to_picks(key, rows):
        r.partial[...] = rows.astype(bf16).reshape(r.partial.shape)
        landing = r.partial_got.at[0 if key == "sum_out" else 1]
        links(key, r.partial, landing).finish()
        return sum_blocks(landing)

    after_attn = r.pick_rows[:, :MODEL_WIDTH] + to_picks(
        "sum_out", mm(attended.astype(bf16), flat_rows_of(r.out_weight))
    )
    r.after_attn[...] = after_attn
    r.normed_mine[...] = (after_attn * inverse_root(after_attn) * r.gain_mlp[...]).astype(bf16)
    links("normed_mlp", r.normed_mine, r.normed_mlp).finish()
    ff_all.finish()
    gate_up = mm(flat_rows_of(r.normed_mlp), r.ff_weight[...].reshape(MODEL_WIDTH, -1))
    r.gate_up[...] = gate_up
    half = gate_up.shape[1] // 2
    gate_part, up_part = gate_up[:, :half], gate_up[:, half:]
    activated = (gate_part * jax.nn.sigmoid(gate_part) * up_part).astype(bf16)
    down_all.finish()
    after_mlp = after_attn + to_picks("sum_mlp", mm(activated, flat_rows_of(r.down_weight)))
    r.after_mlp[...] = after_mlp
    r.final_mine[...] = (after_mlp * inverse_root(after_mlp) * r.gain_final[...]).astype(bf16)
    links("final", r.final_mine, r.final_slot).finish()
    links("final_all", r.final_slot, r.final_all).finish()
    each(n_z, lambda step: along_z(step).wait_send(), 1)
    each(n_z, lambda step: each(n_u, lambda hop: across(hop, step).wait_send(), 1))
    each(n_z, lambda step: each(n_u, lambda hop: to_core(hop, step).wait_send()))


def fall_body(n_u, n_b, r, links, s):
    u, b = lax.axis_index("ulysses"), lax.axis_index("blk")
    n_z = n_b // 2
    z, c = b // 2, lax.rem(b, 2)
    score_scale = HEAD_WIDTH ** (-0.5)
    picks = r.after_mlp.shape[0]
    places = r.key_raw.shape[0]
    r.factors[...] = jnp.zeros_like(r.factors)
    head_rows = links("head_rows", r.head_rows, r.rows_got)
    links("head_stats", r.head_stats, r.stats_got).finish()
    tops = r.stats_got[0, 0:1, :]
    for k in range(1, n_u):
        tops = jnp.maximum(tops, r.stats_got[k, 0:1, :])
    total = jnp.zeros_like(tops)
    for k in range(n_u):
        factor = jnp.exp(r.stats_got[k, 0:1, :] - tops)
        r.factors[k : k + 1, :] = factor
        total += r.stats_got[k, 1:2, :] * factor
    r.slot_stats[...] = jnp.zeros_like(r.slot_stats)
    r.slot_stats[0:1, :] = tops
    r.slot_stats[1:2, :] = total
    slot_part = links("slot_stats", r.slot_stats, r.slot_got)
    by_row = r.factors[...].T
    head_rows.finish()
    rows = r.rows_got[0].astype(f32) * by_row[:, 0:1]
    for k in range(1, n_u):
        rows += r.rows_got[k].astype(f32) * by_row[:, k : k + 1]
    r.partial[...] = rows.astype(bf16).reshape(r.partial.shape)
    back = links("slot_rows", r.partial, r.partial_got.at[0])
    slot_part.finish()
    tops = r.slot_got[0, 0:1, :]
    for k in range(1, n_b):
        tops = jnp.maximum(tops, r.slot_got[k, 0:1, :])
    total = jnp.zeros_like(tops)
    for k in range(n_b):
        factor = jnp.exp(r.slot_got[k, 0:1, :] - tops)
        r.factors[k : k + 1, :] = factor
        total += r.slot_got[k, 1:2, :] * factor
    log_norm = tops + jnp.log(total)
    for k in range(n_b):
        r.factors[k : k + 1, :] = r.factors[k : k + 1, :] / total
    r.factors[n_b : n_b + 1, :] = log_norm
    r.norms_mine[...] = jnp.broadcast_to(log_norm, r.norms_mine.shape)
    norms_part = links("norms", r.norms_mine, r.norms_all)
    r.columns[...] = r.factors[...].T
    mine = r.columns[pl.ds(pl.multiple_of(b * picks, picks), picks), :]
    back.finish()
    target_rows = r.pick_rows[:, MODEL_WIDTH:]
    grad_final = -target_rows
    for k in range(n_b):
        grad_final += r.partial_got[0, k].astype(f32) * mine[:, k : k + 1]
    grad_final = grad_final * r.weights[:, 0:1]
    target_logit = jnp.sum(
        r.final_mine[...].astype(f32) * target_rows, axis=-1, keepdims=True
    )
    r.terms[...] = r.weights[...] * (target_logit - mine[:, n_b : n_b + 1])
    grad_mlp, gain_final = norm_back_rows(r.after_mlp[...], r.gain_final[...], grad_final)
    r.mine_low[...] = grad_mlp.astype(bf16)
    links("branch", r.mine_low, r.grad_all).finish()
    branch = flat_rows_of(r.grad_all)
    gate_up = r.gate_up[...]
    half = gate_up.shape[1] // 2
    gate_part, up_part = gate_up[:, :half], gate_up[:, half:]
    sigmoid_gate = jax.nn.sigmoid(gate_part)
    grad_act = mm_back(branch, flat_rows_of(r.down_weight))
    grad_gate = grad_act * up_part * sigmoid_gate * (1.0 + gate_part * (1.0 - sigmoid_gate))
    grad_up = grad_act * gate_part * sigmoid_gate
    grad_gate_up = jnp.concatenate([grad_gate, grad_up], axis=1).astype(bf16)
    r.partial[...] = (
        mm_back(grad_gate_up, r.ff_weight[...].reshape(MODEL_WIDTH, -1))
        .astype(bf16)
        .reshape(r.partial.shape)
    )
    back = links("sum_ff", r.partial, r.partial_got.at[1])
    activated = (gate_part * sigmoid_gate * up_part).astype(bf16)
    r.grad_down[...] = mm_outer(activated, branch).astype(bf16).reshape(r.grad_down.shape)
    down_part = links("down", r.grad_down, r.down_got)
    r.grad_ff[...] = (
        mm_outer(flat_rows_of(r.normed_mlp), grad_gate_up).astype(bf16).reshape(r.grad_ff.shape)
    )
    ff_part = links("ff", r.grad_ff, r.ff_got)
    back.finish()
    grad_mid, gain_mlp = norm_back_rows(
        r.after_attn[...], r.gain_mlp[...], sum_blocks(r.partial_got.at[1])
    )
    grad_attn = grad_mlp + grad_mid
    r.mine_low[...] = grad_attn.astype(bf16)
    links("branch_attn", r.mine_low, r.branch_all).finish()
    branch = flat_rows_of(r.branch_all)
    grad_low = mm_back(branch, flat_rows_of(r.out_weight)).astype(bf16)
    r.attended_mine[...] = grad_low
    last = links("attended", r.attended_mine, r.attended_all)
    out_cut = r.attended.shape[1] // n_u
    product = r.attended[...] * grad_low.astype(f32)
    group = lax.broadcasted_iota(jnp.int32, product.shape, 1) // out_cut
    lane = lax.broadcasted_iota(jnp.int32, r.deltas.shape, 1)
    sums = jnp.zeros(r.deltas.shape, f32)
    for row in range(n_u):
        one = jnp.sum(jnp.where(group == row, product, 0.0), axis=-1, keepdims=True)
        sums = jnp.where(lane == row, one, sums)
    r.deltas[...] = sums
    r.delta_mine[...] = r.deltas[...].T[:8, :]
    delta_part = links("deltas", r.delta_mine, r.delta_all)
    r.grad_out[...] = (
        mm_outer(r.attended[...].astype(bf16), branch).astype(bf16).reshape(r.grad_out.shape)
    )
    out_part = links("out", r.grad_out, r.out_got)
    wide = flat_rows_of(r.arrived).astype(f32)
    r.normed_keys[...] = (wide * inverse_root(wide) * r.gain_attn[...]).astype(bf16)
    last.finish()
    delta_part.finish()

    allowed = r.key_lim[...] <= r.slot_picked[...]
    width = KEY_VALUE_HEADS * HEAD_WIDTH
    r.gain_key_row[...] = jnp.zeros((1, HEAD_WIDTH), f32)
    heads_each = QUERY_HEADS // KEY_VALUE_HEADS
    for kv_head in range(KEY_VALUE_HEADS):
        part = slice(kv_head * HEAD_WIDTH, (kv_head + 1) * HEAD_WIDTH)
        key, value = r.key_rot[:, part], r.values[:, part]
        grad_key = jnp.zeros(key.shape, f32)
        grad_value = jnp.zeros(key.shape, f32)
        for head in range(kv_head * heads_each, (kv_head + 1) * heads_each):
            query = head_of(r.query_all, head)
            cuts = cuts_of(head, n_u, n_b)
            upstream = jnp.concatenate([r.attended_all[at, :, there] for at, there, _ in cuts], 1)
            row = head // (QUERY_HEADS // n_u)
            delta = sum(r.delta_all[at, row : row + 1, :] for at, _, _ in cuts)
            scores = mm_back(key, query) * score_scale
            probs = jnp.where(allowed, jnp.exp(scores - r.log_total[head : head + 1, :]), 0.0)
            grad_probs = mm_back(value, upstream)
            grad_scores = (probs * (grad_probs - delta) * score_scale).astype(bf16)
            grad_query = mm_outer(grad_scores, key).astype(bf16)
            share = r.query_send.shape[2] // HEAD_WIDTH
            at = head % share * HEAD_WIDTH
            r.query_send[head // share, :, at : at + HEAD_WIDTH] = grad_query
            grad_key += mm(grad_scores, query)
            grad_value += mm(probs.astype(bf16), upstream)
        grad_head, gain_head = norm_back_rows(
            r.key_raw[:, part],
            r.gain_key[...],
            turned(grad_key.astype(bf16).astype(f32), r.rope_cos[:places], -r.rope_sin[:places]),
        )
        r.gain_key_row[...] += gain_head
        r.grad_kv[:, part] = grad_head.astype(bf16)
        r.grad_kv[:, width + kv_head * HEAD_WIDTH : width + (kv_head + 1) * HEAD_WIDTH] = (
            grad_value.astype(bf16)
        )
    query_part = links("grad_queries", r.query_send, r.query_got)

    def place(hop, step):
        return (lax.rem(u + hop, n_u), lax.rem(z + step, n_z))

    def to_core(hop, step):
        row, line = place(hop, step)
        return remote(
            r.kv_grad.at[row, line, 1 - c],
            r.kv_core.at[hop, step],
            s.core_send.at[hop, step],
            s.core_recv.at[hop, step],
            {"blk": z * 2 + 1 - c},
        )

    def across(hop, step):
        return remote(
            r.kv_core.at[hop, step],
            r.kv_cross.at[hop, step],
            s.xy_send.at[hop, step],
            s.xy_recv.at[hop, step],
            {"ulysses": lax.rem(u + hop, n_u)},
        )

    def along_z(step):
        return remote(
            r.kv_plane.at[step],
            r.kv_line.at[step],
            s.z_send.at[step],
            s.z_recv.at[step],
            {"blk": lax.rem(z + step, n_z) * 2 + c},
        )

    block_rows = MODEL_WIDTH // n_u

    def weight_grad(k):
        hop = lax.rem(k + 1, n_u)
        row = lax.rem(u + hop, n_u)
        columns = pl.ds(pl.multiple_of(row * block_rows, block_rows), block_rows)
        r.kv_grad[row] = (
            mm_outer(r.normed_keys[:, columns], r.grad_kv[...])
            .astype(bf16)
            .reshape(r.kv_grad.shape[1:])
        )
        each(n_z, lambda step: to_core(hop, step).start())

    each(n_u, weight_grad)
    query_part.finish()
    upstream = sum_blocks(r.query_got).astype(bf16).astype(f32)
    r.gain_query_row[...] = jnp.zeros((1, HEAD_WIDTH), f32)
    for k in range(upstream.shape[1] // HEAD_WIDTH):
        part = slice(k * HEAD_WIDTH, (k + 1) * HEAD_WIDTH)
        grad_head, gain_head = norm_back_rows(
            r.query_raw[:, part],
            r.gain_query[...],
            turned(upstream[:, part], r.rope_cos[places:], -r.rope_sin[places:]),
        )
        r.grad_low[:, part] = grad_head.astype(bf16)
        r.gain_query_row[...] += gain_head
    r.partial[...] = (
        mm_back(r.grad_low[...], r.q_weight[...].reshape(MODEL_WIDTH, -1))
        .astype(bf16)
        .reshape(r.partial.shape)
    )
    back = links("sum_query", r.partial, r.partial_got.at[2])

    def add_pair(hop):
        def one(step):
            row, line = place(hop, step)
            to_core(hop, step).wait_recv()
            r.kv_core[hop, step] = (
                r.kv_grad[row, line, c].astype(f32) + r.kv_core[hop, step].astype(f32)
            ).astype(bf16)

        return one

    def forward_hop(hop):
        def forward(step):
            add_pair(hop)(step)
            across(hop, step).start()

        each(n_z, forward)

    each(n_u, forward_hop, 1)
    each(n_z, add_pair(0))
    r.grad_q[...] = (
        mm_outer(flat_rows_of(r.normed_slot), r.grad_low[...]).astype(bf16).reshape(r.grad_q.shape)
    )
    q_part = links("q", r.grad_q, r.q_got)
    back.finish()
    grad_mine, gain_attn = norm_back_rows(
        r.pick_rows[:, :MODEL_WIDTH], r.gain_attn[...], sum_blocks(r.partial_got.at[2])
    )
    r.mine_low[...] = (grad_attn + grad_mine).astype(bf16)
    pick_part = links("pick_back", r.mine_low, r.pick_back)

    def row_grad(k):
        columns = pl.ds(pl.multiple_of(k * block_rows, block_rows), block_rows)
        r.grad_wide[:, columns] = mm_back(
            r.grad_kv[...], r.kv_weight[k].reshape(block_rows, -1)
        )

    each(n_u, row_grad)
    grad_rows, gain_keys = norm_back_rows(wide, r.gain_attn[...], r.grad_wide[...])
    pick_part.finish()
    pick_hot = jnp.where(r.key_pos[...] == r.slot_picked[...], 1.0, 0.0).astype(bf16)
    r.rows_send[...] = (
        (grad_rows + mm(pick_hot, flat_rows_of(r.pick_back)))
        .astype(bf16)
        .reshape(r.rows_send.shape)
    )
    rows_part = links("rows", r.rows_send, r.rows_back)

    r.gain_mlp_row[...] = gain_mlp
    r.gain_final_row[...] = gain_final
    r.gain_picks_row[...] = gain_attn
    r.gain_rows_row[...] = gain_keys
    r.gains_mine[...] = jnp.zeros_like(r.gains_mine)
    lines = MODEL_WIDTH // 128
    for j in range(lines):
        part = slice(j * 128, (j + 1) * 128)
        r.gains_mine[j : j + 1, :] = r.gain_picks_row[:, part] + r.gain_rows_row[:, part]
        r.gains_mine[lines + j : lines + j + 1, :] = r.gain_mlp_row[:, part]
        r.gains_mine[2 * lines + j : 2 * lines + j + 1, :] = r.gain_final_row[:, part]
    r.gains_mine[3 * lines : 3 * lines + 1, :] = r.gain_query_row[...]
    r.gains_mine[3 * lines + 1 : 3 * lines + 2, :] = r.gain_key_row[...]
    gains_part = links("gains_blk", r.gains_mine, r.gains_got)

    ff_part.finish()
    r.ff_sum[...] = sum_blocks(r.ff_got).astype(bf16)
    ff_last = links("ff_cols", r.ff_sum, r.ff_out)
    down_part.finish()
    r.down_out[...] = sum_blocks(r.down_got)
    out_part.finish()
    r.out_out[...] = sum_blocks(r.out_got)
    gains_part.finish()
    r.gains_slot[...] = sum_blocks(r.gains_got)
    gains_last = links("gains_ulysses", r.gains_slot, r.gains_all)
    q_part.finish()
    r.q_sum[...] = sum_blocks(r.q_got).astype(bf16)
    q_last = links("q_cols", r.q_sum, r.q_out)

    def plane_sum(step):
        total = r.kv_core[0, step].astype(f32)
        for hop in range(1, n_u):
            across(hop, step).wait_recv()
            total = total + r.kv_cross[hop, step].astype(f32)
        return total

    def add_plane(step):
        r.kv_plane[step] = plane_sum(step).astype(bf16)
        along_z(step).start()

    each(n_z, add_plane, 1)
    total = plane_sum(0)
    for step in range(1, n_z):
        along_z(step).wait_recv()
        total = total + r.kv_line[step].astype(f32)
    r.inflow_out[:, QUERY_WIDTH:] = total
    gains_last.finish()
    gains = sum_blocks(r.gains_all)
    r.gains_out[...] = gains
    for part in (norms_part, ff_last, q_last, rows_part):
        part.finish()
    q_share = r.q_out.shape[2]
    for k in range(n_b):
        r.inflow_out[:, k * q_share : (k + 1) * q_share] = r.q_out[k].astype(f32)
    for k, there, here in ff_cuts(n_u, n_b):
        r.expand_out[:, here] = r.ff_out[k, :, there].astype(f32)
    squares = jnp.sum(gains * gains) / (n_u * n_b)
    for ref in (r.inflow_out, r.expand_out, r.out_out, r.down_out):
        squares += jnp.sum(ref[...] * ref[...])
    r.squares[...] = jnp.full(r.squares.shape, squares, f32)
    each(n_z, lambda step: each(n_u, lambda hop: to_core(hop, step).wait_send()))
    each(n_z, lambda step: each(n_u, lambda hop: across(hop, step).wait_send(), 1))
    each(n_z, lambda step: along_z(step).wait_send(), 1)


def lookup_kernel(slots, fills_ref, ids_ref, table_ref, rows_ref, wide, sem):
    wide[...] = jnp.zeros_like(wide)

    def row_copy(place, row):
        return pltpu.make_async_copy(
            table_ref.at[pl.ds(row, 1), :], wide.at[pl.ds(place, 1), :], sem
        )

    def of_peer(peer, total):
        fill = fills_ref[peer]

        def fetch(k, carry):
            place = peer * slots + k
            row_copy(place, ids_ref[place]).start()
            return carry

        lax.fori_loop(0, fill, fetch, 0)
        return total + fill

    total = lax.fori_loop(0, fills_ref.shape[0], of_peer, 0)

    def drain(k, carry):
        row_copy(0, 0).wait()
        return carry

    lax.fori_loop(0, total, drain, 0)
    rows_ref[...] = wide[...].astype(rows_ref.dtype)


def lookup(fills, ids, table, slots):
    places = ids.shape[0]
    return pl.pallas_call(
        functools.partial(lookup_kernel, slots),
        out_shape=jax.ShapeDtypeStruct((places, table.shape[1]), bf16),
        in_specs=[
            pl.BlockSpec(memory_space=pltpu.SMEM),
            pl.BlockSpec(memory_space=pltpu.SMEM),
            pl.BlockSpec(memory_space=pl.ANY),
        ],
        out_specs=VMEM,
        scratch_shapes=[
            pltpu.VMEM((places, table.shape[1]), f32),
            pltpu.SemaphoreType.DMA,
        ],
        compiler_params=pltpu.CompilerParams(vmem_limit_bytes=40 * 1024 * 1024),
        name="lookup",
    )(fills, ids, table)


def table_tile(share):
    return -(-share // (9 * 16)) * 16


def table_grad_kernel(
    limit, logits, finals, norms, weights, targets, rows, row_ids, grad_out, squares
):
    tile = grad_out.shape[0]
    start = pl.program_id(0) * tile
    ids = start + lax.broadcasted_iota(jnp.int32, (tile, 1), 0)
    grad_logits = (
        weights[...]
        * (jnp.exp(logits[...] - norms[...]) - jnp.where(targets[...] == ids, 1.0, 0.0))
    ).astype(bf16)
    hot = jnp.where(row_ids[...] == ids, 1.0, 0.0).astype(bf16)
    grad = mm(grad_logits, finals[...]) + mm(hot, rows[...])
    grad_out[...] = grad.astype(bf16)

    @pl.when(pl.program_id(0) == 0)
    def _():
        squares[...] = jnp.zeros_like(squares)

    squares[...] += jnp.sum(jnp.where(ids < limit, grad * grad, 0.0), axis=0, keepdims=True)


def table_grad_call(logits, finals, norms, weights, targets, rows, row_ids):
    share, picks = logits.shape
    places, width = rows.shape
    tile = table_tile(share)
    whole = lambda *shape: pl.BlockSpec(shape, lambda i: (0, 0))
    return pl.pallas_call(
        functools.partial(table_grad_kernel, share),
        grid=(pl.cdiv(share, tile),),
        out_shape=[
            jax.ShapeDtypeStruct((share, width), bf16),
            jax.ShapeDtypeStruct((1, width), f32),
        ],
        in_specs=[
            pl.BlockSpec((tile, picks), lambda i: (i, 0)),
            whole(picks, width),
            whole(1, picks),
            whole(1, picks),
            whole(1, picks),
            whole(places, width),
            whole(1, places),
        ],
        out_specs=[
            pl.BlockSpec((tile, width), lambda i: (i, 0)),
            whole(1, width),
        ],
        compiler_params=pltpu.CompilerParams(vmem_limit_bytes=40 * 1024 * 1024),
        cost_estimate=pl.CostEstimate(
            flops=2 * share * width * (picks + places),
            bytes_accessed=share * (4 * picks + 2 * width),
            transcendentals=share * picks,
        ),
        name="table_grad",
    )(logits, finals, norms, weights, targets, rows, row_ids)


def adam_kernel(rate, decay, numbers, weight, first, second, grad, change, new_first, new_second):
    gradient = grad[...].astype(f32) * numbers[0]
    mean = beta_first * first[...] + (1.0 - beta_first) * gradient
    square = beta_second * second[...] + (1.0 - beta_second) * gradient * gradient
    new_first[...] = mean
    new_second[...] = square
    change[...] = -rate * (
        mean * numbers[1] / (jnp.sqrt(square * numbers[2]) + adam_eps) + decay * weight[...]
    )


def layer_adam_kernel(rates, decays, numbers, *refs):
    count = len(rates)
    for k in range(count):
        weight, first, second, grad = refs[4 * k : 4 * k + 4]
        adam_kernel(rates[k], decays[k], numbers, weight, first, second, grad, *refs[4 * count + 3 * k :][:3])


def layer_adam_call(numbers, groups, rates, decays):
    arrays = [array for group in groups for array in group]
    return pl.pallas_call(
        functools.partial(layer_adam_kernel, rates, decays),
        out_shape=[
            jax.ShapeDtypeStruct(group[0].shape, f32) for group in groups for _ in range(3)
        ],
        in_specs=[pl.BlockSpec(memory_space=pltpu.SMEM)] + [VMEM] * len(arrays),
        out_specs=[VMEM] * (3 * len(groups)),
        compiler_params=pltpu.CompilerParams(vmem_limit_bytes=32 * 1024 * 1024),
        name="layer_adam",
    )(numbers, *arrays)


def adam_call(numbers, weight, first, second, grad, rate, decay):
    share, width = weight.shape
    tile = table_tile(share)
    block = pl.BlockSpec((tile, width), lambda i: (i, 0))
    return pl.pallas_call(
        functools.partial(adam_kernel, rate, decay),
        grid=(pl.cdiv(share, tile),),
        out_shape=[jax.ShapeDtypeStruct((share, width), f32)] * 3,
        in_specs=[pl.BlockSpec(memory_space=pltpu.SMEM)] + [block] * 4,
        out_specs=[block] * 3,
        compiler_params=pltpu.CompilerParams(vmem_limit_bytes=48 * 1024 * 1024),
        name="adam",
    )(numbers, weight, first, second, grad)


def local(
    tokens,
    lengths,
    picked,
    targets,
    advantages,
    step_count,
    embedding,
    first_embedding,
    second_embedding,
    inflow,
    inflow_first_moment,
    inflow_second_moment,
    outflow,
    first_outflow,
    second_outflow,
    expand,
    first_expand,
    second_expand,
    contract,
    first_contract,
    second_contract,
    scales,
    first_scales,
    second_scales,
):
    exchange = Exchanger()
    n_u, n_b = lax.axis_size("ulysses"), lax.axis_size("blk")
    n_all = n_u * n_b
    n_z = n_b // 2
    u, b = lax.axis_index("ulysses"), lax.axis_index("blk")
    me = u * n_b + b
    slot_count, block_len = tokens.shape
    assert slot_count == n_u and n_b % 2 == 0
    picks = picked.shape[1]
    slot_picks = picks * n_b
    all_picks = slot_picks * n_u
    row_share = embedding.shape[0]
    group = QUERY_HEADS // KEY_VALUE_HEADS
    score_scale = HEAD_WIDTH ** (-0.5)
    in_rows, out_share, ff_share = inflow.shape[0], outflow.shape[0], contract.shape[0]
    q_share = QUERY_WIDTH // n_b
    heads_share = q_share // HEAD_WIDTH
    ff_mine = n_u * ff_share
    out_cut = QUERY_WIDTH // n_all
    scale_share = scales.shape[0]

    width = KEY_VALUE_HEADS * HEAD_WIDTH
    wants_mean = n_b * (block_len + picks) / n_all
    slots = -(-int(wants_mean + 5.2 * math.sqrt(wants_mean)) // 16) * 16
    places = n_u * slots
    blk_g = ("blk", "g")
    column = ((places, 1), jnp.int32)
    row_wide = ((1, MODEL_WIDTH), f32)
    head_wide = ((1, HEAD_WIDTH), f32)
    begin = named_call(
        exchange,
        functools.partial(begin_body, n_u, n_b, row_share, slots),
        {
            "tokens": blk_g,
            "targets": blk_g,
            "picked": blk_g,
            "advantages": blk_g,
            "near": blk_g,
            "far": ("ulysses", "g"),
        },
        {},
        {
            "tokens": tokens,
            "targets": targets,
            "picked": picked,
            "advantages": advantages,
            "lengths": lengths[:, None],
            "scales": scales[None, :],
        },
        {
            "tokens_all": ((n_b,) + tokens.shape, jnp.int32),
            "targets_all": ((n_b,) + targets.shape, jnp.int32),
            "slot_picked": ((1, slot_picks), jnp.int32),
            "weights": ((1, all_picks), f32),
            "target_ids": ((1, all_picks), jnp.int32),
            "weight_wide": ((picks, 128), f32),
            "row_ids": column,
            "key_pos": column,
            "key_lim": column,
            "target_of": column,
            "positions": ((places + slot_picks, 1), jnp.int32),
            "meta": ((24, 128), f32),
            "gain_attn": row_wide,
            "gain_mlp": row_wide,
            "gain_final": row_wide,
            "gain_query": head_wide,
            "gain_key": head_wide,
        },
        {
            "picked_all": ((n_b,) + picked.shape, jnp.int32),
            "advantages_all": ((n_b,) + advantages.shape, f32),
            "near": ((n_b, 1, scale_share), f32),
            "far": ((n_u, n_b, 1, scale_share), f32),
            "wants": ((n_u, block_len + picks), jnp.int32),
            "masks": ((2 * n_u, block_len + picks), f32),
            "labels": ((2 * n_u, block_len + picks), f32),
            "ranks": ((2 * n_u, block_len + picks), f32),
            "gains": ((1, n_all * scale_share), f32),
        },
        "begin",
    )
    gain_rows = [
        begin.gain_attn,
        begin.gain_mlp,
        begin.gain_final,
        begin.gain_query,
        begin.gain_key,
    ]
    gain_attn, gain_query, gain_key = begin.gain_attn[0], begin.gain_query[0], begin.gain_key[0]
    slot_picked = begin.slot_picked[0]
    rounds = (jnp.max(begin.meta[8 : 8 + n_u, 0]).astype(jnp.int32) + slots - 1) // slots
    count_local = begin.meta[16, 0]
    half = HEAD_WIDTH // 2
    lane = jnp.arange(HEAD_WIDTH, dtype=jnp.int32)
    frequency = rope_base ** (-((lane % half).astype(f32) * 2.0 / HEAD_WIDTH))
    angles = begin.positions.astype(f32) * frequency[None, :]
    rope_cos = jnp.cos(angles)
    rope_sin = jnp.sin(angles) * jnp.where(lane < half, -1.0, 1.0)[None, :]
    query_cos, query_sin = rope_cos[places:], rope_sin[places:]
    ff_width = 2 * ff_mine
    own_cut = n_u * out_cut
    rows_low = (picks, MODEL_WIDTH)
    slot_low = (n_b, picks, MODEL_WIDTH)
    stat_rows = (8, slot_picks)
    weight_wide = begin.weight_wide

    def fetch(fills, row_ids):
        rows = lookup(fills, jnp.maximum(row_ids, 0), embedding, slots)
        return rows.reshape(n_u, slots, MODEL_WIDTH)

    def widen_ff(array):
        return (
            array.astype(f32)
            .reshape(n_b, in_rows, 2, n_u, ff_share)
            .transpose(1, 2, 3, 0, 4)
            .reshape(in_rows, 2 * FF)
        )

    def head_of_table(final_all):
        table_low = embedding.astype(bf16)
        logits = mm_back(table_low, final_all)
        local_max = jnp.max(logits, axis=0)
        head_weights = jnp.exp(logits - local_max[None, :])
        local_sum = jnp.sum(head_weights, axis=0)
        head_rows = mm_outer(head_weights.astype(bf16), table_low).astype(bf16)
        head_stats = jnp.pad(
            jnp.stack([local_max, local_sum]).reshape(2, n_u, slot_picks).transpose(1, 0, 2),
            ((0, 0), (0, 6), (0, 0)),
        )
        return (logits, head_rows.reshape(n_u, slot_picks, MODEL_WIDTH), head_stats)

    def usual_way():
        fills = jnp.minimum(begin.meta[:n_u, 0].astype(jnp.int32), slots)
        lined = {
            "key_pos": begin.key_pos,
            "key_lim": begin.key_lim,
            "slot_picked": begin.slot_picked,
            "gain_attn": gain_rows[0],
            "gain_mlp": gain_rows[1],
            "gain_final": gain_rows[2],
            "gain_query": gain_rows[3],
            "gain_key": gain_rows[4],
            "rope_cos": rope_cos,
            "rope_sin": rope_sin,
        }
        kv_block = (in_rows, 2 * width)
        kv_shape = (n_u, n_z, 2) + kv_block
        q_shape = (n_u, n_b, in_rows, q_share)
        ff_shape = (n_u, n_b, in_rows, ff_width)
        out_shape = (n_u, out_share, MODEL_WIDTH)
        down_shape = (n_u, ff_share, MODEL_WIDTH)
        rows_shape = (n_u, slots, MODEL_WIDTH)
        blk_s, blk_g = ("blk", "s"), ("blk", "g")
        uly_s, uly_g = ("ulysses", "s"), ("ulysses", "g")
        rise = named_call(
            exchange,
            functools.partial(rise_body, n_u, n_b),
            {
                "rows": uly_s,
                "q_split": blk_s,
                "ff_split": blk_s,
                "picks": blk_s,
                "q_all": uly_g,
                "normed": blk_g,
                "queries": blk_g,
                "out_all": uly_g,
                "ff_all": uly_g,
                "down_all": uly_g,
                "parts": blk_s,
                "stats": blk_g,
                "sum_out": blk_s,
                "normed_mlp": blk_g,
                "sum_mlp": blk_s,
                "final": blk_g,
                "final_all": uly_g,
            },
            {
                "z_send": (n_z,),
                "z_recv": (n_z,),
                "own": (1,),
                "xy_send": (n_u, n_z),
                "xy_recv": (n_u, n_z),
                "core_send": (n_u, n_z),
                "core_recv": (n_u, n_z),
            },
            {
                "rows_in": fetch(fills, begin.row_ids.reshape(-1)),
                "inflow": inflow,
                "expand": expand,
                "outflow": outflow,
                "contract": contract,
                "target_of": begin.target_of,
                **lined,
            },
            {
                "arrived": (rows_shape, bf16),
                "kv_weight": (kv_shape, bf16),
                "q_weight": (q_shape, bf16),
                "ff_weight": (ff_shape, bf16),
                "out_weight": (out_shape, bf16),
                "down_weight": (down_shape, bf16),
                "pick_rows": ((picks, 2 * MODEL_WIDTH), f32),
                "normed_slot": (slot_low, bf16),
                "query_raw": ((slot_picks, q_share), f32),
                "query_all": ((n_b, slot_picks, q_share), bf16),
                "key_raw": ((places, width), f32),
                "key_rot": ((places, width), bf16),
                "values": ((places, width), bf16),
                "attended": ((slot_picks, own_cut), f32),
                "log_total": ((QUERY_HEADS, slot_picks), f32),
                "after_attn": (rows_low, f32),
                "normed_mlp": (slot_low, bf16),
                "gate_up": ((slot_picks, ff_width), f32),
                "after_mlp": (rows_low, f32),
                "final_mine": (rows_low, bf16),
                "final_all": ((n_u,) + slot_low, bf16),
            },
            {
                "kv_in": (kv_block, bf16),
                "q_in": (q_shape[1:], bf16),
                "ff_in": (ff_shape[1:], bf16),
                "out_in": (out_shape[1:], bf16),
                "down_in": (down_shape[1:], bf16),
                "q_part": (q_shape[1:], bf16),
                "ff_part": (ff_shape[1:], bf16),
                "pick_send": ((n_b, picks, 2 * MODEL_WIDTH), bf16),
                "pick_got": ((n_b, picks, 2 * MODEL_WIDTH), bf16),
                "normed_mine": (rows_low, bf16),
                "normed_keys": ((places, MODEL_WIDTH), bf16),
                "query_mine": ((slot_picks, q_share), bf16),
                "part_send": ((n_b, slot_picks, own_cut), bf16),
                "part_got": ((n_b, slot_picks, own_cut), bf16),
                "stats": ((2 * QUERY_HEADS, slot_picks), f32),
                "stats_all": ((n_b, 2 * QUERY_HEADS, slot_picks), f32),
                "shares": ((n_b * n_u, slot_picks), f32),
                "partial": (slot_low, bf16),
                "partial_got": ((2,) + slot_low, bf16),
                "final_slot": (slot_low, bf16),
            },
            "rise",
        )
        final_all = rise.final_all.reshape(all_picks, MODEL_WIDTH)
        logits, head_rows, head_stats = head_of_table(final_all)
        kept = (
            "arrived",
            "kv_weight",
            "q_weight",
            "ff_weight",
            "out_weight",
            "down_weight",
            "pick_rows",
            "normed_slot",
            "query_raw",
            "query_all",
            "key_raw",
            "key_rot",
            "values",
            "attended",
            "log_total",
            "after_attn",
            "normed_mlp",
            "gate_up",
            "after_mlp",
            "final_mine",
        )
        fall = named_call(
            exchange,
            functools.partial(fall_body, n_u, n_b),
            {
                "head_rows": uly_s,
                "head_stats": uly_s,
                "slot_stats": blk_g,
                "slot_rows": blk_s,
                "norms": uly_g,
                "branch": blk_g,
                "sum_ff": blk_s,
                "down": uly_s,
                "ff": uly_s,
                "branch_attn": blk_g,
                "attended": blk_g,
                "deltas": blk_g,
                "out": uly_s,
                "grad_queries": blk_s,
                "sum_query": blk_s,
                "q": uly_s,
                "pick_back": blk_g,
                "rows": uly_s,
                "gains_blk": blk_g,
                "gains_ulysses": uly_g,
                "ff_cols": blk_s,
                "q_cols": blk_s,
            },
            {
                "core_send": (n_u, n_z),
                "core_recv": (n_u, n_z),
                "xy_send": (n_u, n_z),
                "xy_recv": (n_u, n_z),
                "z_send": (n_z,),
                "z_recv": (n_z,),
            },
            {
                "head_rows": head_rows,
                "head_stats": head_stats,
                "weights": weight_wide,
                **{key: getattr(rise, key) for key in kept},
                **lined,
            },
            {
                "norms_all": ((n_u,) + stat_rows, f32),
                "terms": ((picks, 128), f32),
                "rows_back": (rows_shape, bf16),
                "inflow_out": (inflow.shape, f32),
                "expand_out": (expand.shape, f32),
                "out_out": (out_shape[1:], f32),
                "down_out": (down_shape[1:], f32),
                "gains_out": ((32, 128), f32),
                "squares": ((8, 128), f32),
            },
            {
                "rows_got": ((n_u, slot_picks, MODEL_WIDTH), bf16),
                "stats_got": ((n_u,) + stat_rows, f32),
                "slot_stats": (stat_rows, f32),
                "slot_got": ((n_b,) + stat_rows, f32),
                "factors": ((n_b + 8, slot_picks), f32),
                "columns": ((slot_picks, n_b + 8), f32),
                "norms_mine": (stat_rows, f32),
                "partial": (slot_low, bf16),
                "partial_got": ((3,) + slot_low, bf16),
                "mine_low": (rows_low, bf16),
                "grad_all": (slot_low, bf16),
                "branch_all": (slot_low, bf16),
                "grad_down": (down_shape, bf16),
                "down_got": (down_shape, bf16),
                "grad_ff": (ff_shape, bf16),
                "ff_got": (ff_shape, bf16),
                "grad_out": (out_shape, bf16),
                "out_got": (out_shape, bf16),
                "attended_mine": ((slot_picks, own_cut), bf16),
                "attended_all": ((n_b, slot_picks, own_cut), bf16),
                "deltas": ((slot_picks, 128), f32),
                "delta_mine": (stat_rows, f32),
                "delta_all": ((n_b,) + stat_rows, f32),
                "normed_keys": ((places, MODEL_WIDTH), bf16),
                "query_send": ((n_b, slot_picks, q_share), bf16),
                "query_got": ((n_b, slot_picks, q_share), bf16),
                "grad_kv": ((places, 2 * width), bf16),
                "kv_grad": (kv_shape, bf16),
                "kv_core": ((n_u, n_z) + kv_block, bf16),
                "kv_cross": ((n_u, n_z) + kv_block, bf16),
                "kv_plane": ((n_z,) + kv_block, bf16),
                "kv_line": ((n_z,) + kv_block, bf16),
                "grad_low": ((slot_picks, q_share), bf16),
                "grad_q": (q_shape, bf16),
                "q_got": (q_shape, bf16),
                "q_sum": (q_shape[1:], bf16),
                "pick_back": (slot_low, bf16),
                "grad_wide": ((places, MODEL_WIDTH), f32),
                "rows_send": (rows_shape, bf16),
                "gain_mlp_row": ((1, MODEL_WIDTH), f32),
                "gain_final_row": ((1, MODEL_WIDTH), f32),
                "gain_picks_row": ((1, MODEL_WIDTH), f32),
                "gain_rows_row": ((1, MODEL_WIDTH), f32),
                "gain_query_row": ((1, HEAD_WIDTH), f32),
                "gain_key_row": ((1, HEAD_WIDTH), f32),
                "gains_mine": ((32, 128), f32),
                "gains_got": ((n_b, 32, 128), f32),
                "gains_slot": ((32, 128), f32),
                "gains_all": ((n_u, 32, 128), f32),
                "ff_sum": (ff_shape[1:], bf16),
                "q_out": (q_shape[1:], bf16),
                "ff_out": (ff_shape[1:], bf16),
            },
            "fall",
        )
        table_grad, table_squares = table_grad_call(
            logits,
            final_all,
            fall.norms_all[:, 0].reshape(1, all_picks),
            begin.weights,
            begin.target_ids,
            fall.rows_back.reshape(places, MODEL_WIDTH),
            begin.row_ids.reshape(1, places),
        )
        return (
            -jnp.sum(fall.terms[:, 0]),
            fall.squares[0, 0] + jnp.sum(table_squares),
            table_grad,
            fall.inflow_out,
            fall.out_out,
            fall.expand_out,
            fall.down_out,
            lax.dynamic_slice_in_dim(fall.gains_out.reshape(-1), me * scale_share, scale_share),
        )

    def long_way():
        inflow_low = inflow.astype(bf16)
        q_cols = inflow_low[:, :QUERY_WIDTH].reshape(in_rows, n_b, q_share).transpose(1, 0, 2)
        ff_cols = (
            expand.astype(bf16)
            .reshape(in_rows, 2, n_u, n_b, ff_share)
            .transpose(3, 0, 1, 2, 4)
            .reshape(n_b, in_rows, 2 * ff_mine)
        )
        wants_block = block_len + picks
        wants_count = n_b * wants_block
        wants = (
            jnp.concatenate([begin.tokens_all, begin.targets_all], axis=2)
            .transpose(1, 0, 2)
            .reshape(n_u, wants_count)
        )
        my_length = lax.dynamic_index_in_dim(lengths, u, 0, keepdims=False)
        owners = wants // row_share
        own_owners = lax.dynamic_index_in_dim(owners, u, 0, keepdims=True)
        sent_mask = owners == me
        got_mask = own_owners == jnp.arange(n_u, dtype=jnp.int32)[:, None] * n_b + b
        masks = jnp.concatenate([sent_mask, got_mask], axis=0)
        totals_sent = jnp.sum(sent_mask.astype(f32), axis=1).astype(jnp.int32)
        lanes = math.gcd(wants_count, 128)
        blocks = masks.astype(bf16).reshape(2 * n_u, wants_count // lanes, lanes)
        before = (jnp.arange(lanes)[:, None] < jnp.arange(lanes)[None, :]).astype(bf16)
        block_sums = jnp.sum(blocks.astype(f32), axis=-1)
        chunk = jnp.arange(wants_count // lanes)
        block_base = mm(block_sums.astype(bf16), (chunk[:, None] < chunk[None, :]).astype(bf16))
        ranks = (
            mm(blocks.reshape(-1, lanes), before).reshape(blocks.shape) + block_base[:, :, None]
        ).reshape(2 * n_u, wants_count)
        ranks = jnp.where(masks, ranks.astype(jnp.int32), -1)
        labels = jnp.concatenate(
            [
                wants - me * row_share,
                jnp.broadcast_to(
                    jnp.arange(wants_count, dtype=jnp.int32)[None, :], (n_u, wants_count)
                ),
            ],
            axis=0,
        )

        def slot_tables(turn, hot):
            slot_rank = turn * slots + jnp.arange(slots, dtype=jnp.int32)
            hit = ranks[:, None, :] == slot_rank[None, :, None]
            found = jnp.sum(jnp.where(hit, labels[:, None, :] + 1, 0), axis=-1) - 1
            fills = jnp.clip(totals_sent - turn * slots, 0, slots)
            row_ids = found[:n_u].reshape(-1)
            entry = found[n_u:].reshape(-1)
            block, inside = entry // wants_block, entry % wants_block
            is_token = (entry >= 0) & (inside < block_len)
            key_pos = jnp.where(is_token, block * block_len + inside, 1 << 30)
            target_of = jnp.where(
                (entry >= 0) & (inside >= block_len), block * picks + inside - block_len, -1
            )
            if not hot:
                return (row_ids, fills, key_pos, None, target_of)
            pick_hot = (slot_picked[:, None] == key_pos[None, :]).astype(bf16)
            target_hot = (jnp.arange(slot_picks)[:, None] == target_of[None, :]).astype(bf16)
            return (row_ids, fills, key_pos, pick_hot, target_hot)

        row_ids, fills, key_pos, pick_hot, target_hot = slot_tables(jnp.int32(0), True)

        arrived, kv_weight, q_weight, ff_split = start_call(
            exchange, fetch(fills, row_ids), inflow_low[:, QUERY_WIDTH:], q_cols, ff_cols
        )
        arrived = arrived.reshape(places, MODEL_WIDTH)
        kv_weight = kv_weight.reshape(MODEL_WIDTH, -1)
        q_weight = q_weight.reshape(MODEL_WIDTH, q_share)
        def picked_rows(pick_hot, target_hot, arrived):
            return jnp.concatenate([mm(pick_hot, arrived), mm(target_hot, arrived)], axis=1)

        refetch_id = [exchange.next_id() for _ in range(5)]

        def refetch(turn, which):
            tables = slot_tables(turn, True)
            (got,) = exchange.many(
                (("ulysses", "s"),), fetch(tables[1], tables[0]), collective_id=refetch_id[which]
            )
            return (tables, got.reshape(places, MODEL_WIDTH))

        def more(state):
            return state[0] < rounds

        def picks_turn(state):
            tables, got = refetch(state[0], 0)
            return (state[0] + 1, state[1] + picked_rows(tables[3], tables[4], got))

        pick_part = picked_rows(pick_hot, target_hot, arrived)
        _, pick_part = lax.while_loop(more, picks_turn, (jnp.int32(1), pick_part))
        got_picks, normed_slot, query_raw, query_all, ff_all, out_all, down_all = fused_call(
            exchange,
            functools.partial(query_body, n_b),
            (("blk", "s"), ("blk", "g"), ("blk", "g")) + (("ulysses", "g"),) * 3,
            (
                pick_part.astype(bf16).reshape(n_b, picks, 2 * MODEL_WIDTH),
                gain_rows[0],
                gain_rows[3],
                q_weight,
                query_cos,
                query_sin,
                ff_split,
                outflow.astype(bf16),
                contract.astype(bf16),
            ),
            (
                ((picks, 2 * MODEL_WIDTH), f32),
                (slot_low, bf16),
                ((slot_picks, q_share), f32),
                ((n_b, slot_picks, q_share), bf16),
                ((n_u, n_b, in_rows, ff_width), bf16),
                ((n_u, out_share, MODEL_WIDTH), bf16),
                ((n_u, ff_share, MODEL_WIDTH), bf16),
            ),
            (
                ((n_b, picks, 2 * MODEL_WIDTH), bf16),
                (rows_low, bf16),
                ((slot_picks, q_share), bf16),
            ),
            "queries",
        )
        ff_weight = ff_all.reshape(MODEL_WIDTH, ff_width)
        out_weight = out_all.reshape(n_u * out_share, MODEL_WIDTH)
        down_weight = down_all.reshape(ff_mine, MODEL_WIDTH)

        def keys_of(arrived, key_pos):
            embedded = arrived.astype(f32)
            normed = (embedded * inverse_root(embedded) * gain_attn).astype(bf16)
            mixed = mm(normed, kv_weight)
            half = KEY_VALUE_HEADS * HEAD_WIDTH
            key_raw = mixed[:, :half].reshape(places, KEY_VALUE_HEADS, HEAD_WIDTH)
            values = mixed[:, half:].reshape(places, KEY_VALUE_HEADS, HEAD_WIDTH)
            angle_tables = rope_angles(jnp.where(key_pos < (1 << 30), key_pos, 0))
            key_rot = rotate(key_raw * inverse_root(key_raw) * gain_key, angle_tables, 1.0)
            return (
                embedded,
                normed,
                key_raw,
                angle_tables,
                key_rot.astype(bf16).transpose(1, 0, 2),
                values.astype(bf16).transpose(1, 0, 2),
            )

        query_pos = jnp.tile(slot_picked, group)

        def allowed_of(key_pos):
            return ((key_pos[None, :] <= query_pos[:, None]) & (key_pos[None, :] < my_length))[None]

        def scores_of(query_groups, key_rot, allowed):
            scores = (
                jnp.einsum("kqd,kjd->kqj", query_groups, key_rot, preferred_element_type=f32)
                * score_scale
            )
            return jnp.where(allowed, scores, masked_score)

        def attend(scores, allowed, values):
            part_max = jnp.max(scores, axis=-1, keepdims=True)
            weights = jnp.where(allowed, jnp.exp(scores - part_max), 0.0)
            out = jnp.einsum("kqj,kjd->kqd", weights.astype(bf16), values, preferred_element_type=f32)
            return (part_max, jnp.sum(weights, axis=-1, keepdims=True), out)

        keys = keys_of(arrived, key_pos)

        query_groups = (
            query_all.reshape(n_b, slot_picks, heads_share, HEAD_WIDTH)
            .transpose(0, 2, 1, 3)
            .reshape(KEY_VALUE_HEADS, group * slot_picks, HEAD_WIDTH)
        )
        allowed = allowed_of(key_pos)
        scores = scores_of(query_groups, keys[4], allowed)

        def attend_turn(state):
            turn, top, total, out = state
            tables, got = refetch(turn, 1)
            keys_now = keys_of(got, tables[2])
            allowed_now = allowed_of(tables[2])
            new = attend(scores_of(query_groups, keys_now[4], allowed_now), allowed_now, keys_now[5])
            both = jnp.maximum(top, new[0])
            old_factor, new_factor = jnp.exp(top - both), jnp.exp(new[0] - both)
            return (
                turn + 1,
                both,
                total * old_factor + new[1] * new_factor,
                out * old_factor + new[2] * new_factor,
            )

        _, part_max, part_sum, part_out = lax.while_loop(
            more, attend_turn, (jnp.int32(1),) + attend(scores, allowed, keys[5])
        )
        part_send = (
            part_out.astype(bf16)
            .reshape(QUERY_HEADS, slot_picks, HEAD_WIDTH)
            .transpose(1, 0, 2)
            .reshape(slot_picks, n_u, n_b, out_cut)
            .transpose(2, 0, 1, 3)
            .reshape(n_b, slot_picks, n_u * out_cut)
        )
        stats = jnp.stack([part_max[..., 0], part_sum[..., 0]]).reshape(2 * QUERY_HEADS, slot_picks)
        (
            attended,
            log_total,
            after_attn,
            normed_mlp,
            gate_up,
            after_mlp,
            final_mine,
            final_all,
        ) = fused_call(
            exchange,
            functools.partial(forward_body, n_u, n_b),
            (("blk", "s"), ("blk", "g"), ("blk", "s"), ("blk", "g"), ("blk", "s"), ("blk", "g"))
            + (("ulysses", "g"),),
            (
                part_send,
                stats,
                got_picks,
                out_weight,
                ff_weight,
                down_weight,
                gain_rows[1],
                gain_rows[2],
            ),
            (
                ((slot_picks, own_cut), f32),
                ((QUERY_HEADS, slot_picks), f32),
                (rows_low, f32),
                (slot_low, bf16),
                ((slot_picks, ff_width), f32),
                (rows_low, f32),
                (rows_low, bf16),
                ((n_u,) + slot_low, bf16),
            ),
            (
                ((n_b, slot_picks, own_cut), bf16),
                ((n_b, 2 * QUERY_HEADS, slot_picks), f32),
                ((n_b * n_u, slot_picks), f32),
                (slot_low, bf16),
                ((2,) + slot_low, bf16),
                (rows_low, bf16),
                (slot_low, bf16),
            ),
            "forward",
        )

        final_all = final_all.reshape(all_picks, MODEL_WIDTH)
        logits, head_rows, head_stats = head_of_table(final_all)
        (
            norms_all,
            terms,
            grad_gain_mlp,
            grad_gain_final,
            grad_ff,
            grad_out,
            grad_down,
            grad_after_attn,
            _,
            got_attended,
            got_delta,
        ) = fused_call(
            exchange,
            functools.partial(backward_body, n_u, n_b),
            (
                ("ulysses", "s"),
                ("ulysses", "s"),
                ("blk", "s"),
                ("blk", "g"),
                ("ulysses", "g"),
                ("blk", "g"),
                ("blk", "s"),
                ("blk", "g"),
                ("blk", "g"),
                ("blk", "g"),
            ),
            (
                head_rows,
                head_stats,
                final_mine,
                got_picks,
                weight_wide,
                after_mlp,
                after_attn,
                gate_up,
                normed_mlp,
                attended,
                out_weight,
                ff_weight,
                down_weight,
                gain_rows[1],
                gain_rows[2],
            ),
            (
                ((n_u,) + stat_rows, f32),
                ((picks, 128), f32),
                ((1, MODEL_WIDTH), f32),
                ((1, MODEL_WIDTH), f32),
                ((n_u, n_b, in_rows, ff_width), bf16),
                ((n_u, out_share, MODEL_WIDTH), bf16),
                ((n_u, ff_share, MODEL_WIDTH), bf16),
                (rows_low, f32),
                (slot_low, bf16),
                ((n_b, slot_picks, own_cut), bf16),
                ((n_b,) + stat_rows, f32),
            ),
            (
                ((n_u, slot_picks, MODEL_WIDTH), bf16),
                ((n_u,) + stat_rows, f32),
                (stat_rows, f32),
                ((n_b,) + stat_rows, f32),
                ((n_b + 8, slot_picks), f32),
                ((slot_picks, n_b + 8), f32),
                (stat_rows, f32),
                (slot_low, bf16),
                ((2,) + slot_low, bf16),
                (rows_low, bf16),
                (slot_low, bf16),
                ((slot_picks, own_cut), bf16),
                ((slot_picks, 128), f32),
                (stat_rows, f32),
            ),
            "backward",
        )
        loss_local = -jnp.sum(terms[:, 0])
        grad_heads = (
            got_attended.reshape(n_b, slot_picks, n_u, out_cut)
            .transpose(1, 2, 0, 3)
            .reshape(slot_picks, QUERY_HEADS, HEAD_WIDTH)
            .transpose(1, 0, 2)
            .reshape(KEY_VALUE_HEADS, group * slot_picks, HEAD_WIDTH)
        )
        row_delta = jnp.sum(
            got_delta[:, :n_u].transpose(1, 0, 2).reshape(QUERY_HEADS, HEAD_WIDTH // out_cut, slot_picks), axis=1
        ).reshape(KEY_VALUE_HEADS, group * slot_picks, 1)
        log_groups = log_total.reshape(KEY_VALUE_HEADS, group * slot_picks, 1)

        def score_grads(scores, allowed, values):
            probs = jnp.where(allowed, jnp.exp(scores - log_groups), 0.0)
            grad_probs = jnp.einsum("kqd,kjd->kqj", grad_heads, values, preferred_element_type=f32)
            return (probs, (probs * (grad_probs - row_delta) * score_scale).astype(bf16))

        def query_grads(grad_scores, key_rot):
            return jnp.einsum("kqj,kjd->kqd", grad_scores, key_rot, preferred_element_type=f32)

        def key_grads(probs, grad_scores, keys):
            grad_key = jnp.einsum(
                "kqj,kqd->kjd", grad_scores, query_groups, preferred_element_type=f32
            )
            grad_value = jnp.einsum(
                "kqj,kqd->kjd", probs.astype(bf16), grad_heads, preferred_element_type=f32
            )
            upstream = rotate(
                grad_key.astype(bf16).astype(f32).transpose(1, 0, 2), keys[3], -1.0
            )
            grad_raw, grad_gain = norm_back(keys[2], gain_key, upstream)
            grad_kv = jnp.concatenate(
                [
                    grad_raw.reshape(places, -1).astype(bf16),
                    grad_value.astype(bf16).transpose(1, 0, 2).reshape(places, -1),
                ],
                axis=1,
            )
            return (grad_kv, grad_gain)

        def row_grads(grad_kv, keys):
            return norm_back(keys[0], gain_attn, mm_back(grad_kv, kv_weight))

        def redo(turn, which):
            tables, got = refetch(turn, which)
            keys_now = keys_of(got, tables[2])
            allowed_now = allowed_of(tables[2])
            scores_now = scores_of(query_groups, keys_now[4], allowed_now)
            return (tables, keys_now) + score_grads(scores_now, allowed_now, keys_now[5])

        def query_turn(state):
            _, keys_now, _, grad_scores_now = redo(state[0], 2)
            return (state[0] + 1, state[1] + query_grads(grad_scores_now, keys_now[4]))

        probs, grad_scores = score_grads(scores, allowed, keys[5])
        _, grad_query_part = lax.while_loop(
            more, query_turn, (jnp.int32(1), query_grads(grad_scores, keys[4]))
        )
        query_send = (
            grad_query_part.astype(bf16)
            .reshape(n_b, heads_share, slot_picks, HEAD_WIDTH)
            .transpose(0, 2, 1, 3)
            .reshape(n_b, slot_picks, q_share)
        )
        (
            grad_gain_query,
            grad_gain_picks,
            grad_q,
            pick_back,
            sum_ff,
            sum_outflow,
            sum_contract,
        ) = fused_call(
            exchange,
            query_back_body,
            (("blk", "s"), ("blk", "s"), ("blk", "g")) + (("ulysses", "s"),) * 3,
            (
                query_send,
                query_raw,
                query_cos,
                query_sin,
                gain_rows[3],
                q_weight,
                normed_slot,
                got_picks,
                gain_rows[0],
                grad_after_attn,
                grad_ff,
                grad_out,
                grad_down,
            ),
            (
                ((1, HEAD_WIDTH), f32),
                ((1, MODEL_WIDTH), f32),
                ((n_u, n_b, in_rows, q_share), bf16),
                (slot_low, bf16),
                ((n_b, in_rows, ff_width), bf16),
                ((out_share, MODEL_WIDTH), f32),
                ((ff_share, MODEL_WIDTH), f32),
            ),
            (
                ((n_b, slot_picks, q_share), bf16),
                ((slot_picks, q_share), bf16),
                (slot_low, bf16),
                (slot_low, bf16),
                (rows_low, bf16),
                ((n_u, n_b, in_rows, ff_width), bf16),
                ((n_u, out_share, MODEL_WIDTH), bf16),
                ((n_u, ff_share, MODEL_WIDTH), bf16),
            ),
            "query_grads",
        )
        pick_back = pick_back.reshape(slot_picks, MODEL_WIDTH)

        grad_kv, grad_gain_key = key_grads(probs, grad_scores, keys)
        grad_kv_weight = mm_outer(keys[1], grad_kv)
        grad_rows, grad_gain_attn = row_grads(grad_kv, keys)

        def weight_turn(state):
            turn, weight_sum, key_sum, attn_sum = state
            _, keys_now, probs_now, grad_scores_now = redo(turn, 3)
            grad_kv_now, gain_key_now = key_grads(probs_now, grad_scores_now, keys_now)
            _, gain_attn_now = row_grads(grad_kv_now, keys_now)
            return (
                turn + 1,
                weight_sum + mm_outer(keys_now[1], grad_kv_now),
                key_sum + gain_key_now,
                attn_sum + gain_attn_now,
            )

        _, grad_kv_weight, grad_gain_key, grad_gain_attn = lax.while_loop(
            more, weight_turn, (jnp.int32(1), grad_kv_weight, grad_gain_key, grad_gain_attn)
        )
        grad_scales = jnp.concatenate(
            [
                grad_gain_attn + grad_gain_picks[0],
                grad_gain_mlp[0],
                grad_gain_final[0],
                grad_gain_query[0],
                grad_gain_key,
            ]
        )

        token_rows = (grad_rows + mm_outer(pick_hot, pick_back)).astype(bf16)
        sum_kv, rows_back, got_q, got_ff, got_scales = settle_call(
            exchange,
            grad_kv_weight.astype(bf16).reshape(n_u, n_z, 2, in_rows, -1),
            token_rows.reshape(n_u, slots, MODEL_WIDTH),
            grad_q,
            sum_ff,
            jnp.pad(
                grad_scales.reshape(n_all, scale_share), ((0, 0), (0, 128 - scale_share))
            ).reshape(n_all, 1, 128),
        )
        sum_q = got_q.astype(f32).transpose(1, 0, 2).reshape(in_rows, QUERY_WIDTH)
        sum_inflow = jnp.concatenate([sum_q, sum_kv], axis=1)
        sum_expand = widen_ff(got_ff)
        sum_scales = jnp.sum(got_scales, axis=0)[0, :scale_share]

        table_grad, table_squares = table_grad_call(
            logits,
            final_all,
            norms_all[:, 0].reshape(1, all_picks),
            begin.weights,
            begin.target_ids,
            rows_back.reshape(places, MODEL_WIDTH),
            row_ids.reshape(1, places),
        )
        return_id = exchange.next_id()

        def return_turn(state):
            turn, so_far, _ = state
            tables, keys_now, probs_now, grad_scores_now = redo(turn, 4)
            grad_kv_now, _ = key_grads(probs_now, grad_scores_now, keys_now)
            rows_now, _ = row_grads(grad_kv_now, keys_now)
            rows_now = (rows_now + mm_outer(tables[3], pick_back)).astype(bf16)
            (back,) = exchange.many(
                (("ulysses", "s"),),
                rows_now.reshape(n_u, slots, MODEL_WIDTH),
                collective_id=return_id,
            )
            hot = (
                jnp.arange(row_share, dtype=jnp.int32)[:, None] == tables[0][None, :]
            ).astype(bf16)
            grown = so_far.astype(f32) + mm(hot, back.reshape(places, MODEL_WIDTH))
            return (turn + 1, grown.astype(bf16), jnp.sum(grown * grown, axis=0, keepdims=True))

        _, table_grad, table_squares = lax.while_loop(
            more, return_turn, (jnp.int32(1), table_grad, table_squares)
        )
        squares = jnp.sum(table_squares)
        for grad_piece in (sum_inflow, sum_outflow, sum_expand, sum_contract, sum_scales):
            squares = squares + jnp.sum(grad_piece * grad_piece)
        return (
            loss_local,
            squares,
            table_grad,
            sum_inflow,
            sum_outflow,
            sum_expand,
            sum_contract,
            sum_scales,
        )

    step_float = step_count[0].astype(f32)
    first_scale = 1.0 / (1.0 - beta_first**step_float)
    second_scale = 1.0 / (1.0 - beta_second**step_float)

    def finish(loss_local, squares, table_grad, *layer_grads):
        totals = named_call(
            exchange,
            totals_body,
            {"near": ("blk", "g"), "far": ("ulysses", "g")},
            {},
            {"mine": jnp.pad(jnp.stack([squares, count_local, loss_local]), (0, 125)).reshape(1, 128)},
            {"total": ((1, 128), f32)},
            {
                "near_all": ((n_b, 1, 128), f32),
                "near": ((1, 128), f32),
                "far_all": ((n_u, 1, 128), f32),
            },
            "totals",
        ).total[0]
        square_total, count_total, loss_total = totals[0], totals[1], totals[2]
        gradient_norm = jnp.sqrt(square_total) / count_total
        factor = jnp.minimum(1.0, clip_limit / gradient_norm) / count_total
        outputs = [loss_total / count_total, gradient_norm]
        numbers = jnp.stack([factor, first_scale, second_scale])
        outputs += adam_call(
            numbers,
            embedding,
            first_embedding,
            second_embedding,
            table_grad,
            learning_rates[0],
            weight_decays[0],
        )
        outputs += layer_adam_call(
            numbers,
            (
                (inflow, inflow_first_moment, inflow_second_moment, layer_grads[0]),
                (outflow, first_outflow, second_outflow, layer_grads[1]),
                (expand, first_expand, second_expand, layer_grads[2]),
                (contract, first_contract, second_contract, layer_grads[3]),
            ),
            learning_rates[1:5],
            weight_decays[1:5],
        )
        outputs += adam_update(
            scales,
            first_scales,
            second_scales,
            layer_grads[4] * factor,
            learning_rates[5],
            weight_decays[5],
            step_float,
        )
        return tuple(outputs)

    _, outputs = lax.while_loop(
        lambda state: state[0],
        lambda state: (jnp.bool_(False), finish(*long_way())),
        (rounds > 1, finish(*usual_way())),
    )
    return outputs


def solution(mesh):
    rows = P(("ulysses", "blk"), None)
    flat_rows = P(("ulysses", "blk"))
    column = P(None, "blk")
    return jax.shard_map(
        local,
        mesh=mesh,
        in_specs=(column, P(), column, column, column, P()) + (rows,) * 15 + (flat_rows,) * 3,
        out_specs=(P(), P()) + (rows,) * 15 + (flat_rows,) * 3,
        check_vma=False,
    )
```

time: 699 us -> 432 us (0.62)
  Pallas kernels: 437 us -> 364 us
  other arithmetic: 71.3 us -> 11.4 us
  local copies, waits for them, and re-layouts: 68.6 us -> 18.1 us
  matrix products: 64.2 us -> 21.3 us
  starting transfers between devices: 14.7 us -> 0 us
  loops' own time: 10.9 us -> 1.03 us
  waiting for transfers between devices: 7.88 us -> 0 us
    pallas_call x23 -> x4, Pallas kernels: 366 us -> 294 us  [remote_call(): pl.pallas_call(kernel, out_shape=shapes, in_specs=[VMEM] * len(arrays), o...]
    reduce_sum x41 -> x3, other arithmetic: 25.9 us -> 3.27 us  [the longest x1 1.36 us: head_of_table(): local_sum = jnp.sum(head_weights, axis=0)]
    dot_general x15 -> x0, matrix products: 20.6 us -> none  [the longest x9 8.67 us: mm(): lax.dot_general(left, right, (((1,), (0,)), ((), ())), preferred_element_...]
    convert_element_type x26 -> x1, other arithmetic: 17.7 us -> 1.13 us  [local(): angles = begin.positions.astype(f32) * frequency[None, :]]
    dot_general x7 -> x1, matrix products: 26.2 us -> 11.1 us  [mm_outer(): lax.dot_general(left, right, (((0,), (0,)), ((), ())), preferred_element_...]
    reshape x21 -> x0, local copies, waits for them, and re-layouts: 14.9 us -> none  [the longest x1 4.02 us: local(): grad_expand.astype(bf16).reshape(n_u, wide_rows, MODEL_WIDTH)]
    all_to_all x3 -> x0, starting transfers between devices: 14.7 us -> none  [the longest x1 5.19 us: local(): lax.all_to_all(sum_layer[:wide_rows].astype(bf16).reshape(n_b, in_rows, 2...]
    mul x9 -> x0, local copies, waits for them, and re-layouts: 12.8 us -> none  [the longest x3 5.36 us: local(): layer_grads[position] * factor]
  transfers between devices with their start and end apart: 3 -> 0, of which waited for: 1 -> 0; matrix products, arithmetic and copies ran while one was open for 8% -> 0% of each run, Pallas kernels for 22% -> 0%
where the time goes in v3:
time: 432 us; the launch traced here: 426 us
  Pallas kernels  364 us (84%)
  matrix products  21.3 us (5%)
  local copies, waits for them, and re-layouts  18.1 us (4%)
  other arithmetic  11.4 us (3%)
  between operations  11 us (3%)
    pallas_call x4, Pallas kernels, remote_call(): pl.pallas_call(kernel, out_shape=shapes, in_specs=[VMEM] * len(arrays), o...  294 us
    pallas_call x1, Pallas kernels, adam_call(): pl.pallas_call(functools.partial(adam_kernel, rate, decay), grid=(pl.cdiv...  42.5 us
    pallas_call x1, Pallas kernels, table_grad_call(): pl.pallas_call(functools.partial(table_grad_kernel, share), grid=(pl.cdiv...  16.8 us
    dot_general x1, matrix products, mm_outer(): lax.dot_general(left, right, (((0,), (0,)), ((), ())), preferred_element_...  11.1 us
    dot_general x1, matrix products, mm_back(): lax.dot_general(left, right, (((1,), (1,)), ((), ())), preferred_element_...  10.2 us

profile of v3, /device:TPU:0, one launch (start us, length us, event | category | flops | bytes accessed | tf_op | source)
XLA Modules:
  0.0 426.5 jit_solution(4857306061074700771)
XLA Ops:
  1.5 1.3 copy.342.refs_4_
  2.8 15.1 %begin.1 = (s32[8,4,256]{2,1,0:T(4,128)}, s32[8,4,16]{2,1,0:T(4,128)}, s32[1,128]{1,0:T(1,128)S(1)}, f32[1,512]{1,0:T(1,128)}, s32[1,512]{1,0:T(1,128)}, /*index...) custom-call(s32[4,256]{1,0:T(4,128)} %refs_0_.2, ...), custom_call_target="tpu_custom_call" | custom-call | tf_op jit(solution)/shard_map/begin/pallas_call | solution.py:219
  17.9 0.0 copy-start.105
  17.9 0.0 copy-start.116
  17.9 1.2 slice.309
  19.2 1.3 slice_reduce_fusion.2
  21.1 1.2 fusion.272
  22.3 0.8 minimum_reduce_fusion.fills_ref
  23.1 1.1 convert_reduce_fusion.2
  24.2 1.3 copy.344
  25.5 1.4 copy.343
  26.9 1.1 fusion.264
  28.0 0.0 copy-start.103
  28.0 0.0 copy-start.104
  28.0 0.7 slice.373
  28.7 0.6 slice.372
  29.4 4.6 %lookup.28 = bf16[448,1024]{1,0:T(8,128)(2,1)S(1)} custom-call(s32[4]{0:T(128)S(1)} %minimum_reduce_fusion.fills_ref, s32[448]{0:T(512)S(1)} %get-tuple-element.2306.ids_ref, f32[4748,1024]{1,0:T(8,128)} %weight.1), custom_call_target="tpu_custom_call" | custom-call | tf_op jit(solution)/shard_map/lookup/pallas_call | solution.py:1679
  34.0 0.0 copy-start.12
  34.0 0.9 copy-done.12
  34.9 130.0 %rise.1 = (bf16[4,112,1024]{2,1,0:T(8,128)(2,1)}, bf16[4,4,2,32,2048]{4,3,2,1,0:T(8,128)(2,1)}, bf16[4,8,32,256]{3,2,1,0:T(8,128)(2,1)}, bf16[4,8,32,768]{3,2,1,...) custom-call(bf16[4,112,1024]{2,1,0:T(8,128)(2,1)} %bitcast.864, ...), custom_call_target="tpu_custom_call" | custom-call | tf_op jit(solution)/shard_map/rise/pallas_call | solution.py:219
  165.0 10.2 %fusion.289 = (f32[512]{0:T(512)S(1)}, f32[512,4748]{0,1:T(8,128)S(1)}) fusion(bf16[512,1024]{1,0:T(8,128)(2,1)} %bitcast.865, f32[4748,1024]{1,0:T(8,128)} %weight.1), kind=kOutput, calls=%fused_computation.574 | convolution fusion | flops 4985931264 | bytes 30222336 | tf_op jit(solution)/shard_map/dot_general | solution.py:81
  175.2 0.0 copy-start.76
  175.2 1.4 fusion.251
  176.6 1.2 pad.20.refs_1_
  177.8 1.2 copy-done.76
  179.0 11.1 %fusion.259 = bf16[512,1024]{1,0:T(8,128)(2,1)} fusion(f32[4748,1024]{1,0:T(8,128)} %weight.1, f32[512]{0:T(512)S(1)} %get-tuple-element.2715, f32[512,4748]{0,1:T(8,128)S(1)} %get-tuple-element.2716), kind=kOutput, calls=%fused_computation.537 | convolution fusion | flops 4988887040 | bytes 30222336 | tf_op jit(solution)/shard_map/dot_general | solution.py:77
  190.2 0.0 copy-done.116
  190.2 136.3 %fall.1 = (f32[4,8,128]{2,1,0:T(8,128)}, f32[16,128]{1,0:T(8,128)}, bf16[4,112,1024]{2,1,0:T(8,128)(2,1)}, f32[32,4096]{1,0:T(8,128)}, f32[32,6144]{1,0:T(8,128)...) custom-call(bf16[4,128,1024]{2,1,0:T(8,128)(2,1)} %bitcast.963, ...), custom_call_target="tpu_custom_call" | custom-call | tf_op jit(solution)/shard_map/fall/pallas_call | solution.py:219
  326.6 1.3 slice_reduce_fusion.1
  328.5 1.2 slice.307
  329.7 0.7 slice_bitcast_fusion.12.norms
  330.4 1.2 copy-done.18
  331.6 16.8 %table_grad.3 = (bf16[4748,1024]{1,0:T(8,128)(2,1)S(1)}, f32[1,1024]{1,0:T(1,128)S(1)}) custom-call(f32[4748,512]{1,0:T(8,128)} %bitcast.932, bf16[512,1024]{1,0:T(8,128)(2,1)S(1)} %bitcast.866, f32[1,512]{1,0:T(1,128)S(1)} %slice_bitcast_fusion.12.norms, f32[1,512]{1,0:T(1,128)} %get-tuple-element.3708.weights, s32[1,512]{1,0:T(1,128)} %get-tuple-element.3709.targets, ...), custom_call_target="tpu_custom_call" | custom-call | flops 9334947840 | bytes 19447808 | tf_op jit(solution)/shard_map/table_grad/pallas_call | solution.py:1727
  348.4 3.7 copy-done.11
  352.1 0.6 reduce_sum.481
  354.0 1.2 fusion.270.refs_0_
  355.2 12.3 %totals.3 = f32[1,128]{1,0:T(1,128)} custom-call(f32[1,128]{1,0:T(1,128)} %fusion.270.refs_0_), custom_call_target="tpu_custom_call" | custom-call | tf_op jit(solution)/shard_map/totals/pallas_call | solution.py:219
  367.6 1.3 fusion.288
  373.0 1.3 add_multiply_fusion.1
  374.3 0.1 pad_maximum_fusion.12.numbers
  374.4 0.0 copy-done.17
  374.4 5.9 %layer_adam.3 = (f32[32,4096]{1,0:T(8,128)}, f32[32,4096]{1,0:T(8,128)}, f32[32,4096]{1,0:T(8,128)}, f32[64,1024]{1,0:T(8,128)}, f32[64,1024]{1,0:T(8,128)}, /*i...) custom-call(f32[3]{0:T(128)S(1)} %pad_maximum_fusion.12.numbers, ...), custom_call_target="tpu_custom_call" | custom-call | tf_op jit(solution)/shard_map/layer_adam/pallas_call | solution.py:1777
  380.3 0.0 copy-start.60
  380.3 0.0 copy-start.70
  380.4 0.0 copy-start.78
  380.4 0.0 copy-start.129
  380.4 42.5 %adam.3 = (f32[4748,1024]{1,0:T(8,128)}, f32[4748,1024]{1,0:T(8,128)}, f32[4748,1024]{1,0:T(8,128)}) custom-call(f32[3]{0:T(128)S(1)} %pad_maximum_fusion.12.numbers, f32[4748,1024]{1,0:T(8,128)} %weight.1, f32[4748,1024]{1,0:T(8,128)} %first.1, f32[4748,1024]{1,0:T(8,128)} %second.1, bf16[4748,1024]{1,0:T(8,128)(2,1)} %copy-done.11), custom_call_target="tpu_custom_call" | custom-call | tf_op jit(solution)/shard_map/adam/pallas_call | solution.py:1793
  423.0 1.0 while.117
  (38 shorter events, 0.1 us)
Async XLA Ops:
  17.9 172.3 %copy-start.105 = (s32[1,128]{1,0:T(1,128)}, s32[1,128]{1,0:T(1,128)S(1)}, u32[]{:S(2)}) copy-start(s32[1,128]{1,0:T(1,128)S(1)} %get-tuple-element.3692.refs_8_.refs_25_) | copy-start | bytes 1540
  17.9 172.3 %copy-start.116 = (f32[1,1024]{1,0:T(1,128)}, f32[1,1024]{1,0:T(1,128)S(1)}, u32[]{:S(2)}) copy-start(f32[1,1024]{1,0:T(1,128)S(1)} %get-tuple-element.3705.refs_10_.refs_27_) | copy-start | bytes 12292
  17.9 172.3 %copy-start.118 = (f32[1,1024]{1,0:T(1,128)}, f32[1,1024]{1,0:T(1,128)S(1)}, u32[]{:S(2)}) copy-start(f32[1,1024]{1,0:T(1,128)S(1)} %get-tuple-element.3706.refs_11_.refs_28_) | copy-start | bytes 12292
  17.9 172.3 %copy-start.120 = (f32[16,128]{1,0:T(8,128)}, f32[16,128]{1,0:T(8,128)S(1)}, u32[]{:S(2)}) copy-start(f32[16,128]{1,0:T(8,128)S(1)} %get-tuple-element.3707.refs_2_) | copy-start | bytes 24580
  17.9 172.3 %copy-start.124 = (f32[1,128]{1,0:T(1,128)}, f32[1,128]{1,0:T(1,128)S(1)}, u32[]{:S(2)}) copy-start(f32[1,128]{1,0:T(1,128)S(1)} %get-tuple-element.3701.refs_12_.refs_29_) | copy-start | bytes 1540
  28.0 5.9 %copy-start.103 = (f32[576,128]{1,0:T(8,128)}, f32[576,128]{1,0:T(8,128)S(1)}, u32[]{:S(2)}) copy-start(f32[576,128]{1,0:T(8,128)S(1)} %get-tuple-element.2710.refs_15_.refs_32_) | copy-start | bytes 884740
  28.0 5.9 %copy-start.104 = (f32[576,128]{1,0:T(8,128)}, f32[576,128]{1,0:T(8,128)S(1)}, u32[]{:S(2)}) copy-start(f32[576,128]{1,0:T(8,128)S(1)} %get-tuple-element.2711.refs_14_.refs_31_) | copy-start | bytes 884740
  29.4 5.6 %copy-start.59 = (f32[32,6144]{1,0:T(8,128)S(1)}, f32[32,6144]{1,0:T(8,128)}, u32[]{:S(2)}) copy-start(f32[32,6144]{1,0:T(8,128)} %refs_8_.1) | copy-start | bytes 2359300
  29.4 5.6 %copy-start.66 = (f32[32,4096]{1,0:T(8,128)S(1)}, f32[32,4096]{1,0:T(8,128)}, u32[]{:S(2)}) copy-start(f32[32,4096]{1,0:T(8,128)} %refs_0_.3) | copy-start | bytes 1572868
  29.4 5.6 %copy-start.69 = (f32[96,1024]{1,0:T(8,128)S(1)}, f32[96,1024]{1,0:T(8,128)}, u32[]{:S(2)}) copy-start(f32[96,1024]{1,0:T(8,128)} %refs_12_.1) | copy-start | bytes 1179652
  29.4 5.6 %copy-start.77 = (f32[64,1024]{1,0:T(8,128)S(1)}, f32[64,1024]{1,0:T(8,128)}, u32[]{:S(2)}) copy-start(f32[64,1024]{1,0:T(8,128)} %refs_4_.3) | copy-start | bytes 786436
  34.0 0.9 copy-start.12
  175.2 3.8 copy-start.76
  190.2 140.2 %copy-start.13 = (bf16[4,8,16,1024]{3,2,1,0:T(8,128)(2,1)S(1)}, bf16[4,8,16,1024]{3,2,1,0:T(8,128)(2,1)}, u32[]{:S(2)}) copy-start(bf16[4,8,16,1024]{3,2,1,0:T(8,128)(2,1)} %get-tuple-element.1653) | copy-start | bytes 3145732
  330.4 1.2 copy-start.18
  331.6 42.8 %copy-start.14 = (f32[32,6144]{1,0:T(8,128)S(1)}, f32[32,6144]{1,0:T(8,128)}, u32[]{:S(2)}) copy-start(f32[32,6144]{1,0:T(8,128)} %get-tuple-element.1688.refs_11_) | copy-start | bytes 2359300
  331.6 42.8 %copy-start.15 = (f32[32,4096]{1,0:T(8,128)S(1)}, f32[32,4096]{1,0:T(8,128)}, u32[]{:S(2)}) copy-start(f32[32,4096]{1,0:T(8,128)} %get-tuple-element.1686.refs_3_) | copy-start | bytes 1572868
  331.6 42.8 %copy-start.16 = (f32[96,1024]{1,0:T(8,128)S(1)}, f32[96,1024]{1,0:T(8,128)}, u32[]{:S(2)}) copy-start(f32[96,1024]{1,0:T(8,128)} %get-tuple-element.1689.refs_15_) | copy-start | bytes 1179652
  331.6 42.8 %copy-start.17 = (f32[64,1024]{1,0:T(8,128)S(1)}, f32[64,1024]{1,0:T(8,128)}, u32[]{:S(2)}) copy-start(f32[64,1024]{1,0:T(8,128)} %get-tuple-element.1687.refs_7_) | copy-start | bytes 786436
  348.4 3.7 copy-start.11
  380.3 42.6 %copy-start.60 = (f32[32,6144]{1,0:T(8,128)S(1)}, f32[32,6144]{1,0:T(8,128)}, u32[]{:S(2)}) copy-start(f32[32,6144]{1,0:T(8,128)} %refs_8_.1) | copy-start | bytes 2359300
  380.3 42.6 %copy-start.70 = (f32[96,1024]{1,0:T(8,128)S(1)}, f32[96,1024]{1,0:T(8,128)}, u32[]{:S(2)}) copy-start(f32[96,1024]{1,0:T(8,128)} %refs_12_.1) | copy-start | bytes 1179652
  380.4 42.6 %copy-start.78 = (f32[64,1024]{1,0:T(8,128)S(1)}, f32[64,1024]{1,0:T(8,128)}, u32[]{:S(2)}) copy-start(f32[64,1024]{1,0:T(8,128)} %refs_4_.3) | copy-start | bytes 786436
  380.4 42.6 %copy-start.106 = (s32[1,128]{1,0:T(1,128)S(1)}, s32[1,128]{1,0:T(1,128)}, u32[]{:S(2)}) copy-start(s32[1,128]{1,0:T(1,128)} %copy-done.105) | copy-start | bytes 1540
  380.4 42.6 %copy-start.114 = (s32[8,4,16]{2,0,1:T(8,128)S(1)}, s32[8,4,16]{2,0,1:T(8,128)}, u32[]{:S(2)}) copy-start(s32[8,4,16]{2,0,1:T(8,128)} %copy.344) | copy-start | bytes 6148
  380.4 42.6 %copy-start.129 = (s32[4]{0:T(128)S(1)}, s32[4]{0:T(128)}, u32[]{:S(2)}) copy-start(s32[4]{0:T(128)} %param.37) | copy-start | bytes 52

commit v4 on v3

--- a/solution.py
+++ b/solution.py
@@ -27,7 +27,8 @@
 
 bf16 = jnp.bfloat16
 f32 = jnp.float32
-BOTH = ("ulysses", "blk")
+BLK, ULY, ALL = "blk", "ulysses", "all"
+SPLIT, WHOLE = "s", "g"
 
 
 def inverse_root(values):
@@ -91,31 +92,20 @@
     )
 
 
-def adam_update(weight_now, first_now, second_now, gradient, rate_value, decay_value, step_float):
-    new_first = beta_first * first_now + (1.0 - beta_first) * gradient
-    new_second = beta_second * second_now + (1.0 - beta_second) * gradient * gradient
-    first_hat = new_first / (1.0 - beta_first**step_float)
-    second_hat = new_second / (1.0 - beta_second**step_float)
-    change = -rate_value * (
-        first_hat / (jnp.sqrt(second_hat) + adam_eps) + decay_value * weight_now
-    )
-    return (change, new_first, new_second)
-
-
 def place_of(axis, blk_count, peer):
-    if axis == "all":
-        return {"ulysses": peer // blk_count, "blk": lax.rem(peer, blk_count)}
+    if axis == ALL:
+        return {ULY: peer // blk_count, BLK: lax.rem(peer, blk_count)}
     return {axis: peer}
 
 
 def rank_of(axis, blk_count):
-    row, column = lax.axis_index("ulysses"), lax.axis_index("blk")
-    return {"ulysses": row, "blk": column, "all": row * blk_count + column}[axis]
+    row, column = lax.axis_index(ULY), lax.axis_index(BLK)
+    return {ULY: row, BLK: column, ALL: row * blk_count + column}[axis]
 
 
 def greet(axes, blk_count, counts):
     barrier = pltpu.get_barrier_semaphore()
-    axes = ("all",) if "all" in axes else tuple(axes)
+    axes = (ALL,) if ALL in axes else tuple(axes)
     total = 0
     for axis in axes:
         me, count = rank_of(axis, blk_count), counts[axis]
@@ -163,7 +153,7 @@
     def copy(self, step):
         peer = lax.rem(self.me + step, self.count)
         return remote(
-            self.source.at[peer] if self.kind == "s" else self.source,
+            self.source.at[peer] if self.kind == SPLIT else self.source,
             self.landing.at[self.me],
             self.send_sems.at[step],
             self.recv_sems.at[step],
@@ -172,7 +162,7 @@
 
     def own(self):
         return pltpu.make_async_copy(
-            self.source.at[self.me] if self.kind == "s" else self.source,
+            self.source.at[self.me] if self.kind == SPLIT else self.source,
             self.landing.at[self.me],
             self.own_sem,
         )
@@ -208,14 +198,15 @@
 
 
 def axis_counts():
-    n_u, n_b = lax.axis_size("ulysses"), lax.axis_size("blk")
-    return {"ulysses": n_u, "blk": n_b, "all": n_u * n_b}
+    n_u, n_b = lax.axis_size(ULY), lax.axis_size(BLK)
+    return {ULY: n_u, BLK: n_b, ALL: n_u * n_b}
 
 
 VMEM = pl.BlockSpec(memory_space=pltpu.VMEM)
 
 
 def remote_call(kernel, collective_id, shapes, scratch, arrays, name):
+    few = lax.axis_size(ULY) * lax.axis_size(BLK) <= 32
     return pl.pallas_call(
         kernel,
         out_shape=shapes,
@@ -225,7 +216,7 @@
         compiler_params=pltpu.CompilerParams(
             collective_id=collective_id,
             has_side_effects=True,
-            vmem_limit_bytes=56 * 1024 * 1024,
+            vmem_limit_bytes=(40 if few else 57) * 1024 * 1024,
         ),
         name=name,
     )(*arrays)
@@ -243,7 +234,7 @@
         counts = axis_counts()
         shapes = [
             jax.ShapeDtypeStruct(
-                array.shape if kind == "s" else (counts[axis],) + array.shape, array.dtype
+                array.shape if kind == SPLIT else (counts[axis],) + array.shape, array.dtype
             )
             for (axis, kind), array in zip(plan, arrays)
         ]
@@ -253,7 +244,7 @@
         if collective_id is None:
             collective_id = self.next_id()
         return remote_call(
-            functools.partial(exchange_kernel, plan, counts["blk"], counts),
+            functools.partial(exchange_kernel, plan, counts[BLK], counts),
             collective_id,
             shapes,
             scratch,
@@ -286,14 +277,14 @@
     core_recv,
     *part_sems,
 ):
-    u, b = lax.axis_index("ulysses"), lax.axis_index("blk")
+    u, b = lax.axis_index(ULY), lax.axis_index(BLK)
     n_u, n_z = kv_out.shape[0], kv_out.shape[1]
     z, c = b // 2, lax.rem(b, 2)
-    greet({"ulysses", "blk"}, blk_count, counts)
-    rows = Part("ulysses", "s", rows_in, rows_out, *part_sems[0:3], blk_count)
-    first_q = Part("blk", "s", q_in, q_split, *part_sems[3:6], blk_count)
-    then_q = Part("ulysses", "g", q_split, q_out, *part_sems[6:9], blk_count)
-    split_ff = Part("blk", "s", ff_in, ff_out, *part_sems[9:12], blk_count)
+    greet({ULY, BLK}, blk_count, counts)
+    rows = Part(ULY, SPLIT, rows_in, rows_out, *part_sems[0:3], blk_count)
+    first_q = Part(BLK, SPLIT, q_in, q_split, *part_sems[3:6], blk_count)
+    then_q = Part(ULY, WHOLE, q_split, q_out, *part_sems[6:9], blk_count)
+    split_ff = Part(BLK, SPLIT, ff_in, ff_out, *part_sems[9:12], blk_count)
 
     def along_z(step):
         mine = kv_out.at[u, z, c]
@@ -302,7 +293,7 @@
             mine,
             z_send.at[step],
             z_recv.at[step],
-            {"blk": lax.rem(z + step, n_z) * 2 + c},
+            {BLK: lax.rem(z + step, n_z) * 2 + c},
         )
 
     def own_copy():
@@ -318,7 +309,7 @@
             place,
             xy_send.at[hop, step],
             xy_recv.at[hop, step],
-            {"ulysses": lax.rem(u + hop, n_u)},
+            {ULY: lax.rem(u + hop, n_u)},
         )
 
     def to_core(hop, step):
@@ -328,7 +319,7 @@
             place,
             core_send.at[hop, step],
             core_recv.at[hop, step],
-            {"blk": z * 2 + 1 - c},
+            {BLK: z * 2 + 1 - c},
         )
 
     own_copy().start()
@@ -367,7 +358,7 @@
 
 def start_call(exchange, rows, kv_low, q_cols, ff_cols):
     counts = axis_counts()
-    n_u, n_b = counts["ulysses"], counts["blk"]
+    n_u, n_b = counts[ULY], counts[BLK]
     n_z = n_b // 2
     dma = pltpu.SemaphoreType.DMA
     return remote_call(
@@ -426,15 +417,15 @@
     z_recv,
     *part_sems,
 ):
-    u, b = lax.axis_index("ulysses"), lax.axis_index("blk")
+    u, b = lax.axis_index(ULY), lax.axis_index(BLK)
     n_u, n_z = kv_in.shape[0], kv_in.shape[1]
     z, c = b // 2, lax.rem(b, 2)
-    greet({"all"}, blk_count, counts)
-    rows = Part("ulysses", "s", rows_in, rows_out, *part_sems[0:3], blk_count)
-    first_q = Part("ulysses", "s", q_in, q_got, *part_sems[3:6], blk_count)
-    then_q = Part("blk", "s", q_sum, q_out, *part_sems[6:9], blk_count)
-    gains = Part("all", "s", gains_in, gains_out, *part_sems[9:12], blk_count)
-    split_ff = Part("blk", "s", ff_in, ff_out, *part_sems[12:15], blk_count)
+    greet({ALL}, blk_count, counts)
+    rows = Part(ULY, SPLIT, rows_in, rows_out, *part_sems[0:3], blk_count)
+    first_q = Part(ULY, SPLIT, q_in, q_got, *part_sems[3:6], blk_count)
+    then_q = Part(BLK, SPLIT, q_sum, q_out, *part_sems[6:9], blk_count)
+    gains = Part(ALL, SPLIT, gains_in, gains_out, *part_sems[9:12], blk_count)
+    split_ff = Part(BLK, SPLIT, ff_in, ff_out, *part_sems[12:15], blk_count)
 
     def place(hop, step):
         return (lax.rem(u + hop, n_u), lax.rem(z + step, n_z))
@@ -446,7 +437,7 @@
             kv_core.at[hop, step],
             core_send.at[hop, step],
             core_recv.at[hop, step],
-            {"blk": z * 2 + 1 - c},
+            {BLK: z * 2 + 1 - c},
         )
 
     def across(hop, step):
@@ -455,7 +446,7 @@
             kv_cross.at[hop, step],
             xy_send.at[hop, step],
             xy_recv.at[hop, step],
-            {"ulysses": lax.rem(u + hop, n_u)},
+            {ULY: lax.rem(u + hop, n_u)},
         )
 
     def along_z(step):
@@ -464,7 +455,7 @@
             kv_line.at[step],
             z_send.at[step],
             z_recv.at[step],
-            {"blk": lax.rem(z + step, n_z) * 2 + c},
+            {BLK: lax.rem(z + step, n_z) * 2 + c},
         )
 
     each(n_z, lambda step: each(n_u, lambda hop: to_core(hop, step).start()))
@@ -522,7 +513,7 @@
 
 def settle_call(exchange, kv_grad, rows, q_grad, ff_grad, gains):
     counts = axis_counts()
-    n_u, n_b = counts["ulysses"], counts["blk"]
+    n_u, n_b = counts[ULY], counts[BLK]
     n_z = n_b // 2
     block = kv_grad.shape[3:]
     dma = pltpu.SemaphoreType.DMA
@@ -596,8 +587,8 @@
         ins, refs = refs[:n_in], refs[n_in:]
         results, refs = refs[:n_out], refs[n_out:]
         kept, sem_refs = refs[:n_scratch], refs[n_scratch:]
-        greet({axis for axis, _ in plan}, counts["blk"], counts)
-        body(Links(plan, counts["blk"], sem_refs), ins, results, kept)
+        greet({axis for axis, _ in plan}, counts[BLK], counts)
+        body(Links(plan, counts[BLK], sem_refs), ins, results, kept)
 
     return remote_call(
         kernel,
@@ -667,7 +658,7 @@
     picks = after_out.shape[0]
     out_cut = attended_out.shape[1] // n_u
     heads_row = QUERY_HEADS // n_u
-    cut_head = (lax.axis_index("blk") * out_cut) // HEAD_WIDTH
+    cut_head = (lax.axis_index(BLK) * out_cut) // HEAD_WIDTH
     sent = links(0, part_send, part_got)
     links.now(1, stats, stats_all)
     full_max = stats_all[0, :QUERY_HEADS]
@@ -764,7 +755,7 @@
     ) = scratch
     picks = after_mlp.shape[0]
     slot_picks = n_b * picks
-    b = lax.axis_index("blk")
+    b = lax.axis_index(BLK)
     factors[...] = jnp.zeros_like(factors)
     first = links(0, head_rows, rows_got)
     links.now(1, head_stats, stats_got)
@@ -939,9 +930,12 @@
         sem_refs = refs[len(names) :]
         for key, ref in zip(extra, sem_refs[3 * len(plan) :]):
             setattr(s, key, ref)
-        base = Links(list(plan.values()), counts["blk"], sem_refs)
-        greet({axis for axis, _ in plan.values()}, counts["blk"], counts)
-        body(r, lambda key, source, landing: base(order[key], source, landing), s)
+        base = Links(list(plan.values()), counts[BLK], sem_refs)
+        links = Named()
+        for key in plan:
+            setattr(links, key, functools.partial(base, order[key]))
+        greet({axis for axis, _ in plan.values()}, counts[BLK], counts)
+        body(r, links, s)
 
     results = remote_call(
         kernel,
@@ -967,18 +961,18 @@
 
 
 def begin_body(n_u, n_b, row_share, slots, r, links, s):
-    u, b = lax.axis_index("ulysses"), lax.axis_index("blk")
+    u, b = lax.axis_index(ULY), lax.axis_index(BLK)
     me = u * n_b + b
     block_len, picks = r.tokens.shape[1], r.picked.shape[1]
     places = n_u * slots
     gathers = [
-        links("tokens", r.tokens, r.tokens_all),
-        links("targets", r.targets, r.targets_all),
-        links("picked", r.picked, r.picked_all),
-        links("advantages", r.advantages, r.advantages_all),
+        links.tokens(r.tokens, r.tokens_all),
+        links.targets(r.targets, r.targets_all),
+        links.picked(r.picked, r.picked_all),
+        links.advantages(r.advantages, r.advantages_all),
     ]
-    links("near", r.scales, r.near).finish()
-    far = links("far", r.near, r.far)
+    links.near(r.scales, r.near).finish()
+    far = links.far(r.near, r.far)
     for part in gathers:
         part.finish()
 
@@ -1067,10 +1061,19 @@
 
 
 def totals_body(r, links, s):
-    links("near", r.mine, r.near_all).finish()
-    r.near[...] = sum_blocks(r.near_all)
-    links("far", r.near, r.far_all).finish()
-    r.total[...] = sum_blocks(r.far_all)
+    lane = lax.broadcasted_iota(jnp.int32, (1, 128), 1)
+    squares = r.tails[0:1, 0:1] + jnp.sum(r.table_squares[...], axis=1, keepdims=True)
+    row = jnp.where(lane == 0, squares, 0.0)
+    row = jnp.where(lane == 1, r.counts[0:1, :], row)
+    r.mine[...] = jnp.where(lane == 2, r.tails[1:2, 0:1], row)
+    links.near(r.mine, r.all).finish()
+    total = sum_blocks(r.all)
+    count = total[:, 1:2]
+    norm = jnp.sqrt(total[:, 0:1]) / count
+    factor = jnp.minimum(1.0, clip_limit / norm) / count
+    row = jnp.where(lane == 0, factor, r.steps[...])
+    row = jnp.where(lane == 3, total[:, 2:3] / count, row)
+    r.numbers[...] = jnp.where(lane == 4, norm, row)
 
 
 def head_of(ref, head):
@@ -1104,7 +1107,7 @@
 
 
 def rise_body(n_u, n_b, r, links, s):
-    u, b = lax.axis_index("ulysses"), lax.axis_index("blk")
+    u, b = lax.axis_index(ULY), lax.axis_index(BLK)
     n_z = n_b // 2
     z, c = b // 2, lax.rem(b, 2)
     score_scale = HEAD_WIDTH ** (-0.5)
@@ -1115,7 +1118,7 @@
             r.kv_weight.at[u, z, c],
             s.z_send.at[step],
             s.z_recv.at[step],
-            {"blk": lax.rem(z + step, n_z) * 2 + c},
+            {BLK: lax.rem(z + step, n_z) * 2 + c},
         )
 
     def own_copy():
@@ -1131,7 +1134,7 @@
             place,
             s.xy_send.at[hop, step],
             s.xy_recv.at[hop, step],
-            {"ulysses": lax.rem(u + hop, n_u)},
+            {ULY: lax.rem(u + hop, n_u)},
         )
 
     def to_core(hop, step):
@@ -1141,25 +1144,25 @@
             place,
             s.core_send.at[hop, step],
             s.core_recv.at[hop, step],
-            {"blk": z * 2 + 1 - c},
+            {BLK: z * 2 + 1 - c},
         )
 
     places = r.key_raw.shape[0]
     half = KEY_VALUE_HEADS * HEAD_WIDTH
     r.kv_in[...] = r.inflow[:, QUERY_WIDTH:].astype(bf16)
     own_copy().start()
-    rows = links("rows", r.rows_in, r.arrived)
+    rows = links.rows(r.rows_in, r.arrived)
     each(n_z, lambda step: along_z(step).start(), 1)
     q_share = r.q_in.shape[2]
     for k in range(n_b):
         r.q_in[k] = r.inflow[:, k * q_share : (k + 1) * q_share].astype(bf16)
-    q_split = links("q_split", r.q_in, r.q_part)
+    q_split = links.q_split(r.q_in, r.q_part)
     own_copy().wait()
     each(n_u, lambda hop: across(hop, 0).start(), 1)
     to_core(0, 0).start()
     for k, there, here in ff_cuts(n_u, n_b):
         r.ff_in[k, :, there] = r.expand[:, here].astype(bf16)
-    ff_split = links("ff_split", r.ff_in, r.ff_part)
+    ff_split = links.ff_split(r.ff_in, r.ff_part)
     r.out_in[...] = r.outflow[...].astype(bf16)
     r.down_in[...] = r.contract[...].astype(bf16)
     rows.finish()
@@ -1174,7 +1177,7 @@
     r.pick_send[:, :, MODEL_WIDTH:] = (
         mm_outer(target_hot, arrived).astype(bf16).reshape(r.normed_slot.shape)
     )
-    picked = links("picks", r.pick_send, r.pick_got)
+    picked = links.picks(r.pick_send, r.pick_got)
 
     def pass_on(step):
         along_z(step).wait_recv()
@@ -1183,7 +1186,7 @@
 
     each(n_z, pass_on, 1)
     q_split.finish()
-    q_all = links("q_all", r.q_part, r.q_weight)
+    q_all = links.q_all(r.q_part, r.q_weight)
     wide = arrived.astype(f32)
     r.normed_keys[...] = (wide * inverse_root(wide) * r.gain_attn[...]).astype(bf16)
     picked.finish()
@@ -1191,7 +1194,7 @@
     r.pick_rows[...] = pick_rows
     mine = pick_rows[:, :MODEL_WIDTH]
     r.normed_mine[...] = (mine * inverse_root(mine) * r.gain_attn[...]).astype(bf16)
-    links("normed", r.normed_mine, r.normed_slot).finish()
+    links.normed(r.normed_mine, r.normed_slot).finish()
     q_all.finish()
     raw = mm(flat_rows_of(r.normed_slot), r.q_weight[...].reshape(MODEL_WIDTH, -1))
     r.query_raw[...] = raw
@@ -1201,7 +1204,7 @@
         r.query_mine[:, part] = turned(
             head * inverse_root(head) * r.gain_query[...], r.rope_cos[places:], r.rope_sin[places:]
         ).astype(bf16)
-    queries = links("queries", r.query_mine, r.query_all)
+    queries = links.queries(r.query_mine, r.query_all)
 
     def share(step):
         def one(hop):
@@ -1211,10 +1214,10 @@
         each(n_u, one, 1)
 
     each(n_z, share)
-    out_all = links("out_all", r.out_in, r.out_weight)
+    out_all = links.out_all(r.out_in, r.out_weight)
     ff_split.finish()
-    ff_all = links("ff_all", r.ff_part, r.ff_weight)
-    down_all = links("down_all", r.down_in, r.down_weight)
+    ff_all = links.ff_all(r.ff_part, r.ff_weight)
+    down_all = links.down_all(r.down_in, r.down_weight)
     each(n_z, lambda step: each(n_u, lambda hop: to_core(hop, step).wait_recv()))
 
     wide_head = 2 * HEAD_WIDTH
@@ -1263,8 +1266,8 @@
     out_cut = r.attended.shape[1] // n_u
     heads_row = QUERY_HEADS // n_u
     cut_head = (b * out_cut) // HEAD_WIDTH
-    sent = links("parts", r.part_send, r.part_got)
-    links("stats", r.stats, r.stats_all).finish()
+    sent = links.parts(r.part_send, r.part_got)
+    links.stats(r.stats, r.stats_all).finish()
     full_max = r.stats_all[0, :QUERY_HEADS]
     for k in range(1, n_b):
         full_max = jnp.maximum(full_max, r.stats_all[k, :QUERY_HEADS])
@@ -1291,18 +1294,18 @@
     r.attended[...] = attended
     out_all.finish()
 
-    def to_picks(key, rows):
+    def to_picks(which, send, rows):
         r.partial[...] = rows.astype(bf16).reshape(r.partial.shape)
-        landing = r.partial_got.at[0 if key == "sum_out" else 1]
-        links(key, r.partial, landing).finish()
+        landing = r.partial_got.at[which]
+        send(r.partial, landing).finish()
         return sum_blocks(landing)
 
     after_attn = r.pick_rows[:, :MODEL_WIDTH] + to_picks(
-        "sum_out", mm(attended.astype(bf16), flat_rows_of(r.out_weight))
+        0, links.sum_out, mm(attended.astype(bf16), flat_rows_of(r.out_weight))
     )
     r.after_attn[...] = after_attn
     r.normed_mine[...] = (after_attn * inverse_root(after_attn) * r.gain_mlp[...]).astype(bf16)
-    links("normed_mlp", r.normed_mine, r.normed_mlp).finish()
+    links.normed_mlp(r.normed_mine, r.normed_mlp).finish()
     ff_all.finish()
     gate_up = mm(flat_rows_of(r.normed_mlp), r.ff_weight[...].reshape(MODEL_WIDTH, -1))
     r.gate_up[...] = gate_up
@@ -1310,26 +1313,26 @@
     gate_part, up_part = gate_up[:, :half], gate_up[:, half:]
     activated = (gate_part * jax.nn.sigmoid(gate_part) * up_part).astype(bf16)
     down_all.finish()
-    after_mlp = after_attn + to_picks("sum_mlp", mm(activated, flat_rows_of(r.down_weight)))
+    after_mlp = after_attn + to_picks(1, links.sum_mlp, mm(activated, flat_rows_of(r.down_weight)))
     r.after_mlp[...] = after_mlp
     r.final_mine[...] = (after_mlp * inverse_root(after_mlp) * r.gain_final[...]).astype(bf16)
-    links("final", r.final_mine, r.final_slot).finish()
-    links("final_all", r.final_slot, r.final_all).finish()
+    links.final(r.final_mine, r.final_slot).finish()
+    links.final_all(r.final_slot, r.final_all).finish()
     each(n_z, lambda step: along_z(step).wait_send(), 1)
     each(n_z, lambda step: each(n_u, lambda hop: across(hop, step).wait_send(), 1))
     each(n_z, lambda step: each(n_u, lambda hop: to_core(hop, step).wait_send()))
 
 
 def fall_body(n_u, n_b, r, links, s):
-    u, b = lax.axis_index("ulysses"), lax.axis_index("blk")
+    u, b = lax.axis_index(ULY), lax.axis_index(BLK)
     n_z = n_b // 2
     z, c = b // 2, lax.rem(b, 2)
     score_scale = HEAD_WIDTH ** (-0.5)
     picks = r.after_mlp.shape[0]
     places = r.key_raw.shape[0]
     r.factors[...] = jnp.zeros_like(r.factors)
-    head_rows = links("head_rows", r.head_rows, r.rows_got)
-    links("head_stats", r.head_stats, r.stats_got).finish()
+    head_rows = links.head_rows(r.head_rows, r.rows_got)
+    links.head_stats(r.head_stats, r.stats_got).finish()
     tops = r.stats_got[0, 0:1, :]
     for k in range(1, n_u):
         tops = jnp.maximum(tops, r.stats_got[k, 0:1, :])
@@ -1341,14 +1344,14 @@
     r.slot_stats[...] = jnp.zeros_like(r.slot_stats)
     r.slot_stats[0:1, :] = tops
     r.slot_stats[1:2, :] = total
-    slot_part = links("slot_stats", r.slot_stats, r.slot_got)
+    slot_part = links.slot_stats(r.slot_stats, r.slot_got)
     by_row = r.factors[...].T
     head_rows.finish()
     rows = r.rows_got[0].astype(f32) * by_row[:, 0:1]
     for k in range(1, n_u):
         rows += r.rows_got[k].astype(f32) * by_row[:, k : k + 1]
     r.partial[...] = rows.astype(bf16).reshape(r.partial.shape)
-    back = links("slot_rows", r.partial, r.partial_got.at[0])
+    back = links.slot_rows(r.partial, r.partial_got.at[0])
     slot_part.finish()
     tops = r.slot_got[0, 0:1, :]
     for k in range(1, n_b):
@@ -1363,7 +1366,7 @@
         r.factors[k : k + 1, :] = r.factors[k : k + 1, :] / total
     r.factors[n_b : n_b + 1, :] = log_norm
     r.norms_mine[...] = jnp.broadcast_to(log_norm, r.norms_mine.shape)
-    norms_part = links("norms", r.norms_mine, r.norms_all)
+    norms_part = links.norms(r.norms_mine, r.norms_all)
     r.columns[...] = r.factors[...].T
     mine = r.columns[pl.ds(pl.multiple_of(b * picks, picks), picks), :]
     back.finish()
@@ -1378,7 +1381,7 @@
     r.terms[...] = r.weights[...] * (target_logit - mine[:, n_b : n_b + 1])
     grad_mlp, gain_final = norm_back_rows(r.after_mlp[...], r.gain_final[...], grad_final)
     r.mine_low[...] = grad_mlp.astype(bf16)
-    links("branch", r.mine_low, r.grad_all).finish()
+    links.branch(r.mine_low, r.grad_all).finish()
     branch = flat_rows_of(r.grad_all)
     gate_up = r.gate_up[...]
     half = gate_up.shape[1] // 2
@@ -1393,25 +1396,25 @@
         .astype(bf16)
         .reshape(r.partial.shape)
     )
-    back = links("sum_ff", r.partial, r.partial_got.at[1])
+    back = links.sum_ff(r.partial, r.partial_got.at[1])
     activated = (gate_part * sigmoid_gate * up_part).astype(bf16)
     r.grad_down[...] = mm_outer(activated, branch).astype(bf16).reshape(r.grad_down.shape)
-    down_part = links("down", r.grad_down, r.down_got)
+    down_part = links.down(r.grad_down, r.down_got)
     r.grad_ff[...] = (
         mm_outer(flat_rows_of(r.normed_mlp), grad_gate_up).astype(bf16).reshape(r.grad_ff.shape)
     )
-    ff_part = links("ff", r.grad_ff, r.ff_got)
+    ff_part = links.ff(r.grad_ff, r.ff_got)
     back.finish()
     grad_mid, gain_mlp = norm_back_rows(
         r.after_attn[...], r.gain_mlp[...], sum_blocks(r.partial_got.at[1])
     )
     grad_attn = grad_mlp + grad_mid
     r.mine_low[...] = grad_attn.astype(bf16)
-    links("branch_attn", r.mine_low, r.branch_all).finish()
+    links.branch_attn(r.mine_low, r.branch_all).finish()
     branch = flat_rows_of(r.branch_all)
     grad_low = mm_back(branch, flat_rows_of(r.out_weight)).astype(bf16)
     r.attended_mine[...] = grad_low
-    last = links("attended", r.attended_mine, r.attended_all)
+    last = links.attended(r.attended_mine, r.attended_all)
     out_cut = r.attended.shape[1] // n_u
     product = r.attended[...] * grad_low.astype(f32)
     group = lax.broadcasted_iota(jnp.int32, product.shape, 1) // out_cut
@@ -1422,11 +1425,11 @@
         sums = jnp.where(lane == row, one, sums)
     r.deltas[...] = sums
     r.delta_mine[...] = r.deltas[...].T[:8, :]
-    delta_part = links("deltas", r.delta_mine, r.delta_all)
+    delta_part = links.deltas(r.delta_mine, r.delta_all)
     r.grad_out[...] = (
         mm_outer(r.attended[...].astype(bf16), branch).astype(bf16).reshape(r.grad_out.shape)
     )
-    out_part = links("out", r.grad_out, r.out_got)
+    out_part = links.out(r.grad_out, r.out_got)
     wide = flat_rows_of(r.arrived).astype(f32)
     r.normed_keys[...] = (wide * inverse_root(wide) * r.gain_attn[...]).astype(bf16)
     last.finish()
@@ -1467,7 +1470,7 @@
         r.grad_kv[:, width + kv_head * HEAD_WIDTH : width + (kv_head + 1) * HEAD_WIDTH] = (
             grad_value.astype(bf16)
         )
-    query_part = links("grad_queries", r.query_send, r.query_got)
+    query_part = links.grad_queries(r.query_send, r.query_got)
 
     def place(hop, step):
         return (lax.rem(u + hop, n_u), lax.rem(z + step, n_z))
@@ -1479,7 +1482,7 @@
             r.kv_core.at[hop, step],
             s.core_send.at[hop, step],
             s.core_recv.at[hop, step],
-            {"blk": z * 2 + 1 - c},
+            {BLK: z * 2 + 1 - c},
         )
 
     def across(hop, step):
@@ -1488,7 +1491,7 @@
             r.kv_cross.at[hop, step],
             s.xy_send.at[hop, step],
             s.xy_recv.at[hop, step],
-            {"ulysses": lax.rem(u + hop, n_u)},
+            {ULY: lax.rem(u + hop, n_u)},
         )
 
     def along_z(step):
@@ -1497,7 +1500,7 @@
             r.kv_line.at[step],
             s.z_send.at[step],
             s.z_recv.at[step],
-            {"blk": lax.rem(z + step, n_z) * 2 + c},
+            {BLK: lax.rem(z + step, n_z) * 2 + c},
         )
 
     block_rows = MODEL_WIDTH // n_u
@@ -1531,7 +1534,7 @@
         .astype(bf16)
         .reshape(r.partial.shape)
     )
-    back = links("sum_query", r.partial, r.partial_got.at[2])
+    back = links.sum_query(r.partial, r.partial_got.at[2])
 
     def add_pair(hop):
         def one(step):
@@ -1555,13 +1558,13 @@
     r.grad_q[...] = (
         mm_outer(flat_rows_of(r.normed_slot), r.grad_low[...]).astype(bf16).reshape(r.grad_q.shape)
     )
-    q_part = links("q", r.grad_q, r.q_got)
+    q_part = links.q(r.grad_q, r.q_got)
     back.finish()
     grad_mine, gain_attn = norm_back_rows(
         r.pick_rows[:, :MODEL_WIDTH], r.gain_attn[...], sum_blocks(r.partial_got.at[2])
     )
     r.mine_low[...] = (grad_attn + grad_mine).astype(bf16)
-    pick_part = links("pick_back", r.mine_low, r.pick_back)
+    pick_part = links.pick_back(r.mine_low, r.pick_back)
 
     def row_grad(k):
         columns = pl.ds(pl.multiple_of(k * block_rows, block_rows), block_rows)
@@ -1578,7 +1581,7 @@
         .astype(bf16)
         .reshape(r.rows_send.shape)
     )
-    rows_part = links("rows", r.rows_send, r.rows_back)
+    rows_part = links.rows(r.rows_send, r.rows_back)
 
     r.gain_mlp_row[...] = gain_mlp
     r.gain_final_row[...] = gain_final
@@ -1593,21 +1596,21 @@
         r.gains_mine[2 * lines + j : 2 * lines + j + 1, :] = r.gain_final_row[:, part]
     r.gains_mine[3 * lines : 3 * lines + 1, :] = r.gain_query_row[...]
     r.gains_mine[3 * lines + 1 : 3 * lines + 2, :] = r.gain_key_row[...]
-    gains_part = links("gains_blk", r.gains_mine, r.gains_got)
+    gains_part = links.gains_blk(r.gains_mine, r.gains_got)
 
     ff_part.finish()
     r.ff_sum[...] = sum_blocks(r.ff_got).astype(bf16)
-    ff_last = links("ff_cols", r.ff_sum, r.ff_out)
+    ff_last = links.ff_cols(r.ff_sum, r.ff_out)
     down_part.finish()
     r.down_out[...] = sum_blocks(r.down_got)
     out_part.finish()
     r.out_out[...] = sum_blocks(r.out_got)
     gains_part.finish()
     r.gains_slot[...] = sum_blocks(r.gains_got)
-    gains_last = links("gains_ulysses", r.gains_slot, r.gains_all)
+    gains_last = links.gains_ulysses(r.gains_slot, r.gains_all)
     q_part.finish()
     r.q_sum[...] = sum_blocks(r.q_got).astype(bf16)
-    q_last = links("q_cols", r.q_sum, r.q_out)
+    q_last = links.q_cols(r.q_sum, r.q_out)
 
     def plane_sum(step):
         total = r.kv_core[0, step].astype(f32)
@@ -1628,7 +1631,6 @@
     r.inflow_out[:, QUERY_WIDTH:] = total
     gains_last.finish()
     gains = sum_blocks(r.gains_all)
-    r.gains_out[...] = gains
     for part in (norms_part, ff_last, q_last, rows_part):
         part.finish()
     q_share = r.q_out.shape[2]
@@ -1639,7 +1641,20 @@
     squares = jnp.sum(gains * gains) / (n_u * n_b)
     for ref in (r.inflow_out, r.expand_out, r.out_out, r.down_out):
         squares += jnp.sum(ref[...] * ref[...])
-    r.squares[...] = jnp.full(r.squares.shape, squares, f32)
+    r.tails[...] = jnp.zeros_like(r.tails)
+    r.tails[0:1, :] = jnp.full((1, 128), squares, f32)
+    r.tails[1:2, :] = jnp.full((1, 128), -jnp.sum(r.terms[:, 0:1]), f32)
+    for row in range(n_u):
+        at = slice(row * n_b * picks, (row + 1) * n_b * picks)
+        r.norms_row[:, at] = r.norms_all[row, 0:1, :]
+    for k in range(gains.shape[0] - 6):
+        r.gains_line[:, k * 128 : (k + 1) * 128] = gains[k : k + 1, :]
+    share = r.gains_out.shape[1]
+    me = u * n_b + b
+    own = jnp.zeros((1, share), f32)
+    for k in range(n_u * n_b):
+        own = jnp.where(me == k, r.gains_line[:, k * share : (k + 1) * share], own)
+    r.gains_out[...] = own
     each(n_z, lambda step: each(n_u, lambda hop: to_core(hop, step).wait_send()))
     each(n_z, lambda step: each(n_u, lambda hop: across(hop, step).wait_send(), 1))
     each(n_z, lambda step: along_z(step).wait_send(), 1)
@@ -1694,8 +1709,73 @@
     )(fills, ids, table)
 
 
-def table_tile(share):
-    return -(-share // (9 * 16)) * 16
+def table_tile(share, count=9):
+    return -(-share // (count * 16)) * 16
+
+
+def head_kernel(share, finals, table, logits, rows, stats, mixed, top, total):
+    tile = table.shape[0]
+    step = pl.program_id(0)
+    known = step * tile + lax.broadcasted_iota(jnp.int32, (tile, 1), 0) < share
+    low = jnp.where(known, table[...], 0.0).astype(bf16)
+    scores = mm_back(low, finals[...])
+    logits[...] = scores
+    scores = jnp.where(known, scores, masked_score)
+
+    @pl.when(step == 0)
+    def _():
+        top[...] = jnp.full(top.shape, masked_score, f32)
+        total[...] = jnp.zeros_like(total)
+        mixed[...] = jnp.zeros_like(mixed)
+
+    new_top = jnp.maximum(top[...], jnp.max(scores, axis=0, keepdims=True))
+    shrink = jnp.exp(top[...] - new_top)
+    weights = jnp.exp(scores - new_top)
+    top[...] = new_top
+    total[...] = total[...] * shrink + jnp.sum(weights, axis=0, keepdims=True)
+    mixed[...] = mixed[...] * shrink + mm_outer(low, weights.astype(bf16))
+
+    @pl.when(step == pl.num_programs(0) - 1)
+    def _():
+        rows[...] = mixed[...].T.astype(bf16)
+        stats[...] = jnp.zeros_like(stats)
+        width = stats.shape[2]
+        for k in range(stats.shape[0]):
+            at = slice(k * width, (k + 1) * width)
+            stats[k, 0:1, :] = top[:, at]
+            stats[k, 1:2, :] = total[:, at]
+
+
+def head_call(finals, table, n_u):
+    share, width = table.shape
+    picks = finals.shape[0]
+    tile = table_tile(share, 6)
+    stats = (n_u, 8, picks // n_u)
+    return pl.pallas_call(
+        functools.partial(head_kernel, share),
+        grid=(pl.cdiv(share, tile),),
+        out_shape=[
+            jax.ShapeDtypeStruct((share, picks), f32),
+            jax.ShapeDtypeStruct((picks, width), bf16),
+            jax.ShapeDtypeStruct(stats, f32),
+        ],
+        in_specs=[
+            pl.BlockSpec((picks, width), lambda i: (0, 0)),
+            pl.BlockSpec((tile, width), lambda i: (i, 0)),
+        ],
+        out_specs=[
+            pl.BlockSpec((tile, picks), lambda i: (i, 0)),
+            pl.BlockSpec((picks, width), lambda i: (0, 0)),
+            pl.BlockSpec(stats, lambda i: (0, 0, 0)),
+        ],
+        scratch_shapes=[
+            pltpu.VMEM((width, picks), f32),
+            pltpu.VMEM((1, picks), f32),
+            pltpu.VMEM((1, picks), f32),
+        ],
+        compiler_params=pltpu.CompilerParams(vmem_limit_bytes=44 * 1024 * 1024),
+        name="head",
+    )(finals, table)
 
 
 def table_grad_kernel(
@@ -1744,7 +1824,7 @@
             pl.BlockSpec((tile, width), lambda i: (i, 0)),
             whole(1, width),
         ],
-        compiler_params=pltpu.CompilerParams(vmem_limit_bytes=40 * 1024 * 1024),
+        compiler_params=pltpu.CompilerParams(vmem_limit_bytes=60 * 1024 * 1024),
         cost_estimate=pl.CostEstimate(
             flops=2 * share * width * (picks + places),
             bytes_accessed=share * (4 * picks + 2 * width),
@@ -1755,13 +1835,14 @@
 
 
 def adam_kernel(rate, decay, numbers, weight, first, second, grad, change, new_first, new_second):
-    gradient = grad[...].astype(f32) * numbers[0]
+    gradient = grad[...].astype(f32) * numbers[:, 0:1]
     mean = beta_first * first[...] + (1.0 - beta_first) * gradient
     square = beta_second * second[...] + (1.0 - beta_second) * gradient * gradient
     new_first[...] = mean
     new_second[...] = square
     change[...] = -rate * (
-        mean * numbers[1] / (jnp.sqrt(square * numbers[2]) + adam_eps) + decay * weight[...]
+        mean * numbers[:, 1:2] / (jnp.sqrt(square * numbers[:, 2:3]) + adam_eps)
+        + decay * weight[...]
     )
 
 
@@ -1779,7 +1860,7 @@
         out_shape=[
             jax.ShapeDtypeStruct(group[0].shape, f32) for group in groups for _ in range(3)
         ],
-        in_specs=[pl.BlockSpec(memory_space=pltpu.SMEM)] + [VMEM] * len(arrays),
+        in_specs=[VMEM] * (1 + len(arrays)),
         out_specs=[VMEM] * (3 * len(groups)),
         compiler_params=pltpu.CompilerParams(vmem_limit_bytes=32 * 1024 * 1024),
         name="layer_adam",
@@ -1794,9 +1875,9 @@
         functools.partial(adam_kernel, rate, decay),
         grid=(pl.cdiv(share, tile),),
         out_shape=[jax.ShapeDtypeStruct((share, width), f32)] * 3,
-        in_specs=[pl.BlockSpec(memory_space=pltpu.SMEM)] + [block] * 4,
+        in_specs=[pl.BlockSpec((1, 128), lambda i: (0, 0))] + [block] * 4,
         out_specs=[block] * 3,
-        compiler_params=pltpu.CompilerParams(vmem_limit_bytes=48 * 1024 * 1024),
+        compiler_params=pltpu.CompilerParams(vmem_limit_bytes=60 * 1024 * 1024),
         name="adam",
     )(numbers, weight, first, second, grad)
 
@@ -1828,10 +1909,10 @@
     second_scales,
 ):
     exchange = Exchanger()
-    n_u, n_b = lax.axis_size("ulysses"), lax.axis_size("blk")
+    n_u, n_b = lax.axis_size(ULY), lax.axis_size(BLK)
     n_all = n_u * n_b
     n_z = n_b // 2
-    u, b = lax.axis_index("ulysses"), lax.axis_index("blk")
+    u, b = lax.axis_index(ULY), lax.axis_index(BLK)
     me = u * n_b + b
     slot_count, block_len = tokens.shape
     assert slot_count == n_u and n_b % 2 == 0
@@ -1852,62 +1933,65 @@
     wants_mean = n_b * (block_len + picks) / n_all
     slots = -(-int(wants_mean + 5.2 * math.sqrt(wants_mean)) // 16) * 16
     places = n_u * slots
-    blk_g = ("blk", "g")
+    blk_g = (BLK, WHOLE)
     column = ((places, 1), jnp.int32)
     row_wide = ((1, MODEL_WIDTH), f32)
     head_wide = ((1, HEAD_WIDTH), f32)
-    begin = named_call(
-        exchange,
-        functools.partial(begin_body, n_u, n_b, row_share, slots),
-        {
-            "tokens": blk_g,
-            "targets": blk_g,
-            "picked": blk_g,
-            "advantages": blk_g,
-            "near": blk_g,
-            "far": ("ulysses", "g"),
-        },
-        {},
-        {
-            "tokens": tokens,
-            "targets": targets,
-            "picked": picked,
-            "advantages": advantages,
-            "lengths": lengths[:, None],
-            "scales": scales[None, :],
-        },
-        {
-            "tokens_all": ((n_b,) + tokens.shape, jnp.int32),
-            "targets_all": ((n_b,) + targets.shape, jnp.int32),
-            "slot_picked": ((1, slot_picks), jnp.int32),
-            "weights": ((1, all_picks), f32),
-            "target_ids": ((1, all_picks), jnp.int32),
-            "weight_wide": ((picks, 128), f32),
-            "row_ids": column,
-            "key_pos": column,
-            "key_lim": column,
-            "target_of": column,
-            "positions": ((places + slot_picks, 1), jnp.int32),
-            "meta": ((24, 128), f32),
-            "gain_attn": row_wide,
-            "gain_mlp": row_wide,
-            "gain_final": row_wide,
-            "gain_query": head_wide,
-            "gain_key": head_wide,
-        },
-        {
-            "picked_all": ((n_b,) + picked.shape, jnp.int32),
-            "advantages_all": ((n_b,) + advantages.shape, f32),
-            "near": ((n_b, 1, scale_share), f32),
-            "far": ((n_u, n_b, 1, scale_share), f32),
-            "wants": ((n_u, block_len + picks), jnp.int32),
-            "masks": ((2 * n_u, block_len + picks), f32),
-            "labels": ((2 * n_u, block_len + picks), f32),
-            "ranks": ((2 * n_u, block_len + picks), f32),
-            "gains": ((1, n_all * scale_share), f32),
-        },
-        "begin",
-    )
+    def begin_call():
+        return named_call(
+            exchange,
+            functools.partial(begin_body, n_u, n_b, row_share, slots),
+            dict(
+                tokens=blk_g,
+                targets=blk_g,
+                picked=blk_g,
+                advantages=blk_g,
+                near=blk_g,
+                far=(ULY, WHOLE),
+            ),
+            {},
+            dict(
+                tokens=tokens,
+                targets=targets,
+                picked=picked,
+                advantages=advantages,
+                lengths=lengths[:, None],
+                scales=scales[None, :],
+            ),
+            dict(
+                tokens_all=((n_b,) + tokens.shape, jnp.int32),
+                targets_all=((n_b,) + targets.shape, jnp.int32),
+                slot_picked=((1, slot_picks), jnp.int32),
+                weights=((1, all_picks), f32),
+                target_ids=((1, all_picks), jnp.int32),
+                weight_wide=((picks, 128), f32),
+                row_ids=column,
+                key_pos=column,
+                key_lim=column,
+                target_of=column,
+                positions=((places + slot_picks, 1), jnp.int32),
+                meta=((24, 128), f32),
+                gain_attn=row_wide,
+                gain_mlp=row_wide,
+                gain_final=row_wide,
+                gain_query=head_wide,
+                gain_key=head_wide,
+            ),
+            dict(
+                picked_all=((n_b,) + picked.shape, jnp.int32),
+                advantages_all=((n_b,) + advantages.shape, f32),
+                near=((n_b, 1, scale_share), f32),
+                far=((n_u, n_b, 1, scale_share), f32),
+                wants=((n_u, block_len + picks), jnp.int32),
+                masks=((2 * n_u, block_len + picks), f32),
+                labels=((2 * n_u, block_len + picks), f32),
+                ranks=((2 * n_u, block_len + picks), f32),
+                gains=((1, n_all * scale_share), f32),
+            ),
+            "begin",
+        )
+
+    begin = begin_call()
     gain_rows = [
         begin.gain_attn,
         begin.gain_mlp,
@@ -1946,32 +2030,23 @@
         )
 
     def head_of_table(final_all):
-        table_low = embedding.astype(bf16)
-        logits = mm_back(table_low, final_all)
-        local_max = jnp.max(logits, axis=0)
-        head_weights = jnp.exp(logits - local_max[None, :])
-        local_sum = jnp.sum(head_weights, axis=0)
-        head_rows = mm_outer(head_weights.astype(bf16), table_low).astype(bf16)
-        head_stats = jnp.pad(
-            jnp.stack([local_max, local_sum]).reshape(2, n_u, slot_picks).transpose(1, 0, 2),
-            ((0, 0), (0, 6), (0, 0)),
-        )
+        logits, head_rows, head_stats = head_call(final_all, embedding, n_u)
         return (logits, head_rows.reshape(n_u, slot_picks, MODEL_WIDTH), head_stats)
 
     def usual_way():
         fills = jnp.minimum(begin.meta[:n_u, 0].astype(jnp.int32), slots)
-        lined = {
-            "key_pos": begin.key_pos,
-            "key_lim": begin.key_lim,
-            "slot_picked": begin.slot_picked,
-            "gain_attn": gain_rows[0],
-            "gain_mlp": gain_rows[1],
-            "gain_final": gain_rows[2],
-            "gain_query": gain_rows[3],
-            "gain_key": gain_rows[4],
-            "rope_cos": rope_cos,
-            "rope_sin": rope_sin,
-        }
+        lined = dict(
+            key_pos=begin.key_pos,
+            key_lim=begin.key_lim,
+            slot_picked=begin.slot_picked,
+            gain_attn=gain_rows[0],
+            gain_mlp=gain_rows[1],
+            gain_final=gain_rows[2],
+            gain_query=gain_rows[3],
+            gain_key=gain_rows[4],
+            rope_cos=rope_cos,
+            rope_sin=rope_sin,
+        )
         kv_block = (in_rows, 2 * width)
         kv_shape = (n_u, n_z, 2) + kv_block
         q_shape = (n_u, n_b, in_rows, q_share)
@@ -1979,246 +2054,245 @@
         out_shape = (n_u, out_share, MODEL_WIDTH)
         down_shape = (n_u, ff_share, MODEL_WIDTH)
         rows_shape = (n_u, slots, MODEL_WIDTH)
-        blk_s, blk_g = ("blk", "s"), ("blk", "g")
-        uly_s, uly_g = ("ulysses", "s"), ("ulysses", "g")
+        blk_s, blk_g = (BLK, SPLIT), (BLK, WHOLE)
+        uly_s, uly_g = (ULY, SPLIT), (ULY, WHOLE)
         rise = named_call(
             exchange,
             functools.partial(rise_body, n_u, n_b),
-            {
-                "rows": uly_s,
-                "q_split": blk_s,
-                "ff_split": blk_s,
-                "picks": blk_s,
-                "q_all": uly_g,
-                "normed": blk_g,
-                "queries": blk_g,
-                "out_all": uly_g,
-                "ff_all": uly_g,
-                "down_all": uly_g,
-                "parts": blk_s,
-                "stats": blk_g,
-                "sum_out": blk_s,
-                "normed_mlp": blk_g,
-                "sum_mlp": blk_s,
-                "final": blk_g,
-                "final_all": uly_g,
-            },
-            {
-                "z_send": (n_z,),
-                "z_recv": (n_z,),
-                "own": (1,),
-                "xy_send": (n_u, n_z),
-                "xy_recv": (n_u, n_z),
-                "core_send": (n_u, n_z),
-                "core_recv": (n_u, n_z),
-            },
-            {
-                "rows_in": fetch(fills, begin.row_ids.reshape(-1)),
-                "inflow": inflow,
-                "expand": expand,
-                "outflow": outflow,
-                "contract": contract,
-                "target_of": begin.target_of,
+            dict(
+                rows=uly_s,
+                q_split=blk_s,
+                ff_split=blk_s,
+                picks=blk_s,
+                q_all=uly_g,
+                normed=blk_g,
+                queries=blk_g,
+                out_all=uly_g,
+                ff_all=uly_g,
+                down_all=uly_g,
+                parts=blk_s,
+                stats=blk_g,
+                sum_out=blk_s,
+                normed_mlp=blk_g,
+                sum_mlp=blk_s,
+                final=blk_g,
+                final_all=uly_g,
+            ),
+            dict(
+                z_send=(n_z,),
+                z_recv=(n_z,),
+                own=(1,),
+                xy_send=(n_u, n_z),
+                xy_recv=(n_u, n_z),
+                core_send=(n_u, n_z),
+                core_recv=(n_u, n_z),
+            ),
+            dict(
+                rows_in=fetch(fills, begin.row_ids.reshape(-1)),
+                inflow=inflow,
+                expand=expand,
+                outflow=outflow,
+                contract=contract,
+                target_of=begin.target_of,
                 **lined,
-            },
-            {
-                "arrived": (rows_shape, bf16),
-                "kv_weight": (kv_shape, bf16),
-                "q_weight": (q_shape, bf16),
-                "ff_weight": (ff_shape, bf16),
-                "out_weight": (out_shape, bf16),
-                "down_weight": (down_shape, bf16),
-                "pick_rows": ((picks, 2 * MODEL_WIDTH), f32),
-                "normed_slot": (slot_low, bf16),
-                "query_raw": ((slot_picks, q_share), f32),
-                "query_all": ((n_b, slot_picks, q_share), bf16),
-                "key_raw": ((places, width), f32),
-                "key_rot": ((places, width), bf16),
-                "values": ((places, width), bf16),
-                "attended": ((slot_picks, own_cut), f32),
-                "log_total": ((QUERY_HEADS, slot_picks), f32),
-                "after_attn": (rows_low, f32),
-                "normed_mlp": (slot_low, bf16),
-                "gate_up": ((slot_picks, ff_width), f32),
-                "after_mlp": (rows_low, f32),
-                "final_mine": (rows_low, bf16),
-                "final_all": ((n_u,) + slot_low, bf16),
-            },
-            {
-                "kv_in": (kv_block, bf16),
-                "q_in": (q_shape[1:], bf16),
-                "ff_in": (ff_shape[1:], bf16),
-                "out_in": (out_shape[1:], bf16),
-                "down_in": (down_shape[1:], bf16),
-                "q_part": (q_shape[1:], bf16),
-                "ff_part": (ff_shape[1:], bf16),
-                "pick_send": ((n_b, picks, 2 * MODEL_WIDTH), bf16),
-                "pick_got": ((n_b, picks, 2 * MODEL_WIDTH), bf16),
-                "normed_mine": (rows_low, bf16),
-                "normed_keys": ((places, MODEL_WIDTH), bf16),
-                "query_mine": ((slot_picks, q_share), bf16),
-                "part_send": ((n_b, slot_picks, own_cut), bf16),
-                "part_got": ((n_b, slot_picks, own_cut), bf16),
-                "stats": ((2 * QUERY_HEADS, slot_picks), f32),
-                "stats_all": ((n_b, 2 * QUERY_HEADS, slot_picks), f32),
-                "shares": ((n_b * n_u, slot_picks), f32),
-                "partial": (slot_low, bf16),
-                "partial_got": ((2,) + slot_low, bf16),
-                "final_slot": (slot_low, bf16),
-            },
+            ),
+            dict(
+                arrived=(rows_shape, bf16),
+                kv_weight=(kv_shape, bf16),
+                q_weight=(q_shape, bf16),
+                ff_weight=(ff_shape, bf16),
+                out_weight=(out_shape, bf16),
+                down_weight=(down_shape, bf16),
+                pick_rows=((picks, 2 * MODEL_WIDTH), f32),
+                normed_slot=(slot_low, bf16),
+                query_raw=((slot_picks, q_share), f32),
+                query_all=((n_b, slot_picks, q_share), bf16),
+                key_raw=((places, width), f32),
+                key_rot=((places, width), bf16),
+                values=((places, width), bf16),
+                attended=((slot_picks, own_cut), f32),
+                log_total=((QUERY_HEADS, slot_picks), f32),
+                after_attn=(rows_low, f32),
+                normed_mlp=(slot_low, bf16),
+                gate_up=((slot_picks, ff_width), f32),
+                after_mlp=(rows_low, f32),
+                final_mine=(rows_low, bf16),
+                final_all=((n_u,) + slot_low, bf16),
+            ),
+            dict(
+                kv_in=(kv_block, bf16),
+                q_in=(q_shape[1:], bf16),
+                ff_in=(ff_shape[1:], bf16),
+                out_in=(out_shape[1:], bf16),
+                down_in=(down_shape[1:], bf16),
+                q_part=(q_shape[1:], bf16),
+                ff_part=(ff_shape[1:], bf16),
+                pick_send=((n_b, picks, 2 * MODEL_WIDTH), bf16),
+                pick_got=((n_b, picks, 2 * MODEL_WIDTH), bf16),
+                normed_mine=(rows_low, bf16),
+                normed_keys=((places, MODEL_WIDTH), bf16),
+                query_mine=((slot_picks, q_share), bf16),
+                part_send=((n_b, slot_picks, own_cut), bf16),
+                part_got=((n_b, slot_picks, own_cut), bf16),
+                stats=((2 * QUERY_HEADS, slot_picks), f32),
+                stats_all=((n_b, 2 * QUERY_HEADS, slot_picks), f32),
+                shares=((n_b * n_u, slot_picks), f32),
+                partial=(slot_low, bf16),
+                partial_got=((2,) + slot_low, bf16),
+                final_slot=(slot_low, bf16),
+            ),
             "rise",
         )
         final_all = rise.final_all.reshape(all_picks, MODEL_WIDTH)
         logits, head_rows, head_stats = head_of_table(final_all)
-        kept = (
-            "arrived",
-            "kv_weight",
-            "q_weight",
-            "ff_weight",
-            "out_weight",
-            "down_weight",
-            "pick_rows",
-            "normed_slot",
-            "query_raw",
-            "query_all",
-            "key_raw",
-            "key_rot",
-            "values",
-            "attended",
-            "log_total",
-            "after_attn",
-            "normed_mlp",
-            "gate_up",
-            "after_mlp",
-            "final_mine",
-        )
         fall = named_call(
             exchange,
             functools.partial(fall_body, n_u, n_b),
-            {
-                "head_rows": uly_s,
-                "head_stats": uly_s,
-                "slot_stats": blk_g,
-                "slot_rows": blk_s,
-                "norms": uly_g,
-                "branch": blk_g,
-                "sum_ff": blk_s,
-                "down": uly_s,
-                "ff": uly_s,
-                "branch_attn": blk_g,
-                "attended": blk_g,
-                "deltas": blk_g,
-                "out": uly_s,
-                "grad_queries": blk_s,
-                "sum_query": blk_s,
-                "q": uly_s,
-                "pick_back": blk_g,
-                "rows": uly_s,
-                "gains_blk": blk_g,
-                "gains_ulysses": uly_g,
-                "ff_cols": blk_s,
-                "q_cols": blk_s,
-            },
-            {
-                "core_send": (n_u, n_z),
-                "core_recv": (n_u, n_z),
-                "xy_send": (n_u, n_z),
-                "xy_recv": (n_u, n_z),
-                "z_send": (n_z,),
-                "z_recv": (n_z,),
-            },
-            {
-                "head_rows": head_rows,
-                "head_stats": head_stats,
-                "weights": weight_wide,
-                **{key: getattr(rise, key) for key in kept},
+            dict(
+                head_rows=uly_s,
+                head_stats=uly_s,
+                slot_stats=blk_g,
+                slot_rows=blk_s,
+                norms=uly_g,
+                branch=blk_g,
+                sum_ff=blk_s,
+                down=uly_s,
+                ff=uly_s,
+                branch_attn=blk_g,
+                attended=blk_g,
+                deltas=blk_g,
+                out=uly_s,
+                grad_queries=blk_s,
+                sum_query=blk_s,
+                q=uly_s,
+                pick_back=blk_g,
+                rows=uly_s,
+                gains_blk=blk_g,
+                gains_ulysses=uly_g,
+                ff_cols=blk_s,
+                q_cols=blk_s,
+            ),
+            dict(
+                core_send=(n_u, n_z),
+                core_recv=(n_u, n_z),
+                xy_send=(n_u, n_z),
+                xy_recv=(n_u, n_z),
+                z_send=(n_z,),
+                z_recv=(n_z,),
+            ),
+            dict(
+                head_rows=head_rows,
+                head_stats=head_stats,
+                weights=weight_wide,
+                arrived=rise.arrived,
+                kv_weight=rise.kv_weight,
+                q_weight=rise.q_weight,
+                ff_weight=rise.ff_weight,
+                out_weight=rise.out_weight,
+                down_weight=rise.down_weight,
+                pick_rows=rise.pick_rows,
+                normed_slot=rise.normed_slot,
+                query_raw=rise.query_raw,
+                query_all=rise.query_all,
+                key_raw=rise.key_raw,
+                key_rot=rise.key_rot,
+                values=rise.values,
+                attended=rise.attended,
+                log_total=rise.log_total,
+                after_attn=rise.after_attn,
+                normed_mlp=rise.normed_mlp,
+                gate_up=rise.gate_up,
+                after_mlp=rise.after_mlp,
+                final_mine=rise.final_mine,
                 **lined,
-            },
-            {
-                "norms_all": ((n_u,) + stat_rows, f32),
-                "terms": ((picks, 128), f32),
-                "rows_back": (rows_shape, bf16),
-                "inflow_out": (inflow.shape, f32),
-                "expand_out": (expand.shape, f32),
-                "out_out": (out_shape[1:], f32),
-                "down_out": (down_shape[1:], f32),
-                "gains_out": ((32, 128), f32),
-                "squares": ((8, 128), f32),
-            },
-            {
-                "rows_got": ((n_u, slot_picks, MODEL_WIDTH), bf16),
-                "stats_got": ((n_u,) + stat_rows, f32),
-                "slot_stats": (stat_rows, f32),
-                "slot_got": ((n_b,) + stat_rows, f32),
-                "factors": ((n_b + 8, slot_picks), f32),
-                "columns": ((slot_picks, n_b + 8), f32),
-                "norms_mine": (stat_rows, f32),
-                "partial": (slot_low, bf16),
-                "partial_got": ((3,) + slot_low, bf16),
-                "mine_low": (rows_low, bf16),
-                "grad_all": (slot_low, bf16),
-                "branch_all": (slot_low, bf16),
-                "grad_down": (down_shape, bf16),
-                "down_got": (down_shape, bf16),
-                "grad_ff": (ff_shape, bf16),
-                "ff_got": (ff_shape, bf16),
-                "grad_out": (out_shape, bf16),
-                "out_got": (out_shape, bf16),
-                "attended_mine": ((slot_picks, own_cut), bf16),
-                "attended_all": ((n_b, slot_picks, own_cut), bf16),
-                "deltas": ((slot_picks, 128), f32),
-                "delta_mine": (stat_rows, f32),
-                "delta_all": ((n_b,) + stat_rows, f32),
-                "normed_keys": ((places, MODEL_WIDTH), bf16),
-                "query_send": ((n_b, slot_picks, q_share), bf16),
-                "query_got": ((n_b, slot_picks, q_share), bf16),
-                "grad_kv": ((places, 2 * width), bf16),
-                "kv_grad": (kv_shape, bf16),
-                "kv_core": ((n_u, n_z) + kv_block, bf16),
-                "kv_cross": ((n_u, n_z) + kv_block, bf16),
-                "kv_plane": ((n_z,) + kv_block, bf16),
-                "kv_line": ((n_z,) + kv_block, bf16),
-                "grad_low": ((slot_picks, q_share), bf16),
-                "grad_q": (q_shape, bf16),
-                "q_got": (q_shape, bf16),
-                "q_sum": (q_shape[1:], bf16),
-                "pick_back": (slot_low, bf16),
-                "grad_wide": ((places, MODEL_WIDTH), f32),
-                "rows_send": (rows_shape, bf16),
-                "gain_mlp_row": ((1, MODEL_WIDTH), f32),
-                "gain_final_row": ((1, MODEL_WIDTH), f32),
-                "gain_picks_row": ((1, MODEL_WIDTH), f32),
-                "gain_rows_row": ((1, MODEL_WIDTH), f32),
-                "gain_query_row": ((1, HEAD_WIDTH), f32),
-                "gain_key_row": ((1, HEAD_WIDTH), f32),
-                "gains_mine": ((32, 128), f32),
-                "gains_got": ((n_b, 32, 128), f32),
-                "gains_slot": ((32, 128), f32),
-                "gains_all": ((n_u, 32, 128), f32),
-                "ff_sum": (ff_shape[1:], bf16),
-                "q_out": (q_shape[1:], bf16),
-                "ff_out": (ff_shape[1:], bf16),
-            },
+            ),
+            dict(
+                rows_back=(rows_shape, bf16),
+                inflow_out=(inflow.shape, f32),
+                expand_out=(expand.shape, f32),
+                out_out=(out_shape[1:], f32),
+                down_out=(down_shape[1:], f32),
+                gains_out=((1, scale_share), f32),
+                tails=((8, 128), f32),
+                norms_row=((1, all_picks), f32),
+            ),
+            dict(
+                rows_got=((n_u, slot_picks, MODEL_WIDTH), bf16),
+                stats_got=((n_u,) + stat_rows, f32),
+                slot_stats=(stat_rows, f32),
+                slot_got=((n_b,) + stat_rows, f32),
+                factors=((n_b + 8, slot_picks), f32),
+                columns=((slot_picks, n_b + 8), f32),
+                norms_mine=(stat_rows, f32),
+                partial=(slot_low, bf16),
+                partial_got=((3,) + slot_low, bf16),
+                mine_low=(rows_low, bf16),
+                grad_all=(slot_low, bf16),
+                branch_all=(slot_low, bf16),
+                grad_down=(down_shape, bf16),
+                down_got=(down_shape, bf16),
+                grad_ff=(ff_shape, bf16),
+                ff_got=(ff_shape, bf16),
+                grad_out=(out_shape, bf16),
+                out_got=(out_shape, bf16),
+                attended_mine=((slot_picks, own_cut), bf16),
+                attended_all=((n_b, slot_picks, own_cut), bf16),
+                deltas=((slot_picks, 128), f32),
+                delta_mine=(stat_rows, f32),
+                delta_all=((n_b,) + stat_rows, f32),
+                normed_keys=((places, MODEL_WIDTH), bf16),
+                query_send=((n_b, slot_picks, q_share), bf16),
+                query_got=((n_b, slot_picks, q_share), bf16),
+                grad_kv=((places, 2 * width), bf16),
+                kv_grad=(kv_shape, bf16),
+                kv_core=((n_u, n_z) + kv_block, bf16),
+                kv_cross=((n_u, n_z) + kv_block, bf16),
+                kv_plane=((n_z,) + kv_block, bf16),
+                kv_line=((n_z,) + kv_block, bf16),
+                grad_low=((slot_picks, q_share), bf16),
+                grad_q=(q_shape, bf16),
+                q_got=(q_shape, bf16),
+                q_sum=(q_shape[1:], bf16),
+                pick_back=(slot_low, bf16),
+                grad_wide=((places, MODEL_WIDTH), f32),
+                rows_send=(rows_shape, bf16),
+                gain_mlp_row=((1, MODEL_WIDTH), f32),
+                gain_final_row=((1, MODEL_WIDTH), f32),
+                gain_picks_row=((1, MODEL_WIDTH), f32),
+                gain_rows_row=((1, MODEL_WIDTH), f32),
+                gain_query_row=((1, HEAD_WIDTH), f32),
+                gain_key_row=((1, HEAD_WIDTH), f32),
+                norms_all=((n_u,) + stat_rows, f32),
+                terms=((picks, 128), f32),
+                gains_line=((1, n_all * scale_share), f32),
+                gains_mine=((32, 128), f32),
+                gains_got=((n_b, 32, 128), f32),
+                gains_slot=((32, 128), f32),
+                gains_all=((n_u, 32, 128), f32),
+                ff_sum=(ff_shape[1:], bf16),
+                q_out=(q_shape[1:], bf16),
+                ff_out=(ff_shape[1:], bf16),
+            ),
             "fall",
         )
         table_grad, table_squares = table_grad_call(
             logits,
             final_all,
-            fall.norms_all[:, 0].reshape(1, all_picks),
+            fall.norms_row,
             begin.weights,
             begin.target_ids,
             fall.rows_back.reshape(places, MODEL_WIDTH),
             begin.row_ids.reshape(1, places),
         )
         return (
-            -jnp.sum(fall.terms[:, 0]),
-            fall.squares[0, 0] + jnp.sum(table_squares),
+            fall.tails,
+            table_squares,
             table_grad,
             fall.inflow_out,
             fall.out_out,
             fall.expand_out,
             fall.down_out,
-            lax.dynamic_slice_in_dim(fall.gains_out.reshape(-1), me * scale_share, scale_share),
+            fall.gains_out,
         )
 
     def long_way():
@@ -2299,7 +2373,7 @@
         def refetch(turn, which):
             tables = slot_tables(turn, True)
             (got,) = exchange.many(
-                (("ulysses", "s"),), fetch(tables[1], tables[0]), collective_id=refetch_id[which]
+                ((ULY, SPLIT),), fetch(tables[1], tables[0]), collective_id=refetch_id[which]
             )
             return (tables, got.reshape(places, MODEL_WIDTH))
 
@@ -2315,7 +2389,7 @@
         got_picks, normed_slot, query_raw, query_all, ff_all, out_all, down_all = fused_call(
             exchange,
             functools.partial(query_body, n_b),
-            (("blk", "s"), ("blk", "g"), ("blk", "g")) + (("ulysses", "g"),) * 3,
+            ((BLK, SPLIT), (BLK, WHOLE), (BLK, WHOLE)) + ((ULY, WHOLE),) * 3,
             (
                 pick_part.astype(bf16).reshape(n_b, picks, 2 * MODEL_WIDTH),
                 gain_rows[0],
@@ -2432,8 +2506,8 @@
         ) = fused_call(
             exchange,
             functools.partial(forward_body, n_u, n_b),
-            (("blk", "s"), ("blk", "g"), ("blk", "s"), ("blk", "g"), ("blk", "s"), ("blk", "g"))
-            + (("ulysses", "g"),),
+            ((BLK, SPLIT), (BLK, WHOLE), (BLK, SPLIT), (BLK, WHOLE), (BLK, SPLIT), (BLK, WHOLE))
+            + ((ULY, WHOLE),),
             (
                 part_send,
                 stats,
@@ -2484,16 +2558,16 @@
             exchange,
             functools.partial(backward_body, n_u, n_b),
             (
-                ("ulysses", "s"),
-                ("ulysses", "s"),
-                ("blk", "s"),
-                ("blk", "g"),
-                ("ulysses", "g"),
-                ("blk", "g"),
-                ("blk", "s"),
-                ("blk", "g"),
-                ("blk", "g"),
-                ("blk", "g"),
+                (ULY, SPLIT),
+                (ULY, SPLIT),
+                (BLK, SPLIT),
+                (BLK, WHOLE),
+                (ULY, WHOLE),
+                (BLK, WHOLE),
+                (BLK, SPLIT),
+                (BLK, WHOLE),
+                (BLK, WHOLE),
+                (BLK, WHOLE),
             ),
             (
                 head_rows,
@@ -2619,7 +2693,7 @@
         ) = fused_call(
             exchange,
             query_back_body,
-            (("blk", "s"), ("blk", "s"), ("blk", "g")) + (("ulysses", "s"),) * 3,
+            ((BLK, SPLIT), (BLK, SPLIT), (BLK, WHOLE)) + ((ULY, SPLIT),) * 3,
             (
                 query_send,
                 query_raw,
@@ -2721,7 +2795,7 @@
             rows_now, _ = row_grads(grad_kv_now, keys_now)
             rows_now = (rows_now + mm_outer(tables[3], pick_back)).astype(bf16)
             (back,) = exchange.many(
-                (("ulysses", "s"),),
+                ((ULY, SPLIT),),
                 rows_now.reshape(n_u, slots, MODEL_WIDTH),
                 collective_id=return_id,
             )
@@ -2734,44 +2808,44 @@
         _, table_grad, table_squares = lax.while_loop(
             more, return_turn, (jnp.int32(1), table_grad, table_squares)
         )
-        squares = jnp.sum(table_squares)
+        squares = jnp.zeros((), f32)
         for grad_piece in (sum_inflow, sum_outflow, sum_expand, sum_contract, sum_scales):
             squares = squares + jnp.sum(grad_piece * grad_piece)
+        tails = jnp.pad(jnp.stack([squares, loss_local]), (0, 6))
         return (
-            loss_local,
-            squares,
+            jnp.broadcast_to(tails[:, None], (8, 128)),
+            table_squares,
             table_grad,
             sum_inflow,
             sum_outflow,
             sum_expand,
             sum_contract,
-            sum_scales,
+            sum_scales[None, :],
         )
 
     step_float = step_count[0].astype(f32)
     first_scale = 1.0 / (1.0 - beta_first**step_float)
     second_scale = 1.0 / (1.0 - beta_second**step_float)
 
-    def finish(loss_local, squares, table_grad, *layer_grads):
-        totals = named_call(
+    steps = jnp.pad(jnp.stack([first_scale, second_scale]), (1, 125)).reshape(1, 128)
+
+    def finish(tails, table_squares, table_grad, *layer_grads):
+        numbers = named_call(
             exchange,
             totals_body,
-            {"near": ("blk", "g"), "far": ("ulysses", "g")},
+            dict(near=(ALL, WHOLE)),
             {},
-            {"mine": jnp.pad(jnp.stack([squares, count_local, loss_local]), (0, 125)).reshape(1, 128)},
-            {"total": ((1, 128), f32)},
-            {
-                "near_all": ((n_b, 1, 128), f32),
-                "near": ((1, 128), f32),
-                "far_all": ((n_u, 1, 128), f32),
-            },
+            dict(
+                tails=tails,
+                table_squares=table_squares,
+                counts=begin.meta[16:],
+                steps=steps,
+            ),
+            dict(numbers=((1, 128), f32)),
+            dict(mine=((1, 128), f32), all=((n_all, 1, 128), f32)),
             "totals",
-        ).total[0]
-        square_total, count_total, loss_total = totals[0], totals[1], totals[2]
-        gradient_norm = jnp.sqrt(square_total) / count_total
-        factor = jnp.minimum(1.0, clip_limit / gradient_norm) / count_total
-        outputs = [loss_total / count_total, gradient_norm]
-        numbers = jnp.stack([factor, first_scale, second_scale])
+        ).numbers
+        outputs = [numbers[0, 3], numbers[0, 4]]
         outputs += adam_call(
             numbers,
             embedding,
@@ -2788,19 +2862,12 @@
                 (outflow, first_outflow, second_outflow, layer_grads[1]),
                 (expand, first_expand, second_expand, layer_grads[2]),
                 (contract, first_contract, second_contract, layer_grads[3]),
+                (scales[None, :], first_scales[None, :], second_scales[None, :], layer_grads[4]),
             ),
-            learning_rates[1:5],
-            weight_decays[1:5],
-        )
-        outputs += adam_update(
-            scales,
-            first_scales,
-            second_scales,
-            layer_grads[4] * factor,
-            learning_rates[5],
-            weight_decays[5],
-            step_float,
-        )
+            learning_rates[1:],
+            weight_decays[1:],
+        )
+        outputs[-3:] = [array[0] for array in outputs[-3:]]
         return tuple(outputs)
 
     _, outputs = lax.while_loop(
@@ -2812,9 +2879,9 @@
 
 
 def solution(mesh):
-    rows = P(("ulysses", "blk"), None)
-    flat_rows = P(("ulysses", "blk"))
-    column = P(None, "blk")
+    rows = P((ULY, BLK), None)
+    flat_rows = P((ULY, BLK))
+    column = P(None, BLK)
     return jax.shard_map(
         local,
         mesh=mesh,

time: 432 us -> 396 us (0.917)
  matrix products: 21.3 us -> 0 us
  Pallas kernels: 364 us -> 377 us
  local copies, waits for them, and re-layouts: 18.1 us -> 7.57 us
  other arithmetic: 11.4 us -> 2.81 us
  between operations: 11 us -> 3.5 us
    dot_general x2 -> x0, matrix products: 21.3 us -> none  [the longest x1 11.1 us: mm_outer(): lax.dot_general(left, right, (((0,), (0,)), ((), ())), preferred_element_...]
    pallas_call x0 -> x1, Pallas kernels: none -> 20.2 us  [head_call(): pl.pallas_call(functools.partial(head_kernel, share), grid=(pl.cdiv(share...]
    pallas_call x4, Pallas kernels: 294 us -> 284 us  [remote_call(): pl.pallas_call(kernel, out_shape=shapes, in_specs=[VMEM] * len(arrays), o...]
where the time goes in v4:
time: 396 us; the launch traced here: 392 us
  Pallas kernels  377 us (95%)
  local copies, waits for them, and re-layouts  7.57 us (2%)
    pallas_call x4, Pallas kernels, remote_call(): pl.pallas_call(kernel, out_shape=shapes, in_specs=[VMEM] * len(arrays), o...  284 us
    pallas_call x1, Pallas kernels, adam_call(): pl.pallas_call(functools.partial(adam_kernel, rate, decay), grid=(pl.cdiv...  45.5 us
    pallas_call x1, Pallas kernels, head_call(): pl.pallas_call(functools.partial(head_kernel, share), grid=(pl.cdiv(share...  20.2 us
    pallas_call x1, Pallas kernels, table_grad_call(): pl.pallas_call(functools.partial(table_grad_kernel, share), grid=(pl.cdiv...  17.7 us

profile of v4, /device:TPU:0, one launch (start us, length us, event | category | flops | bytes accessed | tf_op | source)
XLA Modules:
  0.0 391.9 jit_solution(1034815345424421788)
XLA Ops:
  1.5 0.1 fusion.240.refs_3_
  1.6 0.7 copy.342.refs_4_
  2.3 0.7 copy-done.49
  3.0 0.7 copy-done.51
  3.7 0.7 copy-done.52
  4.4 0.7 copy-done.53
  5.0 14.0 %begin.1 = (s32[8,4,256]{2,1,0:T(4,128)S(1)}, s32[8,4,16]{2,1,0:T(4,128)S(1)}, s32[1,128]{1,0:T(1,128)S(1)}, f32[1,512]{1,0:T(1,128)S(1)}, s32[1,512]{1,0:T(1,12...) custom-call(s32[4,256]{1,0:T(4,128)S(1)} %copy-done.49, ...), custom_call_target="tpu_custom_call" | custom-call | tf_op jit(solution)/shard_map/begin/pallas_call | solution.py:210
  19.1 0.0 copy-start.165
  19.1 0.0 copy-start.167
  19.1 0.0 copy-start.170
  19.1 0.0 copy-start.198
  19.1 0.0 copy-start.200
  19.1 0.6 slice_reduce_fusion.1
  20.4 0.7 fusion.241
  21.1 0.1 minimum_reduce_fusion.fills_ref
  21.2 0.2 convert_reduce_fusion.2
  21.5 1.1 fusion.235
  22.6 0.6 slice.351
  23.2 0.6 slice.350
  23.8 4.5 %lookup.28 = bf16[448,1024]{1,0:T(8,128)(2,1)S(1)} custom-call(s32[4]{0:T(128)S(1)} %minimum_reduce_fusion.fills_ref, s32[448]{0:T(512)S(1)} %get-tuple-element.2298.ids_ref, f32[4748,1024]{1,0:T(8,128)} %weight.1), custom_call_target="tpu_custom_call" | custom-call | tf_op jit(solution)/shard_map/lookup/pallas_call | solution.py:1694
  28.3 0.0 copy-done.111
  28.3 0.0 copy-done.117
  28.3 0.0 copy-done.126
  28.3 0.0 copy-done.136
  28.3 125.2 %rise.1 = (bf16[4,112,1024]{2,1,0:T(8,128)(2,1)S(1)}, bf16[4,4,2,32,2048]{4,3,2,1,0:T(8,128)(2,1)}, bf16[4,8,32,256]{3,2,1,0:T(8,128)(2,1)S(1)}, bf16[4,8,32,768...) custom-call(bf16[4,112,1024]{2,1,0:T(8,128)(2,1)S(1)} %bitcast.848, ...), custom_call_target="tpu_custom_call" | custom-call | tf_op jit(solution)/shard_map/rise/pallas_call | solution.py:210
  153.6 0.0 copy-start.32
  153.6 0.0 copy-start.39
  153.6 20.2 %head.3 = (f32[4748,512]{1,0:T(8,128)}, bf16[512,1024]{1,0:T(8,128)(2,1)S(1)}, f32[4,8,128]{2,1,0:T(8,128)S(1)}) custom-call(bf16[512,1024]{1,0:T(8,128)(2,1)S(1)} %bitcast.850, f32[4748,1024]{1,0:T(8,128)} %weight.1), custom_call_target="tpu_custom_call" | custom-call | tf_op jit(solution)/shard_map/head/pallas_call | solution.py:1754
  173.8 0.0 copy-done.32
  173.8 0.0 copy-done.39
  173.8 134.8 %fall.1 = (bf16[4,112,1024]{2,1,0:T(8,128)(2,1)S(1)}, f32[32,4096]{1,0:T(8,128)S(1)}, f32[32,6144]{1,0:T(8,128)S(1)}, f32[64,1024]{1,0:T(8,128)S(1)}, f32[96,102...) custom-call(bf16[4,128,1024]{2,1,0:T(8,128)(2,1)S(1)} %bitcast.852, ...), custom_call_target="tpu_custom_call" | custom-call | tf_op jit(solution)/shard_map/fall/pallas_call | solution.py:210
  308.7 0.0 copy-start.54
  308.7 0.9 copy-done.54
  309.6 0.6 copy-done.56
  310.2 0.0 copy-done.200
  310.2 0.0 copy-start.186
  310.2 0.0 copy-start.188
  310.2 17.7 %table_grad.3 = (bf16[4748,1024]{1,0:T(8,128)(2,1)}, f32[1,1024]{1,0:T(1,128)}) custom-call(f32[4748,512]{1,0:T(8,128)} %get-tuple-element.1679.logits, bf16[512,1024]{1,0:T(8,128)(2,1)} %bitcast.851, f32[1,512]{1,0:T(1,128)} %copy-done.56, f32[1,512]{1,0:T(1,128)S(1)} %get-tuple-element.3684.weights, s32[1,512]{1,0:T(1,128)S(1)} %get-tuple-element.3685.targets, ...), custom_call_target="tpu_custom_call" | custom-call | flops 9334947840 | bytes 19447808 | tf_op jit(solution)/shard_map/table_grad/pallas_call | solution.py:1807
  327.9 0.7 copy-done.50
  328.6 9.6 %totals.3.numbers = f32[1,128]{1,0:T(1,128)S(1)} custom-call(f32[8,128]{1,0:T(8,128)S(1)} %get-tuple-element.1678.refs_0_, f32[1,1024]{1,0:T(1,128)S(1)} %copy-done.50, f32[8,128]{1,0:T(8,128)S(1)} %slice.289.refs_2_, f32[1,128]{1,0:T(1,128)S(1)} %fusion.240.refs_3_), custom_call_target="tpu_custom_call" | custom-call | tf_op jit(solution)/shard_map/totals/pallas_call | solution.py:210
  338.3 0.6 fusion.254
  338.8 0.0 copy-done.186
  338.9 5.6 %layer_adam.3 = (f32[32,4096]{1,0:T(8,128)}, f32[32,4096]{1,0:T(8,128)}, f32[32,4096]{1,0:T(8,128)}, f32[64,1024]{1,0:T(8,128)}, f32[64,1024]{1,0:T(8,128)}, /*i...) custom-call(f32[1,128]{1,0:T(1,128)S(1)} %totals.3.numbers, ...), custom_call_target="tpu_custom_call" | custom-call | tf_op jit(solution)/shard_map/layer_adam/pallas_call | solution.py:1858
  344.5 0.0 copy-done.47
  344.5 0.0 copy-start.193
  344.5 45.5 %adam.3 = (f32[4748,1024]{1,0:T(8,128)}, f32[4748,1024]{1,0:T(8,128)}, f32[4748,1024]{1,0:T(8,128)}) custom-call(f32[1,128]{1,0:T(1,128)} %copy-done.47, f32[4748,1024]{1,0:T(8,128)} %weight.1, f32[4748,1024]{1,0:T(8,128)} %first.1, f32[4748,1024]{1,0:T(8,128)} %second.1, bf16[4748,1024]{1,0:T(8,128)(2,1)} %get-tuple-element.1685.grad), custom_call_target="tpu_custom_call" | custom-call | tf_op jit(solution)/shard_map/adam/pallas_call | solution.py:1874
  390.0 0.0 copy-done.193
  390.0 0.8 while.117
  (26 shorter events, 0.1 us)
Async XLA Ops:
  1.5 326.4 %copy-start.190 = (f32[1,128]{1,0:T(1,128)}, f32[1,128]{1,0:T(1,128)S(1)}, u32[]{:S(2)}) copy-start(f32[1,128]{1,0:T(1,128)S(1)} %fusion.240.refs_3_) | copy-start | bytes 1540
  2.3 0.7 copy-start.49
  3.0 0.7 copy-start.51
  3.7 0.7 copy-start.52
  4.4 0.7 copy-start.53
  19.1 154.7 %copy-start.165 = (f32[1,1024]{1,0:T(1,128)}, f32[1,1024]{1,0:T(1,128)S(1)}, u32[]{:S(2)}) copy-start(f32[1,1024]{1,0:T(1,128)S(1)} %get-tuple-element.3681.refs_10_.refs_27_) | copy-start | bytes 12292
  19.1 154.7 %copy-start.167 = (f32[1,1024]{1,0:T(1,128)}, f32[1,1024]{1,0:T(1,128)S(1)}, u32[]{:S(2)}) copy-start(f32[1,1024]{1,0:T(1,128)S(1)} %get-tuple-element.3682.refs_11_.refs_28_) | copy-start | bytes 12292
  19.1 154.7 %copy-start.170 = (f32[16,128]{1,0:T(8,128)}, f32[16,128]{1,0:T(8,128)S(1)}, u32[]{:S(2)}) copy-start(f32[16,128]{1,0:T(8,128)S(1)} %get-tuple-element.3683.refs_2_) | copy-start | bytes 24580
  19.1 291.1 %copy-start.198 = (f32[1,512]{1,0:T(1,128)}, f32[1,512]{1,0:T(1,128)S(1)}, u32[]{:S(2)}) copy-start(f32[1,512]{1,0:T(1,128)S(1)} %get-tuple-element.3684.weights) | copy-start | bytes 6148
  19.1 291.1 %copy-start.200 = (s32[1,512]{1,0:T(1,128)}, s32[1,512]{1,0:T(1,128)S(1)}, u32[]{:S(2)}) copy-start(s32[1,512]{1,0:T(1,128)S(1)} %get-tuple-element.3685.targets) | copy-start | bytes 6148
  23.8 4.5 %copy-start.111 = (f32[32,6144]{1,0:T(8,128)S(1)}, f32[32,6144]{1,0:T(8,128)}, u32[]{:S(2)}) copy-start(f32[32,6144]{1,0:T(8,128)} %refs_8_.1) | copy-start | bytes 2359300
  23.8 4.5 %copy-start.117 = (f32[32,4096]{1,0:T(8,128)S(1)}, f32[32,4096]{1,0:T(8,128)}, u32[]{:S(2)}) copy-start(f32[32,4096]{1,0:T(8,128)} %refs_0_.3) | copy-start | bytes 1572868
  23.8 4.5 %copy-start.126 = (f32[96,1024]{1,0:T(8,128)S(1)}, f32[96,1024]{1,0:T(8,128)}, u32[]{:S(2)}) copy-start(f32[96,1024]{1,0:T(8,128)} %refs_12_.1) | copy-start | bytes 1179652
  23.8 4.5 %copy-start.136 = (f32[64,1024]{1,0:T(8,128)S(1)}, f32[64,1024]{1,0:T(8,128)}, u32[]{:S(2)}) copy-start(f32[64,1024]{1,0:T(8,128)} %refs_4_.3) | copy-start | bytes 786436
  153.6 20.2 %copy-start.32 = (f32[448,1024]{1,0:T(8,128)}, f32[448,1024]{1,0:T(8,128)S(1)}, u32[]{:S(2)}) copy-start(f32[448,1024]{1,0:T(8,128)S(1)} %get-tuple-element.1668.refs_13_) | copy-start | bytes 5505028
  153.6 20.2 %copy-start.39 = (bf16[4,8,16,1024]{3,2,1,0:T(8,128)(2,1)}, bf16[4,8,16,1024]{3,2,1,0:T(8,128)(2,1)S(1)}, u32[]{:S(2)}) copy-start(bf16[4,8,16,1024]{3,2,1,0:T(8,128)(2,1)S(1)} %get-tuple-element.1654) | copy-start | bytes 3145732
  308.7 0.9 copy-start.54
  309.6 0.6 copy-start.56
  310.2 28.7 %copy-start.127 = (f32[96,1024]{1,0:T(8,128)S(1)}, f32[96,1024]{1,0:T(8,128)}, u32[]{:S(2)}) copy-start(f32[96,1024]{1,0:T(8,128)} %refs_12_.1) | copy-start | bytes 1179652
  310.2 28.7 %copy-start.184 = (f32[104]{0:T(128)S(1)}, f32[104]{0:T(128)}, u32[]{:S(2)}) copy-start(f32[104]{0:T(128)} %param.57) | copy-start | bytes 1252
  310.2 28.7 %copy-start.186 = (f32[104]{0:T(128)S(1)}, f32[104]{0:T(128)}, u32[]{:S(2)}) copy-start(f32[104]{0:T(128)} %param.58) | copy-start | bytes 1252
  310.2 28.7 %copy-start.188 = (f32[104]{0:T(128)S(1)}, f32[104]{0:T(128)}, u32[]{:S(2)}) copy-start(f32[104]{0:T(128)} %param.59) | copy-start | bytes 1252
  327.9 0.7 copy-start.50
  338.2 6.2 %copy-start.47 = (f32[1,128]{1,0:T(1,128)}, f32[1,128]{1,0:T(1,128)S(1)}, u32[]{:S(2)}) copy-start(f32[1,128]{1,0:T(1,128)S(1)} %totals.3.numbers) | copy-start | bytes 1540
  344.5 45.5 %copy-start.193 = (s32[4]{0:T(128)S(1)}, s32[4]{0:T(128)}, u32[]{:S(2)}) copy-start(s32[4]{0:T(128)} %param.37) | copy-start | bytes 52

commit v5 on v4

--- a/solution.py
+++ b/solution.py
@@ -205,7 +205,7 @@
 VMEM = pl.BlockSpec(memory_space=pltpu.VMEM)
 
 
-def remote_call(kernel, collective_id, shapes, scratch, arrays, name):
+def remote_call(kernel, collective_id, shapes, scratch, arrays, name, grant=40):
     few = lax.axis_size(ULY) * lax.axis_size(BLK) <= 32
     return pl.pallas_call(
         kernel,
@@ -216,7 +216,7 @@
         compiler_params=pltpu.CompilerParams(
             collective_id=collective_id,
             has_side_effects=True,
-            vmem_limit_bytes=(40 if few else 57) * 1024 * 1024,
+            vmem_limit_bytes=(grant if few or grant < 40 else 57) * 1024 * 1024,
         ),
         name=name,
     )(*arrays)
@@ -914,7 +914,7 @@
     pass
 
 
-def named_call(exchange, body, plan, extra_sems, ins, outs, scratch, name):
+def named_call(exchange, body, plan, extra_sems, ins, outs, scratch, name, grant=40):
     counts = axis_counts()
     sem_shapes = []
     for axis, _ in plan.values():
@@ -946,6 +946,7 @@
         + [pltpu.SemaphoreType.DMA(extra_sems[key]) for key in extra],
         list(ins.values()),
         name,
+        grant,
     )
     found = Named()
     for key, value in zip(outs, results):
@@ -1171,13 +1172,9 @@
     pick_hot = jnp.where(r.key_pos[...] == r.slot_picked[...], 1.0, 0.0).astype(bf16)
     pick_lane = lax.broadcasted_iota(jnp.int32, pick_hot.shape, 1)
     target_hot = jnp.where(r.target_of[...] == pick_lane, 1.0, 0.0).astype(bf16)
-    r.pick_send[:, :, :MODEL_WIDTH] = (
-        mm_outer(pick_hot, arrived).astype(bf16).reshape(r.normed_slot.shape)
-    )
-    r.pick_send[:, :, MODEL_WIDTH:] = (
-        mm_outer(target_hot, arrived).astype(bf16).reshape(r.normed_slot.shape)
-    )
+    r.pick_send[...] = mm_outer(pick_hot, arrived).astype(bf16).reshape(r.pick_send.shape)
     picked = links.picks(r.pick_send, r.pick_got)
+    r.aim_send[...] = mm_outer(target_hot, arrived).astype(bf16).reshape(r.aim_send.shape)
 
     def pass_on(step):
         along_z(step).wait_recv()
@@ -1190,9 +1187,8 @@
     wide = arrived.astype(f32)
     r.normed_keys[...] = (wide * inverse_root(wide) * r.gain_attn[...]).astype(bf16)
     picked.finish()
-    pick_rows = sum_blocks(r.pick_got)
-    r.pick_rows[...] = pick_rows
-    mine = pick_rows[:, :MODEL_WIDTH]
+    mine = sum_blocks(r.pick_got)
+    r.pick_rows[:, :MODEL_WIDTH] = mine
     r.normed_mine[...] = (mine * inverse_root(mine) * r.gain_attn[...]).astype(bf16)
     links.normed(r.normed_mine, r.normed_slot).finish()
     q_all.finish()
@@ -1317,7 +1313,11 @@
     r.after_mlp[...] = after_mlp
     r.final_mine[...] = (after_mlp * inverse_root(after_mlp) * r.gain_final[...]).astype(bf16)
     links.final(r.final_mine, r.final_slot).finish()
-    links.final_all(r.final_slot, r.final_all).finish()
+    final_all = links.final_all(r.final_slot, r.final_all)
+    aims = links.aims(r.aim_send, r.aim_got)
+    aims.finish()
+    r.pick_rows[:, MODEL_WIDTH:] = sum_blocks(r.aim_got)
+    final_all.finish()
     each(n_z, lambda step: along_z(step).wait_send(), 1)
     each(n_z, lambda step: each(n_u, lambda hop: across(hop, step).wait_send(), 1))
     each(n_z, lambda step: each(n_u, lambda hop: to_core(hop, step).wait_send()))
@@ -1435,6 +1435,10 @@
     last.finish()
     delta_part.finish()
 
+    ff_part.finish()
+    r.ff_sum[...] = sum_blocks(r.ff_got).astype(bf16)
+    ff_last = links.ff_cols(r.ff_sum, r.ff_out)
+
     allowed = r.key_lim[...] <= r.slot_picked[...]
     width = KEY_VALUE_HEADS * HEAD_WIDTH
     r.gain_key_row[...] = jnp.zeros((1, HEAD_WIDTH), f32)
@@ -1517,6 +1521,28 @@
         each(n_z, lambda step: to_core(hop, step).start())
 
     each(n_u, weight_grad)
+    def add_pair(hop, step):
+        row, line = place(hop, step)
+        to_core(hop, step).wait_recv()
+        r.kv_core[hop, step] = (
+            r.kv_grad[row, line, c].astype(f32) + r.kv_core[hop, step].astype(f32)
+        ).astype(bf16)
+
+    def send_pairs(k):
+        step = lax.rem(k + 1, n_z)
+
+        def one(hop):
+            add_pair(hop, step)
+            across(hop, step).start()
+
+        each(n_u, one, 1)
+        add_pair(0, step)
+
+    each(n_z, send_pairs)
+    down_part.finish()
+    r.down_out[...] = sum_blocks(r.down_got)
+    out_part.finish()
+    r.out_out[...] = sum_blocks(r.out_got)
     query_part.finish()
     upstream = sum_blocks(r.query_got).astype(bf16).astype(f32)
     r.gain_query_row[...] = jnp.zeros((1, HEAD_WIDTH), f32)
@@ -1536,25 +1562,6 @@
     )
     back = links.sum_query(r.partial, r.partial_got.at[2])
 
-    def add_pair(hop):
-        def one(step):
-            row, line = place(hop, step)
-            to_core(hop, step).wait_recv()
-            r.kv_core[hop, step] = (
-                r.kv_grad[row, line, c].astype(f32) + r.kv_core[hop, step].astype(f32)
-            ).astype(bf16)
-
-        return one
-
-    def forward_hop(hop):
-        def forward(step):
-            add_pair(hop)(step)
-            across(hop, step).start()
-
-        each(n_z, forward)
-
-    each(n_u, forward_hop, 1)
-    each(n_z, add_pair(0))
     r.grad_q[...] = (
         mm_outer(flat_rows_of(r.normed_slot), r.grad_low[...]).astype(bf16).reshape(r.grad_q.shape)
     )
@@ -1574,6 +1581,18 @@
 
     each(n_u, row_grad)
     grad_rows, gain_keys = norm_back_rows(wide, r.gain_attn[...], r.grad_wide[...])
+    def plane_sum(step):
+        total = r.kv_core[0, step].astype(f32)
+        for hop in range(1, n_u):
+            across(hop, step).wait_recv()
+            total = total + r.kv_cross[hop, step].astype(f32)
+        return total
+
+    def add_plane(step):
+        r.kv_plane[step] = plane_sum(step).astype(bf16)
+        along_z(step).start()
+
+    each(n_z, add_plane, 1)
     pick_part.finish()
     pick_hot = jnp.where(r.key_pos[...] == r.slot_picked[...], 1.0, 0.0).astype(bf16)
     r.rows_send[...] = (
@@ -1598,13 +1617,6 @@
     r.gains_mine[3 * lines + 1 : 3 * lines + 2, :] = r.gain_key_row[...]
     gains_part = links.gains_blk(r.gains_mine, r.gains_got)
 
-    ff_part.finish()
-    r.ff_sum[...] = sum_blocks(r.ff_got).astype(bf16)
-    ff_last = links.ff_cols(r.ff_sum, r.ff_out)
-    down_part.finish()
-    r.down_out[...] = sum_blocks(r.down_got)
-    out_part.finish()
-    r.out_out[...] = sum_blocks(r.out_got)
     gains_part.finish()
     r.gains_slot[...] = sum_blocks(r.gains_got)
     gains_last = links.gains_ulysses(r.gains_slot, r.gains_all)
@@ -1612,18 +1624,6 @@
     r.q_sum[...] = sum_blocks(r.q_got).astype(bf16)
     q_last = links.q_cols(r.q_sum, r.q_out)
 
-    def plane_sum(step):
-        total = r.kv_core[0, step].astype(f32)
-        for hop in range(1, n_u):
-            across(hop, step).wait_recv()
-            total = total + r.kv_cross[hop, step].astype(f32)
-        return total
-
-    def add_plane(step):
-        r.kv_plane[step] = plane_sum(step).astype(bf16)
-        along_z(step).start()
-
-    each(n_z, add_plane, 1)
     total = plane_sum(0)
     for step in range(1, n_z):
         along_z(step).wait_recv()
@@ -1824,7 +1824,7 @@
             pl.BlockSpec((tile, width), lambda i: (i, 0)),
             whole(1, width),
         ],
-        compiler_params=pltpu.CompilerParams(vmem_limit_bytes=60 * 1024 * 1024),
+        compiler_params=pltpu.CompilerParams(vmem_limit_bytes=32 * 1024 * 1024),
         cost_estimate=pl.CostEstimate(
             flops=2 * share * width * (picks + places),
             bytes_accessed=share * (4 * picks + 2 * width),
@@ -1877,7 +1877,7 @@
         out_shape=[jax.ShapeDtypeStruct((share, width), f32)] * 3,
         in_specs=[pl.BlockSpec((1, 128), lambda i: (0, 0))] + [block] * 4,
         out_specs=[block] * 3,
-        compiler_params=pltpu.CompilerParams(vmem_limit_bytes=60 * 1024 * 1024),
+        compiler_params=pltpu.CompilerParams(vmem_limit_bytes=40 * 1024 * 1024),
         name="adam",
     )(numbers, weight, first, second, grad)
 
@@ -2064,6 +2064,7 @@
                 q_split=blk_s,
                 ff_split=blk_s,
                 picks=blk_s,
+                aims=blk_s,
                 q_all=uly_g,
                 normed=blk_g,
                 queries=blk_g,
@@ -2127,8 +2128,10 @@
                 down_in=(down_shape[1:], bf16),
                 q_part=(q_shape[1:], bf16),
                 ff_part=(ff_shape[1:], bf16),
-                pick_send=((n_b, picks, 2 * MODEL_WIDTH), bf16),
-                pick_got=((n_b, picks, 2 * MODEL_WIDTH), bf16),
+                pick_send=(slot_low, bf16),
+                pick_got=(slot_low, bf16),
+                aim_send=(slot_low, bf16),
+                aim_got=(slot_low, bf16),
                 normed_mine=(rows_low, bf16),
                 normed_keys=((places, MODEL_WIDTH), bf16),
                 query_mine=((slot_picks, q_share), bf16),
@@ -2844,6 +2847,7 @@
             dict(numbers=((1, 128), f32)),
             dict(mine=((1, 128), f32), all=((n_all, 1, 128), f32)),
             "totals",
+            8,
         ).numbers
         outputs = [numbers[0, 3], numbers[0, 4]]
         outputs += adam_call(

time: 396 us -> 379 us (0.957)
  Pallas kernels: 377 us -> 358 us
    pallas_call x4, Pallas kernels: 284 us -> 272 us  [remote_call(): pl.pallas_call(kernel, out_shape=shapes, in_specs=[VMEM] * len(arrays), o...]
where the time goes in v5:
time: 379 us; the launch traced here: 375 us
  Pallas kernels  358 us (94%)
  local copies, waits for them, and re-layouts  9.23 us (2%)
    pallas_call x4, Pallas kernels, remote_call(): pl.pallas_call(kernel, out_shape=shapes, in_specs=[VMEM] * len(arrays), o...  272 us
    pallas_call x1, Pallas kernels, adam_call(): pl.pallas_call(functools.partial(adam_kernel, rate, decay), grid=(pl.cdiv...  43.2 us
    pallas_call x1, Pallas kernels, head_call(): pl.pallas_call(functools.partial(head_kernel, share), grid=(pl.cdiv(share...  19.9 us
    pallas_call x1, Pallas kernels, table_grad_call(): pl.pallas_call(functools.partial(table_grad_kernel, share), grid=(pl.cdiv...  15.1 us

profile of v5, /device:TPU:0, one launch (start us, length us, event | category | flops | bytes accessed | tf_op | source)
XLA Modules:
  0.0 374.8 jit_solution(14174031715995756693)
XLA Ops:
  1.5 0.7 fusion.240.refs_3_
  2.1 0.7 copy.342.refs_4_
  2.9 0.7 copy-done.49
  3.6 0.7 copy-done.50
  4.3 0.7 copy-done.51
  4.9 0.7 copy-done.52
  5.6 14.5 %begin.1 = (s32[8,4,256]{2,1,0:T(4,128)S(1)}, s32[8,4,16]{2,1,0:T(4,128)S(1)}, s32[1,128]{1,0:T(1,128)S(1)}, f32[1,512]{1,0:T(1,128)}, s32[1,512]{1,0:T(1,128)},...) custom-call(s32[4,256]{1,0:T(4,128)S(1)} %copy-done.49, ...), custom_call_target="tpu_custom_call" | custom-call | tf_op jit(solution)/shard_map/begin/pallas_call | solution.py:210
  20.1 0.0 copy-start.186
  20.2 0.6 slice_reduce_fusion.1
  21.5 0.2 fusion.241
  21.7 0.1 minimum_reduce_fusion.fills_ref
  21.8 0.2 convert_reduce_fusion.2
  22.0 1.1 fusion.235
  23.1 0.6 slice.351
  23.8 0.6 slice.350
  24.4 4.5 %lookup.28 = bf16[448,1024]{1,0:T(8,128)(2,1)S(1)} custom-call(s32[4]{0:T(128)S(1)} %minimum_reduce_fusion.fills_ref, s32[448]{0:T(512)S(1)} %get-tuple-element.2298.ids_ref, f32[4748,1024]{1,0:T(8,128)} %weight.1), custom_call_target="tpu_custom_call" | custom-call | tf_op jit(solution)/shard_map/lookup/pallas_call | solution.py:1694
  29.0 123.0 %rise.1 = (bf16[4,112,1024]{2,1,0:T(8,128)(2,1)S(1)}, bf16[4,4,2,32,2048]{4,3,2,1,0:T(8,128)(2,1)}, bf16[4,8,32,256]{3,2,1,0:T(8,128)(2,1)S(1)}, bf16[4,8,32,768...) custom-call(bf16[4,112,1024]{2,1,0:T(8,128)(2,1)S(1)} %bitcast.848, ...), custom_call_target="tpu_custom_call" | custom-call | tf_op jit(solution)/shard_map/rise/pallas_call | solution.py:210
  152.0 0.0 copy-start.33
  152.0 19.9 %head.3 = (f32[4748,512]{1,0:T(8,128)}, bf16[512,1024]{1,0:T(8,128)(2,1)S(1)}, f32[4,8,128]{2,1,0:T(8,128)S(1)}) custom-call(bf16[512,1024]{1,0:T(8,128)(2,1)S(1)} %bitcast.850, f32[4748,1024]{1,0:T(8,128)} %weight.1), custom_call_target="tpu_custom_call" | custom-call | tf_op jit(solution)/shard_map/head/pallas_call | solution.py:1754
  171.9 125.7 %fall.1 = (bf16[4,112,1024]{2,1,0:T(8,128)(2,1)S(1)}, f32[32,4096]{1,0:T(8,128)S(1)}, f32[32,6144]{1,0:T(8,128)S(1)}, f32[64,1024]{1,0:T(8,128)S(1)}, f32[96,102...) custom-call(bf16[4,128,1024]{2,1,0:T(8,128)(2,1)S(1)} %bitcast.852, ...), custom_call_target="tpu_custom_call" | custom-call | tf_op jit(solution)/shard_map/fall/pallas_call | solution.py:210
  297.6 0.0 copy-done.201
  297.6 0.0 copy-done.203
  297.6 0.0 copy-start.54
  297.6 3.8 %copy-done.54 = f32[4748,512]{1,0:T(8,128)S(1)} copy-done((f32[4748,512]{1,0:T(8,128)S(1)}, f32[4748,512]{1,0:T(8,128)}, u32[]{:S(2)}) %copy-start.54) | copy-done | bytes 9723928
  301.4 0.0 copy-start.146
  301.4 0.0 copy-start.147
  301.4 0.0 copy-start.148
  301.4 0.0 copy-start.152
  301.5 0.0 copy-start.153
  301.5 0.0 copy-start.187
  301.5 0.0 copy-start.189
  301.5 0.0 copy-start.191
  301.5 15.1 %table_grad.3 = (bf16[4748,1024]{1,0:T(8,128)(2,1)S(1)}, f32[1,1024]{1,0:T(1,128)S(1)}) custom-call(f32[4748,512]{1,0:T(8,128)S(1)} %copy-done.54, bf16[512,1024]{1,0:T(8,128)(2,1)S(1)} %bitcast.851, f32[1,512]{1,0:T(1,128)S(1)} %get-tuple-element.1680.norms, f32[1,512]{1,0:T(1,128)S(1)} %copy-done.201, s32[1,512]{1,0:T(1,128)S(1)} %copy-done.203, ...), custom_call_target="tpu_custom_call" | custom-call | flops 9334947840 | bytes 19447808 | tf_op jit(solution)/shard_map/table_grad/pallas_call | solution.py:1807
  316.6 0.0 copy-done.193
  316.6 8.9 %totals.3.numbers = f32[1,128]{1,0:T(1,128)S(1)} custom-call(f32[8,128]{1,0:T(8,128)S(1)} %get-tuple-element.1678.refs_0_, f32[1,1024]{1,0:T(1,128)S(1)} %get-tuple-element.1684.refs_1_, f32[8,128]{1,0:T(8,128)S(1)} %slice.289.refs_2_, f32[1,128]{1,0:T(1,128)S(1)} %copy-done.193), custom_call_target="tpu_custom_call" | custom-call | tf_op jit(solution)/shard_map/totals/pallas_call | solution.py:210
  325.6 0.6 fusion.254
  326.2 0.0 copy-done.145
  326.2 0.0 copy-done.146
  326.2 0.0 copy-done.147
  326.2 0.0 copy-done.148
  326.2 0.0 copy-done.152
  326.2 0.0 copy-done.153
  326.2 0.0 copy-done.187
  326.2 0.0 copy-done.189
  326.2 0.0 copy-done.191
  326.3 3.5 layer_adam.3
  329.8 43.2 %adam.3 = (f32[4748,1024]{1,0:T(8,128)}, f32[4748,1024]{1,0:T(8,128)}, f32[4748,1024]{1,0:T(8,128)}) custom-call(f32[1,128]{1,0:T(1,128)S(1)} %totals.3.numbers, f32[4748,1024]{1,0:T(8,128)} %weight.1, f32[4748,1024]{1,0:T(8,128)} %first.1, f32[4748,1024]{1,0:T(8,128)} %second.1, bf16[4748,1024]{1,0:T(8,128)(2,1)S(1)} %get-tuple-element.1685.grad), custom_call_target="tpu_custom_call" | custom-call | tf_op jit(solution)/shard_map/adam/pallas_call | solution.py:1874
  373.0 0.8 while.117
  (34 shorter events, 0.1 us)
Async XLA Ops:
  2.9 0.7 copy-start.49
  3.6 0.7 copy-start.50
  4.3 0.7 copy-start.51
  4.9 0.7 copy-start.52
  20.1 8.8 %copy-start.186 = (f32[24,128]{1,0:T(8,128)}, f32[24,128]{1,0:T(8,128)S(1)}, u32[]{:S(2)}) copy-start(f32[24,128]{1,0:T(8,128)S(1)} %get-tuple-element.3686) | copy-start | bytes 36868
  20.1 151.7 %copy-start.170 = (f32[1,1024]{1,0:T(1,128)}, f32[1,1024]{1,0:T(1,128)S(1)}, u32[]{:S(2)}) copy-start(f32[1,1024]{1,0:T(1,128)S(1)} %get-tuple-element.3681.refs_10_.refs_27_) | copy-start | bytes 12292
  20.2 151.7 %copy-start.172 = (f32[1,1024]{1,0:T(1,128)}, f32[1,1024]{1,0:T(1,128)S(1)}, u32[]{:S(2)}) copy-start(f32[1,1024]{1,0:T(1,128)S(1)} %get-tuple-element.3682.refs_11_.refs_28_) | copy-start | bytes 12292
  20.2 151.7 %copy-start.175 = (f32[16,128]{1,0:T(8,128)}, f32[16,128]{1,0:T(8,128)S(1)}, u32[]{:S(2)}) copy-start(f32[16,128]{1,0:T(8,128)S(1)} %get-tuple-element.3683.refs_2_) | copy-start | bytes 24580
  24.4 4.5 %copy-start.109 = (f32[32,6144]{1,0:T(8,128)S(1)}, f32[32,6144]{1,0:T(8,128)}, u32[]{:S(2)}) copy-start(f32[32,6144]{1,0:T(8,128)} %refs_8_.1) | copy-start | bytes 2359300
  24.4 4.5 %copy-start.115 = (f32[32,4096]{1,0:T(8,128)S(1)}, f32[32,4096]{1,0:T(8,128)}, u32[]{:S(2)}) copy-start(f32[32,4096]{1,0:T(8,128)} %refs_0_.3) | copy-start | bytes 1572868
  24.4 4.5 %copy-start.124 = (f32[96,1024]{1,0:T(8,128)S(1)}, f32[96,1024]{1,0:T(8,128)}, u32[]{:S(2)}) copy-start(f32[96,1024]{1,0:T(8,128)} %refs_12_.1) | copy-start | bytes 1179652
  24.4 4.6 %copy-start.133 = (f32[64,1024]{1,0:T(8,128)S(1)}, f32[64,1024]{1,0:T(8,128)}, u32[]{:S(2)}) copy-start(f32[64,1024]{1,0:T(8,128)} %refs_4_.3) | copy-start | bytes 786436
  152.0 19.9 %copy-start.33 = (f32[448,1024]{1,0:T(8,128)}, f32[448,1024]{1,0:T(8,128)S(1)}, u32[]{:S(2)}) copy-start(f32[448,1024]{1,0:T(8,128)S(1)} %get-tuple-element.1668.refs_13_) | copy-start | bytes 5505028
  171.9 125.7 %copy-start.201 = (f32[1,512]{1,0:T(1,128)S(1)}, f32[1,512]{1,0:T(1,128)}, u32[]{:S(2)}) copy-start(f32[1,512]{1,0:T(1,128)} %get-tuple-element.3684.weights) | copy-start | bytes 6148
  171.9 125.7 %copy-start.203 = (s32[1,512]{1,0:T(1,128)S(1)}, s32[1,512]{1,0:T(1,128)}, u32[]{:S(2)}) copy-start(s32[1,512]{1,0:T(1,128)} %get-tuple-element.3685.targets) | copy-start | bytes 6148
  297.6 3.8 %copy-start.54 = (f32[4748,512]{1,0:T(8,128)S(1)}, f32[4748,512]{1,0:T(8,128)}, u32[]{:S(2)}) copy-start(f32[4748,512]{1,0:T(8,128)} %get-tuple-element.1679.logits) | copy-start | bytes 29171716
  301.4 15.2 %copy-start.193 = (f32[1,128]{1,0:T(1,128)S(1)}, f32[1,128]{1,0:T(1,128)}, u32[]{:S(2)}) copy-start(f32[1,128]{1,0:T(1,128)} %fusion.240.refs_3_) | copy-start | bytes 1540
  301.4 24.8 %copy-start.135 = (f32[32,6144]{1,0:T(8,128)S(1)}, f32[32,6144]{1,0:T(8,128)}, u32[]{:S(2)}) copy-start(f32[32,6144]{1,0:T(8,128)} %refs_9_.1) | copy-start | bytes 2359300
  301.4 24.8 %copy-start.136 = (f32[32,6144]{1,0:T(8,128)S(1)}, f32[32,6144]{1,0:T(8,128)}, u32[]{:S(2)}) copy-start(f32[32,6144]{1,0:T(8,128)} %refs_10_.1) | copy-start | bytes 2359300
  301.4 24.8 %copy-start.145 = (f32[32,4096]{1,0:T(8,128)S(1)}, f32[32,4096]{1,0:T(8,128)}, u32[]{:S(2)}) copy-start(f32[32,4096]{1,0:T(8,128)} %refs_1_.5) | copy-start | bytes 1572868
  301.4 24.8 %copy-start.146 = (f32[32,4096]{1,0:T(8,128)S(1)}, f32[32,4096]{1,0:T(8,128)}, u32[]{:S(2)}) copy-start(f32[32,4096]{1,0:T(8,128)} %refs_2_.5) | copy-start | bytes 1572868
  301.4 24.8 %copy-start.147 = (f32[96,1024]{1,0:T(8,128)S(1)}, f32[96,1024]{1,0:T(8,128)}, u32[]{:S(2)}) copy-start(f32[96,1024]{1,0:T(8,128)} %refs_13_.1) | copy-start | bytes 1179652
  301.4 24.8 %copy-start.148 = (f32[96,1024]{1,0:T(8,128)S(1)}, f32[96,1024]{1,0:T(8,128)}, u32[]{:S(2)}) copy-start(f32[96,1024]{1,0:T(8,128)} %refs_14_.1) | copy-start | bytes 1179652
  301.4 24.8 %copy-start.152 = (f32[64,1024]{1,0:T(8,128)S(1)}, f32[64,1024]{1,0:T(8,128)}, u32[]{:S(2)}) copy-start(f32[64,1024]{1,0:T(8,128)} %refs_5_.1) | copy-start | bytes 786436
  301.5 24.8 %copy-start.153 = (f32[64,1024]{1,0:T(8,128)S(1)}, f32[64,1024]{1,0:T(8,128)}, u32[]{:S(2)}) copy-start(f32[64,1024]{1,0:T(8,128)} %refs_6_.1) | copy-start | bytes 786436
  301.5 24.8 %copy-start.187 = (f32[104]{0:T(128)S(1)}, f32[104]{0:T(128)}, u32[]{:S(2)}) copy-start(f32[104]{0:T(128)} %param.57) | copy-start | bytes 1252
  301.5 24.8 %copy-start.189 = (f32[104]{0:T(128)S(1)}, f32[104]{0:T(128)}, u32[]{:S(2)}) copy-start(f32[104]{0:T(128)} %param.58) | copy-start | bytes 1252
  301.5 24.8 %copy-start.191 = (f32[104]{0:T(128)S(1)}, f32[104]{0:T(128)}, u32[]{:S(2)}) copy-start(f32[104]{0:T(128)} %param.59) | copy-start | bytes 1252
  329.8 43.2 %copy-start.196 = (s32[4]{0:T(128)S(1)}, s32[4]{0:T(128)}, u32[]{:S(2)}) copy-start(s32[4]{0:T(128)} %param.37) | copy-start | bytes 52

commit v6 on v5

--- a/solution.py
+++ b/solution.py
@@ -1153,11 +1153,11 @@
     r.kv_in[...] = r.inflow[:, QUERY_WIDTH:].astype(bf16)
     own_copy().start()
     rows = links.rows(r.rows_in, r.arrived)
-    each(n_z, lambda step: along_z(step).start(), 1)
     q_share = r.q_in.shape[2]
     for k in range(n_b):
         r.q_in[k] = r.inflow[:, k * q_share : (k + 1) * q_share].astype(bf16)
     q_split = links.q_split(r.q_in, r.q_part)
+    each(n_z, lambda step: along_z(step).start(), 1)
     own_copy().wait()
     each(n_u, lambda hop: across(hop, 0).start(), 1)
     to_core(0, 0).start()
@@ -1166,6 +1166,8 @@
     ff_split = links.ff_split(r.ff_in, r.ff_part)
     r.out_in[...] = r.outflow[...].astype(bf16)
     r.down_in[...] = r.contract[...].astype(bf16)
+    q_split.finish()
+    q_all = links.q_all(r.q_part, r.q_weight)
     rows.finish()
 
     arrived = flat_rows_of(r.arrived)
@@ -1182,8 +1184,6 @@
         to_core(0, step).start()
 
     each(n_z, pass_on, 1)
-    q_split.finish()
-    q_all = links.q_all(r.q_part, r.q_weight)
     wide = arrived.astype(f32)
     r.normed_keys[...] = (wide * inverse_root(wide) * r.gain_attn[...]).astype(bf16)
     picked.finish()

time: 379 us -> 376 us (level)
  no operation moved by 1% of the time
where the time goes in v6:
time: 376 us; the launch traced here: 372 us
  Pallas kernels  355 us (94%)
  local copies, waits for them, and re-layouts  9.23 us (2%)
    pallas_call x4, Pallas kernels, remote_call(): pl.pallas_call(kernel, out_shape=shapes, in_specs=[VMEM] * len(arrays), o...  269 us
    pallas_call x1, Pallas kernels, adam_call(): pl.pallas_call(functools.partial(adam_kernel, rate, decay), grid=(pl.cdiv...  43.2 us
    pallas_call x1, Pallas kernels, head_call(): pl.pallas_call(functools.partial(head_kernel, share), grid=(pl.cdiv(share...  19.9 us
    pallas_call x1, Pallas kernels, table_grad_call(): pl.pallas_call(functools.partial(table_grad_kernel, share), grid=(pl.cdiv...  15.1 us

profile of v6, /device:TPU:0, one launch (start us, length us, event | category | flops | bytes accessed | tf_op | source)
XLA Modules:
  0.0 371.9 jit_solution(9072609715996336016)
XLA Ops:
  1.5 0.7 fusion.240.refs_3_
  2.1 0.7 copy.342.refs_4_
  2.9 0.7 copy-done.49
  3.6 0.7 copy-done.50
  4.3 0.7 copy-done.51
  4.9 0.7 copy-done.52
  5.6 14.5 %begin.1 = (s32[8,4,256]{2,1,0:T(4,128)S(1)}, s32[8,4,16]{2,1,0:T(4,128)S(1)}, s32[1,128]{1,0:T(1,128)S(1)}, f32[1,512]{1,0:T(1,128)}, s32[1,512]{1,0:T(1,128)},...) custom-call(s32[4,256]{1,0:T(4,128)S(1)} %copy-done.49, ...), custom_call_target="tpu_custom_call" | custom-call | tf_op jit(solution)/shard_map/begin/pallas_call | solution.py:210
  20.1 0.0 copy-start.186
  20.1 0.0 copy-start.170
  20.2 0.0 copy-start.172
  20.2 0.0 copy-start.175
  20.2 0.6 slice_reduce_fusion.1
  21.5 0.2 fusion.241
  21.7 0.1 minimum_reduce_fusion.fills_ref
  21.8 0.2 convert_reduce_fusion.2
  22.0 1.1 fusion.235
  23.1 0.6 slice.351
  23.8 0.6 slice.350
  24.4 4.4 %lookup.28 = bf16[448,1024]{1,0:T(8,128)(2,1)S(1)} custom-call(s32[4]{0:T(128)S(1)} %minimum_reduce_fusion.fills_ref, s32[448]{0:T(512)S(1)} %get-tuple-element.2298.ids_ref, f32[4748,1024]{1,0:T(8,128)} %weight.1), custom_call_target="tpu_custom_call" | custom-call | tf_op jit(solution)/shard_map/lookup/pallas_call | solution.py:1694
  28.8 0.0 copy-done.186
  28.8 0.0 copy-done.109
  28.8 0.0 copy-done.115
  28.8 0.0 copy-done.124
  28.8 0.0 copy-done.133
  28.8 120.9 %rise.1 = (bf16[4,112,1024]{2,1,0:T(8,128)(2,1)S(1)}, bf16[4,4,2,32,2048]{4,3,2,1,0:T(8,128)(2,1)}, bf16[4,8,32,256]{3,2,1,0:T(8,128)(2,1)S(1)}, bf16[4,8,32,768...) custom-call(bf16[4,112,1024]{2,1,0:T(8,128)(2,1)S(1)} %bitcast.848, ...), custom_call_target="tpu_custom_call" | custom-call | tf_op jit(solution)/shard_map/rise/pallas_call | solution.py:210
  149.8 0.0 copy-start.33
  149.8 19.9 %head.3 = (f32[4748,512]{1,0:T(8,128)}, bf16[512,1024]{1,0:T(8,128)(2,1)S(1)}, f32[4,8,128]{2,1,0:T(8,128)S(1)}) custom-call(bf16[512,1024]{1,0:T(8,128)(2,1)S(1)} %bitcast.850, f32[4748,1024]{1,0:T(8,128)} %weight.1), custom_call_target="tpu_custom_call" | custom-call | tf_op jit(solution)/shard_map/head/pallas_call | solution.py:1754
  169.7 0.0 copy-done.33
  169.7 0.0 copy-done.175
  169.7 0.0 copy-start.201
  169.7 0.0 copy-start.203
  169.7 124.9 %fall.1 = (bf16[4,112,1024]{2,1,0:T(8,128)(2,1)S(1)}, f32[32,4096]{1,0:T(8,128)S(1)}, f32[32,6144]{1,0:T(8,128)S(1)}, f32[64,1024]{1,0:T(8,128)S(1)}, f32[96,102...) custom-call(bf16[4,128,1024]{2,1,0:T(8,128)(2,1)S(1)} %bitcast.852, ...), custom_call_target="tpu_custom_call" | custom-call | tf_op jit(solution)/shard_map/fall/pallas_call | solution.py:210
  294.6 0.0 copy-start.54
  294.7 3.8 %copy-done.54 = f32[4748,512]{1,0:T(8,128)S(1)} copy-done((f32[4748,512]{1,0:T(8,128)S(1)}, f32[4748,512]{1,0:T(8,128)}, u32[]{:S(2)}) %copy-start.54) | copy-done | bytes 9723928
  298.4 0.0 copy-start.146
  298.4 0.0 copy-start.147
  298.4 0.0 copy-start.148
  298.5 0.0 copy-start.152
  298.5 0.0 copy-start.153
  298.5 0.0 copy-start.187
  298.5 0.0 copy-start.189
  298.5 0.0 copy-start.191
  298.5 15.1 %table_grad.3 = (bf16[4748,1024]{1,0:T(8,128)(2,1)S(1)}, f32[1,1024]{1,0:T(1,128)S(1)}) custom-call(f32[4748,512]{1,0:T(8,128)S(1)} %copy-done.54, bf16[512,1024]{1,0:T(8,128)(2,1)S(1)} %bitcast.851, f32[1,512]{1,0:T(1,128)S(1)} %get-tuple-element.1680.norms, f32[1,512]{1,0:T(1,128)S(1)} %copy-done.201, s32[1,512]{1,0:T(1,128)S(1)} %copy-done.203, ...), custom_call_target="tpu_custom_call" | custom-call | flops 9334947840 | bytes 19447808 | tf_op jit(solution)/shard_map/table_grad/pallas_call | solution.py:1807
  313.6 8.9 %totals.3.numbers = f32[1,128]{1,0:T(1,128)S(1)} custom-call(f32[8,128]{1,0:T(8,128)S(1)} %get-tuple-element.1678.refs_0_, f32[1,1024]{1,0:T(1,128)S(1)} %get-tuple-element.1684.refs_1_, f32[8,128]{1,0:T(8,128)S(1)} %slice.289.refs_2_, f32[1,128]{1,0:T(1,128)S(1)} %copy-done.193), custom_call_target="tpu_custom_call" | custom-call | tf_op jit(solution)/shard_map/totals/pallas_call | solution.py:210
  322.6 0.6 fusion.254
  323.3 3.5 layer_adam.3
  326.8 43.2 %adam.3 = (f32[4748,1024]{1,0:T(8,128)}, f32[4748,1024]{1,0:T(8,128)}, f32[4748,1024]{1,0:T(8,128)}) custom-call(f32[1,128]{1,0:T(1,128)S(1)} %totals.3.numbers, f32[4748,1024]{1,0:T(8,128)} %weight.1, f32[4748,1024]{1,0:T(8,128)} %first.1, f32[4748,1024]{1,0:T(8,128)} %second.1, bf16[4748,1024]{1,0:T(8,128)(2,1)S(1)} %get-tuple-element.1685.grad), custom_call_target="tpu_custom_call" | custom-call | tf_op jit(solution)/shard_map/adam/pallas_call | solution.py:1874
  370.0 0.8 while.117
  (34 shorter events, 0.1 us)
Async XLA Ops:
  2.9 0.7 copy-start.49
  3.6 0.7 copy-start.50
  4.3 0.7 copy-start.51
  4.9 0.7 copy-start.52
  20.1 8.6 %copy-start.186 = (f32[24,128]{1,0:T(8,128)}, f32[24,128]{1,0:T(8,128)S(1)}, u32[]{:S(2)}) copy-start(f32[24,128]{1,0:T(8,128)S(1)} %get-tuple-element.3686) | copy-start | bytes 36868
  20.1 149.5 %copy-start.170 = (f32[1,1024]{1,0:T(1,128)}, f32[1,1024]{1,0:T(1,128)S(1)}, u32[]{:S(2)}) copy-start(f32[1,1024]{1,0:T(1,128)S(1)} %get-tuple-element.3681.refs_10_.refs_27_) | copy-start | bytes 12292
  20.2 149.5 %copy-start.172 = (f32[1,1024]{1,0:T(1,128)}, f32[1,1024]{1,0:T(1,128)S(1)}, u32[]{:S(2)}) copy-start(f32[1,1024]{1,0:T(1,128)S(1)} %get-tuple-element.3682.refs_11_.refs_28_) | copy-start | bytes 12292
  20.2 149.5 %copy-start.175 = (f32[16,128]{1,0:T(8,128)}, f32[16,128]{1,0:T(8,128)S(1)}, u32[]{:S(2)}) copy-start(f32[16,128]{1,0:T(8,128)S(1)} %get-tuple-element.3683.refs_2_) | copy-start | bytes 24580
  24.4 4.4 %copy-start.109 = (f32[32,6144]{1,0:T(8,128)S(1)}, f32[32,6144]{1,0:T(8,128)}, u32[]{:S(2)}) copy-start(f32[32,6144]{1,0:T(8,128)} %refs_8_.1) | copy-start | bytes 2359300
  24.4 4.4 %copy-start.115 = (f32[32,4096]{1,0:T(8,128)S(1)}, f32[32,4096]{1,0:T(8,128)}, u32[]{:S(2)}) copy-start(f32[32,4096]{1,0:T(8,128)} %refs_0_.3) | copy-start | bytes 1572868
  24.4 4.4 %copy-start.124 = (f32[96,1024]{1,0:T(8,128)S(1)}, f32[96,1024]{1,0:T(8,128)}, u32[]{:S(2)}) copy-start(f32[96,1024]{1,0:T(8,128)} %refs_12_.1) | copy-start | bytes 1179652
  24.4 4.4 %copy-start.133 = (f32[64,1024]{1,0:T(8,128)S(1)}, f32[64,1024]{1,0:T(8,128)}, u32[]{:S(2)}) copy-start(f32[64,1024]{1,0:T(8,128)} %refs_4_.3) | copy-start | bytes 786436
  149.8 19.9 %copy-start.33 = (f32[448,1024]{1,0:T(8,128)}, f32[448,1024]{1,0:T(8,128)S(1)}, u32[]{:S(2)}) copy-start(f32[448,1024]{1,0:T(8,128)S(1)} %get-tuple-element.1668.refs_13_) | copy-start | bytes 5505028
  169.7 125.0 %copy-start.201 = (f32[1,512]{1,0:T(1,128)S(1)}, f32[1,512]{1,0:T(1,128)}, u32[]{:S(2)}) copy-start(f32[1,512]{1,0:T(1,128)} %get-tuple-element.3684.weights) | copy-start | bytes 6148
  169.7 125.0 %copy-start.203 = (s32[1,512]{1,0:T(1,128)S(1)}, s32[1,512]{1,0:T(1,128)}, u32[]{:S(2)}) copy-start(s32[1,512]{1,0:T(1,128)} %get-tuple-element.3685.targets) | copy-start | bytes 6148
  294.6 3.8 %copy-start.54 = (f32[4748,512]{1,0:T(8,128)S(1)}, f32[4748,512]{1,0:T(8,128)}, u32[]{:S(2)}) copy-start(f32[4748,512]{1,0:T(8,128)} %get-tuple-element.1679.logits) | copy-start | bytes 29171716
  298.4 15.2 %copy-start.193 = (f32[1,128]{1,0:T(1,128)S(1)}, f32[1,128]{1,0:T(1,128)}, u32[]{:S(2)}) copy-start(f32[1,128]{1,0:T(1,128)} %fusion.240.refs_3_) | copy-start | bytes 1540
  298.4 24.8 %copy-start.135 = (f32[32,6144]{1,0:T(8,128)S(1)}, f32[32,6144]{1,0:T(8,128)}, u32[]{:S(2)}) copy-start(f32[32,6144]{1,0:T(8,128)} %refs_9_.1) | copy-start | bytes 2359300
  298.4 24.8 %copy-start.136 = (f32[32,6144]{1,0:T(8,128)S(1)}, f32[32,6144]{1,0:T(8,128)}, u32[]{:S(2)}) copy-start(f32[32,6144]{1,0:T(8,128)} %refs_10_.1) | copy-start | bytes 2359300
  298.4 24.8 %copy-start.145 = (f32[32,4096]{1,0:T(8,128)S(1)}, f32[32,4096]{1,0:T(8,128)}, u32[]{:S(2)}) copy-start(f32[32,4096]{1,0:T(8,128)} %refs_1_.5) | copy-start | bytes 1572868
  298.4 24.8 %copy-start.146 = (f32[32,4096]{1,0:T(8,128)S(1)}, f32[32,4096]{1,0:T(8,128)}, u32[]{:S(2)}) copy-start(f32[32,4096]{1,0:T(8,128)} %refs_2_.5) | copy-start | bytes 1572868
  298.4 24.8 %copy-start.147 = (f32[96,1024]{1,0:T(8,128)S(1)}, f32[96,1024]{1,0:T(8,128)}, u32[]{:S(2)}) copy-start(f32[96,1024]{1,0:T(8,128)} %refs_13_.1) | copy-start | bytes 1179652
  298.4 24.8 %copy-start.148 = (f32[96,1024]{1,0:T(8,128)S(1)}, f32[96,1024]{1,0:T(8,128)}, u32[]{:S(2)}) copy-start(f32[96,1024]{1,0:T(8,128)} %refs_14_.1) | copy-start | bytes 1179652
  298.5 24.8 %copy-start.152 = (f32[64,1024]{1,0:T(8,128)S(1)}, f32[64,1024]{1,0:T(8,128)}, u32[]{:S(2)}) copy-start(f32[64,1024]{1,0:T(8,128)} %refs_5_.1) | copy-start | bytes 786436
  298.5 24.8 %copy-start.153 = (f32[64,1024]{1,0:T(8,128)S(1)}, f32[64,1024]{1,0:T(8,128)}, u32[]{:S(2)}) copy-start(f32[64,1024]{1,0:T(8,128)} %refs_6_.1) | copy-start | bytes 786436
  298.5 24.8 %copy-start.187 = (f32[104]{0:T(128)S(1)}, f32[104]{0:T(128)}, u32[]{:S(2)}) copy-start(f32[104]{0:T(128)} %param.57) | copy-start | bytes 1252
  298.5 24.8 %copy-start.189 = (f32[104]{0:T(128)S(1)}, f32[104]{0:T(128)}, u32[]{:S(2)}) copy-start(f32[104]{0:T(128)} %param.58) | copy-start | bytes 1252
  298.5 24.8 %copy-start.191 = (f32[104]{0:T(128)S(1)}, f32[104]{0:T(128)}, u32[]{:S(2)}) copy-start(f32[104]{0:T(128)} %param.59) | copy-start | bytes 1252
  326.8 43.2 %copy-start.196 = (s32[4]{0:T(128)S(1)}, s32[4]{0:T(128)}, u32[]{:S(2)}) copy-start(s32[4]{0:T(128)} %param.37) | copy-start | bytes 52
